TPU v7x, 32 devices: a whole 2x2x4 slice. The times are simulated.
32 devices in a mesh: crop: 4 (over y, x), row: 8 (over z, core).
Axes of the slice: x: 2, y: 2, z: 4, core: 2. Of those that a mesh axis runs over, the one named last changes fastest.
Arguments:
- pair: bfloat16 [4, 256, 256, 128], P('crop', 'row'), may hold values from -6 to 6
- single: bfloat16 [4, 256, 384], P('crop', 'row'), may hold values from -6 to 6
- lengths: int32 [4], P('crop'), may hold values from 192 to 256, as said below
- params: float32 [3070464], P('row'), as said below
- moment_one: float32 [3070464], P('row'), as said below
- moment_two: float32 [3070464], P('row'), as said below
- pair_cotangent: bfloat16 [4, 256, 256, 128], P('crop', 'row'), may hold values from -6 to 6
- single_cotangent: bfloat16 [4, 256, 384], P('crop', 'row'), may hold values from -6 to 6
Outputs:
- pair_out: bfloat16 [4, 256, 256, 128], P('crop', 'row')
- single_out: bfloat16 [4, 256, 384], P('crop', 'row')
- pair_grad: float32 [4, 256, 256, 128], P('crop', 'row')
- single_grad: float32 [4, 256, 384], P('crop', 'row')
- new_params: float32 [3070464], P('row')
- new_first: float32 [3070464], P('row')
- new_second: float32 [3070464], P('row')
- clip_norm: float32 [], replicated
Inputs may be any that keep to these rules, and one draw needn't show every extreme that they name: `lengths`: one crop has all 256 tokens live. `params`: matrices about one over the root of their rows (outputs of attention four times that), gains 0.5 to 1.5, biases about 0.3. `moment_one`: both signs. `moment_two`: positive.
All inputs are finite; a program needn't handle non-finite values.
Results may differ from a plain program's by a relative error of at most 0.022.
Values may be sent and summed in bfloat16 or wider, within the bound.
No kernel may reach another device: no remote copies, remote signals or barrier semaphores. Data moves between devices by JAX's collectives and lax.ppermute only.
A program may use at most 768 MiB of HBM per device.

v0:
```python
import functools
import math

import jax
import jax.numpy as jnp
import numpy as np
from jax import lax
from jax.experimental import pallas as pl
from jax.experimental.pallas import tpu as pltpu
from jax.sharding import PartitionSpec as P

C = 128
H = 128
S = 384
TA_HEADS = 4
SA_HEADS = 16
STEP = 10
STRIDE = 128
LENGTH = 256

OUTGOING, INCOMING, STARTING, ENDING, PAIR, ATTEND, SINGLE = range(7)
(
    NORM_GAIN,
    NORM_BIAS,
    PROJ_GATE,
    OUT_GAIN,
    OUT_BIAS,
    PROJ_OUT,
    GATE_OUT,
    QKVG,
    BIAS_PROJ,
    OUTPUT,
    UP,
    DOWN,
    PAIR_GAIN,
    PAIR_BIAS,
    PAIR_PROJ,
    COLS,
    BIAS_W,
    BIAS_T,
    VECTORS,
    T,
) = range(7, 27)


EPSILON = 1e-05
MASKED = 1000000000.0
BETA_ONE = 0.9
BETA_TWO = 0.95
ADAM_EPS = 1e-08
CLIP = 1.0


def layout(pair_width, hidden_width, single_width, tri_heads, att_heads):
    entries = []
    for prefix in (OUTGOING, INCOMING):
        entries += [
            ((prefix, NORM_GAIN), (pair_width,)),
            ((prefix, NORM_BIAS), (pair_width,)),
            ((prefix, PROJ_GATE), (pair_width, 4 * hidden_width)),
            ((prefix, OUT_GAIN), (hidden_width,)),
            ((prefix, OUT_BIAS), (hidden_width,)),
            ((prefix, PROJ_OUT), (hidden_width, pair_width)),
            ((prefix, GATE_OUT), (pair_width, pair_width)),
        ]
    for prefix in (STARTING, ENDING):
        entries += [
            ((prefix, NORM_GAIN), (pair_width,)),
            ((prefix, NORM_BIAS), (pair_width,)),
            ((prefix, QKVG), (pair_width, 4 * pair_width)),
            ((prefix, BIAS_PROJ), (pair_width, tri_heads)),
            ((prefix, OUTPUT), (pair_width, pair_width)),
        ]
    entries += [
        ((PAIR, NORM_GAIN), (pair_width,)),
        ((PAIR, NORM_BIAS), (pair_width,)),
        ((PAIR, UP), (pair_width, 8 * pair_width)),
        ((PAIR, DOWN), (4 * pair_width, pair_width)),
        ((ATTEND, NORM_GAIN), (single_width,)),
        ((ATTEND, NORM_BIAS), (single_width,)),
        ((ATTEND, QKVG), (single_width, 4 * single_width)),
        ((ATTEND, PAIR_GAIN), (pair_width,)),
        ((ATTEND, PAIR_BIAS), (pair_width,)),
        ((ATTEND, PAIR_PROJ), (pair_width, att_heads)),
        ((ATTEND, OUTPUT), (single_width, single_width)),
        ((SINGLE, NORM_GAIN), (single_width,)),
        ((SINGLE, NORM_BIAS), (single_width,)),
        ((SINGLE, UP), (single_width, 8 * single_width)),
        ((SINGLE, DOWN), (4 * single_width, single_width)),
    ]
    return entries


def logical_order(flat):
    return flat.reshape(-1, STRIDE).T.reshape(-1)


def stored_order(vector):
    return vector.reshape(STRIDE, -1).T.reshape(-1)


def rate_tables(entries):
    rates = []
    decays = []
    for name, shape in entries:
        count = math.prod(shape)
        if len(shape) == 1:
            rates.append(np.full(count, 0.5, np.float32))
            decays.append(np.zeros(count, np.float32))
        else:
            rates.append(np.full(count, 2.0 / math.sqrt(shape[0]), np.float32))
            decays.append(np.full(count, 0.01, np.float32))
    rates = np.concatenate(rates)
    decays = np.concatenate(decays)
    return (rates.reshape(STRIDE, -1).T.reshape(-1), decays.reshape(STRIDE, -1).T.reshape(-1))


def unpack(flat, entries):
    pieces = {}
    offset = 0
    for name, shape in entries:
        count = math.prod(shape)
        pieces[name] = flat[offset : offset + count].reshape(shape)
        offset += count
    return pieces


def layer_norm(values, gain, shift):
    centred = values - jnp.mean(values, axis=-1, keepdims=True)
    spread = jnp.mean(centred * centred, axis=-1, keepdims=True)
    return centred * lax.rsqrt(spread + EPSILON) * gain + shift


def norm_backward(values, gain, shift, grad):
    _, pullback = jax.vjp(layer_norm, values, gain, shift)
    return pullback(grad)


def norm_pair(weights, prefix):
    return (
        weights[(prefix, NORM_GAIN)].astype(jnp.float32),
        weights[(prefix, NORM_BIAS)].astype(jnp.float32),
    )


def gated_pair(project, pair_mask):
    half = project.shape[-1] // 2
    return project[..., :half] * jax.nn.sigmoid(project[..., half:]) * pair_mask[..., None]


def gated_output(values, gate):
    return values * jax.nn.sigmoid(gate)


def swiglu(hidden):
    half = hidden.shape[-1] // 2
    return jax.nn.silu(hidden[..., :half]) * hidden[..., half:]


def matmul(left, right):
    return jnp.dot(left, right, preferred_element_type=jnp.float32)


def outer_sum(left, right):
    return jnp.einsum(
        "nc,nd->cd",
        left.reshape(-1, left.shape[-1]),
        right.reshape(-1, right.shape[-1]),
        preferred_element_type=jnp.float32,
    )


def flip(values):
    moved = lax.all_to_all(values, "row", split_axis=1, concat_axis=0, tiled=True)
    return jnp.swapaxes(moved, 0, 1)


def channel_forward(first, second, incoming):
    whole_first, whole_second = (
        lax.all_to_all(first, "row", split_axis=2, concat_axis=0, tiled=True),
        lax.all_to_all(second, "row", split_axis=2, concat_axis=0, tiled=True),
    )
    if incoming:
        local_tri = jnp.einsum(
            "kih,kjh->ijh", whole_first, whole_second, preferred_element_type=jnp.float32
        )
        local_tri = local_tri.astype(jnp.bfloat16).astype(jnp.float32)
    else:
        local_tri = jnp.einsum(
            "ikh,jkh->ijh", whole_first, whole_second, preferred_element_type=jnp.float32
        )
    tri = lax.all_to_all(
        local_tri.astype(jnp.bfloat16), "row", split_axis=0, concat_axis=2, tiled=True
    ).astype(local_tri.dtype)
    return (tri, whole_first, whole_second)


def channel_backward(grad_tri, whole_first, whole_second, incoming):
    whole_grad = lax.all_to_all(grad_tri, "row", split_axis=2, concat_axis=0, tiled=True)
    if incoming:
        grad_a = jnp.einsum(
            "ijh,kjh->kih", whole_grad, whole_second, preferred_element_type=jnp.float32
        )
        grad_b = jnp.einsum(
            "ijh,kih->kjh", whole_grad, whole_first, preferred_element_type=jnp.float32
        )
    else:
        grad_a = jnp.einsum(
            "ijh,jkh->ikh", whole_grad, whole_second, preferred_element_type=jnp.float32
        )
        grad_b = jnp.einsum(
            "ijh,ikh->jkh", whole_grad, whole_first, preferred_element_type=jnp.float32
        )
    return (
        lax.all_to_all(
            grad_a.astype(jnp.bfloat16), "row", split_axis=0, concat_axis=2, tiled=True
        ).astype(grad_a.dtype),
        lax.all_to_all(
            grad_b.astype(jnp.bfloat16), "row", split_axis=0, concat_axis=2, tiled=True
        ).astype(grad_b.dtype),
    )


def triangle_forward(state, pair_mask, weights, prefix, incoming):
    gain, shift = norm_pair(weights, prefix)
    lowered = layer_norm(state, gain, shift).astype(jnp.bfloat16)
    project = matmul(lowered, weights[(prefix, PROJ_GATE)])
    product = gated_pair(project, pair_mask).astype(jnp.bfloat16)
    half = product.shape[-1] // 2
    tri, own, other = channel_forward(product[..., :half], product[..., half:], incoming)
    out_gain = weights[(prefix, OUT_GAIN)].astype(jnp.float32)
    out_shift = weights[(prefix, OUT_BIAS)].astype(jnp.float32)
    out_low = layer_norm(tri, out_gain, out_shift).astype(jnp.bfloat16)
    output = matmul(out_low, weights[(prefix, PROJ_OUT)])
    gate_out = matmul(lowered, weights[(prefix, GATE_OUT)])
    update = gated_output(output, gate_out)
    return (update, (state, lowered, lowered, project, own, other, tri, out_low, output, gate_out))


def triangle_backward(saved, grad_update, pair_mask, weights, prefix, incoming, grads):
    state, lowered, framed, project, own, other, tri, out_low, output, gate_out = saved
    _, pullback = jax.vjp(gated_output, output, gate_out)
    grad_output, grad_gate = pullback(grad_update)
    grad_output = grad_output.astype(jnp.bfloat16)
    grad_gate = grad_gate.astype(jnp.bfloat16)
    grads[(prefix, PROJ_OUT)] = outer_sum(out_low, grad_output)
    grads[(prefix, GATE_OUT)] = outer_sum(lowered, grad_gate)
    grad_normed = matmul(grad_output, weights[(prefix, PROJ_OUT)].T)
    out_gain = weights[(prefix, OUT_GAIN)].astype(jnp.float32)
    out_shift = weights[(prefix, OUT_BIAS)].astype(jnp.float32)
    grad_tri, grads[(prefix, OUT_GAIN)], grads[(prefix, OUT_BIAS)] = norm_backward(
        tri, out_gain, out_shift, grad_normed
    )
    grad_tri = grad_tri.astype(jnp.bfloat16)
    grad_first, grad_second = channel_backward(grad_tri, own, other, incoming)
    _, pullback = jax.vjp(lambda values: gated_pair(values, pair_mask), project)
    (grad_project,) = pullback(jnp.concatenate([grad_first, grad_second], axis=-1))
    grad_project = grad_project.astype(jnp.bfloat16)
    grads[(prefix, PROJ_GATE)] = outer_sum(framed, grad_project)
    grad_framed = matmul(grad_project, weights[(prefix, PROJ_GATE)].T)
    if incoming:
        grad_framed = grad_framed.astype(jnp.bfloat16).astype(jnp.float32)
    grad_lowered = grad_framed + matmul(grad_gate, weights[(prefix, GATE_OUT)].T)
    gain, shift = norm_pair(weights, prefix)
    grad_state, grads[(prefix, NORM_GAIN)], grads[(prefix, NORM_BIAS)] = norm_backward(
        state, gain, shift, grad_lowered
    )
    return grad_state


def row_scores(query, key, bias, penalty, scale):
    scores = jnp.einsum("jhd,khd->hjk", query, key, preferred_element_type=jnp.float32) * scale
    return scores + bias.astype(jnp.float32) + penalty[None, None, :]


def attention_forward(state, penalty, weights, prefix, ending):
    gain, shift = norm_pair(weights, prefix)
    lowered = layer_norm(state, gain, shift).astype(jnp.bfloat16)
    framed = flip(lowered) if ending else lowered
    rows, length, width = framed.shape
    size = width // TA_HEADS
    scale = size ** (-0.5)
    qkvg = matmul(framed, weights[(prefix, QKVG)])
    queries = qkvg[..., :width].astype(jnp.bfloat16).reshape(rows, length, TA_HEADS, size)
    keys = qkvg[..., width : 2 * width].astype(jnp.bfloat16).reshape(rows, length, TA_HEADS, size)
    values = (
        qkvg[..., 2 * width : 3 * width].astype(jnp.bfloat16).reshape(rows, length, TA_HEADS, size)
    )
    gate = qkvg[..., 3 * width :]
    local_bias = (
        matmul(framed, weights[(prefix, BIAS_PROJ)]).astype(jnp.bfloat16).transpose(2, 0, 1)
    )
    bias = lax.all_gather(local_bias, "row", axis=1, tiled=True)

    def forward_row(items):
        query, key, value = items
        scores = row_scores(query, key, bias, penalty, scale)
        top = jnp.max(scores, axis=-1, keepdims=True)
        shifted = jnp.exp(scores - top)
        total = jnp.sum(shifted, axis=-1, keepdims=True)
        probs = (shifted / total).astype(jnp.bfloat16)
        mixed = jnp.einsum("hjk,khd->jhd", probs, value, preferred_element_type=jnp.float32)
        return (mixed, top[..., 0] + jnp.log(total[..., 0]))

    mixed, log_totals = lax.map(forward_row, (queries, keys, values))
    mixed = mixed.reshape(rows, length, width)
    gated_low = gated_output(mixed, gate).astype(jnp.bfloat16)
    returned = flip(gated_low) if ending else gated_low
    update = matmul(returned, weights[(prefix, OUTPUT)])
    return (update, (state, framed, queries, keys, values, gate, bias, mixed, log_totals, returned))


def attention_backward(saved, grad_update, penalty, weights, prefix, ending, grads):
    state, framed, queries, keys, values, gate, bias, mixed, log_totals, returned = saved
    rows, length, width = framed.shape
    size = width // TA_HEADS
    scale = size ** (-0.5)
    grad_low = grad_update.astype(jnp.bfloat16)
    grads[(prefix, OUTPUT)] = outer_sum(returned, grad_low)
    grad_gated = matmul(grad_low, weights[(prefix, OUTPUT)].T)
    if ending:
        grad_gated = flip(grad_gated.astype(jnp.bfloat16)).astype(jnp.float32)
    _, pullback = jax.vjp(gated_output, mixed, gate)
    grad_mixed, grad_gate = pullback(grad_gated)
    grad_mixed = grad_mixed.astype(jnp.bfloat16).reshape(rows, length, TA_HEADS, size)

    def back_row(carry, items):
        query, key, value, log_total, grad_row = items
        scores = row_scores(query, key, bias, penalty, scale)
        probs = jnp.exp(scores - log_total[..., None])
        grad_probs = jnp.einsum("jhd,khd->hjk", grad_row, value, preferred_element_type=jnp.float32)
        delta = jnp.sum(probs * grad_probs, axis=-1, keepdims=True)
        grad_scores = (probs * (grad_probs - delta)).astype(jnp.bfloat16)
        grad_query = (
            jnp.einsum("hjk,khd->jhd", grad_scores, key, preferred_element_type=jnp.float32) * scale
        )
        grad_key = (
            jnp.einsum("hjk,jhd->khd", grad_scores, query, preferred_element_type=jnp.float32)
            * scale
        )
        grad_value = jnp.einsum(
            "hjk,jhd->khd", probs.astype(jnp.bfloat16), grad_row, preferred_element_type=jnp.float32
        )
        return (carry + grad_scores.astype(jnp.float32), (grad_query, grad_key, grad_value))

    empty = jnp.zeros(bias.shape, jnp.float32)
    grad_bias, (grad_query, grad_key, grad_value) = lax.scan(
        back_row, empty, (queries, keys, values, log_totals, grad_mixed)
    )
    grad_bias = lax.psum_scatter(grad_bias, "row", scatter_dimension=1, tiled=True)
    grad_bias = grad_bias.transpose(1, 2, 0).astype(jnp.bfloat16)
    grad_qkvg = jnp.concatenate(
        [
            grad_query.reshape(rows, length, width),
            grad_key.reshape(rows, length, width),
            grad_value.reshape(rows, length, width),
            grad_gate,
        ],
        axis=-1,
    ).astype(jnp.bfloat16)
    grads[(prefix, QKVG)] = outer_sum(framed, grad_qkvg)
    grads[(prefix, BIAS_PROJ)] = outer_sum(framed, grad_bias)
    grad_framed = matmul(grad_qkvg, weights[(prefix, QKVG)].T) + matmul(
        grad_bias, weights[(prefix, BIAS_PROJ)].T
    )
    if ending:
        grad_framed = flip(grad_framed.astype(jnp.bfloat16)).astype(jnp.float32)
    gain, shift = norm_pair(weights, prefix)
    grad_state, grads[(prefix, NORM_GAIN)], grads[(prefix, NORM_BIAS)] = norm_backward(
        state, gain, shift, grad_framed
    )
    return grad_state


def transition_forward(state, weights, prefix):
    gain, shift = norm_pair(weights, prefix)
    lowered = layer_norm(state, gain, shift).astype(jnp.bfloat16)
    hidden = matmul(lowered, weights[(prefix, UP)])
    mixed_low = swiglu(hidden).astype(jnp.bfloat16)
    update = matmul(mixed_low, weights[(prefix, DOWN)])
    return (update, (state, lowered, hidden, mixed_low))


def transition_backward(saved, grad_update, weights, prefix, grads):
    state, lowered, hidden, mixed_low = saved
    grad_low = grad_update.astype(jnp.bfloat16)
    grads[(prefix, DOWN)] = outer_sum(mixed_low, grad_low)
    grad_mixed = matmul(grad_low, weights[(prefix, DOWN)].T)
    _, pullback = jax.vjp(swiglu, hidden)
    (grad_hidden,) = pullback(grad_mixed)
    grad_hidden = grad_hidden.astype(jnp.bfloat16)
    grads[(prefix, UP)] = outer_sum(lowered, grad_hidden)
    grad_lowered = matmul(grad_hidden, weights[(prefix, UP)].T)
    gain, shift = norm_pair(weights, prefix)
    grad_state, grads[(prefix, NORM_GAIN)], grads[(prefix, NORM_BIAS)] = norm_backward(
        state, gain, shift, grad_lowered
    )
    return grad_state


def single_forward(single_state, pair_state, penalty, weights):
    gain, shift = norm_pair(weights, ATTEND)
    lowered = layer_norm(single_state, gain, shift).astype(jnp.bfloat16)
    rows, width = lowered.shape
    size = width // SA_HEADS
    qkvg = matmul(lowered, weights[(ATTEND, QKVG)])
    query = qkvg[:, :width].astype(jnp.bfloat16).reshape(rows, SA_HEADS, size)
    key = qkvg[:, width : 2 * width].astype(jnp.bfloat16)
    value = qkvg[:, 2 * width : 3 * width].astype(jnp.bfloat16)
    gate = qkvg[:, 3 * width :]
    keys_all, values_all = (
        lax.all_gather(key, "row", axis=0, tiled=True),
        lax.all_gather(value, "row", axis=0, tiled=True),
    )
    keys_all = keys_all.reshape(-1, SA_HEADS, size)
    values_all = values_all.reshape(-1, SA_HEADS, size)
    pair_gain = weights[(ATTEND, PAIR_GAIN)].astype(jnp.float32)
    pair_shift = weights[(ATTEND, PAIR_BIAS)].astype(jnp.float32)
    pair_low = layer_norm(pair_state, pair_gain, pair_shift).astype(jnp.bfloat16)
    bias = matmul(pair_low, weights[(ATTEND, PAIR_PROJ)]).transpose(2, 0, 1)
    scores = jnp.einsum(
        "ihd,jhd->hij", query, keys_all, preferred_element_type=jnp.float32
    ) * size ** (-0.5)
    scores = scores + bias + penalty[None, None, :]
    probs = jax.nn.softmax(scores, axis=-1)
    probs_low = probs.astype(jnp.bfloat16)
    mixed = jnp.einsum(
        "hij,jhd->ihd", probs_low, values_all, preferred_element_type=jnp.float32
    ).reshape(rows, width)
    gated_low = gated_output(mixed, gate).astype(jnp.bfloat16)
    update = matmul(gated_low, weights[(ATTEND, OUTPUT)])
    return (
        update,
        (
            single_state,
            pair_state,
            lowered,
            query,
            keys_all,
            values_all,
            gate,
            pair_low,
            probs,
            probs_low,
            mixed,
            gated_low,
        ),
    )


def single_backward(saved, grad_update, weights, grads):
    (
        single_state,
        pair_state,
        lowered,
        query,
        keys_all,
        values_all,
        gate,
        pair_low,
        probs,
        probs_low,
        mixed,
        gated_low,
    ) = saved
    rows, width = lowered.shape
    size = width // SA_HEADS
    scale = size ** (-0.5)
    grad_low = grad_update.astype(jnp.bfloat16)
    grads[(ATTEND, OUTPUT)] = outer_sum(gated_low, grad_low)
    grad_gated = matmul(grad_low, weights[(ATTEND, OUTPUT)].T)
    _, pullback = jax.vjp(gated_output, mixed, gate)
    grad_mixed, grad_gate = pullback(grad_gated)
    grad_mixed = grad_mixed.astype(jnp.bfloat16).reshape(rows, SA_HEADS, size)
    grad_probs = jnp.einsum(
        "ihd,jhd->hij", grad_mixed, values_all, preferred_element_type=jnp.float32
    )
    delta = jnp.sum(probs * grad_probs, axis=-1, keepdims=True)
    grad_scores = (probs * (grad_probs - delta)).astype(jnp.bfloat16)
    grad_query = (
        jnp.einsum("hij,jhd->ihd", grad_scores, keys_all, preferred_element_type=jnp.float32)
        * scale
    )
    key_part = (
        jnp.einsum("hij,ihd->jhd", grad_scores, query, preferred_element_type=jnp.float32) * scale
    )
    value_part = jnp.einsum(
        "hij,ihd->jhd", probs_low, grad_mixed, preferred_element_type=jnp.float32
    )
    grad_key, grad_value = (
        lax.psum_scatter(key_part.reshape(-1, width), "row", scatter_dimension=0, tiled=True),
        lax.psum_scatter(value_part.reshape(-1, width), "row", scatter_dimension=0, tiled=True),
    )
    grad_qkvg = jnp.concatenate(
        [grad_query.reshape(rows, width), grad_key, grad_value, grad_gate], axis=-1
    ).astype(jnp.bfloat16)
    grads[(ATTEND, QKVG)] = outer_sum(lowered, grad_qkvg)
    grad_lowered = matmul(grad_qkvg, weights[(ATTEND, QKVG)].T)
    gain, shift = norm_pair(weights, ATTEND)
    grad_single, grads[(ATTEND, NORM_GAIN)], grads[(ATTEND, NORM_BIAS)] = norm_backward(
        single_state, gain, shift, grad_lowered
    )
    grad_bias = grad_scores.transpose(1, 2, 0)
    grads[(ATTEND, PAIR_PROJ)] = outer_sum(pair_low, grad_bias)
    grad_pair_low = matmul(grad_bias, weights[(ATTEND, PAIR_PROJ)].T)
    pair_gain = weights[(ATTEND, PAIR_GAIN)].astype(jnp.float32)
    pair_shift = weights[(ATTEND, PAIR_BIAS)].astype(jnp.float32)
    grad_pair, grads[(ATTEND, PAIR_GAIN)], grads[(ATTEND, PAIR_BIAS)] = norm_backward(
        pair_state, pair_gain, pair_shift, grad_pair_low
    )
    return (grad_single, grad_pair)


def shards(pair, single, lengths, params, moment_one, moment_two, pair_cotangent, single_cotangent):
    entries = layout(C, H, S, TA_HEADS, SA_HEADS)
    full = lax.all_gather(params.astype(jnp.bfloat16), "row", axis=0, tiled=True)
    weights = unpack(logical_order(full), entries)
    rows = pair.shape[1]
    length = pair.shape[2]
    first_row = lax.axis_index("row") * rows
    mask = (jnp.arange(length, dtype=jnp.int32) < lengths[0]).astype(jnp.float32)
    mask_rows = lax.dynamic_slice_in_dim(mask, first_row, rows)
    pair_mask = mask_rows[:, None] * mask[None, :]
    penalty = (mask - 1.0) * MASKED
    state = pair[0].astype(jnp.float32)
    saved = {}
    for prefix, incoming in ((OUTGOING, False), (INCOMING, True)):
        update, saved[prefix] = triangle_forward(state, pair_mask, weights, prefix, incoming)
        state = state + update
    for prefix, ending in ((STARTING, False), (ENDING, True)):
        update, saved[prefix] = attention_forward(state, penalty, weights, prefix, ending)
        state = state + update
    update, saved[PAIR] = transition_forward(state, weights, PAIR)
    pair_final = state + update
    single_state = single[0].astype(jnp.float32)
    update, saved[ATTEND] = single_forward(single_state, pair_final, penalty, weights)
    single_mid = single_state + update
    update, saved[SINGLE] = transition_forward(single_mid, weights, SINGLE)
    single_final = single_mid + update
    grads = {}
    grad_single = single_cotangent[0].astype(jnp.float32)
    grad_single = grad_single + transition_backward(
        saved[SINGLE], grad_single, weights, SINGLE, grads
    )
    from_single, from_pair = single_backward(saved[ATTEND], grad_single, weights, grads)
    grad_single = grad_single + from_single
    grad_pair = pair_cotangent[0].astype(jnp.float32) + from_pair
    grad_pair = grad_pair + transition_backward(saved[PAIR], grad_pair, weights, PAIR, grads)
    for prefix, ending in ((ENDING, True), (STARTING, False)):
        grad_pair = grad_pair + attention_backward(
            saved[prefix], grad_pair, penalty, weights, prefix, ending, grads
        )
    for prefix, incoming in ((INCOMING, True), (OUTGOING, False)):
        grad_pair = grad_pair + triangle_backward(
            saved[prefix], grad_pair, pair_mask, weights, prefix, incoming, grads
        )
    flat = stored_order(jnp.concatenate([grads[name].reshape(-1) for name, shape in entries]))
    shard_size = params.shape[0]
    row_index = lax.axis_index("row")
    total = lax.psum(flat, ("crop", "row"))
    shard = lax.dynamic_slice_in_dim(total, row_index * shard_size, shard_size)
    norm_squared = jnp.sum(total * total)
    clip_norm = jnp.sqrt(norm_squared)
    clipped = shard * (CLIP / jnp.maximum(clip_norm, CLIP))
    new_first = BETA_ONE * moment_one + (1.0 - BETA_ONE) * clipped
    new_second = BETA_TWO * moment_two + (1.0 - BETA_TWO) * clipped * clipped
    rates, decays = rate_tables(entries)
    rate_shard = lax.dynamic_slice_in_dim(jnp.asarray(rates), row_index * shard_size, shard_size)
    decay_shard = lax.dynamic_slice_in_dim(jnp.asarray(decays), row_index * shard_size, shard_size)
    first_hat = new_first / (1.0 - BETA_ONE**STEP)
    second_hat = new_second / (1.0 - BETA_TWO**STEP)
    new_params = params - rate_shard * (
        first_hat / (jnp.sqrt(second_hat) + ADAM_EPS) + decay_shard * params
    )
    return (
        pair_final.astype(jnp.bfloat16)[None],
        single_final.astype(jnp.bfloat16)[None],
        grad_pair[None],
        grad_single[None],
        new_params,
        new_first,
        new_second,
        clip_norm,
    )


F32 = jnp.float32
BF16 = jnp.bfloat16
LOG2E = 1.4426950408889634
VMEM_LIMIT = 56 * 1024 * 1024


def mm(left, right):
    return lax.dot_general(left, right, (((1,), (0,)), ((), ())), preferred_element_type=F32)


def mm_nt(left, right):
    return lax.dot_general(left, right, (((1,), (1,)), ((), ())), preferred_element_type=F32)


def mm_tn(left, right):
    return lax.dot_general(left, right, (((0,), (0,)), ((), ())), preferred_element_type=F32)


def standardize(values):
    centred = values - jnp.mean(values, axis=0, keepdims=True)
    spread = jnp.mean(centred * centred, axis=0, keepdims=True)
    inverse = lax.rsqrt(spread + EPSILON)
    return centred * inverse, inverse


def standardize_back(unit, inverse, grad_unit):
    first = jnp.mean(grad_unit, axis=0, keepdims=True)
    second = jnp.mean(grad_unit * unit, axis=0, keepdims=True)
    return inverse * (grad_unit - first - unit * second)


def sigmoid(values):
    return 0.5 * jnp.tanh(0.5 * values) + 0.5


def column(ref, index):
    return ref[:, index : index + 1]


def live_pair(info, alive, row):
    return jnp.where(info[row] > 0, alive[0:1], 0.0)


def each_row(count, body):
    def step(index, carry):
        body(index)
        return carry

    lax.fori_loop(0, count, step, 0)


def spec_full(shape):
    return pl.BlockSpec(shape, lambda step: (0,) * len(shape))


def spec_rows(shape, block, axis):
    sizes = tuple(block if place == axis else size for place, size in enumerate(shape))
    return pl.BlockSpec(
        sizes, lambda step: tuple(step if place == axis else 0 for place in range(len(shape)))
    )


def run_rows(kernel, name, steps, ins, outs, scratch):
    in_specs = []
    for array, axis in ins:
        if axis == "smem":
            in_specs.append(pl.BlockSpec(memory_space=pltpu.SMEM))
        elif axis is None:
            in_specs.append(spec_full(array.shape))
        else:
            in_specs.append(spec_rows(array.shape, array.shape[axis] // steps, axis))
    out_specs = []
    for shape, dtype, axis in outs:
        if axis is None:
            out_specs.append(spec_full(shape))
        else:
            out_specs.append(spec_rows(shape, shape[axis] // steps, axis))
    return pl.pallas_call(
        kernel,
        grid=(steps,),
        in_specs=in_specs,
        out_specs=out_specs,
        out_shape=[jax.ShapeDtypeStruct(shape, dtype) for shape, dtype, axis in outs],
        scratch_shapes=[pltpu.VMEM(shape, dtype) for shape, dtype in scratch],
        compiler_params=pltpu.CompilerParams(vmem_limit_bytes=VMEM_LIMIT),
        name=name,
    )(*[array for array, axis in ins])


def zero_first(*refs):
    @pl.when(pl.program_id(0) == 0)
    def _():
        for ref in refs:
            ref[...] = jnp.zeros(ref.shape, ref.dtype)


def lane_sums(ref):
    return jnp.sum(ref[...].T, axis=0, keepdims=True)


def on_last(steps, body):
    @pl.when(pl.program_id(0) == steps - 1)
    def _():
        body()


def read_plain(ref, row):
    return ref[row].astype(F32)


def reorder(values, order):
    size = values.shape[0] // len(order)
    return jnp.concatenate([values[place * size : (place + 1) * size] for place in order], axis=0)


def read_tokens(order, ref, row):
    return reorder(ref[row].astype(F32), order).T


def read_flipped(ref, row):
    parts = ref[:, row]
    return parts.reshape(-1, parts.shape[-1]).astype(F32).T


def read_turned(order, ref, row):
    parts = ref[:, row]
    return reorder(parts.reshape(-1, parts.shape[-1]).astype(F32), order).T


def tri_pre_row(info, alive, row, state, cols, first, proj_t):
    unit, inverse = standardize(state)
    lowered = (unit * column(cols, first) + column(cols, first + 1)).astype(BF16)
    project = mm(proj_t[...], lowered)
    half = project.shape[0] // 2
    return project[:half] * sigmoid(project[half:]) * live_pair(info, alive, row)


def store_product(out, scratch, devices):
    hidden = scratch.shape[0] // 2
    part = hidden // devices

    def one(device, carry):
        out[device, 0] = scratch[pl.ds(device * part, part)].astype(BF16)
        out[device, 1] = scratch[pl.ds(hidden + device * part, part)].astype(BF16)
        return carry

    lax.fori_loop(0, devices, one, 0)


def copy_blocks(target, source, count):
    def one(index, carry):
        target[index] = source[index].astype(target.dtype)
        return carry

    lax.fori_loop(0, count, one, 0)


def store_flipped(out, scratch):
    devices, part = out.shape[0], out.shape[1]

    def one(device, carry):
        out[device] = scratch[pl.ds(device * part, part)].astype(out.dtype)
        return carry

    lax.fori_loop(0, devices, one, 0)


def tri_post_row(state, tri, cols, proj_t, gate_t):
    unit, inverse = standardize(state)
    lowered = (unit * column(cols, 0) + column(cols, 1)).astype(BF16)
    tri_unit, tri_inverse = standardize(tri)
    out_low = (tri_unit * column(cols, 2) + column(cols, 3)).astype(BF16)
    output = mm(proj_t[...], out_low)
    gate = sigmoid(mm(gate_t[...], lowered))
    return unit, inverse, lowered, tri_unit, tri_inverse, out_low, output, gate


def row_base(rows):
    return pl.program_id(0) * rows


def tri_pre_first_kernel(devices, read, info, alive, pair, cols, proj_t, out, scratch):
    rows = pair.shape[0]

    def body(row):
        scratch[:, row, :] = tri_pre_row(
            info, alive, row_base(rows) + row, read(pair, row), cols, 0, proj_t
        )

    each_row(rows, body)
    store_product(out, scratch, devices)


def tri_product_kernel(incoming, operands, out):
    def body(channel):
        length = operands.shape[-1]
        first = operands[:, 0, channel].reshape(length, length)
        second = operands[:, 1, channel].reshape(length, length)
        tri = mm_tn(first, second) if incoming else mm_nt(first, second)
        out[:, channel] = tri.astype(BF16).reshape(out.shape[0], out.shape[2], length)

    each_row(operands.shape[2], body)


def tri_join_kernel(
    devices, read, info, alive, source, tri_in, cols, proj_t, gate_t, next_cols, next_proj_t,
    state_out, out, tri_scratch, scratch,
):
    rows = state_out.shape[0]
    copy_blocks(tri_scratch, tri_in, tri_in.shape[0])

    def body(row):
        state = read(source, row)
        pieces = tri_post_row(state, tri_scratch[:, row, :], cols, proj_t, gate_t)
        state = state + pieces[6] * pieces[7]
        state_out[row] = state
        scratch[:, row, :] = tri_pre_row(
            info, alive, row_base(rows) + row, state, next_cols, 0, next_proj_t
        )

    each_row(rows, body)
    store_product(out, scratch, devices)


def tri_last_kernel(
    source, tri_in, cols, proj_t, gate_t, next_cols, bias_t, state_out, bias_out, tri_scratch, scratch
):
    rows = state_out.shape[0]
    copy_blocks(tri_scratch, tri_in, tri_in.shape[0])

    def body(row):
        state = source[row]
        pieces = tri_post_row(state, tri_scratch[:, row, :], cols, proj_t, gate_t)
        state = state + pieces[6] * pieces[7]
        state_out[row] = state
        unit, inverse = standardize(state)
        lowered = (unit * column(next_cols, 0) + column(next_cols, 1)).astype(BF16)
        scratch[:, row, :] = mm(bias_t[...], lowered)

    each_row(rows, body)
    bias_out[...] = scratch[: bias_out.shape[0]].astype(BF16)


def flipped_bias_kernel(source, cols, bias_t, bias_out, scratch):
    rows = source.shape[1]

    def body(row):
        unit, inverse = standardize(read_flipped(source, row))
        lowered = (unit * column(cols, 0) + column(cols, 1)).astype(BF16)
        scratch[:, row, :] = mm(bias_t[...], lowered)

    each_row(rows, body)
    bias_out[...] = scratch[: bias_out.shape[0]].astype(BF16)


def fill_bias(alive, bias_in, table):
    @pl.when(pl.program_id(0) == 0)
    def _():
        length = table.shape[1]
        penalty = (alive[0:1] - 1.0) * (MASKED * LOG2E)
        for head in range(table.shape[0]):
            values = bias_in[:, head].reshape(length, length).astype(F32)
            table[head] = (values * LOG2E + penalty).T


def attention_row(state, cols, proj_t):
    unit, inverse = standardize(state)
    lowered = (unit * column(cols, 0) + column(cols, 1)).astype(BF16)
    project = mm(proj_t[...], lowered)
    width = project.shape[0] // 4
    size = width // TA_HEADS
    query = (project[:width] * (size**-0.5 * LOG2E)).astype(BF16)
    key = project[width : 2 * width].astype(BF16)
    value = project[2 * width : 3 * width].astype(BF16)
    gate = sigmoid(project[3 * width :])
    return unit, inverse, lowered, query, key, value, gate


def attend_rows(state, cols, proj_t, output_t, table, save_total, save_mixed):
    unit, inverse, lowered, query, key, value, gate = attention_row(state, cols, proj_t)
    size = query.shape[0] // TA_HEADS
    mixed = []
    totals = []
    for head in range(TA_HEADS):
        part = slice(head * size, (head + 1) * size)
        scores = mm_tn(key[part], query[part]) + table[head]
        top = jnp.max(scores, axis=0, keepdims=True)
        shifted = jnp.exp2(scores - top)
        total = jnp.sum(shifted, axis=0, keepdims=True)
        mixed.append(mm(value[part], shifted.astype(BF16)) / total)
        totals.append(top + jnp.log2(total))
    mixed = jnp.concatenate(mixed, axis=0)
    save_total(jnp.concatenate(totals, axis=0))
    save_mixed(mixed.astype(BF16))
    return state + mm(output_t[...], (mixed * gate).astype(BF16))


def starting_kernel(
    alive, source, bias_in, cols, proj_t, output_t, out, totals, mixed, table, scratch
):
    fill_bias(alive, bias_in, table)
    rows = source.shape[0]

    def body(row):
        def save_total(values):
            totals[row] = values

        def save_mixed(values):
            mixed[row] = values

        state = attend_rows(source[row], cols, proj_t, output_t, table, save_total, save_mixed)
        scratch[:, row, :] = state.T

    each_row(rows, body)
    store_flipped(out, scratch)


def ending_kernel(alive, source, bias_in, cols, proj_t, output_t, out, totals, mixed, table):
    fill_bias(alive, bias_in, table)
    rows = source.shape[1]

    def body(row):
        def save_total(values):
            totals[row] = values

        def save_mixed(values):
            mixed[row] = values

        out[row] = attend_rows(
            read_flipped(source, row), cols, proj_t, output_t, table, save_total, save_mixed
        )

    each_row(rows, body)


def transition_kernel(
    order, source, cols, up_t, down_t, next_cols, bias_t, state_out, pair_out, bias_out, scratch, bias_scratch
):
    rows = source.shape[0]

    def body(row):
        state = source[row]
        unit, inverse = standardize(state)
        lowered = (unit * column(cols, 0) + column(cols, 1)).astype(BF16)
        hidden = mm(up_t[...], lowered)
        half = hidden.shape[0] // 2
        first = hidden[:half]
        mixed = (first * sigmoid(first) * hidden[half:]).astype(BF16)
        state = state + mm(down_t[...], mixed)
        state_out[row] = state
        scratch[:, row, :] = state.T
        unit, inverse = standardize(state)
        lowered = (unit * column(next_cols, 0) + column(next_cols, 1)).astype(BF16)
        bias_scratch[:, row, :] = mm(bias_t[...], lowered)

    each_row(rows, body)
    size = pair_out.shape[0] // len(order)
    for place, held in enumerate(order):
        pair_out[place * size : (place + 1) * size] = scratch[held * size : (held + 1) * size].astype(BF16)
    bias_out[...] = bias_scratch[...].astype(BF16)


def transition_back_kernel(
    steps, read, mid, final, cotangent, bias_grad, cols, up_t, up, down, next_cols, bias_w,
    grad_out, up_grad, down_grad, bias_w_grad, vecs, norm_gain, norm_bias, pair_gain, pair_bias, bias_scratch,
):
    zero_first(up_grad, down_grad, bias_w_grad, norm_gain, norm_bias, pair_gain, pair_bias)
    rows = mid.shape[0]
    bias_scratch[...] = bias_grad[...].astype(F32)

    def body(row):
        grad = read(cotangent, row)
        unit, inverse = standardize(final[row])
        gain = column(next_cols, 0)
        lowered = (unit * gain + column(next_cols, 1)).astype(BF16)
        grad_bias = bias_scratch[:, row, :].astype(BF16)
        bias_w_grad[...] += mm_nt(lowered, grad_bias)
        grad_lowered = mm(bias_w[...], grad_bias)
        pair_gain[...] += grad_lowered * unit
        pair_bias[...] += grad_lowered
        grad = grad + standardize_back(unit, inverse, grad_lowered * gain)
        unit, inverse = standardize(mid[row])
        gain = column(cols, 0)
        lowered = (unit * gain + column(cols, 1)).astype(BF16)
        hidden = mm(up_t[...], lowered)
        half = hidden.shape[0] // 2
        first, second = hidden[:half], hidden[half:]
        slope = sigmoid(first)
        silu = first * slope
        grad_low = grad.astype(BF16)
        grad_mixed = mm(down[...], grad_low)
        down_grad[...] += mm_nt((silu * second).astype(BF16), grad_low)
        grad_hidden = jnp.concatenate(
            [
                (grad_mixed * second * (slope + silu * (1.0 - slope))).astype(BF16),
                (grad_mixed * silu).astype(BF16),
            ],
            axis=0,
        )
        up_grad[...] += mm_nt(lowered, grad_hidden)
        grad_lowered = mm(up[...], grad_hidden)
        norm_gain[...] += grad_lowered * unit
        norm_bias[...] += grad_lowered
        grad_out[row] = grad + standardize_back(unit, inverse, grad_lowered * gain)

    each_row(rows, body)

    def finish():
        vecs[0:1] = lane_sums(norm_gain)
        vecs[1:2] = lane_sums(norm_bias)
        vecs[2:3] = lane_sums(pair_gain)
        vecs[3:4] = lane_sums(pair_bias)

    on_last(steps, finish)


def attention_back_kernel(
    steps, read, read_grad, alive, source, grad_in, bias_in, totals, mixed_in, cols, proj_t, proj, output,
    grad_out, bias_out, proj_grad, output_grad, table, grad_table,
):
    fill_bias(alive, bias_in, table)
    zero_first(proj_grad, output_grad, grad_table)
    rows = grad_out.shape[0]

    def body(row):
        unit, inverse, lowered, query, key, value, gate = attention_row(
            read(source, row), cols, proj_t
        )
        mixed = mixed_in[row].astype(F32)
        total = totals[row]
        grad_low = read_grad(grad_in, row).astype(BF16)
        gated = mixed * gate
        output_grad[...] += mm_nt(gated.astype(BF16), grad_low)
        grad_gated = mm(output[...], grad_low)
        grad_gate = grad_gated * gated * (1.0 - gate)
        grad_mixed = grad_gated * gate
        grad_mixed_low = grad_mixed.astype(BF16)
        product = grad_mixed_low.astype(F32) * mixed
        size = query.shape[0] // TA_HEADS
        grad_query, grad_key, grad_value = [], [], []
        for head in range(TA_HEADS):
            part = slice(head * size, (head + 1) * size)
            scores = mm_tn(key[part], query[part]) + table[head]
            probs = jnp.exp2(scores - total[head : head + 1])
            grad_probs = mm_tn(value[part], grad_mixed_low[part])
            delta = jnp.sum(product[part], axis=0, keepdims=True)
            grad_scores = probs * (grad_probs - delta)
            grad_table[head] += grad_scores
            grad_scores = grad_scores.astype(BF16)
            grad_query.append(mm(key[part], grad_scores) * size**-0.5)
            grad_key.append(mm_nt(query[part], grad_scores) * (1.0 / LOG2E))
            grad_value.append(mm_nt(grad_mixed_low[part], probs.astype(BF16)))
        grad_project = jnp.concatenate(
            grad_query + grad_key + grad_value + [grad_gate], axis=0
        ).astype(BF16)
        proj_grad[...] += mm_nt(lowered, grad_project)
        grad_out[row] = mm(proj[...], grad_project).astype(grad_out.dtype)

    each_row(rows, body)

    def finish():
        for head in range(TA_HEADS):
            bias_out[:, head] = (
                grad_table[head].T.astype(BF16).reshape(bias_out.shape[0], bias_out.shape[2], -1)
            )

    on_last(steps, finish)


def attention_end_row(
    state, grad, grad_lowered, grad_bias, cols, bias_w, bias_w_grad, norm_gain, norm_bias
):
    unit, inverse = standardize(state)
    gain = column(cols, 0)
    lowered = (unit * gain + column(cols, 1)).astype(BF16)
    bias_w_grad[...] += mm_nt(lowered, grad_bias)
    grad_lowered = grad_lowered + mm(bias_w[...], grad_bias)
    norm_gain[...] += grad_lowered * unit
    norm_bias[...] += grad_lowered
    return grad + standardize_back(unit, inverse, grad_lowered * gain)


def fill_bias_grad(scratch, bias_grad):
    heads = bias_grad.shape[1]
    total = bias_grad[0].astype(F32)
    for device in range(1, bias_grad.shape[0]):
        total = total + bias_grad[device].astype(F32)
    scratch[:heads] = total
    scratch[heads:] = jnp.zeros((scratch.shape[0] - heads,) + scratch.shape[1:], F32)


def ending_end_kernel(
    steps, source, grad_in, grad_lowered, bias_grad, cols, bias_w,
    grad_out, bias_w_grad, vecs, norm_gain, norm_bias, bias_scratch, scratch,
):
    zero_first(bias_w_grad, norm_gain, norm_bias)
    fill_bias_grad(bias_scratch, bias_grad)
    rows = grad_in.shape[0]

    def body(row):
        grad = attention_end_row(
            read_flipped(source, row), grad_in[row], grad_lowered[row].astype(F32),
            bias_scratch[:, row, :].astype(BF16), cols, bias_w, bias_w_grad, norm_gain, norm_bias,
        )
        scratch[:, row, :] = grad.T

    each_row(rows, body)
    store_flipped(grad_out, scratch)

    def finish():
        vecs[0:1] = lane_sums(norm_gain)
        vecs[1:2] = lane_sums(norm_bias)

    on_last(steps, finish)


def tri_post_back_row(
    state, tri, grad, cols, proj_t, gate_t, proj, gate_w, proj_grad, gate_grad, out_gain, out_bias
):
    unit, inverse, lowered, tri_unit, tri_inverse, out_low, output, gate = tri_post_row(
        state, tri, cols, proj_t, gate_t
    )
    grad_output = grad * gate
    grad_gate = (grad_output * output * (1.0 - gate)).astype(BF16)
    grad_output = grad_output.astype(BF16)
    proj_grad[...] += mm_nt(out_low, grad_output)
    gate_grad[...] += mm_nt(lowered, grad_gate)
    grad_normed = mm(proj[...], grad_output)
    out_gain[...] += grad_normed * tri_unit
    out_bias[...] += grad_normed
    grad_tri = standardize_back(tri_unit, tri_inverse, grad_normed * column(cols, 2))
    return grad_tri, mm(gate_w[...], grad_gate)


def starting_end_kernel(
    steps, source, grad_in, grad_lowered, bias_grad, cols, bias_w,
    below, tri_in, tri_cols, proj_t, gate_t, proj, gate_w,
    grad_out, tri_out, gate_back, bias_w_grad, proj_grad, gate_grad, vecs,
    norm_gain, norm_bias, out_gain, out_bias, bias_scratch, tri_scratch,
):
    zero_first(bias_w_grad, proj_grad, gate_grad, norm_gain, norm_bias, out_gain, out_bias)
    fill_bias_grad(bias_scratch, bias_grad)
    copy_blocks(tri_scratch, tri_in, tri_in.shape[0])
    rows = source.shape[0]

    def body(row):
        grad = attention_end_row(
            source[row], read_flipped(grad_in, row), grad_lowered[row].astype(F32),
            bias_scratch[:, row, :].astype(BF16), cols, bias_w, bias_w_grad, norm_gain, norm_bias,
        )
        grad_out[row] = grad
        grad_tri, back = tri_post_back_row(
            below[row], tri_scratch[:, row, :], grad, tri_cols, proj_t, gate_t, proj, gate_w,
            proj_grad, gate_grad, out_gain, out_bias,
        )
        gate_back[row] = back.astype(gate_back.dtype)
        tri_scratch[:, row, :] = grad_tri

    each_row(rows, body)
    copy_blocks(tri_out, tri_scratch, tri_out.shape[0])

    def finish():
        vecs[0:1] = lane_sums(norm_gain)
        vecs[1:2] = lane_sums(norm_bias)
        vecs[2:3] = lane_sums(out_gain)
        vecs[3:4] = lane_sums(out_bias)

    on_last(steps, finish)


def tri_product_back_kernel(incoming, grad, operands, out):
    def body(channel):
        length = operands.shape[-1]
        first = operands[:, 0, channel].reshape(length, length)
        second = operands[:, 1, channel].reshape(length, length)
        tri = grad[:, channel].reshape(length, length)
        if incoming:
            grad_first = mm_nt(second, tri)
            grad_second = mm(first, tri)
        else:
            grad_first = mm(tri, second)
            grad_second = mm_tn(tri, first)
        shape = (out.shape[0], out.shape[3], length)
        out[:, 0, channel] = grad_first.astype(BF16).reshape(shape)
        out[:, 1, channel] = grad_second.astype(BF16).reshape(shape)

    each_row(operands.shape[2], body)


def tri_pre_back_row(
    info, alive, row, state, product_grad, gate_back, grad, cols, proj_t, proj, proj_grad, norm_gain, norm_bias
):
    unit, inverse = standardize(state)
    gain = column(cols, 0)
    lowered = (unit * gain + column(cols, 1)).astype(BF16)
    project = mm(proj_t[...], lowered)
    half = project.shape[0] // 2
    gate = sigmoid(project[half:])
    grad_first = product_grad * gate * live_pair(info, alive, row)
    grad_second = grad_first * project[:half] * (1.0 - gate)
    grad_project = jnp.concatenate([grad_first.astype(BF16), grad_second.astype(BF16)], axis=0)
    proj_grad[...] += mm_nt(lowered, grad_project)
    grad_lowered = mm(proj[...], grad_project) + gate_back
    norm_gain[...] += grad_lowered * unit
    norm_bias[...] += grad_lowered
    return grad + standardize_back(unit, inverse, grad_lowered * gain)


def fill_product_grad(scratch, product_grad):
    devices, part = product_grad.shape[0], product_grad.shape[2]

    def one(device, carry):
        scratch[pl.ds(device * part, part)] = product_grad[device, 0].astype(F32)
        scratch[pl.ds((devices + device) * part, part)] = product_grad[device, 1].astype(F32)
        return carry

    lax.fori_loop(0, devices, one, 0)


def tri_join_back_kernel(
    steps, read, info, alive, source, product_grad, gate_in, grad_in, cols, proj_t, proj,
    below, tri_in, tri_cols, out_t, gate_t, out_w, gate_w,
    grad_out, tri_out, gate_back, proj_grad, out_grad, gate_grad, vecs,
    norm_gain, norm_bias, out_gain, out_bias, scratch, tri_scratch,
):
    zero_first(proj_grad, out_grad, gate_grad, norm_gain, norm_bias, out_gain, out_bias)
    fill_product_grad(scratch, product_grad)
    copy_blocks(tri_scratch, tri_in, tri_in.shape[0])
    rows = source.shape[0]

    def body(row):
        grad = tri_pre_back_row(
            info, alive, row_base(rows) + row, source[row], scratch[:, row, :], gate_in[row].astype(F32),
            grad_in[row], cols, proj_t, proj, proj_grad, norm_gain, norm_bias,
        )
        grad_out[row] = grad
        grad_tri, back = tri_post_back_row(
            read(below, row), tri_scratch[:, row, :], grad, tri_cols, out_t, gate_t, out_w, gate_w,
            out_grad, gate_grad, out_gain, out_bias,
        )
        gate_back[row] = back.astype(gate_back.dtype)
        tri_scratch[:, row, :] = grad_tri

    each_row(rows, body)
    copy_blocks(tri_out, tri_scratch, tri_out.shape[0])

    def finish():
        vecs[0:1] = lane_sums(norm_gain)
        vecs[1:2] = lane_sums(norm_bias)
        vecs[2:3] = lane_sums(out_gain)
        vecs[3:4] = lane_sums(out_bias)

    on_last(steps, finish)


def tri_first_back_kernel(
    steps, read, order, info, alive, source, product_grad, gate_in, grad_in, cols, proj_t, proj,
    grad_out, proj_grad, vecs, norm_gain, norm_bias, scratch,
):
    zero_first(proj_grad, norm_gain, norm_bias)
    fill_product_grad(scratch, product_grad)
    rows = source.shape[0]

    def body(row):
        grad = tri_pre_back_row(
            info, alive, row_base(rows) + row, read(source, row), scratch[:, row, :],
            gate_in[row].astype(F32), grad_in[row], cols, proj_t, proj, proj_grad, norm_gain, norm_bias,
        )
        grad_out[row] = reorder(grad.T, order).astype(grad_out.dtype)

    each_row(rows, body)

    def finish():
        vecs[0:1] = lane_sums(norm_gain)
        vecs[1:2] = lane_sums(norm_bias)

    on_last(steps, finish)


RUN = 24


def table_of(entries):
    table = {}
    offset = 0
    for name, shape in entries:
        table[name] = (offset // STRIDE, shape)
        offset += math.prod(shape)
    return table, offset


def runs_kernel(info, shard, out, scratch):
    def one(block, carry):
        scratch[:, block, :] = shard[pl.ds(block * STRIDE, STRIDE), :].T
        return carry

    lax.fori_loop(0, RUN, one, 0)
    half = STRIDE // 2
    turn = info[0] * half

    def move(lane, carry):
        out[lane] = scratch[lax.rem(lane + turn, STRIDE)].astype(BF16)
        return carry

    lax.fori_loop(0, STRIDE, move, 0)


def run_place(shards, total, lane, shard):
    count = total // STRIDE
    whole = total // shards
    step, odd = whole // STRIDE, (whole % STRIDE) // (STRIDE // 2)
    extra = lax.div(shard * odd + jnp.where(lane < STRIDE // 2, 1, 0), 2)
    start = lane * count + shard * step + extra
    return lax.div(start, STRIDE), lax.rem(start, STRIDE)


def rows_from_runs(runs, rows, first_lane, total):
    shards, lanes = runs.shape[0], runs.shape[1]
    base = first_lane * (total // STRIDE) // STRIDE

    def one(index, carry):
        lane, shard = lax.div(index, shards), lax.rem(index, shards)
        row, shift = run_place(shards, total, first_lane + lane, shard)
        row = row - base
        turned = pltpu.roll(runs[shard, lane].astype(F32), shift, 1)
        place = lax.broadcasted_iota(jnp.int32, (RUN + 1, STRIDE), 1)
        last, before = carry
        joint = jnp.where(row - before == RUN, last[2:3], last[1:2])
        below = jnp.concatenate([joint, turned], axis=0)
        above = jnp.concatenate([turned, turned[RUN - 1 :]], axis=0)
        values = jnp.where(place < shift, below, above)
        rows[pl.ds(row, RUN + 1), :] = values
        return values[RUN - 2 :], row

    lax.fori_loop(0, shards * lanes, one, (jnp.zeros((3, STRIDE), F32), -RUN), unroll=4)


def runs_from_rows(rows, out, first_lane, base, total):
    shards, lanes = out.shape[0], out.shape[1]

    def one(index, carry):
        lane, shard = lax.div(index, shards), lax.rem(index, shards)
        row, shift = run_place(shards, total, first_lane + lane, shard)
        turned = pltpu.roll(rows[pl.ds(row - base, RUN + 1), :], (STRIDE - shift) % STRIDE, 1)
        place = lax.broadcasted_iota(jnp.int32, (RUN, STRIDE), 1)
        out[shard, lane] = jnp.where(
            place < STRIDE - shift, turned[:RUN], turned[1:]
        ).astype(BF16)
        return carry

    lax.fori_loop(0, shards * lanes, one, 0, unroll=4)


def row_height(base, first_lane, last_lane, total):
    end = (last_lane * (total // STRIDE)) // STRIDE + RUN + 2
    return -(-(end - base) // 8) * 8


def take_matrix(rows, first, shape):
    blocks = shape[1] // STRIDE
    return [
        rows[pl.ds(first + block, shape[0], stride=blocks), :]
        if blocks > 1
        else rows[first : first + shape[0], :]
        for block in range(blocks)
    ]


def put_matrix(rows, first, matrix):
    height, width = matrix.shape
    blocks = width // STRIDE
    for block in range(blocks):
        part = matrix[:, block * STRIDE : (block + 1) * STRIDE]
        if blocks > 1:
            rows[pl.ds(first + block, height, stride=blocks), :] = part
        else:
            rows[first : first + height, :] = part


def spread(index, heads, rows):
    lane = lax.broadcasted_iota(jnp.int32, (STRIDE, STRIDE), 0)
    channel = lax.broadcasted_iota(jnp.int32, (STRIDE, STRIDE), 1)
    return (channel == index * (STRIDE // heads) + lane // heads).astype(BF16)


def take_narrow(rows, first, heads, high):
    total = jnp.zeros((high, STRIDE), F32)
    head = lax.broadcasted_iota(jnp.int32, (high, STRIDE), 0)
    lane = lax.broadcasted_iota(jnp.int32, (high, STRIDE), 1)
    for index in range(heads):
        line = rows[first + index : first + index + 1, :]
        picked = jnp.where(lane % heads == head, line, 0.0).astype(BF16)
        total = total + mm(picked, spread(index, heads, rows))
    return total


def put_narrow(rows, first, heads, matrix):
    turned = matrix.T.astype(BF16)
    high = turned.shape[0]
    head = lax.broadcasted_iota(jnp.int32, (high, STRIDE), 0)
    lane = lax.broadcasted_iota(jnp.int32, (high, STRIDE), 1)
    for index in range(heads):
        wide = mm_nt(turned, spread(index, heads, rows))
        rows[first + index : first + index + 1, :] = jnp.sum(
            jnp.where(lane % heads == head, wide, 0.0), axis=0, keepdims=True
        )


PAIR_MATRICES = (
    (OUTGOING, PROJ_GATE), (OUTGOING, PROJ_OUT), (OUTGOING, GATE_OUT),
    (INCOMING, PROJ_GATE), (INCOMING, PROJ_OUT), (INCOMING, GATE_OUT),
    (STARTING, QKVG), (STARTING, OUTPUT), (ENDING, QKVG), (ENDING, OUTPUT), (PAIR, UP), (PAIR, DOWN),
)
PAIR_COLUMNS = (
    (OUTGOING, ((OUTGOING, NORM_GAIN), (OUTGOING, NORM_BIAS), (OUTGOING, OUT_GAIN), (OUTGOING, OUT_BIAS))),
    (INCOMING, ((INCOMING, NORM_GAIN), (INCOMING, NORM_BIAS), (INCOMING, OUT_GAIN), (INCOMING, OUT_BIAS))),
    (STARTING, ((STARTING, NORM_GAIN), (STARTING, NORM_BIAS))),
    (ENDING, ((ENDING, NORM_GAIN), (ENDING, NORM_BIAS))),
    (PAIR, ((PAIR, NORM_GAIN), (PAIR, NORM_BIAS))),
)
SINGLE_MATRICES = ((ATTEND, QKVG), (ATTEND, OUTPUT), (SINGLE, UP), (SINGLE, DOWN))
SINGLE_VECTORS = ((ATTEND, NORM_GAIN), (ATTEND, NORM_BIAS), (SINGLE, NORM_GAIN), (SINGLE, NORM_BIAS))


def put_columns(rows, out, table, base, names):
    out[...] = jnp.zeros(out.shape, F32)
    lines = [rows[table[name][0] - base : table[name][0] - base + 1, :] for name in names]
    lines.append(jnp.zeros((8 - len(lines), STRIDE), F32))
    out[...] = jnp.concatenate(lines, axis=0).T


def unpack_pair_kernel(table, total, runs, *refs):
    rows = refs[-1]
    outs = list(refs[:-1])
    rows_from_runs(runs, rows, 0, total)
    for name in PAIR_MATRICES:
        first, shape = table[name]
        plain, turned = outs.pop(0), outs.pop(0)
        for block, part in enumerate(take_matrix(rows, first, shape)):
            place = slice(block * STRIDE, (block + 1) * STRIDE)
            plain[:, place] = part.astype(BF16)
            turned[place, :] = part.T.astype(BF16)
    for prefix in (STARTING, ENDING):
        plain, turned = outs.pop(0), outs.pop(0)
        first, shape = table[(prefix, BIAS_PROJ)]
        matrix = take_narrow(rows, first, shape[1], 8)
        turned[...] = matrix.astype(BF16)
        plain[...] = matrix.T.astype(BF16)
    for prefix, names in PAIR_COLUMNS:
        put_columns(rows, outs.pop(0), table, 0, names)


def unpack_single_kernel(table, total, first_lane, runs, *refs):
    rows = refs[-1]
    outs = list(refs[:-1])
    rows_from_runs(runs, rows, first_lane, total)
    base = first_lane * (total // STRIDE) // STRIDE
    for name in SINGLE_MATRICES:
        first, shape = table[name]
        out = outs.pop(0)
        for block, part in enumerate(take_matrix(rows, first - base, shape)):
            out[:, block * STRIDE : (block + 1) * STRIDE] = part.astype(BF16)
    first, shape = table[(ATTEND, PAIR_PROJ)]
    matrix = take_narrow(rows, first - base, shape[1], shape[1])
    plain, turned = outs.pop(0), outs.pop(0)
    turned[...] = matrix.astype(BF16)
    plain[...] = matrix.T.astype(BF16)
    put_columns(rows, outs.pop(0), table, base, ((ATTEND, PAIR_GAIN), (ATTEND, PAIR_BIAS)))
    lines = outs.pop(0)
    lines[...] = jnp.zeros(lines.shape, F32)
    for index, name in enumerate(SINGLE_VECTORS):
        first, shape = table[name]
        for block in range(shape[0] // STRIDE):
            lines[index : index + 1, block * STRIDE : (block + 1) * STRIDE] = rows[
                first - base + block : first - base + block + 1, :
            ]


def pack_kernel(table, total, first_lane, base, names, *refs):
    ins, out, rows = refs[: len(names)], refs[-2], refs[-1]
    for name, ref in zip(names, ins):
        if isinstance(name, tuple):
            first, shape = table[name]
            if shape[1] % STRIDE:
                put_narrow(rows, first - base, shape[1], ref[...])
            else:
                put_matrix(rows, first - base, ref)
        else:
            for index, vector in name:
                first, shape = table[vector]
                for block in range(shape[0] // STRIDE):
                    rows[first + block - base : first + block - base + 1, :] = ref[
                        index : index + 1, block * STRIDE : (block + 1) * STRIDE
                    ]
    runs_from_rows(rows, out, first_lane, base, total)


def shard_kernel(whole, info, runs, out, squares):
    half = STRIDE // 2
    squares[...] = jnp.zeros(squares.shape, F32)

    def one(block, carry):
        first = runs[pl.ds(info[0] * half, half), block, :]
        second = runs[pl.ds(half - info[0] * half, half), block, :]
        values = jnp.concatenate([first, second], axis=0).T
        row = block * STRIDE + lax.broadcasted_iota(jnp.int32, values.shape, 0)
        lane = lax.broadcasted_iota(jnp.int32, values.shape, 1)
        values = jnp.where(row * STRIDE + lane < whole, values, 0.0)
        out[pl.ds(block * STRIDE, STRIDE), :] = values
        squares[...] += jnp.sum((values * values).reshape(-1, 8, STRIDE), axis=0)
        return carry

    lax.fori_loop(0, RUN, one, 0)


def whole_call(kernel, name, ins, outs, scratch):
    def spec(axis):
        return pl.BlockSpec(memory_space=pltpu.SMEM if axis == "smem" else pltpu.VMEM)

    return pl.pallas_call(
        kernel,
        in_specs=[spec(axis) for array, axis in ins],
        out_specs=[pl.BlockSpec(memory_space=pltpu.VMEM) for shape, dtype in outs],
        out_shape=[jax.ShapeDtypeStruct(shape, dtype) for shape, dtype in outs],
        scratch_shapes=[pltpu.VMEM(shape, dtype) for shape, dtype in scratch],
        compiler_params=pltpu.CompilerParams(vmem_limit_bytes=VMEM_LIMIT),
        name=name,
    )(*[array for array, axis in ins])


def unpack_pair(table, total, runs):
    outs = []
    names = []
    for name in PAIR_MATRICES:
        shape = table[name][1]
        outs += [(shape, BF16), (shape[::-1], BF16)]
        names += [name, (name, T)]
    for prefix in (STARTING, ENDING):
        outs += [((STRIDE, 8), BF16), ((8, STRIDE), BF16)]
        names += [(prefix, BIAS_W), (prefix, BIAS_T)]
    for prefix, parts in PAIR_COLUMNS:
        outs.append(((STRIDE, 8), F32))
        names.append((prefix, COLS))
    height = row_height(0, 0, runs.shape[1], total)
    values = whole_call(
        functools.partial(unpack_pair_kernel, table, total), "pair_weights", [(runs, None)], outs,
        [((height, STRIDE), F32)],
    )
    return dict(zip(names, values))


def unpack_single(table, total, first_lane, runs):
    outs = [(table[name][1], BF16) for name in SINGLE_MATRICES]
    names = list(SINGLE_MATRICES)
    shape = table[(ATTEND, PAIR_PROJ)][1]
    outs += [(shape, BF16), (shape[::-1], BF16), ((STRIDE, 8), F32), ((8, S), F32)]
    names += [(ATTEND, PAIR_PROJ), ((ATTEND, PAIR_PROJ), T), (ATTEND, COLS), (SINGLE, VECTORS)]
    base = first_lane * (total // STRIDE) // STRIDE
    height = row_height(base, first_lane, first_lane + runs.shape[1], total)
    values = whole_call(
        functools.partial(unpack_single_kernel, table, total, first_lane), "single_weights",
        [(runs, None)], outs, [((height, STRIDE), F32)],
    )
    return dict(zip(names, values))


def pack(name, table, total, shards, lanes, base, parts):
    height = row_height(base, *lanes, total)
    for held, array in parts:
        if isinstance(held, tuple):
            end = table[held][0] - base + array.shape[0] * max(1, array.shape[1] // STRIDE)
            height = max(height, -(-end // 8) * 8)
    return whole_call(
        functools.partial(pack_kernel, table, total, lanes[0], base, [held for held, array in parts]),
        name, [(array, None) for held, array in parts],
        [((shards, lanes[1] - lanes[0], RUN, STRIDE), BF16)], [((height, STRIDE), F32)],
    )[0]


def swap(values, group):
    return lax.all_to_all(values, group, split_axis=0, concat_axis=0, tiled=True)


def single_attend(single_state, bias, penalty, weights, group):
    gain, shift = norm_pair(weights, ATTEND)
    lowered = layer_norm(single_state, gain, shift).astype(BF16)
    rows, width = lowered.shape
    size = width // SA_HEADS
    qkvg = matmul(lowered, weights[(ATTEND, QKVG)])
    query = qkvg[:, :width].astype(BF16).reshape(rows, SA_HEADS, size)
    gate = qkvg[:, 3 * width :]
    both = lax.all_gather(qkvg[:, width : 3 * width].astype(BF16), group, axis=0, tiled=True)
    keys_all = both[:, :width].reshape(-1, SA_HEADS, size)
    values_all = both[:, width:].reshape(-1, SA_HEADS, size)
    scores = jnp.einsum(
        "ihd,jhd->hij", query, keys_all, preferred_element_type=F32
    ) * size ** (-0.5)
    scores = scores + bias + penalty[None, None, :]
    probs = jax.nn.softmax(scores, axis=-1)
    probs_low = probs.astype(BF16)
    mixed = jnp.einsum("hij,jhd->ihd", probs_low, values_all, preferred_element_type=F32)
    mixed = mixed.reshape(rows, width)
    gated_low = gated_output(mixed, gate).astype(BF16)
    update = matmul(gated_low, weights[(ATTEND, OUTPUT)])
    return (
        update,
        (single_state, lowered, query, keys_all, values_all, gate, probs, probs_low, mixed, gated_low),
    )


def single_attend_back(saved, grad_update, weights, grads, group):
    single_state, lowered, query, keys_all, values_all, gate, probs, probs_low, mixed, gated_low = saved
    rows, width = lowered.shape
    size = width // SA_HEADS
    scale = size ** (-0.5)
    grad_low = grad_update.astype(BF16)
    grads[(ATTEND, OUTPUT)] = outer_sum(gated_low, grad_low)
    grad_gated = matmul(grad_low, weights[(ATTEND, OUTPUT)].T)
    _, pullback = jax.vjp(gated_output, mixed, gate)
    grad_mixed, grad_gate = pullback(grad_gated)
    grad_mixed = grad_mixed.astype(BF16).reshape(rows, SA_HEADS, size)
    grad_probs = jnp.einsum("ihd,jhd->hij", grad_mixed, values_all, preferred_element_type=F32)
    delta = jnp.sum(probs * grad_probs, axis=-1, keepdims=True)
    grad_scores = (probs * (grad_probs - delta)).astype(BF16)
    grad_query = (
        jnp.einsum("hij,jhd->ihd", grad_scores, keys_all, preferred_element_type=F32) * scale
    )
    key_part = jnp.einsum("hij,ihd->jhd", grad_scores, query, preferred_element_type=F32) * scale
    value_part = jnp.einsum("hij,ihd->jhd", probs_low, grad_mixed, preferred_element_type=F32)
    parts = jnp.concatenate(
        [key_part.reshape(-1, rows, width), value_part.reshape(-1, rows, width)], axis=-1
    )
    grad_both = jnp.sum(swap(parts.astype(BF16), group).astype(F32), axis=0)
    grad_qkvg = jnp.concatenate(
        [grad_query.reshape(rows, width), grad_both, grad_gate], axis=-1
    ).astype(BF16)
    grads[(ATTEND, QKVG)] = outer_sum(lowered, grad_qkvg)
    grad_lowered = matmul(grad_qkvg, weights[(ATTEND, QKVG)].T)
    gain, shift = norm_pair(weights, ATTEND)
    grad_single, grads[(ATTEND, NORM_GAIN)], grads[(ATTEND, NORM_BIAS)] = norm_backward(
        single_state, gain, shift, grad_lowered
    )
    return grad_single, grad_scores


def to_plane(values, parts):
    shape = values.shape
    values = swap(values.reshape((parts, -1) + shape[1:]), "crop")
    return swap(values, "z").reshape(shape)


def from_plane(values, parts):
    shape = values.shape
    values = swap(values.reshape((parts, -1) + shape[1:]), "z")
    return swap(values, "crop").reshape(shape)


def after(values, *others):
    held = lax.optimization_barrier((values,) + others)
    return held


def pair_path(pair, info, alive, orders, weights, cotangent, middle, group, parts):
    rows, length, width = pair.shape
    hidden = weights[(OUTGOING, PROJ_OUT)].shape[0]
    devices = length // rows
    cores = devices // parts
    order, order_back = orders
    read_first = functools.partial(read_tokens, order)
    read_last = functools.partial(read_turned, order)
    part = hidden // devices
    steps = rows // 16
    state_shape = (rows, width, length)
    flip_shape = (devices, rows, rows, width)
    product_shape = (devices, 2, part, rows, length)
    tri_shape = (devices, part, rows, length)
    block = rows // steps
    channel_block = math.gcd(part, 4)

    def products(name, kernel, arrays, out_shape):
        axes = {4: 1, 5: 2}
        return run_rows(
            kernel, name, part // channel_block,
            [(array, axes[array.ndim]) for array in arrays],
            [(out_shape, BF16, axes[len(out_shape)])], [],
        )[0]

    def cols(prefix):
        return weights[(prefix, COLS)]

    tri_cols = cols

    def turned(name):
        return weights[(name, T)]

    tri_scratch = ((hidden, block, length), F32)
    product_scratch = ((2 * hidden, block, length), F32)
    head_scratch = ((8, block, length), F32)
    wide = ((width, length), F32)
    flip_scratch = ((length, block, width), F32)
    table = ((TA_HEADS, length, length), F32)
    attend_saves = [((rows, TA_HEADS, length), F32, 0), (state_shape, BF16, 0)]

    (product,) = run_rows(
        functools.partial(tri_pre_first_kernel, devices, read_first), "outgoing_in", steps,
        [
            (info, "smem"), (alive, None), (pair, 0), (tri_cols(OUTGOING), None),
            (turned((OUTGOING, PROJ_GATE)), None),
        ],
        [(product_shape, BF16, 3)], [product_scratch],
    )
    product_one = swap(product, group)
    tri_one = products(
        "outgoing_product", functools.partial(tri_product_kernel, False), [product_one], tri_shape
    )
    tri_one = swap(tri_one, group).reshape(hidden, rows, length)
    state_one, product = run_rows(
        functools.partial(tri_join_kernel, devices, read_first), "outgoing_out_incoming_in", steps,
        [
            (info, "smem"), (alive, None), (pair, 0), (tri_one, 1), (tri_cols(OUTGOING), None),
            (turned((OUTGOING, PROJ_OUT)), None), (turned((OUTGOING, GATE_OUT)), None),
            (tri_cols(INCOMING), None), (turned((INCOMING, PROJ_GATE)), None),
        ],
        [(state_shape, F32, 0), (product_shape, BF16, 3)], [tri_scratch, product_scratch],
    )
    product_two = swap(product, group)
    tri_two = products(
        "incoming_product", functools.partial(tri_product_kernel, True), [product_two], tri_shape
    )
    tri_two = swap(tri_two, group).reshape(hidden, rows, length)
    state_two, bias = run_rows(
        tri_last_kernel, "incoming_out_starting_bias", steps,
        [
            (state_one, 0), (tri_two, 1), (tri_cols(INCOMING), None),
            (turned((INCOMING, PROJ_OUT)), None), (turned((INCOMING, GATE_OUT)), None),
            (cols(STARTING), None), (weights[(STARTING, BIAS_T)], None),
        ],
        [(state_shape, F32, 0), ((TA_HEADS, rows, length), BF16, 1)], [tri_scratch, head_scratch],
    )
    bias_one = lax.all_gather(bias, group, axis=0, tiled=False)
    cotangent = cotangent.reshape(rows, parts, cores, parts, -1, width).transpose(3, 2, 1, 4, 0, 5)
    cotangent = swap(cotangent.reshape(flip_shape), group)
    cotangent = swap(cotangent.reshape((parts, cores) + flip_shape[1:]), "z").reshape(flip_shape)
    flipped, totals_one, mixed_one = run_rows(
        starting_kernel, "starting_attention", steps,
        [
            (alive, None), (state_two, 0), (bias_one, None), (cols(STARTING), None),
            (turned((STARTING, QKVG)), None), (turned((STARTING, OUTPUT)), None),
        ],
        [(flip_shape, BF16, 2)] + attend_saves, [table, flip_scratch],
    )
    state_three = swap(flipped, group)
    (bias,) = run_rows(
        flipped_bias_kernel, "ending_bias", steps,
        [(state_three, 1), (cols(ENDING), None), (weights[(ENDING, BIAS_T)], None)],
        [((TA_HEADS, rows, length), BF16, 1)], [head_scratch],
    )
    bias_two = lax.all_gather(bias, group, axis=0, tiled=False)
    state_four, totals_two, mixed_two = run_rows(
        ending_kernel, "ending_attention", steps,
        [
            (alive, None), (state_three, 1), (bias_two, None), (cols(ENDING), None),
            (turned((ENDING, QKVG)), None), (turned((ENDING, OUTPUT)), None),
        ],
        [(state_shape, F32, 0)] + attend_saves, [table],
    )
    pair_cols, attend_cols = cols(PAIR), cols(ATTEND)
    state_four, cotangent = after(state_four, cotangent)
    state_five, pair_out, single_bias = run_rows(
        functools.partial(transition_kernel, order_back), "pair_transition", steps,
        [
            (state_four, 0), (pair_cols, None), (turned((PAIR, UP)), None), (turned((PAIR, DOWN)), None),
            (attend_cols, None), (turned((ATTEND, PAIR_PROJ)), None),
        ],
        [(state_shape, F32, 0), ((length, rows, width), BF16, 1), ((SA_HEADS, rows, length), BF16, 1)],
        [flip_scratch, ((SA_HEADS, block, length), F32)],
    )
    pair_out = swap(pair_out.reshape((parts, -1) + pair_out.shape[1:]), "z")

    def turn(values):
        heads = values.shape[0]
        sent = values.reshape(heads, rows, devices, rows).transpose(2, 0, 3, 1)
        return swap(sent, group).transpose(1, 2, 0, 3).reshape(heads, rows, length)

    single_grad_scores = middle(turn(single_bias).astype(F32))
    grads = {}
    grad_four, grads[(PAIR, UP)], grads[(PAIR, DOWN)], grads[(ATTEND, PAIR_PROJ)], vecs = run_rows(
        functools.partial(transition_back_kernel, steps, read_last), "pair_transition_back", steps,
        [
            (state_four, 0), (state_five, 0), (cotangent, 1), (turn(single_grad_scores), 1),
            (pair_cols, None), (turned((PAIR, UP)), None), (weights[(PAIR, UP)], None),
            (weights[(PAIR, DOWN)], None), (attend_cols, None), (weights[(ATTEND, PAIR_PROJ)], None),
        ],
        [
            (state_shape, F32, 0), (weights[(PAIR, UP)].shape, F32, None),
            (weights[(PAIR, DOWN)].shape, F32, None), (weights[(ATTEND, PAIR_PROJ)].shape, F32, None),
            ((8, width), F32, None),
        ],
        [wide, wide, wide, wide, ((SA_HEADS, block, length), F32)],
    )
    grads[(PAIR, VECTORS)] = vecs

    grad_four, pair_out = after(grad_four, pair_out)
    pair_out = swap(pair_out.reshape(flip_shape), group)

    def attention_back(prefix, read, read_grad, source, source_axis, grad, grad_axis, bias, totals, mixed):
        lowered_grad, bias_grad, grads[(prefix, QKVG)], grads[(prefix, OUTPUT)] = run_rows(
            functools.partial(attention_back_kernel, steps, read, read_grad),
            "attention_back", steps,
            [
                (alive, None), (source, source_axis), (grad, grad_axis), (bias, None), (totals, 0),
                (mixed, 0), (cols(prefix), None), (turned((prefix, QKVG)), None),
                (weights[(prefix, QKVG)], None), (weights[(prefix, OUTPUT)], None),
            ],
            [
                (state_shape, BF16, 0), ((devices, TA_HEADS, rows, length), BF16, None),
                (weights[(prefix, QKVG)].shape, F32, None), (weights[(prefix, OUTPUT)].shape, F32, None),
            ],
            [table, table],
        )
        return lowered_grad, swap(bias_grad, group)

    lowered_grad, bias_grad = attention_back(
        ENDING, read_flipped, read_plain, state_three, 1, grad_four, 0, bias_two, totals_two, mixed_two
    )
    bias_grad, pair_out = after(bias_grad, pair_out)
    pair_out = pair_out.reshape(parts, cores, rows, parts, -1, width).transpose(2, 3, 1, 0, 4, 5)
    pair_out = pair_out.reshape(rows, length, width)
    flipped, bias_w_grad, vecs = run_rows(
        functools.partial(ending_end_kernel, steps), "ending_attention_end", steps,
        [
            (state_three, 1), (grad_four, 0), (lowered_grad, 0), (bias_grad, 2), (cols(ENDING), None),
            (weights[(ENDING, BIAS_W)], None),
        ],
        [(flip_shape, BF16, 2), ((width, 8), F32, None), ((8, width), F32, None)],
        [wide, wide, head_scratch, flip_scratch],
    )
    grads[(ENDING, BIAS_PROJ)], grads[(ENDING, VECTORS)] = bias_w_grad, vecs
    grad_three = swap(flipped, group)
    lowered_grad, bias_grad = attention_back(
        STARTING, read_plain, read_flipped, state_two, 0, grad_three, 1, bias_one, totals_one, mixed_one
    )
    square = weights[(INCOMING, GATE_OUT)].shape
    (
        grad_two, grad_tri, gate_back, bias_w_grad, grads[(INCOMING, PROJ_OUT)], grads[(INCOMING, GATE_OUT)], vecs,
    ) = run_rows(
        functools.partial(starting_end_kernel, steps), "starting_end_incoming_out_back", steps,
        [
            (state_two, 0), (grad_three, 1), (lowered_grad, 0), (bias_grad, 2), (cols(STARTING), None),
            (weights[(STARTING, BIAS_W)], None), (state_one, 0), (tri_two, 1), (tri_cols(INCOMING), None),
            (turned((INCOMING, PROJ_OUT)), None), (turned((INCOMING, GATE_OUT)), None),
            (weights[(INCOMING, PROJ_OUT)], None), (weights[(INCOMING, GATE_OUT)], None),
        ],
        [
            (state_shape, F32, 0), ((hidden, rows, length), BF16, 1), (state_shape, BF16, 0),
            ((width, 8), F32, None), (square, F32, None), (square, F32, None), ((8, width), F32, None),
        ],
        [wide, wide, wide, wide, head_scratch, tri_scratch],
    )
    grads[(STARTING, BIAS_PROJ)], grads[(STARTING, VECTORS)] = bias_w_grad, vecs
    grad_tri = swap(grad_tri.reshape(tri_shape), group)
    product_grad = swap(
        products(
            "incoming_product_back", functools.partial(tri_product_back_kernel, True),
            [grad_tri, product_two], product_shape,
        ),
        group,
    )
    (
        grad_one, grad_tri, gate_back, grads[(INCOMING, PROJ_GATE)], grads[(OUTGOING, PROJ_OUT)],
        grads[(OUTGOING, GATE_OUT)], vecs,
    ) = run_rows(
        functools.partial(tri_join_back_kernel, steps, read_first), "incoming_in_outgoing_out_back", steps,
        [
            (info, "smem"), (alive, None), (state_one, 0), (product_grad, 3), (gate_back, 0), (grad_two, 0),
            (tri_cols(INCOMING), None), (turned((INCOMING, PROJ_GATE)), None),
            (weights[(INCOMING, PROJ_GATE)], None), (pair, 0), (tri_one, 1), (tri_cols(OUTGOING), None),
            (turned((OUTGOING, PROJ_OUT)), None), (turned((OUTGOING, GATE_OUT)), None),
            (weights[(OUTGOING, PROJ_OUT)], None), (weights[(OUTGOING, GATE_OUT)], None),
        ],
        [
            (state_shape, F32, 0), ((hidden, rows, length), BF16, 1), (state_shape, BF16, 0),
            (weights[(INCOMING, PROJ_GATE)].shape, F32, None), (square, F32, None), (square, F32, None),
            ((8, width), F32, None),
        ],
        [wide, wide, wide, wide, product_scratch, tri_scratch],
    )
    grads[(INCOMING, VECTORS)] = vecs
    grad_tri = swap(grad_tri.reshape(tri_shape), group)
    product_grad = swap(
        products(
            "outgoing_product_back", functools.partial(tri_product_back_kernel, False),
            [grad_tri, product_one], product_shape,
        ),
        group,
    )
    pair_grad, grads[(OUTGOING, PROJ_GATE)], vecs = run_rows(
        functools.partial(tri_first_back_kernel, steps, read_first, order_back), "outgoing_in_back", steps,
        [
            (info, "smem"), (alive, None), (pair, 0), (product_grad, 3), (gate_back, 0), (grad_one, 0),
            (tri_cols(OUTGOING), None), (turned((OUTGOING, PROJ_GATE)), None),
            (weights[(OUTGOING, PROJ_GATE)], None),
        ],
        [
            ((rows, length, width), BF16, 0), (weights[(OUTGOING, PROJ_GATE)].shape, F32, None),
            ((8, width), F32, None),
        ],
        [wide, wide, product_scratch],
    )
    grads[(OUTGOING, VECTORS)] = vecs
    return pair_out, pair_grad, grads


HELD = {
    (PAIR, VECTORS): ((PAIR, NORM_GAIN), (PAIR, NORM_BIAS), (ATTEND, PAIR_GAIN), (ATTEND, PAIR_BIAS)),
    (ENDING, VECTORS): ((ENDING, NORM_GAIN), (ENDING, NORM_BIAS)),
    (STARTING, VECTORS): (
        (STARTING, NORM_GAIN), (STARTING, NORM_BIAS), (INCOMING, OUT_GAIN), (INCOMING, OUT_BIAS)
    ),
    (INCOMING, VECTORS): (
        (INCOMING, NORM_GAIN), (INCOMING, NORM_BIAS), (OUTGOING, OUT_GAIN), (OUTGOING, OUT_BIAS)
    ),
    (OUTGOING, VECTORS): ((OUTGOING, NORM_GAIN), (OUTGOING, NORM_BIAS)),
}


def vector_part(grads, name, prefix):
    pairs = [(row, held) for row, held in enumerate(HELD[name]) if prefix in (None, held[0])]
    return (pairs, grads[name])


def fast_shards(parts, cores, pair, single, lengths, params, moment_one, moment_two, pair_cotangent, single_cotangent):
    entries = layout(C, H, S, TA_HEADS, SA_HEADS)
    table, total = table_of(entries)
    count = total // STRIDE
    shard_size = params.shape[0]
    attend = table[(ATTEND, NORM_GAIN)][0]
    pair_lanes = -(-attend * STRIDE // count)
    single_lane = attend * STRIDE // count
    devices = parts * cores
    line, group = ("z", "core"), ("crop", "core")
    row_index = lax.axis_index(line)
    odd = ((row_index * shard_size) % STRIDE) // (STRIDE // 2)
    place = jnp.stack([odd, odd]).astype(jnp.int32)
    shard_rows = jnp.pad(params, (0, RUN * STRIDE * STRIDE - shard_size)).reshape(-1, STRIDE)
    (runs,) = whole_call(
        runs_kernel, "parameter_runs", [(place, "smem"), (shard_rows, None)],
        [((STRIDE, RUN, STRIDE), BF16)], [((STRIDE, RUN, STRIDE), F32)],
    )
    weights = unpack_pair(table, total, lax.all_gather(runs[:pair_lanes], line))
    weights.update(
        unpack_single(table, total, single_lane, lax.all_gather(runs[single_lane:], line))
    )
    for index, name in enumerate(SINGLE_VECTORS):
        weights[name] = weights[(SINGLE, VECTORS)][index]
    rows, length = pair.shape[1:3]
    size = rows // parts
    blocks = np.arange(length // size).reshape(parts, cores, parts)
    order = blocks.transpose(2, 1, 0).reshape(-1)
    orders = (order.tolist(), np.argsort(order).tolist())
    tokens = (order[:, None] * size + np.arange(size)).reshape(-1)
    width = single.shape[2]
    length_lanes = jnp.broadcast_to(lengths.astype(BF16), (rows, STRIDE))
    both = jnp.concatenate([single[0], single_cotangent[0], length_lanes], axis=1)
    both = to_plane(both, parts).astype(F32)
    single_state, single_back, live = both[:, :width], both[:, width : 2 * width], both[0, 2 * width]
    mask = (tokens.astype(np.float32) < live).astype(F32)
    info = lax.dynamic_slice_in_dim(mask, lax.axis_index(group) * rows, rows).astype(jnp.int32)
    alive = jnp.broadcast_to(mask, (8, length))
    penalty = (mask - 1.0) * MASKED
    results = {}
    single_grads = {}

    def middle(bias):
        update, saved = single_attend(single_state, bias, penalty, weights, group)
        single_mid = single_state + update
        update, saved_last = transition_forward(single_mid, weights, SINGLE)
        results[SINGLE] = single_mid + update
        grad = single_back
        grad = grad + transition_backward(saved_last, grad, weights, SINGLE, single_grads)
        more, grad_scores = single_attend_back(saved, grad, weights, single_grads, group)
        results["single_grad"] = grad + more
        return grad_scores

    pair_out, pair_grad, grads = pair_path(
        to_plane(pair[0], parts), info, alive, orders, weights, pair_cotangent[0], middle, group, parts
    )
    pair_grad = from_plane(pair_grad, parts).astype(F32)
    both = from_plane(jnp.concatenate([results[SINGLE], results["single_grad"]], axis=1), parts)
    single_out, single_grad = both[:, :width].astype(BF16), both[:, width:]
    grads.update(single_grads)
    lines = jnp.concatenate([grads[name].reshape(1, S) for name in SINGLE_VECTORS], axis=0)
    lines = (list(enumerate(SINGLE_VECTORS)), jnp.pad(lines, ((0, 8 - len(SINGLE_VECTORS)), (0, 0))))
    single_runs = pack(
        "single_gradient", table, total, devices, (pair_lanes, STRIDE), attend,
        [(name, grads[name]) for name in SINGLE_MATRICES + ((ATTEND, PAIR_PROJ),)]
        + [vector_part(grads, (PAIR, VECTORS), ATTEND), lines],
    )
    single_runs = lax.psum(
        lax.psum_scatter(single_runs, line, scatter_dimension=0, tiled=False), "crop"
    ).astype(F32)
    early = -(-(pair_lanes * count - (attend + 2 * S // STRIDE) * STRIDE) // table[(ATTEND, QKVG)][1][1])
    pair_runs = pack(
        "pair_gradient", table, total, devices, (0, pair_lanes), 0,
        [(name, grads[name]) for name in PAIR_MATRICES + ((STARTING, BIAS_PROJ), (ENDING, BIAS_PROJ))]
        + [vector_part(grads, name, None) for name in HELD if name != (PAIR, VECTORS)]
        + [vector_part(grads, (PAIR, VECTORS), PAIR)]
        + [((lines[0][:2]), lines[1]), ((ATTEND, QKVG), grads[(ATTEND, QKVG)][: -(-early // 8) * 8])],
    )
    pair_runs = jnp.sum(swap(pair_runs, line).astype(F32), axis=0)
    pair_runs = jnp.sum(lax.all_gather(pair_runs, "crop"), axis=0)
    shard, squares = whole_call(
        functools.partial(shard_kernel, shard_size), "gradient_share",
        [(place, "smem"), (jnp.concatenate([pair_runs, single_runs], axis=0), None)],
        [((RUN * STRIDE, STRIDE), F32), ((8, STRIDE), F32)], [],
    )
    shard = shard.reshape(-1)[:shard_size]
    clip_norm = jnp.sqrt(jnp.sum(lax.all_gather(squares, line)))
    clipped = shard * (CLIP / jnp.maximum(clip_norm, CLIP))
    new_first = BETA_ONE * moment_one + (1.0 - BETA_ONE) * clipped
    new_second = BETA_TWO * moment_two + (1.0 - BETA_TWO) * clipped * clipped
    rates, decays = rate_tables(entries)
    rate_shard = lax.dynamic_slice_in_dim(jnp.asarray(rates), row_index * shard_size, shard_size)
    decay_shard = lax.dynamic_slice_in_dim(jnp.asarray(decays), row_index * shard_size, shard_size)
    first_hat = new_first / (1.0 - BETA_ONE**STEP)
    second_hat = new_second / (1.0 - BETA_TWO**STEP)
    new_params = params - rate_shard * (
        first_hat / (jnp.sqrt(second_hat) + ADAM_EPS) + decay_shard * params
    )
    return (
        pair_out[None],
        single_out[None],
        pair_grad[None],
        single_grad[None],
        new_params,
        new_first,
        new_second,
        clip_norm,
    )


def solution(mesh):
    crops, devices = mesh.devices.shape
    count = table_of(layout(C, H, S, TA_HEADS, SA_HEADS))[1] // STRIDE
    fast = devices == 2 * crops and LENGTH % (devices * 16) == 0 and count // devices + 2 <= RUN * STRIDE
    row = "row"
    if fast:
        mesh = jax.sharding.Mesh(mesh.devices.reshape(crops, crops, 2), ("crop", "z", "core"))
        row = ("z", "core")
    split = [P("crop", row, None, None), P("crop", row, None), P("crop"), P(row)]
    pair, single, lengths, share = split
    return jax.shard_map(
        functools.partial(fast_shards, crops, 2) if fast else shards,
        mesh=mesh,
        in_specs=(pair, single, lengths, share, share, share, pair, single),
        out_specs=(pair, single, pair, single, share, share, share, P()),
        check_vma=False,
    )
```

profile of v0, /device:TPU:0, one launch (start us, length us, event | category | flops | bytes accessed | tf_op | source)
XLA Modules:
  0.0 1452.3 jit_solution(2952762411967502291)
XLA Ops:
  8.6 9.8 all_to_all.140
  18.4 10.4 all_to_all.141
  28.8 27.2 %all_to_all.142 = bf16[4,8,256,128]{3,2,1,0:T(8,128)(2,1)} all-to-all(bf16[4,8,256,128]{3,2,1,0:T(8,128)(2,1)} %bitcast.129), channel_id=1, replica_groups=mesh['crop'=4,'z'=4,'core'=2] {'crop'}, dimensions={0} | all-to-all | bytes 4194304 | tf_op jit(solution)/shard_map/all_to_all | solution.py:1567
  56.0 3.6 all-to-all-start.3
  63.0 5.9 parameter_runs.1
  72.3 33.2 %all-gather.10.cloned.1.call-done = bf16[192,24,128]{2,1,0:T(8,128)(2,1)} async-done(((bf16[24,24,128]{2,1,0:T(8,128)(2,1)}), bf16[192,24,128]{2,1,0:T(8,128)(2,1)}) %all-gather.10.cloned.1.call-update) | async-done | bytes 1179664 | tf_op jit(solution)/shard_map/all_gather | solution.py:1936
  105.5 7.9 pair_weights.1
  114.7 18.0 %outgoing_in.1 = bf16[8,2,16,32,256]{4,3,2,1,0:T(8,128)(2,1)} custom-call(s32[32]{0:T(128)} %dynamic-slice_convert_fusion.info, f32[8,256]{1,0:T(8,128)} %broadcast_in_dim.17.alive, bf16[32,256,128]{2,1,0:T(8,128)(2,1)} %bitcast.108, f32[128,8]{1,0:T(8,128)} %get-tuple-element.103.cols.tri_cols, bf16[512,128]{1,0:T(8,128)(2,1)} %get-tuple-element.104.proj_t), custom_call_target="tpu_custom_call" | custom-call | tf_op jit(solution)/shard_map/outgoing_in/pallas_call | solution.py:664
  132.8 53.5 %all_to_all.143.operands = bf16[8,2,16,32,256]{4,3,2,1,0:T(8,128)(2,1)} all-to-all(bf16[8,2,16,32,256]{4,3,2,1,0:T(8,128)(2,1)} %outgoing_in.1), channel_id=1, replica_groups=mesh['crop'=4,'z'=4,'core'=2] {'crop','core'}, dimensions={0} | all-to-all | bytes 8388608 | tf_op jit(solution)/shard_map/all_to_all | solution.py:1567
  186.3 6.2 outgoing_product.1
  192.6 30.9 %all_to_all.144 = bf16[8,16,32,256]{3,2,1,0:T(8,128)(2,1)} all-to-all(bf16[8,16,32,256]{3,2,1,0:T(8,128)(2,1)} %outgoing_product.1), channel_id=1, replica_groups=mesh['crop'=4,'z'=4,'core'=2] {'crop','core'}, dimensions={0} | all-to-all | bytes 4194304 | tf_op jit(solution)/shard_map/all_to_all | solution.py:1567
  223.5 29.5 %outgoing_out_incoming_in.1 = (f32[32,128,256]{2,1,0:T(8,128)}, bf16[8,2,16,32,256]{4,3,2,1,0:T(8,128)(2,1)}) custom-call(s32[32]{0:T(128)} %dynamic-slice_convert_fusion.info, f32[8,256]{1,0:T(8,128)} %broadcast_in_dim.17.alive, bf16[32,256,128]{2,1,0:T(8,128)(2,1)} %bitcast.109, bf16[128,32,256]{2,1,0:T(8,128)(2,1)} %bitcast.112, ...), custom_call_target="tpu_custom_call" | custom-call | tf_op jit(solution)/shard_map/outgoing_out_incoming_in/pallas_call | solution.py:664
  253.0 4.7 all-to-all-start.6
  258.7 48.1 %all-to-all-done.6.operands = bf16[8,2,16,32,256]{4,3,2,1,0:T(8,128)(2,1)} async-done(((bf16[8,2,16,32,256]{4,3,2,1,0:T(8,128)(2,1)}), bf16[8,2,16,32,256]{4,3,2,1,0:T(8,128)(2,1)}, u32[]{:S(2)}, u32[]{:S(2)}) %all-to-all-start.6) | async-done | bytes 4194336 | tf_op jit(solution)/shard_map/all_to_all | solution.py:1567
  306.9 6.3 incoming_product.1
  316.8 5.4 copy.70
  322.2 21.2 %all-to-all-done.7 = bf16[8,16,32,256]{3,2,1,0:T(8,128)(2,1)S(1)} async-done(((bf16[8,16,32,256]{3,2,1,0:T(8,128)(2,1)}), bf16[8,16,32,256]{3,2,1,0:T(8,128)(2,1)S(1)}, u32[]{:S(2)}, u32[]{:S(2)}) %all-to-all-start.7) | async-done | bytes 2097184 | tf_op jit(solution)/shard_map/all_to_all | solution.py:1567
  344.7 4.4 all-to-all-start.9
  349.1 21.7 %incoming_out_starting_bias.1 = (f32[32,128,256]{2,1,0:T(8,128)}, bf16[4,32,256]{2,1,0:T(8,128)(2,1)}) custom-call(f32[32,128,256]{2,1,0:T(8,128)} %get-tuple-element.109.source.below, bf16[128,32,256]{2,1,0:T(8,128)(2,1)} %bitcast.114, f32[128,8]{1,0:T(8,128)} %get-tuple-element.107.next_cols.cols.tri_cols, bf16[128,128]{1,0:T(8,128)(2,1)} %get-tuple-element.111.proj_t, ...), custom_call_target="tpu_custom_call" | custom-call | tf_op jit(solution)/shard_map/incoming_out_starting_bias/pallas_call | solution.py:664
  370.8 12.1 all-gather.1
  382.9 58.7 %starting_attention.1 = (bf16[8,32,32,128]{3,2,1,0:T(8,128)(2,1)}, f32[32,4,256]{2,1,0:T(4,128)}, bf16[32,128,256]{2,1,0:T(8,128)(2,1)}) custom-call(f32[8,256]{1,0:T(8,128)} %broadcast_in_dim.17.alive, f32[32,128,256]{2,1,0:T(8,128)} %get-tuple-element.115.source, bf16[8,4,32,256]{3,2,1,0:T(8,128)(2,1)} %bitcast.122, ...), custom_call_target="tpu_custom_call" | custom-call | tf_op jit(solution)/shard_map/starting_attention/pallas_call | solution.py:664
  441.6 30.9 %all_to_all.145.source = bf16[8,32,32,128]{3,2,1,0:T(8,128)(2,1)} all-to-all(bf16[8,32,32,128]{3,2,1,0:T(8,128)(2,1)} %get-tuple-element.119), channel_id=1, replica_groups=mesh['crop'=4,'z'=4,'core'=2] {'crop','core'}, dimensions={0} | all-to-all | bytes 4194304 | tf_op jit(solution)/shard_map/all_to_all | solution.py:1567
  472.5 5.5 all-to-all-start.10
  479.0 28.3 %single_weights.1 = (bf16[384,1536]{1,0:T(8,128)(2,1)}, bf16[384,384]{1,0:T(8,128)(2,1)}, bf16[384,3072]{1,0:T(8,128)(2,1)}, bf16[1536,384]{1,0:T(8,128)(2,1)}, ...) custom-call(bf16[8,105,24,128]{3,2,1,0:T(8,128)(2,1)} %bitcast.121), custom_call_target="tpu_custom_call" | custom-call | tf_op jit(solution)/shard_map/single_weights/pallas_call | solution.py:1506
  511.3 9.1 all_gather.47
  520.4 11.1 ending_bias.1
  531.5 10.8 all-gather.2
  542.3 56.1 %ending_attention.1 = (f32[32,128,256]{2,1,0:T(8,128)}, f32[32,4,256]{2,1,0:T(4,128)}, bf16[32,128,256]{2,1,0:T(8,128)(2,1)}) custom-call(f32[8,256]{1,0:T(8,128)} %broadcast_in_dim.17.alive, bf16[8,32,32,128]{3,2,1,0:T(8,128)(2,1)} %all_to_all.145.source, bf16[8,4,32,256]{3,2,1,0:T(8,128)(2,1)} %bitcast.124, f32[128,8]{1,0:T(8,128)} %get-tuple-element.120.cols, ...), custom_call_target="tpu_custom_call" | custom-call | tf_op jit(solution)/shard_map/ending_attention/pallas_call | solution.py:664
  598.4 30.6 %pair_transition.1 = (f32[32,128,256]{2,1,0:T(8,128)}, bf16[256,32,128]{2,1,0:T(8,128)(2,1)}, bf16[16,32,256]{2,1,0:T(8,128)(2,1)}) custom-call(f32[32,128,256]{2,1,0:T(8,128)} %get-tuple-element.125.source.mid, f32[128,8]{1,0:T(8,128)} %get-tuple-element.126.cols, bf16[1024,128]{1,0:T(8,128)(2,1)} %get-tuple-element.127.up_t, ...), custom_call_target="tpu_custom_call" | custom-call | tf_op jit(solution)/shard_map/pair_transition/pallas_call | solution.py:664
  637.0 5.8 all-to-all-done.11
  663.5 10.0 all_to_all.146
  673.5 5.3 all-to-all-start.13
  685.0 32.3 %pair_transition_back.1 = (f32[32,128,256]{2,1,0:T(8,128)}, f32[128,1024]{1,0:T(8,128)}, f32[512,128]{1,0:T(8,128)}, f32[128,16]{1,0:T(8,128)}, f32[8,128]{1,0:T(8,128)}) custom-call(f32[32,128,256]{2,1,0:T(8,128)} %get-tuple-element.125.source.mid, f32[32,128,256]{2,1,0:T(8,128)} %get-tuple-element.131.final, bf16[8,32,32,128]{3,2,1,0:T(8,128)(2,1)} %bitcast.120, ...), custom_call_target="tpu_custom_call" | custom-call | tf_op jit(solution)/shard_map/pair_transition_back/pallas_call | solution.py:664
  717.3 9.0 all-to-all-done.13
  726.3 66.8 %attention_back.2 = (bf16[32,128,256]{2,1,0:T(8,128)(2,1)}, bf16[8,4,32,256]{3,2,1,0:T(8,128)(2,1)}, f32[128,512]{1,0:T(8,128)}, f32[128,128]{1,0:T(8,128)}) custom-call(f32[8,256]{1,0:T(8,128)} %broadcast_in_dim.17.alive, bf16[8,32,32,128]{3,2,1,0:T(8,128)(2,1)} %all_to_all.145.source, f32[32,128,256]{2,1,0:T(8,128)} %get-tuple-element.144.grad_in, ...), custom_call_target="tpu_custom_call" | custom-call | tf_op jit(solution)/shard_map/attention_back/pallas_call | solution.py:664
  793.1 13.9 all_to_all.147.bias_grad
  807.0 29.8 %all_to_all.148 = bf16[8,32,32,128]{3,2,1,0:T(8,128)(2,1)} all-to-all(bf16[8,32,32,128]{3,2,1,0:T(8,128)(2,1)S(1)} %bitcast.118), channel_id=1, replica_groups=mesh['crop'=4,'z'=4,'core'=2] {'crop','core'}, dimensions={0} | all-to-all | bytes 4194304 | tf_op jit(solution)/shard_map/all_to_all | solution.py:1567
  836.7 15.7 %ending_attention_end.1 = (bf16[8,32,32,128]{3,2,1,0:T(8,128)(2,1)}, f32[128,8]{1,0:T(8,128)}, f32[8,128]{1,0:T(8,128)}) custom-call(bf16[8,32,32,128]{3,2,1,0:T(8,128)(2,1)} %all_to_all.145.source, f32[32,128,256]{2,1,0:T(8,128)} %get-tuple-element.144.grad_in, bf16[32,128,256]{2,1,0:T(8,128)(2,1)} %get-tuple-element.152.grad_lowered, ...), custom_call_target="tpu_custom_call" | custom-call | tf_op jit(solution)/shard_map/ending_attention_end/pallas_call | solution.py:664
  852.5 31.0 %all_to_all.149.grad_in = bf16[8,32,32,128]{3,2,1,0:T(8,128)(2,1)} all-to-all(bf16[8,32,32,128]{3,2,1,0:T(8,128)(2,1)} %get-tuple-element.155), channel_id=1, replica_groups=mesh['crop'=4,'z'=4,'core'=2] {'crop','core'}, dimensions={0} | all-to-all | bytes 4194304 | tf_op jit(solution)/shard_map/all_to_all | solution.py:1567
  883.4 65.2 %attention_back.3 = (bf16[32,128,256]{2,1,0:T(8,128)(2,1)}, bf16[8,4,32,256]{3,2,1,0:T(8,128)(2,1)}, f32[128,512]{1,0:T(8,128)}, f32[128,128]{1,0:T(8,128)}) custom-call(f32[8,256]{1,0:T(8,128)} %broadcast_in_dim.17.alive, f32[32,128,256]{2,1,0:T(8,128)} %get-tuple-element.115.source, bf16[8,32,32,128]{3,2,1,0:T(8,128)(2,1)} %all_to_all.149.grad_in, ...), custom_call_target="tpu_custom_call" | custom-call | tf_op jit(solution)/shard_map/attention_back/pallas_call | solution.py:664
  948.7 13.9 all_to_all.150.bias_grad
  962.5 31.7 %starting_end_incoming_out_back.1 = (f32[32,128,256]{2,1,0:T(8,128)}, bf16[128,32,256]{2,1,0:T(8,128)(2,1)}, bf16[32,128,256]{2,1,0:T(8,128)(2,1)}, f32[128,8]{1...) custom-call(f32[32,128,256]{2,1,0:T(8,128)} %get-tuple-element.115.source, ...), custom_call_target="tpu_custom_call" | custom-call | tf_op jit(solution)/shard_map/starting_end_incoming_out_back/pallas_call | solution.py:664
  994.2 4.0 all-to-all-start.21
  1008.7 16.0 %all-to-all-done.21.grad = bf16[8,16,32,256]{3,2,1,0:T(8,128)(2,1)S(1)} async-done(((bf16[8,16,32,256]{3,2,1,0:T(8,128)(2,1)}), bf16[8,16,32,256]{3,2,1,0:T(8,128)(2,1)S(1)}, u32[]{:S(2)}, u32[]{:S(2)}) %all-to-all-start.21) | async-done | bytes 2097184 | tf_op jit(solution)/shard_map/all_to_all | solution.py:1567
  1028.2 7.4 incoming_product_back.1
  1036.5 4.6 all-to-all-start.22
  1051.6 30.2 %single_gradient.1 = bf16[8,104,24,128]{3,2,1,0:T(8,128)(2,1)} custom-call(f32[384,1536]{1,0:T(8,128)} %fusion.21.refs_0_, f32[384,384]{1,0:T(8,128)} %fusion.27.refs_1_, f32[384,3072]{1,0:T(8,128)} %fusion.23.refs_2_, f32[1536,384]{1,0:T(8,128)} %fusion.31.refs_3_, f32[128,16]{1,0:T(8,128)} %get-tuple-element.195.refs_4_, ...), custom_call_target="tpu_custom_call" | custom-call | tf_op jit(solution)/shard_map/single_gradient/pallas_call | solution.py:1506
  1081.8 8.4 all-to-all-done.22.product_grad
  1090.2 47.2 %incoming_in_outgoing_out_back.1 = (f32[32,128,256]{2,1,0:T(8,128)}, bf16[128,32,256]{2,1,0:T(8,128)(2,1)}, bf16[32,128,256]{2,1,0:T(8,128)(2,1)}, f32[128,512]{...) custom-call(s32[32]{0:T(128)} %dynamic-slice_convert_fusion.info, ...), custom_call_target="tpu_custom_call" | custom-call | tf_op jit(solution)/shard_map/incoming_in_outgoing_out_back/pallas_call | solution.py:664
  1137.4 3.8 all-to-all-start.23
  1144.2 23.6 %all-to-all-done.23.grad = bf16[8,16,32,256]{3,2,1,0:T(8,128)(2,1)S(1)} async-done(((bf16[8,16,32,256]{3,2,1,0:T(8,128)(2,1)}), bf16[8,16,32,256]{3,2,1,0:T(8,128)(2,1)S(1)}, u32[]{:S(2)}, u32[]{:S(2)}) %all-to-all-start.23) | async-done | bytes 2097184 | tf_op jit(solution)/shard_map/all_to_all | solution.py:1567
  1167.8 3.9 all-to-all-start.17
  1171.7 7.2 outgoing_product_back.1
  1179.0 53.6 %all_to_all.151.product_grad = bf16[8,2,16,32,256]{4,3,2,1,0:T(8,128)(2,1)} all-to-all(bf16[8,2,16,32,256]{4,3,2,1,0:T(8,128)(2,1)} %outgoing_product_back.1), channel_id=1, replica_groups=mesh['crop'=4,'z'=4,'core'=2] {'crop','core'}, dimensions={0} | all-to-all | bytes 8388608 | tf_op jit(solution)/shard_map/all_to_all | solution.py:1567
  1237.4 32.1 %outgoing_in_back.1 = (bf16[32,256,128]{2,1,0:T(8,128)(2,1)}, f32[128,512]{1,0:T(8,128)}, f32[8,128]{1,0:T(8,128)}) custom-call(s32[32]{0:T(128)} %dynamic-slice_convert_fusion.info, f32[8,256]{1,0:T(8,128)} %broadcast_in_dim.17.alive, bf16[32,256,128]{2,1,0:T(8,128)(2,1)} %bitcast.111, bf16[8,2,16,32,256]{4,3,2,1,0:T(8,128)(2,1)} %all_to_all.151.product_grad, ...), custom_call_target="tpu_custom_call" | custom-call | tf_op jit(solution)/shard_map/outgoing_in_back/pallas_call | solution.py:664
  1269.5 8.3 pair_gradient.1
  1277.8 34.4 %all_to_all.152 = bf16[8,24,24,128]{3,2,1,0:T(8,128)(2,1)S(1)} all-to-all(bf16[8,24,24,128]{3,2,1,0:T(8,128)(2,1)} %pair_gradient.1), channel_id=1, replica_groups=mesh['crop'=4,'z'=4,'core'=2] {'z','core'}, dimensions={0} | all-to-all | bytes 2359296 | tf_op jit(solution)/shard_map/all_to_all | solution.py:1567
  1312.2 4.5 all-to-all-start.25
  1321.4 47.7 %all-reduce.6.cloned.1.call-done = bf16[104,24,128]{2,1,0:T(8,128)(2,1)} async-done(((bf16[104,24,128]{2,1,0:T(8,128)(2,1)}), bf16[104,24,128]{2,1,0:T(8,128)(2,1)}) %all-reduce.6.cloned.1.call-update) | async-done | bytes 638992 | tf_op jit(solution)/shard_map/psum | solution.py:1985
  1370.3 3.6 all-to-all-start.26
  1373.9 35.0 %all-gather.14.cloned.1.call-done = f32[96,24,128]{2,1,0:T(8,128)} async-done(((f32[24,24,128]{2,1,0:T(8,128)}), f32[96,24,128]{2,1,0:T(8,128)}) %all-gather.14.cloned.1.call-update) | async-done | bytes 1179664 | tf_op jit(solution)/shard_map/all_gather | solution.py:1997
  1413.1 5.2 gradient_share.1
  1418.4 14.4 all-gather.5
  1434.1 7.5 multiply_subtract_fusion
  (220 shorter events, 100.1 us)
Async XLA Ops:
  56.0 57.4 %all-to-all-start.3 = ((bf16[4,8,256,128]{3,2,1,0:T(8,128)(2,1)}), bf16[4,8,256,128]{3,2,1,0:T(8,128)(2,1)S(1)}, u32[]{:S(2)}, u32[]{:S(2)}) async-start(bf16[4,8,256,128]{3,2,1,0:T(8,128)(2,1)} %all_to_all.142), calls=%async_computation.3 | async-start | bytes 4194304 | tf_op jit(solution)/shard_map/all_to_all | solution.py:1567
  59.6 45.8 %all-gather.10.cloned.1.call-start = ((), (), s32[]{:S(2)}) async-start(), calls=%async_computation.31 | async-start | bytes 1327104 | tf_op jit(solution)/shard_map/all_gather | solution.py:1936
  63.0 8.1 copy-start.48
  253.0 4.8 copy-start.8
  253.0 53.8 %all-to-all-start.6 = ((bf16[8,2,16,32,256]{4,3,2,1,0:T(8,128)(2,1)}), bf16[8,2,16,32,256]{4,3,2,1,0:T(8,128)(2,1)}, u32[]{:S(2)}, u32[]{:S(2)}) async-start(bf16[8,2,16,32,256]{4,3,2,1,0:T(8,128)(2,1)} %get-tuple-element.110), calls=%async_computation.6 | async-start | bytes 8388608 | tf_op jit(solution)/shard_map/all_to_all | solution.py:1567
  257.8 221.3 %all-gather.12.cloned.1.call-start = ((), (), s32[]{:S(2)}) async-start(), calls=%async_computation.32 | async-start | bytes 5806080 | tf_op jit(solution)/shard_map/all_gather | solution.py:1938
  313.2 30.2 %all-to-all-start.7 = ((bf16[8,16,32,256]{3,2,1,0:T(8,128)(2,1)}), bf16[8,16,32,256]{3,2,1,0:T(8,128)(2,1)S(1)}, u32[]{:S(2)}, u32[]{:S(2)}) async-start(bf16[8,16,32,256]{3,2,1,0:T(8,128)(2,1)} %incoming_product.1), calls=%async_computation.7 | async-start | bytes 4194304 | tf_op jit(solution)/shard_map/all_to_all | solution.py:1567
  344.7 96.9 %all-to-all-start.9 = ((bf16[8,32,32,128]{3,2,1,0:T(8,128)(2,1)}), bf16[8,32,32,128]{3,2,1,0:T(8,128)(2,1)}, u32[]{:S(2)}, u32[]{:S(2)}) async-start(bf16[8,32,32,128]{3,2,1,0:T(8,128)(2,1)} %bitcast.119), calls=%async_computation.9 | async-start | bytes 4194304 | tf_op jit(solution)/shard_map/all_to_all | solution.py:1567
  472.5 125.9 %all-to-all-start.10 = ((bf16[4,2,32,32,128]{4,3,2,1,0:T(8,128)(2,1)}), bf16[4,2,32,32,128]{4,3,2,1,0:T(8,128)(2,1)S(1)}, u32[]{:S(2)}, u32[]{:S(2)}) async-start(bf16[4,2,32,32,128]{4,3,2,1,0:T(8,128)(2,1)} %bitcast.17), calls=%async_computation.10 | async-start | bytes 4194304 | tf_op jit(solution)/shard_map/all_to_all | solution.py:1567
  478.1 30.1 %copy-start.38 = (f32[32]{0:T(128)}, f32[32]{0:T(128)S(1)}, u32[]{:S(2)}) copy-start(f32[32]{0:T(128)S(1)} %broadcast_multiply_fusion.1) | copy-start | bytes 388
  478.3 29.0 %copy-start.49 = (f32[32]{0:T(128)}, f32[32]{0:T(128)S(1)}, u32[]{:S(2)}) copy-start(f32[32]{0:T(128)S(1)} %multiply_reduce_fusion.6) | copy-start | bytes 388
  478.3 29.9 %copy-start.42 = (f32[32]{0:T(128)}, f32[32]{0:T(128)S(1)}, u32[]{:S(2)}) copy-start(f32[32]{0:T(128)S(1)} %fusion.33) | copy-start | bytes 388
  508.2 23.3 %copy-start.36 = (f32[384]{0:T(512)}, f32[384]{0:T(512)S(1)}, u32[]{:S(2)}) copy-start(f32[384]{0:T(512)S(1)} %get-tuple-element.206) | copy-start | bytes 4612
  508.2 146.1 %copy-start.34 = (f32[384]{0:T(512)}, f32[384]{0:T(512)S(1)}, u32[]{:S(2)}) copy-start(f32[384]{0:T(512)S(1)} %get-tuple-element.205) | copy-start | bytes 4612
  598.4 30.6 %copy-start.6 = (bf16[4,2,32,32,128]{4,3,2,1,0:T(8,128)(2,1)}, bf16[4,2,32,32,128]{4,3,2,1,0:T(8,128)(2,1)S(1)}, u32[]{:S(2)}) copy-start(bf16[4,2,32,32,128]{4,3,2,1,0:T(8,128)(2,1)S(1)} %all-to-all-done.10) | copy-start | bytes 6291460
  632.5 10.3 all-to-all-start.11
  636.2 11.4 copy-start.13
  648.8 5.3 copy-start.11
  648.8 5.5 copy-start.2
  649.8 9.2 copy-start.32
  651.9 3.0 copy-start.16
  652.8 3.2 copy-start.28
  654.1 3.3 copy-start.9
  654.1 3.3 copy-start.40
  654.3 3.1 copy-start.44
  656.0 2.8 copy-start.19
  656.0 2.8 copy-start.21
  656.0 3.0 copy-start.12
  673.5 52.8 %all-to-all-start.13 = ((bf16[4,64,32,128]{3,2,1,0:T(8,128)(2,1)}), bf16[4,64,32,128]{3,2,1,0:T(8,128)(2,1)S(1)}, u32[]{:S(2)}, u32[]{:S(2)}) async-start(bf16[4,64,32,128]{3,2,1,0:T(8,128)(2,1)} %bitcast.131), calls=%async_computation.13 | async-start | bytes 4194304 | tf_op jit(solution)/shard_map/all_to_all | solution.py:1567
  994.2 4.0 copy-start.31
  994.2 4.0 copy-start.33
  994.2 30.5 %all-to-all-start.21 = ((bf16[8,16,32,256]{3,2,1,0:T(8,128)(2,1)}), bf16[8,16,32,256]{3,2,1,0:T(8,128)(2,1)S(1)}, u32[]{:S(2)}, u32[]{:S(2)}) async-start(bf16[8,16,32,256]{3,2,1,0:T(8,128)(2,1)} %bitcast.134), calls=%async_computation.21 | async-start | bytes 4194304 | tf_op jit(solution)/shard_map/all_to_all | solution.py:1567
  998.2 5.4 copy-start.18
  1024.8 3.5 copy-start.4
  1024.8 11.7 all-to-all-start.16
  1035.7 5.5 copy-start.14
  1035.7 5.8 copy-start.47
  1035.7 5.9 copy-start.46
  1035.7 5.9 copy-start.25
  1035.7 5.9 copy-start.29
  1035.7 6.9 copy-start.27
  1036.5 53.7 %all-to-all-start.22 = ((bf16[8,2,16,32,256]{4,3,2,1,0:T(8,128)(2,1)}), bf16[8,2,16,32,256]{4,3,2,1,0:T(8,128)(2,1)}, u32[]{:S(2)}, u32[]{:S(2)}) async-start(bf16[8,2,16,32,256]{4,3,2,1,0:T(8,128)(2,1)} %incoming_product_back.1), calls=%async_computation.22 | async-start | bytes 8388608 | tf_op jit(solution)/shard_map/all_to_all | solution.py:1567
  1041.1 3.5 copy-start.10
  1041.1 3.5 copy-start.20
  1041.1 3.5 copy-start.22
  1041.1 3.4 copy-start.35
  1041.1 3.4 copy-start.41
  1041.1 3.4 copy-start.45
  1041.1 275.6 %reduce-scatter.2.cloned.1.call-start = ((), (), s32[]{:S(2)}) async-start(), calls=%async_computation.29 | async-start | bytes 5750784 | tf_op jit(solution)/shard_map/reduce_scatter | solution.py:1986
  1044.6 3.1 copy-start.7
  1044.6 3.1 copy-start.39
  1044.6 3.1 copy-start.43
  1044.6 5.0 copy-start.37
  1137.4 3.8 copy-start.17
  1137.4 5.0 copy-start.50
  1137.4 6.0 copy-start.26
  1137.4 30.3 %all-to-all-start.23 = ((bf16[8,16,32,256]{3,2,1,0:T(8,128)(2,1)}), bf16[8,16,32,256]{3,2,1,0:T(8,128)(2,1)S(1)}, u32[]{:S(2)}, u32[]{:S(2)}) async-start(bf16[8,16,32,256]{3,2,1,0:T(8,128)(2,1)} %bitcast.133), calls=%async_computation.23 | async-start | bytes 4194304 | tf_op jit(solution)/shard_map/all_to_all | solution.py:1567
  1167.8 3.9 copy-start.3
  1167.8 11.2 all-to-all-start.17
  1232.5 45.3 %all-to-all-start.18 = ((f32[4,8,768]{2,1,0:T(8,128)}), f32[4,8,768]{2,1,0:T(8,128)S(1)}, u32[]{:S(2)}, u32[]{:S(2)}) async-start(f32[4,8,768]{2,1,0:T(8,128)} %all-to-all-done.17), calls=%async_computation.18 | async-start | bytes 196608 | tf_op jit(solution)/shard_map/all_to_all | solution.py:1567
  1312.2 58.0 %all-to-all-start.25 = ((bf16[4,8,256,128]{3,2,1,0:T(8,128)(2,1)}), bf16[4,8,256,128]{3,2,1,0:T(8,128)(2,1)}, u32[]{:S(2)}, u32[]{:S(2)}) async-start(bf16[4,8,256,128]{3,2,1,0:T(8,128)(2,1)} %bitcast.44), calls=%async_computation.25 | async-start | bytes 4194304 | tf_op jit(solution)/shard_map/all_to_all | solution.py:1567
  1316.7 52.4 %all-reduce.6.cloned.1.call-start = ((), (), s32[]{:S(2)}) async-start(), calls=%async_computation.30 | async-start | bytes 1277952 | tf_op jit(solution)/shard_map/psum | solution.py:1985
  1317.3 91.6 %all-gather.14.cloned.1.call-start = ((), (), s32[]{:S(2)}) async-start(), calls=%async_computation.33 | async-start | bytes 1474560 | tf_op jit(solution)/shard_map/all_gather | solution.py:1997
  1370.3 71.4 %all-to-all-start.26 = ((bf16[4,8,256,128]{3,2,1,0:T(8,128)(2,1)}), bf16[4,8,256,128]{3,2,1,0:T(8,128)(2,1)S(1)}, u32[]{:S(2)}, u32[]{:S(2)}) async-start(bf16[4,8,256,128]{3,2,1,0:T(8,128)(2,1)} %all-to-all-done.25), calls=%async_computation.26 | async-start | bytes 4194304 | tf_op jit(solution)/shard_map/all_to_all | solution.py:1567
  (7 other events, 13.6 us)
Sparse Core Ops, SparseCore 0:
  70.6 34.7 all-gather.9
  260.8 57.5 all-gather.11
  1081.9 58.1 reduce-scatter.1
  1320.6 48.4 all-reduce.5
  1371.5 37.3 all-gather.13
where the time goes:
time: 1460 us; the launch traced here: 1450 us
  Pallas kernels  630 us (43%)
  blocking collectives  396 us (27%)
  waiting for transfers between devices  249 us (17%)
  starting transfers between devices  61.7 us (4%)
  local copies, waits for them, and re-layouts  41.6 us (3%)
  other arithmetic  29.5 us (2%)
  matrix products  26.5 us (2%)
  between operations  17.8 us (1%)
    pallas_call x18, Pallas kernels, run_rows(): pl.pallas_call(kernel, grid=(steps,), in_specs=in_specs, out_specs=out_sp...  544 us
    all_to_all x13, blocking collectives, swap(): lax.all_to_all(values, group, split_axis=0, concat_axis=0, tiled=True)  349 us
    all_to_all x15, waiting for transfers between devices, swap(): lax.all_to_all(values, group, split_axis=0, concat_axis=0, tiled=True)  133 us
    pallas_call x6, Pallas kernels, whole_call(): pl.pallas_call(kernel, in_specs=[spec(axis) for array, axis in ins], out_...  85.8 us
    all_to_all x15, starting transfers between devices, swap(): lax.all_to_all(values, group, split_axis=0, concat_axis=0, tiled=True)  61.4 us
    psum x1, waiting for transfers between devices, fast_shards(): lax.psum(lax.psum_scatter(single_runs, line, scatter_dimension=0, tiled=F...  47.7 us
    all_gather x1, waiting for transfers between devices, fast_shards(): pair_runs = jnp.sum(lax.all_gather(pair_runs, 'crop'), axis=0)  35 us
    all_gather x1, waiting for transfers between devices, fast_shards(): weights = unpack_pair(table, total, lax.all_gather(runs[:pair_lanes], line))  33.2 us
  transfers between devices with their start and end apart: 20, of which 11 were waited for; matrix products, arithmetic and copies ran while one was open for 5% of the time, Pallas kernels for 25%

commit v1 on v0

--- a/solution.py
+++ b/solution.py
@@ -624,15 +624,61 @@
 
 
 def live_pair(info, alive, row):
-    return jnp.where(info[row] > 0, alive[0:1], 0.0)
-
-
-def each_row(count, body):
+    return jnp.concatenate(
+        [jnp.where(info[row + place] > 0, alive[0:1], 0.0) for place in range(GROUP)], axis=1
+    )
+
+
+GROUP = 4
+LAG = 4
+
+
+def each_group(count, body):
+    def step(index, carry):
+        body(index * GROUP)
+        return carry
+
+    lax.fori_loop(0, count // GROUP, step, 0)
+
+
+def each_channel(count, body):
     def step(index, carry):
         body(index)
         return carry
 
     lax.fori_loop(0, count, step, 0)
+
+
+def join(read, ref, row):
+    return jnp.concatenate([read(ref, row + place) for place in range(GROUP)], axis=1)
+
+
+def pieces_of(values):
+    length = values.shape[1] // GROUP
+    return [values[:, place * length : (place + 1) * length] for place in range(GROUP)]
+
+
+def put_rows(ref, row, values):
+    for place, part in enumerate(pieces_of(values)):
+        ref[row + place] = part.astype(ref.dtype)
+
+
+def put_inner(scratch, row, values):
+    for place, part in enumerate(pieces_of(values)):
+        scratch[:, row + place, :] = part
+
+
+def read_inner(scratch, row):
+    return scratch[:, row, :]
+
+
+def put_turned(scratch, row, values):
+    for place, part in enumerate(pieces_of(values)):
+        scratch[:, row + place, :] = part.T
+
+
+def add_lanes(ref, values):
+    ref[...] += sum(pieces_of(values))
 
 
 def spec_full(shape):
@@ -646,7 +692,13 @@
     )
 
 
-def run_rows(kernel, name, steps, ins, outs, scratch):
+def cost(microseconds):
+    return pl.CostEstimate(
+        flops=int(microseconds * 1e9), bytes_accessed=int(microseconds * 3e6), transcendentals=0
+    )
+
+
+def run_rows(kernel, name, steps, ins, outs, scratch, time=15):
     in_specs = []
     for array, axis in ins:
         if axis == "smem":
@@ -669,6 +721,7 @@
         out_shape=[jax.ShapeDtypeStruct(shape, dtype) for shape, dtype, axis in outs],
         scratch_shapes=[pltpu.VMEM(shape, dtype) for shape, dtype in scratch],
         compiler_params=pltpu.CompilerParams(vmem_limit_bytes=VMEM_LIMIT),
+        cost_estimate=cost(time),
         name=name,
     )(*[array for array, axis in ins])
 
@@ -769,11 +822,12 @@
     rows = pair.shape[0]
 
     def body(row):
-        scratch[:, row, :] = tri_pre_row(
-            info, alive, row_base(rows) + row, read(pair, row), cols, 0, proj_t
-        )
-
-    each_row(rows, body)
+        product = tri_pre_row(
+            info, alive, row_base(rows) + row, join(read, pair, row), cols, 0, proj_t
+        )
+        put_inner(scratch, row, product)
+
+    each_group(rows, body)
     store_product(out, scratch, devices)
 
 
@@ -785,7 +839,7 @@
         tri = mm_tn(first, second) if incoming else mm_nt(first, second)
         out[:, channel] = tri.astype(BF16).reshape(out.shape[0], out.shape[2], length)
 
-    each_row(operands.shape[2], body)
+    each_channel(operands.shape[2], body)
 
 
 def tri_join_kernel(
@@ -796,15 +850,16 @@
     copy_blocks(tri_scratch, tri_in, tri_in.shape[0])
 
     def body(row):
-        state = read(source, row)
-        pieces = tri_post_row(state, tri_scratch[:, row, :], cols, proj_t, gate_t)
+        state = join(read, source, row)
+        pieces = tri_post_row(state, join(read_inner, tri_scratch, row), cols, proj_t, gate_t)
         state = state + pieces[6] * pieces[7]
-        state_out[row] = state
-        scratch[:, row, :] = tri_pre_row(
+        put_rows(state_out, row, state)
+        product = tri_pre_row(
             info, alive, row_base(rows) + row, state, next_cols, 0, next_proj_t
         )
-
-    each_row(rows, body)
+        put_inner(scratch, row, product)
+
+    each_group(rows, body)
     store_product(out, scratch, devices)
 
 
@@ -815,15 +870,15 @@
     copy_blocks(tri_scratch, tri_in, tri_in.shape[0])
 
     def body(row):
-        state = source[row]
-        pieces = tri_post_row(state, tri_scratch[:, row, :], cols, proj_t, gate_t)
+        state = join(read_plain, source, row)
+        pieces = tri_post_row(state, join(read_inner, tri_scratch, row), cols, proj_t, gate_t)
         state = state + pieces[6] * pieces[7]
-        state_out[row] = state
+        put_rows(state_out, row, state)
         unit, inverse = standardize(state)
         lowered = (unit * column(next_cols, 0) + column(next_cols, 1)).astype(BF16)
-        scratch[:, row, :] = mm(bias_t[...], lowered)
-
-    each_row(rows, body)
+        put_inner(scratch, row, mm(bias_t[...], lowered))
+
+    each_group(rows, body)
     bias_out[...] = scratch[: bias_out.shape[0]].astype(BF16)
 
 
@@ -831,11 +886,11 @@
     rows = source.shape[1]
 
     def body(row):
-        unit, inverse = standardize(read_flipped(source, row))
+        unit, inverse = standardize(join(read_flipped, source, row))
         lowered = (unit * column(cols, 0) + column(cols, 1)).astype(BF16)
-        scratch[:, row, :] = mm(bias_t[...], lowered)
-
-    each_row(rows, body)
+        put_inner(scratch, row, mm(bias_t[...], lowered))
+
+    each_group(rows, body)
     bias_out[...] = scratch[: bias_out.shape[0]].astype(BF16)
 
 
@@ -862,22 +917,62 @@
     return unit, inverse, lowered, query, key, value, gate
 
 
-def attend_rows(state, cols, proj_t, output_t, table, save_total, save_mixed):
+def in_stages(blocks, first, second, third):
+    early, late, done = {}, {}, {}
+    count = len(blocks)
+    for step in range(count + 2 * LAG):
+        if step < count:
+            early[step] = first(*blocks[step])
+        if 0 <= step - LAG < count:
+            late[step - LAG] = second(*blocks[step - LAG], early.pop(step - LAG))
+        if 0 <= step - 2 * LAG < count:
+            place = step - 2 * LAG
+            done[blocks[place]] = third(*blocks[place], late.pop(place))
+    return done
+
+
+def head_rows(values, place, head):
+    size, length = values.shape[0] // TA_HEADS, values.shape[1] // GROUP
+    return values[head * size : (head + 1) * size, place * length : (place + 1) * length]
+
+
+def gather_heads(done):
+    return jnp.concatenate(
+        [
+            jnp.concatenate([done[place, head] for head in range(TA_HEADS)], axis=0)
+            for place in range(GROUP)
+        ],
+        axis=1,
+    )
+
+
+ROW_BLOCKS = [(place, head) for place in range(GROUP) for head in range(TA_HEADS)]
+HEAD_BLOCKS = [(place, head) for head in range(TA_HEADS) for place in range(GROUP)]
+
+
+def attend_rows(state, row, cols, proj_t, output_t, table, totals, mixed_out):
     unit, inverse, lowered, query, key, value, gate = attention_row(state, cols, proj_t)
-    size = query.shape[0] // TA_HEADS
-    mixed = []
-    totals = []
-    for head in range(TA_HEADS):
-        part = slice(head * size, (head + 1) * size)
-        scores = mm_tn(key[part], query[part]) + table[head]
+
+    def score(place, head):
+        return mm_tn(head_rows(key, place, head), head_rows(query, place, head)) + table[head]
+
+    def shift(place, head, scores):
         top = jnp.max(scores, axis=0, keepdims=True)
-        shifted = jnp.exp2(scores - top)
-        total = jnp.sum(shifted, axis=0, keepdims=True)
-        mixed.append(mm(value[part], shifted.astype(BF16)) / total)
-        totals.append(top + jnp.log2(total))
-    mixed = jnp.concatenate(mixed, axis=0)
-    save_total(jnp.concatenate(totals, axis=0))
-    save_mixed(mixed.astype(BF16))
+        return top, jnp.exp2(scores - top).astype(BF16)
+
+    def mix(place, head, items):
+        top, shifted = items
+        values = head_rows(value, place, head)
+        size = values.shape[0]
+        values = jnp.concatenate([values, jnp.ones((16, values.shape[1]), BF16)], axis=0)
+        result = mm(values, shifted)
+        total = result[size : size + 1]
+        return result[:size] / total, top + jnp.log2(total)
+
+    done = in_stages(ROW_BLOCKS, score, shift, mix)
+    mixed = gather_heads({block: items[0] for block, items in done.items()})
+    put_rows(totals, row, gather_heads({block: items[1] for block, items in done.items()}))
+    put_rows(mixed_out, row, mixed)
     return state + mm(output_t[...], (mixed * gate).astype(BF16))
 
 
@@ -888,16 +983,12 @@
     rows = source.shape[0]
 
     def body(row):
-        def save_total(values):
-            totals[row] = values
-
-        def save_mixed(values):
-            mixed[row] = values
-
-        state = attend_rows(source[row], cols, proj_t, output_t, table, save_total, save_mixed)
-        scratch[:, row, :] = state.T
-
-    each_row(rows, body)
+        state = attend_rows(
+            join(read_plain, source, row), row, cols, proj_t, output_t, table, totals, mixed
+        )
+        put_turned(scratch, row, state)
+
+    each_group(rows, body)
     store_flipped(out, scratch)
 
 
@@ -906,17 +997,12 @@
     rows = source.shape[1]
 
     def body(row):
-        def save_total(values):
-            totals[row] = values
-
-        def save_mixed(values):
-            mixed[row] = values
-
-        out[row] = attend_rows(
-            read_flipped(source, row), cols, proj_t, output_t, table, save_total, save_mixed
-        )
-
-    each_row(rows, body)
+        state = attend_rows(
+            join(read_flipped, source, row), row, cols, proj_t, output_t, table, totals, mixed
+        )
+        put_rows(out, row, state)
+
+    each_group(rows, body)
 
 
 def transition_kernel(
@@ -925,7 +1011,7 @@
     rows = source.shape[0]
 
     def body(row):
-        state = source[row]
+        state = join(read_plain, source, row)
         unit, inverse = standardize(state)
         lowered = (unit * column(cols, 0) + column(cols, 1)).astype(BF16)
         hidden = mm(up_t[...], lowered)
@@ -933,13 +1019,13 @@
         first = hidden[:half]
         mixed = (first * sigmoid(first) * hidden[half:]).astype(BF16)
         state = state + mm(down_t[...], mixed)
-        state_out[row] = state
-        scratch[:, row, :] = state.T
+        put_rows(state_out, row, state)
+        put_turned(scratch, row, state)
         unit, inverse = standardize(state)
         lowered = (unit * column(next_cols, 0) + column(next_cols, 1)).astype(BF16)
-        bias_scratch[:, row, :] = mm(bias_t[...], lowered)
-
-    each_row(rows, body)
+        put_inner(bias_scratch, row, mm(bias_t[...], lowered))
+
+    each_group(rows, body)
     size = pair_out.shape[0] // len(order)
     for place, held in enumerate(order):
         pair_out[place * size : (place + 1) * size] = scratch[held * size : (held + 1) * size].astype(BF16)
@@ -955,17 +1041,17 @@
     bias_scratch[...] = bias_grad[...].astype(F32)
 
     def body(row):
-        grad = read(cotangent, row)
-        unit, inverse = standardize(final[row])
+        grad = join(read, cotangent, row)
+        unit, inverse = standardize(join(read_plain, final, row))
         gain = column(next_cols, 0)
         lowered = (unit * gain + column(next_cols, 1)).astype(BF16)
-        grad_bias = bias_scratch[:, row, :].astype(BF16)
+        grad_bias = join(read_inner, bias_scratch, row).astype(BF16)
         bias_w_grad[...] += mm_nt(lowered, grad_bias)
         grad_lowered = mm(bias_w[...], grad_bias)
-        pair_gain[...] += grad_lowered * unit
-        pair_bias[...] += grad_lowered
+        add_lanes(pair_gain, grad_lowered * unit)
+        add_lanes(pair_bias, grad_lowered)
         grad = grad + standardize_back(unit, inverse, grad_lowered * gain)
-        unit, inverse = standardize(mid[row])
+        unit, inverse = standardize(join(read_plain, mid, row))
         gain = column(cols, 0)
         lowered = (unit * gain + column(cols, 1)).astype(BF16)
         hidden = mm(up_t[...], lowered)
@@ -985,11 +1071,11 @@
         )
         up_grad[...] += mm_nt(lowered, grad_hidden)
         grad_lowered = mm(up[...], grad_hidden)
-        norm_gain[...] += grad_lowered * unit
-        norm_bias[...] += grad_lowered
-        grad_out[row] = grad + standardize_back(unit, inverse, grad_lowered * gain)
-
-    each_row(rows, body)
+        add_lanes(norm_gain, grad_lowered * unit)
+        add_lanes(norm_bias, grad_lowered)
+        put_rows(grad_out, row, grad + standardize_back(unit, inverse, grad_lowered * gain))
+
+    each_group(rows, body)
 
     def finish():
         vecs[0:1] = lane_sums(norm_gain)
@@ -1010,39 +1096,53 @@
 
     def body(row):
         unit, inverse, lowered, query, key, value, gate = attention_row(
-            read(source, row), cols, proj_t
-        )
-        mixed = mixed_in[row].astype(F32)
-        total = totals[row]
-        grad_low = read_grad(grad_in, row).astype(BF16)
+            join(read, source, row), cols, proj_t
+        )
+        mixed = join(read_plain, mixed_in, row)
+        total = join(read_plain, totals, row)
+        grad_low = join(read_grad, grad_in, row).astype(BF16)
         gated = mixed * gate
         output_grad[...] += mm_nt(gated.astype(BF16), grad_low)
         grad_gated = mm(output[...], grad_low)
         grad_gate = grad_gated * gated * (1.0 - gate)
-        grad_mixed = grad_gated * gate
-        grad_mixed_low = grad_mixed.astype(BF16)
-        product = grad_mixed_low.astype(F32) * mixed
+        grad_mixed = (grad_gated * gate).astype(BF16)
+        product = grad_mixed.astype(F32) * mixed
         size = query.shape[0] // TA_HEADS
-        grad_query, grad_key, grad_value = [], [], []
-        for head in range(TA_HEADS):
-            part = slice(head * size, (head + 1) * size)
-            scores = mm_tn(key[part], query[part]) + table[head]
-            probs = jnp.exp2(scores - total[head : head + 1])
-            grad_probs = mm_tn(value[part], grad_mixed_low[part])
-            delta = jnp.sum(product[part], axis=0, keepdims=True)
-            grad_scores = probs * (grad_probs - delta)
+
+        def score(place, head):
+            scores = mm_tn(head_rows(key, place, head), head_rows(query, place, head))
+            grads = mm_tn(head_rows(value, place, head), head_rows(grad_mixed, place, head))
+            return scores + table[head], grads
+
+        def slope(place, head, items):
+            scores, grads = items
+            probs = jnp.exp2(scores - head_rows(total, place, head))
+            delta = jnp.sum(head_rows(product, place, head), axis=0, keepdims=True)
+            grad_scores = probs * (grads - delta)
             grad_table[head] += grad_scores
-            grad_scores = grad_scores.astype(BF16)
-            grad_query.append(mm(key[part], grad_scores) * size**-0.5)
-            grad_key.append(mm_nt(query[part], grad_scores) * (1.0 / LOG2E))
-            grad_value.append(mm_nt(grad_mixed_low[part], probs.astype(BF16)))
+            return probs.astype(BF16), grad_scores.astype(BF16)
+
+        def back(place, head, items):
+            probs, grad_scores = items
+            return (
+                mm(head_rows(key, place, head), grad_scores) * size**-0.5,
+                mm_nt(head_rows(query, place, head), grad_scores) * (1.0 / LOG2E),
+                mm_nt(head_rows(grad_mixed, place, head), probs),
+            )
+
+        done = in_stages(HEAD_BLOCKS, score, slope, back)
         grad_project = jnp.concatenate(
-            grad_query + grad_key + grad_value + [grad_gate], axis=0
+            [
+                gather_heads({block: items[part] for block, items in done.items()})
+                for part in range(3)
+            ]
+            + [grad_gate],
+            axis=0,
         ).astype(BF16)
         proj_grad[...] += mm_nt(lowered, grad_project)
-        grad_out[row] = mm(proj[...], grad_project).astype(grad_out.dtype)
-
-    each_row(rows, body)
+        put_rows(grad_out, row, mm(proj[...], grad_project))
+
+    each_group(rows, body)
 
     def finish():
         for head in range(TA_HEADS):
@@ -1061,8 +1161,8 @@
     lowered = (unit * gain + column(cols, 1)).astype(BF16)
     bias_w_grad[...] += mm_nt(lowered, grad_bias)
     grad_lowered = grad_lowered + mm(bias_w[...], grad_bias)
-    norm_gain[...] += grad_lowered * unit
-    norm_bias[...] += grad_lowered
+    add_lanes(norm_gain, grad_lowered * unit)
+    add_lanes(norm_bias, grad_lowered)
     return grad + standardize_back(unit, inverse, grad_lowered * gain)
 
 
@@ -1085,12 +1185,12 @@
 
     def body(row):
         grad = attention_end_row(
-            read_flipped(source, row), grad_in[row], grad_lowered[row].astype(F32),
-            bias_scratch[:, row, :].astype(BF16), cols, bias_w, bias_w_grad, norm_gain, norm_bias,
-        )
-        scratch[:, row, :] = grad.T
-
-    each_row(rows, body)
+            join(read_flipped, source, row), join(read_plain, grad_in, row),
+            join(read_plain, grad_lowered, row), join(read_inner, bias_scratch, row).astype(BF16), cols, bias_w, bias_w_grad, norm_gain, norm_bias,
+        )
+        put_turned(scratch, row, grad)
+
+    each_group(rows, body)
     store_flipped(grad_out, scratch)
 
     def finish():
@@ -1112,8 +1212,8 @@
     proj_grad[...] += mm_nt(out_low, grad_output)
     gate_grad[...] += mm_nt(lowered, grad_gate)
     grad_normed = mm(proj[...], grad_output)
-    out_gain[...] += grad_normed * tri_unit
-    out_bias[...] += grad_normed
+    add_lanes(out_gain, grad_normed * tri_unit)
+    add_lanes(out_bias, grad_normed)
     grad_tri = standardize_back(tri_unit, tri_inverse, grad_normed * column(cols, 2))
     return grad_tri, mm(gate_w[...], grad_gate)
 
@@ -1131,18 +1231,18 @@
 
     def body(row):
         grad = attention_end_row(
-            source[row], read_flipped(grad_in, row), grad_lowered[row].astype(F32),
-            bias_scratch[:, row, :].astype(BF16), cols, bias_w, bias_w_grad, norm_gain, norm_bias,
-        )
-        grad_out[row] = grad
+            join(read_plain, source, row), join(read_flipped, grad_in, row),
+            join(read_plain, grad_lowered, row), join(read_inner, bias_scratch, row).astype(BF16), cols, bias_w, bias_w_grad, norm_gain, norm_bias,
+        )
+        put_rows(grad_out, row, grad)
         grad_tri, back = tri_post_back_row(
-            below[row], tri_scratch[:, row, :], grad, tri_cols, proj_t, gate_t, proj, gate_w,
+            join(read_plain, below, row), join(read_inner, tri_scratch, row), grad, tri_cols, proj_t, gate_t, proj, gate_w,
             proj_grad, gate_grad, out_gain, out_bias,
         )
-        gate_back[row] = back.astype(gate_back.dtype)
-        tri_scratch[:, row, :] = grad_tri
-
-    each_row(rows, body)
+        put_rows(gate_back, row, back)
+        put_inner(tri_scratch, row, grad_tri)
+
+    each_group(rows, body)
     copy_blocks(tri_out, tri_scratch, tri_out.shape[0])
 
     def finish():
@@ -1170,7 +1270,7 @@
         out[:, 0, channel] = grad_first.astype(BF16).reshape(shape)
         out[:, 1, channel] = grad_second.astype(BF16).reshape(shape)
 
-    each_row(operands.shape[2], body)
+    each_channel(operands.shape[2], body)
 
 
 def tri_pre_back_row(
@@ -1187,8 +1287,8 @@
     grad_project = jnp.concatenate([grad_first.astype(BF16), grad_second.astype(BF16)], axis=0)
     proj_grad[...] += mm_nt(lowered, grad_project)
     grad_lowered = mm(proj[...], grad_project) + gate_back
-    norm_gain[...] += grad_lowered * unit
-    norm_bias[...] += grad_lowered
+    add_lanes(norm_gain, grad_lowered * unit)
+    add_lanes(norm_bias, grad_lowered)
     return grad + standardize_back(unit, inverse, grad_lowered * gain)
 
 
@@ -1216,18 +1316,19 @@
 
     def body(row):
         grad = tri_pre_back_row(
-            info, alive, row_base(rows) + row, source[row], scratch[:, row, :], gate_in[row].astype(F32),
-            grad_in[row], cols, proj_t, proj, proj_grad, norm_gain, norm_bias,
-        )
-        grad_out[row] = grad
+            info, alive, row_base(rows) + row, join(read_plain, source, row),
+            join(read_inner, scratch, row), join(read_plain, gate_in, row),
+            join(read_plain, grad_in, row), cols, proj_t, proj, proj_grad, norm_gain, norm_bias,
+        )
+        put_rows(grad_out, row, grad)
         grad_tri, back = tri_post_back_row(
-            read(below, row), tri_scratch[:, row, :], grad, tri_cols, out_t, gate_t, out_w, gate_w,
+            join(read, below, row), join(read_inner, tri_scratch, row), grad, tri_cols, out_t, gate_t, out_w, gate_w,
             out_grad, gate_grad, out_gain, out_bias,
         )
-        gate_back[row] = back.astype(gate_back.dtype)
-        tri_scratch[:, row, :] = grad_tri
-
-    each_row(rows, body)
+        put_rows(gate_back, row, back)
+        put_inner(tri_scratch, row, grad_tri)
+
+    each_group(rows, body)
     copy_blocks(tri_out, tri_scratch, tri_out.shape[0])
 
     def finish():
@@ -1249,12 +1350,14 @@
 
     def body(row):
         grad = tri_pre_back_row(
-            info, alive, row_base(rows) + row, read(source, row), scratch[:, row, :],
-            gate_in[row].astype(F32), grad_in[row], cols, proj_t, proj, proj_grad, norm_gain, norm_bias,
-        )
-        grad_out[row] = reorder(grad.T, order).astype(grad_out.dtype)
-
-    each_row(rows, body)
+            info, alive, row_base(rows) + row, join(read, source, row),
+            join(read_inner, scratch, row), join(read_plain, gate_in, row),
+            join(read_plain, grad_in, row), cols, proj_t, proj, proj_grad, norm_gain, norm_bias,
+        )
+        for place, part in enumerate(pieces_of(grad)):
+            grad_out[row + place] = reorder(part.T, order).astype(grad_out.dtype)
+
+    each_group(rows, body)
 
     def finish():
         vecs[0:1] = lane_sums(norm_gain)
@@ -1499,7 +1602,7 @@
     lax.fori_loop(0, RUN, one, 0)
 
 
-def whole_call(kernel, name, ins, outs, scratch):
+def whole_call(kernel, name, ins, outs, scratch, time=8):
     def spec(axis):
         return pl.BlockSpec(memory_space=pltpu.SMEM if axis == "smem" else pltpu.VMEM)
 
@@ -1510,6 +1613,7 @@
         out_shape=[jax.ShapeDtypeStruct(shape, dtype) for shape, dtype in outs],
         scratch_shapes=[pltpu.VMEM(shape, dtype) for shape, dtype in scratch],
         compiler_params=pltpu.CompilerParams(vmem_limit_bytes=VMEM_LIMIT),
+        cost_estimate=cost(time),
         name=name,
     )(*[array for array, axis in ins])
 
@@ -1646,7 +1750,7 @@
     return held
 
 
-def pair_path(pair, info, alive, orders, weights, cotangent, middle, group, parts):
+def pair_path(pair, info, alive, orders, weights, cotangent, middle, between, group, parts):
     rows, length, width = pair.shape
     hidden = weights[(OUTGOING, PROJ_OUT)].shape[0]
     devices = length // rows
@@ -1823,6 +1927,7 @@
     )
     grads[(ENDING, BIAS_PROJ)], grads[(ENDING, VECTORS)] = bias_w_grad, vecs
     grad_three = swap(flipped, group)
+    grad_three, *_ = after(grad_three, between(0, grads))
     lowered_grad, bias_grad = attention_back(
         STARTING, read_plain, read_flipped, state_two, 0, grad_three, 1, bias_one, totals_one, mixed_one
     )
@@ -1872,6 +1977,7 @@
         [wide, wide, wide, wide, product_scratch, tri_scratch],
     )
     grads[(INCOMING, VECTORS)] = vecs
+    between(1, grads)
     grad_tri = swap(grad_tri.reshape(tri_shape), group)
     product_grad = swap(
         products(
@@ -1933,23 +2039,26 @@
         runs_kernel, "parameter_runs", [(place, "smem"), (shard_rows, None)],
         [((STRIDE, RUN, STRIDE), BF16)], [((STRIDE, RUN, STRIDE), F32)],
     )
-    weights = unpack_pair(table, total, lax.all_gather(runs[:pair_lanes], line))
-    weights.update(
-        unpack_single(table, total, single_lane, lax.all_gather(runs[single_lane:], line))
-    )
+    rows, length, width = pair.shape[1:]
+    pair_in = swap(pair[0].reshape(parts, -1, length, width), "crop")
+    pair_in, first_runs, live = after(
+        pair_in, runs[:pair_lanes], swap(jnp.broadcast_to(lengths.astype(F32), (parts, STRIDE)), "crop")
+    )
+    pair_in = swap(pair_in, "z").reshape(rows, length, width)
+    weights = unpack_pair(table, total, lax.all_gather(first_runs, line))
+    pair_in, last_runs = after(pair_in, runs[single_lane:])
+    weights.update(unpack_single(table, total, single_lane, lax.all_gather(last_runs, line)))
     for index, name in enumerate(SINGLE_VECTORS):
         weights[name] = weights[(SINGLE, VECTORS)][index]
-    rows, length = pair.shape[1:3]
     size = rows // parts
     blocks = np.arange(length // size).reshape(parts, cores, parts)
     order = blocks.transpose(2, 1, 0).reshape(-1)
     orders = (order.tolist(), np.argsort(order).tolist())
     tokens = (order[:, None] * size + np.arange(size)).reshape(-1)
+    live = live[lax.axis_index("z"), 0]
     width = single.shape[2]
-    length_lanes = jnp.broadcast_to(lengths.astype(BF16), (rows, STRIDE))
-    both = jnp.concatenate([single[0], single_cotangent[0], length_lanes], axis=1)
-    both = to_plane(both, parts).astype(F32)
-    single_state, single_back, live = both[:, :width], both[:, width : 2 * width], both[0, 2 * width]
+    both = to_plane(jnp.concatenate([single[0], single_cotangent[0]], axis=1), parts).astype(F32)
+    single_state, single_back = both[:, :width], both[:, width:]
     mask = (tokens.astype(np.float32) < live).astype(F32)
     info = lax.dynamic_slice_in_dim(mask, lax.axis_index(group) * rows, rows).astype(jnp.int32)
     alive = jnp.broadcast_to(mask, (8, length))
@@ -1968,36 +2077,63 @@
         results["single_grad"] = grad + more
         return grad_scores
 
+    def reduce_runs(sent):
+        part = jnp.sum(swap(sent, line).astype(F32), axis=0).astype(BF16)
+        return jnp.sum(lax.all_gather(part, "crop").astype(F32), axis=0)
+
+    reduced = {}
+    lines_held = list(enumerate(SINGLE_VECTORS))
+    late_lanes = -(-table[(INCOMING, NORM_GAIN)][0] * STRIDE // count)
+
+    def lines():
+        values = jnp.concatenate([single_grads[name].reshape(1, S) for name in SINGLE_VECTORS], axis=0)
+        return jnp.pad(values, ((0, 8 - len(SINGLE_VECTORS)), (0, 0)))
+
+    def between(number, grads):
+        if number == 0:
+            sent = pack(
+                "single_gradient", table, total, devices, (pair_lanes, STRIDE), attend,
+                [(name, single_grads[name]) for name in SINGLE_MATRICES]
+                + [((ATTEND, PAIR_PROJ), grads[(ATTEND, PAIR_PROJ)])]
+                + [vector_part(grads, (PAIR, VECTORS), ATTEND), (lines_held, lines())],
+            )
+            reduced[2] = lax.psum(
+                lax.psum_scatter(sent, line, scatter_dimension=0, tiled=False), "crop"
+            ).astype(F32)
+            return sent
+        taken = -(-(pair_lanes * count - (attend + 2 * S // STRIDE) * STRIDE) // (4 * S))
+        first = table[(INCOMING, NORM_GAIN)][0]
+        sent = pack(
+            "pair_gradient", table, total, devices, (late_lanes, pair_lanes), first,
+            [(name, grads[name]) for name in PAIR_MATRICES if table[name][0] >= first]
+            + [(name, grads[name]) for name in ((STARTING, BIAS_PROJ), (ENDING, BIAS_PROJ))]
+            + [vector_part(grads, name, None) for name in ((ENDING, VECTORS), (STARTING, VECTORS))]
+            + [vector_part(grads, (INCOMING, VECTORS), INCOMING)]
+            + [vector_part(grads, (PAIR, VECTORS), PAIR)]
+            + [(lines_held[:2], lines()), ((ATTEND, QKVG), single_grads[(ATTEND, QKVG)][: -(-taken // 8) * 8])],
+        )
+        reduced[1] = reduce_runs(sent)
+        return sent
+
     pair_out, pair_grad, grads = pair_path(
-        to_plane(pair[0], parts), info, alive, orders, weights, pair_cotangent[0], middle, group, parts
+        pair_in, info, alive, orders, weights, pair_cotangent[0], middle, between, group, parts
     )
     pair_grad = from_plane(pair_grad, parts).astype(F32)
     both = from_plane(jnp.concatenate([results[SINGLE], results["single_grad"]], axis=1), parts)
     single_out, single_grad = both[:, :width].astype(BF16), both[:, width:]
-    grads.update(single_grads)
-    lines = jnp.concatenate([grads[name].reshape(1, S) for name in SINGLE_VECTORS], axis=0)
-    lines = (list(enumerate(SINGLE_VECTORS)), jnp.pad(lines, ((0, 8 - len(SINGLE_VECTORS)), (0, 0))))
-    single_runs = pack(
-        "single_gradient", table, total, devices, (pair_lanes, STRIDE), attend,
-        [(name, grads[name]) for name in SINGLE_MATRICES + ((ATTEND, PAIR_PROJ),)]
-        + [vector_part(grads, (PAIR, VECTORS), ATTEND), lines],
-    )
-    single_runs = lax.psum(
-        lax.psum_scatter(single_runs, line, scatter_dimension=0, tiled=False), "crop"
-    ).astype(F32)
-    early = -(-(pair_lanes * count - (attend + 2 * S // STRIDE) * STRIDE) // table[(ATTEND, QKVG)][1][1])
-    pair_runs = pack(
-        "pair_gradient", table, total, devices, (0, pair_lanes), 0,
-        [(name, grads[name]) for name in PAIR_MATRICES + ((STARTING, BIAS_PROJ), (ENDING, BIAS_PROJ))]
-        + [vector_part(grads, name, None) for name in HELD if name != (PAIR, VECTORS)]
-        + [vector_part(grads, (PAIR, VECTORS), PAIR)]
-        + [((lines[0][:2]), lines[1]), ((ATTEND, QKVG), grads[(ATTEND, QKVG)][: -(-early // 8) * 8])],
-    )
-    pair_runs = jnp.sum(swap(pair_runs, line).astype(F32), axis=0)
-    pair_runs = jnp.sum(lax.all_gather(pair_runs, "crop"), axis=0)
+    first = table[(INCOMING, NORM_GAIN)][0]
+    taken = -(-(late_lanes * count - (first + 2) * STRIDE) // (4 * H))
+    sent = pack(
+        "outgoing_gradient", table, total, devices, (0, late_lanes), 0,
+        [(name, grads[name]) for name in PAIR_MATRICES if table[name][0] < first]
+        + [vector_part(grads, (OUTGOING, VECTORS), None)]
+        + [vector_part(grads, (INCOMING, VECTORS), None)]
+        + [((INCOMING, PROJ_GATE), grads[(INCOMING, PROJ_GATE)][: -(-taken // 8) * 8])],
+    )
+    reduced[0] = reduce_runs(sent)
     shard, squares = whole_call(
         functools.partial(shard_kernel, shard_size), "gradient_share",
-        [(place, "smem"), (jnp.concatenate([pair_runs, single_runs], axis=0), None)],
+        [(place, "smem"), (jnp.concatenate([reduced[part] for part in range(3)], axis=0), None)],
         [((RUN * STRIDE, STRIDE), F32), ((8, STRIDE), F32)], [],
     )
     shard = shard.reshape(-1)[:shard_size]

time: 1460 us -> 1230 us (0.84)
  Pallas kernels: 630 us -> 415 us
  blocking collectives: 396 us -> 217 us
  waiting for transfers between devices: 249 us -> 359 us
  starting transfers between devices: 61.7 us -> 99.5 us
    pallas_call x18, Pallas kernels: 544 us -> 328 us  [run_rows(): pl.pallas_call(kernel, grid=(steps,), in_specs=in_specs, out_specs=out_sp...]
    all_to_all x13 -> x7, blocking collectives: 349 us -> 145 us  [swap(): lax.all_to_all(values, group, split_axis=0, concat_axis=0, tiled=True)]
    all_to_all x15 -> x23, waiting for transfers between devices: 133 us -> 278 us  [swap(): lax.all_to_all(values, group, split_axis=0, concat_axis=0, tiled=True)]
    all_to_all x15 -> x23, starting transfers between devices: 61.4 us -> 99.4 us  [swap(): lax.all_to_all(values, group, split_axis=0, concat_axis=0, tiled=True)]
    all_gather x3 -> x2, waiting for transfers between devices: 68.1 us -> 31.7 us  [the longest x1 31.7 us: fast_shards(): weights = unpack_pair(table, total, lax.all_gather(first_runs, line))]
    all_gather x0 -> x2, blocking collectives: none -> 17.5 us  [reduce_runs(): return jnp.sum(lax.all_gather(part, 'crop').astype(F32), axis=0)]
    pallas_call x6 -> x7, Pallas kernels: 85.8 us -> 87.5 us  [whole_call(): pl.pallas_call(kernel, in_specs=[spec(axis) for array, axis in ins], out_...]
  transfers between devices with their start and end apart: 20 -> 27, of which waited for: 11 -> 16; matrix products, arithmetic and copies ran while one was open for 5% -> 6% of each run, Pallas kernels for 25% -> 23%
where the time goes in v1:
time: 1230 us; the launch traced here: 1220 us
  Pallas kernels  415 us (34%)
  waiting for transfers between devices  359 us (29%)
  blocking collectives  217 us (18%)
  starting transfers between devices  99.5 us (8%)
  local copies, waits for them, and re-layouts  51.2 us (4%)
  matrix products  33.7 us (3%)
  other arithmetic  25.4 us (2%)
  between operations  17.4 us (1%)
    pallas_call x18, Pallas kernels, run_rows(): pl.pallas_call(kernel, grid=(steps,), in_specs=in_specs, out_specs=out_sp...  328 us
    all_to_all x23, waiting for transfers between devices, swap(): lax.all_to_all(values, group, split_axis=0, concat_axis=0, tiled=True)  278 us
    all_to_all x7, blocking collectives, swap(): lax.all_to_all(values, group, split_axis=0, concat_axis=0, tiled=True)  145 us
    all_to_all x23, starting transfers between devices, swap(): lax.all_to_all(values, group, split_axis=0, concat_axis=0, tiled=True)  99.4 us
    pallas_call x7, Pallas kernels, whole_call(): pl.pallas_call(kernel, in_specs=[spec(axis) for array, axis in ins], out_...  87.5 us
    psum x1, waiting for transfers between devices, between(): lax.psum(lax.psum_scatter(sent, line, scatter_dimension=0, tiled=False),...  46.4 us
    all_gather x1, waiting for transfers between devices, fast_shards(): weights = unpack_pair(table, total, lax.all_gather(first_runs, line))  31.7 us
  transfers between devices with their start and end apart: 27, of which 16 were waited for; matrix products, arithmetic and copies ran while one was open for 6% of the time, Pallas kernels for 23%

profile of v1, /device:TPU:0, one launch (start us, length us, event | category | flops | bytes accessed | tf_op | source)
XLA Modules:
  0.0 1218.8 jit_solution(4903933576700068046)
XLA Ops:
  7.8 9.6 all_to_all.154
  17.4 4.6 all-to-all-start
  23.9 5.9 parameter_runs.1
  31.4 14.4 %all-to-all-done = bf16[4,8,256,128]{3,2,1,0:T(8,128)(2,1)} async-done(((bf16[4,8,256,128]{3,2,1,0:T(8,128)(2,1)}), bf16[4,8,256,128]{3,2,1,0:T(8,128)(2,1)}, u32[]{:S(2)}, u32[]{:S(2)}) %all-to-all-start) | async-done | bytes 2097184 | tf_op jit(solution)/shard_map/all_to_all | solution.py:1671
  45.8 5.0 all-to-all-start.2
  54.3 31.7 %all-gather.10.cloned.1.call-done = bf16[192,24,128]{2,1,0:T(8,128)(2,1)} async-done(((bf16[24,24,128]{2,1,0:T(8,128)(2,1)}), bf16[192,24,128]{2,1,0:T(8,128)(2,1)}) %all-gather.10.cloned.1.call-update) | async-done | bytes 1179664 | tf_op jit(solution)/shard_map/all_gather | solution.py:2048
  86.0 7.9 pair_weights.1
  93.9 13.7 %all-to-all-done.2 = bf16[4,8,256,128]{3,2,1,0:T(8,128)(2,1)S(1)} async-done(((bf16[4,8,256,128]{3,2,1,0:T(8,128)(2,1)}), bf16[4,8,256,128]{3,2,1,0:T(8,128)(2,1)S(1)}, u32[]{:S(2)}, u32[]{:S(2)}) %all-to-all-start.2) | async-done | bytes 2097184 | tf_op jit(solution)/shard_map/all_to_all | solution.py:1671
  109.0 12.8 %outgoing_in.1 = bf16[8,2,16,32,256]{4,3,2,1,0:T(8,128)(2,1)} custom-call(s32[32]{0:T(128)} %dynamic-slice_convert_fusion.info, f32[8,256]{1,0:T(8,128)} %broadcast_in_dim.17.alive, bf16[32,256,128]{2,1,0:T(8,128)(2,1)} %bitcast.120, f32[128,8]{1,0:T(8,128)} %get-tuple-element.113.cols.tri_cols, bf16[512,128]{1,0:T(8,128)(2,1)} %get-tuple-element.114.proj_t), custom_call_target="tpu_custom_call" | custom-call | flops 15000000512 | bytes 45000000 | tf_op jit(solution)/shard_map/outgoing_in/pallas_call | solution.py:716
  121.7 53.5 %all_to_all.155.operands = bf16[8,2,16,32,256]{4,3,2,1,0:T(8,128)(2,1)} all-to-all(bf16[8,2,16,32,256]{4,3,2,1,0:T(8,128)(2,1)} %outgoing_in.1), channel_id=1, replica_groups=mesh['crop'=4,'z'=4,'core'=2] {'crop','core'}, dimensions={0} | all-to-all | bytes 8388608 | tf_op jit(solution)/shard_map/all_to_all | solution.py:1671
  175.3 6.2 outgoing_product.1
  185.9 25.9 %all-to-all-done.4 = bf16[8,16,32,256]{3,2,1,0:T(8,128)(2,1)S(1)} async-done(((bf16[8,16,32,256]{3,2,1,0:T(8,128)(2,1)}), bf16[8,16,32,256]{3,2,1,0:T(8,128)(2,1)S(1)}, u32[]{:S(2)}, u32[]{:S(2)}) %all-to-all-start.4) | async-done | bytes 2097184 | tf_op jit(solution)/shard_map/all_to_all | solution.py:1671
  215.7 21.4 %outgoing_out_incoming_in.1 = (f32[32,128,256]{2,1,0:T(8,128)}, bf16[8,2,16,32,256]{4,3,2,1,0:T(8,128)(2,1)}) custom-call(s32[32]{0:T(128)} %dynamic-slice_convert_fusion.info, f32[8,256]{1,0:T(8,128)} %broadcast_in_dim.17.alive, bf16[32,256,128]{2,1,0:T(8,128)(2,1)} %bitcast.121, bf16[128,32,256]{2,1,0:T(8,128)(2,1)} %bitcast.124, ...), custom_call_target="tpu_custom_call" | custom-call | flops 15000000512 | bytes 45000000 | tf_op jit(solution)/shard_map/outgoing_out_incoming_in/pallas_call | solution.py:716
  237.1 4.6 all-to-all-start.5
  242.5 48.4 %all-to-all-done.5.operands = bf16[8,2,16,32,256]{4,3,2,1,0:T(8,128)(2,1)} async-done(((bf16[8,2,16,32,256]{4,3,2,1,0:T(8,128)(2,1)}), bf16[8,2,16,32,256]{4,3,2,1,0:T(8,128)(2,1)}, u32[]{:S(2)}, u32[]{:S(2)}) %all-to-all-start.5) | async-done | bytes 4194336 | tf_op jit(solution)/shard_map/all_to_all | solution.py:1671
  290.9 5.2 all-to-all-start.11
  296.0 6.3 incoming_product.1
  302.3 4.5 all-to-all-start.6
  310.6 22.9 %all-to-all-done.6 = bf16[8,16,32,256]{3,2,1,0:T(8,128)(2,1)} async-done(((bf16[8,16,32,256]{3,2,1,0:T(8,128)(2,1)}), bf16[8,16,32,256]{3,2,1,0:T(8,128)(2,1)}, u32[]{:S(2)}, u32[]{:S(2)}) %all-to-all-start.6) | async-done | bytes 2097184 | tf_op jit(solution)/shard_map/all_to_all | solution.py:1671
  337.8 13.9 %incoming_out_starting_bias.1 = (f32[32,128,256]{2,1,0:T(8,128)}, bf16[4,32,256]{2,1,0:T(8,128)(2,1)}) custom-call(f32[32,128,256]{2,1,0:T(8,128)} %get-tuple-element.119.source.below, bf16[128,32,256]{2,1,0:T(8,128)(2,1)} %bitcast.9.tri_in, f32[128,8]{1,0:T(8,128)} %get-tuple-element.117.next_cols.cols.tri_cols, ...), custom_call_target="tpu_custom_call" | custom-call | flops 15000000512 | bytes 45000000 | tf_op jit(solution)/shard_map/incoming_out_starting_bias/pallas_call | solution.py:716
  351.7 17.8 %all-gather.1 = bf16[32,32,256]{2,1,0:T(8,128)(2,1)} all-gather(bf16[4,32,256]{2,1,0:T(8,128)(2,1)} %get-tuple-element.126), channel_id=3, replica_groups=mesh['crop'=4,'z'=4,'core'=2] {'crop','core'}, dimensions={0}, use_global_device_ids=true | all-gather | bytes 589824 | tf_op jit(solution)/shard_map/all_gather | solution.py:1830
  369.6 20.4 %starting_attention.1 = (bf16[8,32,32,128]{3,2,1,0:T(8,128)(2,1)}, f32[32,4,256]{2,1,0:T(4,128)}, bf16[32,128,256]{2,1,0:T(8,128)(2,1)}) custom-call(f32[8,256]{1,0:T(8,128)} %broadcast_in_dim.17.alive, f32[32,128,256]{2,1,0:T(8,128)} %get-tuple-element.125.source, bf16[8,4,32,256]{3,2,1,0:T(8,128)(2,1)} %bitcast.138, ...), custom_call_target="tpu_custom_call" | custom-call | flops 15000000512 | bytes 45000000 | tf_op jit(solution)/shard_map/starting_attention/pallas_call | solution.py:716
  394.6 28.3 %single_weights.1 = (bf16[384,1536]{1,0:T(8,128)(2,1)}, bf16[384,384]{1,0:T(8,128)(2,1)}, bf16[384,3072]{1,0:T(8,128)(2,1)}, bf16[1536,384]{1,0:T(8,128)(2,1)}, ...) custom-call(bf16[8,105,24,128]{3,2,1,0:T(8,128)(2,1)} %bitcast.154), custom_call_target="tpu_custom_call" | custom-call | flops 8000000000 | bytes 24000000 | tf_op jit(solution)/shard_map/single_weights/pallas_call | solution.py:1609
  425.7 5.1 all-to-all-start.9
  432.6 11.0 all_gather.53
  443.6 5.1 ending_bias.1
  448.8 11.1 all-gather.2
  459.9 19.1 %ending_attention.1 = (f32[32,128,256]{2,1,0:T(8,128)}, f32[32,4,256]{2,1,0:T(4,128)}, bf16[32,128,256]{2,1,0:T(8,128)(2,1)}) custom-call(f32[8,256]{1,0:T(8,128)} %broadcast_in_dim.17.alive, bf16[8,32,32,128]{3,2,1,0:T(8,128)(2,1)} %copy-done.12, bf16[8,4,32,256]{3,2,1,0:T(8,128)(2,1)} %bitcast.140, f32[128,8]{1,0:T(8,128)} %get-tuple-element.130.cols, ...), custom_call_target="tpu_custom_call" | custom-call | flops 15000000512 | bytes 45000000 | tf_op jit(solution)/shard_map/ending_attention/pallas_call | solution.py:716
  479.7 14.9 %pair_transition.1 = (f32[32,128,256]{2,1,0:T(8,128)}, bf16[256,32,128]{2,1,0:T(8,128)(2,1)}, bf16[16,32,256]{2,1,0:T(8,128)(2,1)}) custom-call(f32[32,128,256]{2,1,0:T(8,128)} %get-tuple-element.135.source.mid, f32[128,8]{1,0:T(8,128)} %get-tuple-element.136.cols, bf16[1024,128]{1,0:T(8,128)(2,1)} %get-tuple-element.137.up_t, ...), custom_call_target="tpu_custom_call" | custom-call | flops 15000000512 | bytes 45000000 | tf_op jit(solution)/shard_map/pair_transition/pallas_call | solution.py:716
  498.1 4.5 all-to-all-start.12
  503.6 5.8 all-to-all-done.12
  535.1 10.0 all_to_all.156
  557.4 30.8 %pair_transition_back.1 = (f32[32,128,256]{2,1,0:T(8,128)}, f32[128,1024]{1,0:T(8,128)}, f32[512,128]{1,0:T(8,128)}, f32[128,16]{1,0:T(8,128)}, f32[8,128]{1,0:T(8,128)}) custom-call(f32[32,128,256]{2,1,0:T(8,128)} %get-tuple-element.135.source.mid, f32[32,128,256]{2,1,0:T(8,128)} %get-tuple-element.142.final, bf16[8,32,32,128]{3,2,1,0:T(8,128)(2,1)} %bitcast.16.cotangent, ...), custom_call_target="tpu_custom_call" | custom-call | flops 15000000512 | bytes 45000000 | tf_op jit(solution)/shard_map/pair_transition_back/pallas_call | solution.py:716
  588.2 8.6 all-to-all-done.14
  596.8 33.8 %attention_back.2 = (bf16[32,128,256]{2,1,0:T(8,128)(2,1)}, bf16[8,4,32,256]{3,2,1,0:T(8,128)(2,1)}, f32[128,512]{1,0:T(8,128)}, f32[128,128]{1,0:T(8,128)}) custom-call(f32[8,256]{1,0:T(8,128)} %broadcast_in_dim.17.alive, bf16[8,32,32,128]{3,2,1,0:T(8,128)(2,1)} %copy-done.12, f32[32,128,256]{2,1,0:T(8,128)} %get-tuple-element.155.grad_in, ...), custom_call_target="tpu_custom_call" | custom-call | flops 15000000512 | bytes 45000000 | tf_op jit(solution)/shard_map/attention_back/pallas_call | solution.py:716
  630.6 13.9 %all_to_all.157.bias_grad = bf16[8,4,32,256]{3,2,1,0:T(8,128)(2,1)} all-to-all(bf16[8,4,32,256]{3,2,1,0:T(8,128)(2,1)} %get-tuple-element.160), channel_id=1, replica_groups=mesh['crop'=4,'z'=4,'core'=2] {'crop','core'}, dimensions={0} | all-to-all | bytes 1048576 | tf_op jit(solution)/shard_map/all_to_all | solution.py:1671
  668.3 6.5 all-to-all-done.16
  678.9 12.0 ending_attention_end.1
  708.5 30.3 %single_gradient.1 = bf16[8,104,24,128]{3,2,1,0:T(8,128)(2,1)} custom-call(f32[384,1536]{1,0:T(8,128)} %fusion.21.refs_0_, f32[384,384]{1,0:T(8,128)} %fusion.27.refs_1_, f32[384,3072]{1,0:T(8,128)} %fusion.23.refs_2_, f32[1536,384]{1,0:T(8,128)} %fusion.31.refs_3_, f32[128,16]{1,0:T(8,128)} %get-tuple-element.167.refs_4_, ...), custom_call_target="tpu_custom_call" | custom-call | flops 8000000000 | bytes 24000000 | tf_op jit(solution)/shard_map/single_gradient/pallas_call | solution.py:1609
  738.8 33.5 %attention_back.3 = (bf16[32,128,256]{2,1,0:T(8,128)(2,1)}, bf16[8,4,32,256]{3,2,1,0:T(8,128)(2,1)}, f32[128,512]{1,0:T(8,128)}, f32[128,128]{1,0:T(8,128)}) custom-call(f32[8,256]{1,0:T(8,128)} %broadcast_in_dim.17.alive, f32[32,128,256]{2,1,0:T(8,128)} %get-tuple-element.125.source, bf16[8,32,32,128]{3,2,1,0:T(8,128)(2,1)} %all-to-all-done.20.grad_in, ...), custom_call_target="tpu_custom_call" | custom-call | flops 15000000512 | bytes 45000000 | tf_op jit(solution)/shard_map/attention_back/pallas_call | solution.py:716
  772.3 14.4 %all_to_all.158.bias_grad = bf16[8,4,32,256]{3,2,1,0:T(8,128)(2,1)} all-to-all(bf16[8,4,32,256]{3,2,1,0:T(8,128)(2,1)} %get-tuple-element.175), channel_id=1, replica_groups=mesh['crop'=4,'z'=4,'core'=2] {'crop','core'}, dimensions={0} | all-to-all | bytes 1048576 | tf_op jit(solution)/shard_map/all_to_all | solution.py:1671
  786.7 26.6 %starting_end_incoming_out_back.1 = (f32[32,128,256]{2,1,0:T(8,128)}, bf16[128,32,256]{2,1,0:T(8,128)(2,1)}, bf16[32,128,256]{2,1,0:T(8,128)(2,1)}, f32[128,8]{1...) custom-call(f32[32,128,256]{2,1,0:T(8,128)} %get-tuple-element.125.source, ...), custom_call_target="tpu_custom_call" | custom-call | flops 15000000512 | bytes 45000000 | tf_op jit(solution)/shard_map/starting_end_incoming_out_back/pallas_call | solution.py:716
  813.3 30.9 %all_to_all.159.grad = bf16[8,16,32,256]{3,2,1,0:T(8,128)(2,1)} all-to-all(bf16[8,16,32,256]{3,2,1,0:T(8,128)(2,1)} %bitcast.130), channel_id=1, replica_groups=mesh['crop'=4,'z'=4,'core'=2] {'crop','core'}, dimensions={0} | all-to-all | bytes 4194304 | tf_op jit(solution)/shard_map/all_to_all | solution.py:1671
  844.2 7.3 incoming_product_back.1
  851.6 4.7 all-to-all-start.23
  858.5 46.9 %all-to-all-done.23.product_grad = bf16[8,2,16,32,256]{4,3,2,1,0:T(8,128)(2,1)} async-done(((bf16[8,2,16,32,256]{4,3,2,1,0:T(8,128)(2,1)}), bf16[8,2,16,32,256]{4,3,2,1,0:T(8,128)(2,1)}, u32[]{:S(2)}, u32[]{:S(2)}) %all-to-all-start.23) | async-done | bytes 4194336 | tf_op jit(solution)/shard_map/all_to_all | solution.py:1671
  909.4 36.6 %incoming_in_outgoing_out_back.1 = (f32[32,128,256]{2,1,0:T(8,128)}, bf16[128,32,256]{2,1,0:T(8,128)(2,1)}, bf16[32,128,256]{2,1,0:T(8,128)(2,1)}, f32[128,512]{...) custom-call(s32[32]{0:T(128)} %dynamic-slice_convert_fusion.info, ...), custom_call_target="tpu_custom_call" | custom-call | flops 15000000512 | bytes 45000000 | tf_op jit(solution)/shard_map/incoming_in_outgoing_out_back/pallas_call | solution.py:716
  946.0 4.4 all-to-all-start.24
  951.1 25.9 %all-to-all-done.24.grad = bf16[8,16,32,256]{3,2,1,0:T(8,128)(2,1)} async-done(((bf16[8,16,32,256]{3,2,1,0:T(8,128)(2,1)}), bf16[8,16,32,256]{3,2,1,0:T(8,128)(2,1)}, u32[]{:S(2)}, u32[]{:S(2)}) %all-to-all-start.24) | async-done | bytes 2097184 | tf_op jit(solution)/shard_map/all_to_all | solution.py:1671
  980.3 7.3 outgoing_product_back.1
  987.6 4.6 all-to-all-start.25
  995.2 7.0 pair_gradient.1
  1002.2 39.1 %all-to-all-done.25.product_grad = bf16[8,2,16,32,256]{4,3,2,1,0:T(8,128)(2,1)} async-done(((bf16[8,2,16,32,256]{4,3,2,1,0:T(8,128)(2,1)}), bf16[8,2,16,32,256]{4,3,2,1,0:T(8,128)(2,1)}, u32[]{:S(2)}, u32[]{:S(2)}) %all-to-all-start.25) | async-done | bytes 4194336 | tf_op jit(solution)/shard_map/all_to_all | solution.py:1671
  1041.3 5.0 all-to-all-start.29
  1046.3 19.9 %outgoing_in_back.1 = (bf16[32,256,128]{2,1,0:T(8,128)(2,1)}, f32[128,512]{1,0:T(8,128)}, f32[8,128]{1,0:T(8,128)}) custom-call(s32[32]{0:T(128)} %dynamic-slice_convert_fusion.info, f32[8,256]{1,0:T(8,128)} %broadcast_in_dim.17.alive, bf16[32,256,128]{2,1,0:T(8,128)(2,1)} %bitcast.123, bf16[8,2,16,32,256]{4,3,2,1,0:T(8,128)(2,1)} %all-to-all-done.25.product_grad, ...), custom_call_target="tpu_custom_call" | custom-call | flops 15000000512 | bytes 45000000 | tf_op jit(solution)/shard_map/outgoing_in_back/pallas_call | solution.py:716
  1070.5 13.1 %all_to_all.160 = bf16[8,5,24,128]{3,2,1,0:T(8,128)(2,1)S(1)} all-to-all(bf16[8,5,24,128]{3,2,1,0:T(8,128)(2,1)} %outgoing_gradient.1), channel_id=1, replica_groups=mesh['crop'=4,'z'=4,'core'=2] {'z','core'}, dimensions={0} | all-to-all | bytes 491520 | tf_op jit(solution)/shard_map/all_to_all | solution.py:1671
  1083.6 4.5 all-to-all-start.26
  1091.8 46.4 %all-reduce.6.cloned.1.call-done = bf16[104,24,128]{2,1,0:T(8,128)(2,1)} async-done(((bf16[104,24,128]{2,1,0:T(8,128)(2,1)}), bf16[104,24,128]{2,1,0:T(8,128)(2,1)}) %all-reduce.6.cloned.1.call-update) | async-done | bytes 638992 | tf_op jit(solution)/shard_map/psum | solution.py:2100
  1139.4 9.8 all-gather.5
  1149.3 7.7 all-gather.4
  1158.3 5.2 gradient_share.1
  1163.6 14.3 %all-gather.6 = f32[64,128]{1,0:T(8,128)S(1)} all-gather(f32[8,128]{1,0:T(8,128)} %get-tuple-element.209), channel_id=8, replica_groups=mesh['crop'=4,'z'=4,'core'=2] {'z','core'}, dimensions={0}, use_global_device_ids=true | all-gather | bytes 36864 | tf_op jit(solution)/shard_map/all_gather | solution.py:2140
  1182.9 7.5 multiply_subtract_fusion
  1190.4 18.1 %all-to-all-done.27 = bf16[4,8,256,128]{3,2,1,0:T(8,128)(2,1)S(1)} async-done(((bf16[4,8,256,128]{3,2,1,0:T(8,128)(2,1)}), bf16[4,8,256,128]{3,2,1,0:T(8,128)(2,1)S(1)}, u32[]{:S(2)}, u32[]{:S(2)}) %all-to-all-start.27) | async-done | bytes 2097184 | tf_op jit(solution)/shard_map/all_to_all | solution.py:1671
  (224 shorter events, 153.2 us)
Async XLA Ops:
  17.4 5.2 copy-start.2
  17.4 28.4 %all-to-all-start = ((bf16[4,8,256,128]{3,2,1,0:T(8,128)(2,1)}), bf16[4,8,256,128]{3,2,1,0:T(8,128)(2,1)}, u32[]{:S(2)}, u32[]{:S(2)}) async-start(bf16[4,8,256,128]{3,2,1,0:T(8,128)(2,1)} %bitcast.118), calls=%async_computation | async-start | bytes 4194304 | tf_op jit(solution)/shard_map/all_to_all | solution.py:1671
  45.8 5.7 copy-start.20
  45.8 7.2 copy-start.43
  45.8 61.8 %all-to-all-start.2 = ((bf16[4,8,256,128]{3,2,1,0:T(8,128)(2,1)}), bf16[4,8,256,128]{3,2,1,0:T(8,128)(2,1)S(1)}, u32[]{:S(2)}, u32[]{:S(2)}) async-start(bf16[4,8,256,128]{3,2,1,0:T(8,128)(2,1)} %all-to-all-done), calls=%async_computation.2 | async-start | bytes 4194304 | tf_op jit(solution)/shard_map/all_to_all | solution.py:1671
  50.8 35.1 %all-gather.10.cloned.1.call-start = ((), (), s32[]{:S(2)}) async-start(), calls=%async_computation.33 | async-start | bytes 1327104 | tf_op jit(solution)/shard_map/all_gather | solution.py:2048
  181.5 3.8 copy-start.30
  181.5 3.8 copy-start.31
  181.5 30.3 %all-to-all-start.4 = ((bf16[8,16,32,256]{3,2,1,0:T(8,128)(2,1)}), bf16[8,16,32,256]{3,2,1,0:T(8,128)(2,1)S(1)}, u32[]{:S(2)}, u32[]{:S(2)}) async-start(bf16[8,16,32,256]{3,2,1,0:T(8,128)(2,1)} %outgoing_product.1), calls=%async_computation.4 | async-start | bytes 4194304 | tf_op jit(solution)/shard_map/all_to_all | solution.py:1671
  211.8 3.9 copy-start.11
  211.8 25.3 %all-to-all-start.10 = ((bf16[4,8,768]{2,1,0:T(8,128)(2,1)}), bf16[4,8,768]{2,1,0:T(8,128)(2,1)}, u32[]{:S(2)}, u32[]{:S(2)}) async-start(bf16[4,8,768]{2,1,0:T(8,128)(2,1)} %pad_maximum_fusion.3), calls=%async_computation.10 | async-start | bytes 98304 | tf_op jit(solution)/shard_map/all_to_all | solution.py:1671
  237.1 53.7 %all-to-all-start.5 = ((bf16[8,2,16,32,256]{4,3,2,1,0:T(8,128)(2,1)}), bf16[8,2,16,32,256]{4,3,2,1,0:T(8,128)(2,1)}, u32[]{:S(2)}, u32[]{:S(2)}) async-start(bf16[8,2,16,32,256]{4,3,2,1,0:T(8,128)(2,1)} %get-tuple-element.120), calls=%async_computation.5 | async-start | bytes 8388608 | tf_op jit(solution)/shard_map/all_to_all | solution.py:1671
  241.7 152.9 %all-gather.12.cloned.1.call-start = ((), (), s32[]{:S(2)}) async-start(), calls=%async_computation.34 | async-start | bytes 5806080 | tf_op jit(solution)/shard_map/all_gather | solution.py:2050
  290.9 11.5 all-to-all-start.11
  302.3 4.5 copy-start.9
  302.3 31.1 %all-to-all-start.6 = ((bf16[8,16,32,256]{3,2,1,0:T(8,128)(2,1)}), bf16[8,16,32,256]{3,2,1,0:T(8,128)(2,1)}, u32[]{:S(2)}, u32[]{:S(2)}) async-start(bf16[8,16,32,256]{3,2,1,0:T(8,128)(2,1)} %incoming_product.1), calls=%async_computation.6 | async-start | bytes 4194304 | tf_op jit(solution)/shard_map/all_to_all | solution.py:1671
  333.5 56.4 %all-to-all-start.8 = ((bf16[8,32,32,128]{3,2,1,0:T(8,128)(2,1)}), bf16[8,32,32,128]{3,2,1,0:T(8,128)(2,1)}, u32[]{:S(2)}, u32[]{:S(2)}) async-start(bf16[8,32,32,128]{3,2,1,0:T(8,128)(2,1)} %bitcast.14), calls=%async_computation.8 | async-start | bytes 4194304 | tf_op jit(solution)/shard_map/all_to_all | solution.py:1671
  389.9 34.4 %all-to-all-start.7 = ((bf16[8,32,32,128]{3,2,1,0:T(8,128)(2,1)}), bf16[8,32,32,128]{3,2,1,0:T(8,128)(2,1)S(1)}, u32[]{:S(2)}, u32[]{:S(2)}) async-start(bf16[8,32,32,128]{3,2,1,0:T(8,128)(2,1)} %get-tuple-element.129), calls=%async_computation.7 | async-start | bytes 4194304 | tf_op jit(solution)/shard_map/all_to_all | solution.py:1671
  393.6 37.2 %copy-start.4 = (f32[32,768]{1,0:T(8,128)}, f32[32,768]{1,0:T(8,128)S(1)}, u32[]{:S(2)}) copy-start(f32[32,768]{1,0:T(8,128)S(1)} %bitcast_convert_fusion.1) | copy-start | bytes 294916
  393.7 37.1 %copy-start.35 = (f32[32]{0:T(128)}, f32[32]{0:T(128)S(1)}, u32[]{:S(2)}) copy-start(f32[32]{0:T(128)S(1)} %broadcast_multiply_fusion.1) | copy-start | bytes 388
  393.9 29.0 %copy-start.44 = (f32[32]{0:T(128)}, f32[32]{0:T(128)S(1)}, u32[]{:S(2)}) copy-start(f32[32]{0:T(128)S(1)} %multiply_reduce_fusion.6) | copy-start | bytes 388
  393.9 36.9 %copy-start.38 = (f32[32]{0:T(128)}, f32[32]{0:T(128)S(1)}, u32[]{:S(2)}) copy-start(f32[32]{0:T(128)S(1)} %fusion.33) | copy-start | bytes 388
  424.3 6.5 copy-start.33
  424.3 6.5 copy-start.3
  425.7 54.0 %all-to-all-start.9 = ((bf16[4,2,32,32,128]{4,3,2,1,0:T(8,128)(2,1)}), bf16[4,2,32,32,128]{4,3,2,1,0:T(8,128)(2,1)}, u32[]{:S(2)}, u32[]{:S(2)}) async-start(bf16[4,2,32,32,128]{4,3,2,1,0:T(8,128)(2,1)} %bitcast.15), calls=%async_computation.9 | async-start | bytes 4194304 | tf_op jit(solution)/shard_map/all_to_all | solution.py:1671
  496.5 6.1 copy-start.16
  498.1 11.4 all-to-all-start.12
  502.8 12.2 %copy-start.15 = (bf16[256,384]{0,1:T(8,128)(2,1)}, bf16[256,384]{0,1:T(8,128)(2,1)S(1)}, u32[]{:S(2)}) copy-start(bf16[256,384]{0,1:T(8,128)(2,1)S(1)} %copy.71) | copy-start | bytes 589828
  517.2 8.0 copy-start
  522.8 3.7 copy-start.5
  522.8 3.7 copy-start.18
  525.0 4.0 copy-start.7
  525.0 4.0 copy-start.37
  525.2 3.8 copy-start.41
  528.9 3.7 copy-start.14
  545.1 51.7 %all-to-all-start.14 = ((bf16[4,64,32,128]{3,2,1,0:T(8,128)(2,1)}), bf16[4,64,32,128]{3,2,1,0:T(8,128)(2,1)S(1)}, u32[]{:S(2)}, u32[]{:S(2)}) async-start(bf16[4,64,32,128]{3,2,1,0:T(8,128)(2,1)} %bitcast.126), calls=%async_computation.14 | async-start | bytes 4194304 | tf_op jit(solution)/shard_map/all_to_all | solution.py:1671
  596.8 33.8 %copy-start.1 = (bf16[4,64,32,128]{3,2,1,0:T(8,128)(2,1)}, bf16[4,64,32,128]{3,2,1,0:T(8,128)(2,1)S(1)}, u32[]{:S(2)}) copy-start(bf16[4,64,32,128]{3,2,1,0:T(8,128)(2,1)S(1)} %all-to-all-done.14) | copy-start | bytes 6291460
  644.4 30.4 %all-to-all-start.16 = ((bf16[8,32,32,128]{3,2,1,0:T(8,128)(2,1)}), bf16[8,32,32,128]{3,2,1,0:T(8,128)(2,1)S(1)}, u32[]{:S(2)}, u32[]{:S(2)}) async-start(bf16[8,32,32,128]{3,2,1,0:T(8,128)(2,1)} %bitcast.114), calls=%async_computation.16 | async-start | bytes 4194304 | tf_op jit(solution)/shard_map/all_to_all | solution.py:1671
  674.8 16.1 %all-to-all-start.17 = ((bf16[8,32,768]{2,1,0:T(8,128)(2,1)}), bf16[8,32,768]{2,1,0:T(8,128)(2,1)}, u32[]{:S(2)}, u32[]{:S(2)}) async-start(bf16[8,32,768]{2,1,0:T(8,128)(2,1)} %pad_maximum_fusion.1), calls=%async_computation.17 | async-start | bytes 786432 | tf_op jit(solution)/shard_map/all_to_all | solution.py:1671
  691.0 7.8 copy-start.42
  691.0 7.8 copy-start.32
  691.0 47.8 %all-to-all-start.20 = ((bf16[8,32,32,128]{3,2,1,0:T(8,128)(2,1)}), bf16[8,32,32,128]{3,2,1,0:T(8,128)(2,1)}, u32[]{:S(2)}, u32[]{:S(2)}) async-start(bf16[8,32,32,128]{3,2,1,0:T(8,128)(2,1)} %get-tuple-element.166), calls=%async_computation.20 | async-start | bytes 4194304 | tf_op jit(solution)/shard_map/all_to_all | solution.py:1671
  698.8 5.2 copy-start.6
  698.8 5.2 copy-start.26
  698.8 5.2 copy-start.36
  698.8 5.2 copy-start.39
  698.8 7.6 copy-start.34
  851.5 4.8 copy-start.8
  851.5 4.8 copy-start.19
  851.5 6.0 copy-start.45
  851.5 6.0 copy-start.46
  851.6 6.0 copy-start.28
  851.6 6.0 copy-start.40
  851.6 6.2 copy-start.24
  851.6 53.8 %all-to-all-start.23 = ((bf16[8,2,16,32,256]{4,3,2,1,0:T(8,128)(2,1)}), bf16[8,2,16,32,256]{4,3,2,1,0:T(8,128)(2,1)}, u32[]{:S(2)}, u32[]{:S(2)}) async-start(bf16[8,2,16,32,256]{4,3,2,1,0:T(8,128)(2,1)} %incoming_product_back.1), calls=%async_computation.23 | async-start | bytes 8388608 | tf_op jit(solution)/shard_map/all_to_all | solution.py:1671
  905.4 40.6 %all-to-all-start.18 = ((f32[4,8,768]{2,1,0:T(8,128)}), f32[4,8,768]{2,1,0:T(8,128)}, u32[]{:S(2)}, u32[]{:S(2)}) async-start(f32[4,8,768]{2,1,0:T(8,128)} %maximum_bitcast_fusion), calls=%async_computation.18 | async-start | bytes 196608 | tf_op jit(solution)/shard_map/all_to_all | solution.py:1671
  946.0 31.0 %all-to-all-start.24 = ((bf16[8,16,32,256]{3,2,1,0:T(8,128)(2,1)}), bf16[8,16,32,256]{3,2,1,0:T(8,128)(2,1)}, u32[]{:S(2)}, u32[]{:S(2)}) async-start(bf16[8,16,32,256]{3,2,1,0:T(8,128)(2,1)} %bitcast.129), calls=%async_computation.24 | async-start | bytes 4194304 | tf_op jit(solution)/shard_map/all_to_all | solution.py:1671
  950.4 137.7 %reduce-scatter.2.cloned.1.call-start = ((), (), s32[]{:S(2)}) async-start(), calls=%async_computation.31 | async-start | bytes 5750784 | tf_op jit(solution)/shard_map/reduce_scatter | solution.py:2101
  977.0 10.6 all-to-all-start.19
  987.6 53.7 %all-to-all-start.25 = ((bf16[8,2,16,32,256]{4,3,2,1,0:T(8,128)(2,1)}), bf16[8,2,16,32,256]{4,3,2,1,0:T(8,128)(2,1)}, u32[]{:S(2)}, u32[]{:S(2)}) async-start(bf16[8,2,16,32,256]{4,3,2,1,0:T(8,128)(2,1)} %outgoing_product_back.1), calls=%async_computation.25 | async-start | bytes 8388608 | tf_op jit(solution)/shard_map/all_to_all | solution.py:1671
  1041.3 29.2 %all-to-all-start.29 = ((bf16[8,19,24,128]{3,2,1,0:T(8,128)(2,1)}), bf16[8,19,24,128]{3,2,1,0:T(8,128)(2,1)S(1)}, u32[]{:S(2)}, u32[]{:S(2)}) async-start(bf16[8,19,24,128]{3,2,1,0:T(8,128)(2,1)} %pair_gradient.1), calls=%async_computation.29 | async-start | bytes 1867776 | tf_op jit(solution)/shard_map/all_to_all | solution.py:1671
  1083.6 95.7 %all-to-all-start.26 = ((bf16[4,8,256,128]{3,2,1,0:T(8,128)(2,1)}), bf16[4,8,256,128]{3,2,1,0:T(8,128)(2,1)}, u32[]{:S(2)}, u32[]{:S(2)}) async-start(bf16[4,8,256,128]{3,2,1,0:T(8,128)(2,1)} %bitcast.127), calls=%async_computation.26 | async-start | bytes 4194304 | tf_op jit(solution)/shard_map/all_to_all | solution.py:1671
  1088.0 50.1 %all-reduce.6.cloned.1.call-start = ((), (), s32[]{:S(2)}) async-start(), calls=%async_computation.32 | async-start | bytes 1277952 | tf_op jit(solution)/shard_map/psum | solution.py:2100
  1179.3 29.2 %all-to-all-start.27 = ((bf16[4,8,256,128]{3,2,1,0:T(8,128)(2,1)}), bf16[4,8,256,128]{3,2,1,0:T(8,128)(2,1)S(1)}, u32[]{:S(2)}, u32[]{:S(2)}) async-start(bf16[4,8,256,128]{3,2,1,0:T(8,128)(2,1)} %all-to-all-done.26), calls=%async_computation.27 | async-start | bytes 4194304 | tf_op jit(solution)/shard_map/all_to_all | solution.py:1671
  (10 other events, 18.6 us)
Sparse Core Ops, SparseCore 0:
  53.9 32.0 all-gather.9
  244.8 58.0 all-gather.11
  953.5 60.4 reduce-scatter.1
  1091.9 46.1 all-reduce.5

commit v2 on v1

--- a/solution.py
+++ b/solution.py
@@ -685,45 +685,109 @@
     return pl.BlockSpec(shape, lambda step: (0,) * len(shape))
 
 
-def spec_rows(shape, block, axis):
-    sizes = tuple(block if place == axis else size for place, size in enumerate(shape))
-    return pl.BlockSpec(
-        sizes, lambda step: tuple(step if place == axis else 0 for place in range(len(shape)))
-    )
-
-
 def cost(microseconds):
     return pl.CostEstimate(
         flops=int(microseconds * 1e9), bytes_accessed=int(microseconds * 3e6), transcendentals=0
     )
 
 
-def run_rows(kernel, name, steps, ins, outs, scratch, time=15):
-    in_specs = []
+class Both(list):
+    pass
+
+
+def all_rows(ins, outs):
+    extents = [shape[axis] for shape, dtype, axis in outs if axis is not None]
     for array, axis in ins:
-        if axis == "smem":
-            in_specs.append(pl.BlockSpec(memory_space=pltpu.SMEM))
-        elif axis is None:
-            in_specs.append(spec_full(array.shape))
-        else:
-            in_specs.append(spec_rows(array.shape, array.shape[axis] // steps, axis))
-    out_specs = []
-    for shape, dtype, axis in outs:
+        if isinstance(axis, int):
+            extents += [member.shape[axis] for member in (array if isinstance(array, list) else [array])]
+    return max(extents)
+
+
+def run_rows(kernel, name, steps, ins, outs, scratch, time=15, half=None, before=None):
+    grid = steps if half is None else steps // 2
+    offset = grid * (half or 0)
+    flat = []
+    groups = []
+    for array, axis in ins:
+        members = array if isinstance(array, Both) else [array]
+        flat += [(member, axis) for member in members]
+        groups.append((len(members), isinstance(array, Both)))
+    full = all_rows(flat, outs)
+
+    def spec(shape, axis):
         if axis is None:
-            out_specs.append(spec_full(shape))
-        else:
-            out_specs.append(spec_rows(shape, shape[axis] // steps, axis))
+            return spec_full(shape)
+        size = full // steps
+        first = offset if shape[axis] == full else 0
+        sizes = tuple(size if place == axis else extent for place, extent in enumerate(shape))
+        return pl.BlockSpec(
+            sizes,
+            lambda step: tuple(step + first if place == axis else 0 for place in range(len(shape))),
+        )
+
+    in_specs = [
+        pl.BlockSpec(memory_space=pltpu.SMEM) if axis == "smem" else spec(array.shape, axis)
+        for array, axis in flat
+    ]
+    out_specs = [spec(shape, axis) for shape, dtype, axis in outs]
+    arrays = [array for array, axis in flat]
+    aliases = {}
+    kept = []
+    for place, (shape, dtype, axis) in enumerate(outs):
+        if before is not None and (axis is None or shape[axis] == full):
+            aliases[len(arrays)] = place
+            kept.append(place)
+            arrays.append(before[place])
+            in_specs.append(spec_full(shape) if axis is None else pl.BlockSpec(memory_space=pl.ANY))
+
+    def run(*refs):
+        taken = iter(refs)
+        given = []
+        for number, together in groups:
+            members = [next(taken) for _ in range(number)]
+            given.append(members if together else members[0])
+        held = {place: next(taken) for place in kept}
+        results = [next(taken) for _ in outs]
+
+        @pl.when(pl.program_id(0) == 0)
+        def _():
+            for place, (shape, dtype, axis) in enumerate(outs):
+                if axis is None:
+                    results[place][...] = (
+                        held[place][...] if place in held else jnp.zeros(shape, dtype)
+                    )
+
+        kernel(*given, *results, *taken)
+
     return pl.pallas_call(
-        kernel,
-        grid=(steps,),
+        run,
+        grid=(grid,),
         in_specs=in_specs,
         out_specs=out_specs,
         out_shape=[jax.ShapeDtypeStruct(shape, dtype) for shape, dtype, axis in outs],
         scratch_shapes=[pltpu.VMEM(shape, dtype) for shape, dtype in scratch],
+        input_output_aliases=aliases,
         compiler_params=pltpu.CompilerParams(vmem_limit_bytes=VMEM_LIMIT),
-        cost_estimate=cost(time),
+        cost_estimate=cost(time if half is None else time / 2),
         name=name,
-    )(*[array for array, axis in ins])
+    )(*arrays)
+
+
+def run_halves(kernel, name, steps, ins, outs, scratch, time=15):
+    results = []
+    for half in range(2):
+        chosen = [
+            (array[half] if type(array) is list else array, axis) for array, axis in ins
+        ]
+        before = results[0] if half else None
+        results.append(run_rows(kernel, name, steps, chosen, outs, scratch, time, half, before))
+    full = all_rows(ins, outs)
+    return [
+        [results[0][place], results[1][place]]
+        if axis is not None and shape[axis] != full
+        else results[1][place]
+        for place, (shape, dtype, axis) in enumerate(outs)
+    ]
 
 
 def zero_first(*refs):
@@ -737,8 +801,8 @@
     return jnp.sum(ref[...].T, axis=0, keepdims=True)
 
 
-def on_last(steps, body):
-    @pl.when(pl.program_id(0) == steps - 1)
+def on_last(body):
+    @pl.when(pl.program_id(0) == pl.num_programs(0) - 1)
     def _():
         body()
 
@@ -756,8 +820,8 @@
     return reorder(ref[row].astype(F32), order).T
 
 
-def read_flipped(ref, row):
-    parts = ref[:, row]
+def read_flipped(refs, row):
+    parts = jnp.concatenate([ref[:, row] for ref in refs], axis=1)
     return parts.reshape(-1, parts.shape[-1]).astype(F32).T
 
 
@@ -831,15 +895,26 @@
     store_product(out, scratch, devices)
 
 
-def tri_product_kernel(incoming, operands, out):
+def whole_rows(refs, *place):
+    parts = jnp.concatenate([ref[(slice(None),) + place] for ref in refs], axis=1)
+    return parts.reshape(-1, parts.shape[-1])
+
+
+def split_rows(values, outs, *place):
+    part = outs[0].shape[-2]
+    parts = values.astype(BF16).reshape(outs[0].shape[0], -1, values.shape[-1])
+    for half, out in enumerate(outs):
+        out[(slice(None),) + place] = parts[:, half * part : (half + 1) * part]
+
+
+def tri_product_kernel(incoming, operands, first_out, second_out):
     def body(channel):
-        length = operands.shape[-1]
-        first = operands[:, 0, channel].reshape(length, length)
-        second = operands[:, 1, channel].reshape(length, length)
+        first = whole_rows(operands, 0, channel)
+        second = whole_rows(operands, 1, channel)
         tri = mm_tn(first, second) if incoming else mm_nt(first, second)
-        out[:, channel] = tri.astype(BF16).reshape(out.shape[0], out.shape[2], length)
-
-    each_channel(operands.shape[2], body)
+        split_rows(tri, (first_out, second_out), channel)
+
+    each_channel(operands[0].shape[2], body)
 
 
 def tri_join_kernel(
@@ -883,7 +958,7 @@
 
 
 def flipped_bias_kernel(source, cols, bias_t, bias_out, scratch):
-    rows = source.shape[1]
+    rows = source[0].shape[1]
 
     def body(row):
         unit, inverse = standardize(join(read_flipped, source, row))
@@ -994,7 +1069,7 @@
 
 def ending_kernel(alive, source, bias_in, cols, proj_t, output_t, out, totals, mixed, table):
     fill_bias(alive, bias_in, table)
-    rows = source.shape[1]
+    rows = source[0].shape[1]
 
     def body(row):
         state = attend_rows(
@@ -1033,10 +1108,10 @@
 
 
 def transition_back_kernel(
-    steps, read, mid, final, cotangent, bias_grad, cols, up_t, up, down, next_cols, bias_w,
+    read, mid, final, cotangent, bias_grad, cols, up_t, up, down, next_cols, bias_w,
     grad_out, up_grad, down_grad, bias_w_grad, vecs, norm_gain, norm_bias, pair_gain, pair_bias, bias_scratch,
 ):
-    zero_first(up_grad, down_grad, bias_w_grad, norm_gain, norm_bias, pair_gain, pair_bias)
+    zero_first(norm_gain, norm_bias, pair_gain, pair_bias)
     rows = mid.shape[0]
     bias_scratch[...] = bias_grad[...].astype(F32)
 
@@ -1078,20 +1153,20 @@
     each_group(rows, body)
 
     def finish():
-        vecs[0:1] = lane_sums(norm_gain)
-        vecs[1:2] = lane_sums(norm_bias)
-        vecs[2:3] = lane_sums(pair_gain)
-        vecs[3:4] = lane_sums(pair_bias)
-
-    on_last(steps, finish)
+        vecs[0:1] += lane_sums(norm_gain)
+        vecs[1:2] += lane_sums(norm_bias)
+        vecs[2:3] += lane_sums(pair_gain)
+        vecs[3:4] += lane_sums(pair_bias)
+
+    on_last(finish)
 
 
 def attention_back_kernel(
-    steps, read, read_grad, alive, source, grad_in, bias_in, totals, mixed_in, cols, proj_t, proj, output,
+    read, read_grad, alive, source, grad_in, bias_in, totals, mixed_in, cols, proj_t, proj, output,
     grad_out, bias_out, proj_grad, output_grad, table, grad_table,
 ):
     fill_bias(alive, bias_in, table)
-    zero_first(proj_grad, output_grad, grad_table)
+    zero_first(grad_table)
     rows = grad_out.shape[0]
 
     def body(row):
@@ -1150,7 +1225,7 @@
                 grad_table[head].T.astype(BF16).reshape(bias_out.shape[0], bias_out.shape[2], -1)
             )
 
-    on_last(steps, finish)
+    on_last(finish)
 
 
 def attention_end_row(
@@ -1176,10 +1251,10 @@
 
 
 def ending_end_kernel(
-    steps, source, grad_in, grad_lowered, bias_grad, cols, bias_w,
+    source, grad_in, grad_lowered, bias_grad, cols, bias_w,
     grad_out, bias_w_grad, vecs, norm_gain, norm_bias, bias_scratch, scratch,
 ):
-    zero_first(bias_w_grad, norm_gain, norm_bias)
+    zero_first(norm_gain, norm_bias)
     fill_bias_grad(bias_scratch, bias_grad)
     rows = grad_in.shape[0]
 
@@ -1194,10 +1269,10 @@
     store_flipped(grad_out, scratch)
 
     def finish():
-        vecs[0:1] = lane_sums(norm_gain)
-        vecs[1:2] = lane_sums(norm_bias)
-
-    on_last(steps, finish)
+        vecs[0:1] += lane_sums(norm_gain)
+        vecs[1:2] += lane_sums(norm_bias)
+
+    on_last(finish)
 
 
 def tri_post_back_row(
@@ -1219,12 +1294,12 @@
 
 
 def starting_end_kernel(
-    steps, source, grad_in, grad_lowered, bias_grad, cols, bias_w,
+    source, grad_in, grad_lowered, bias_grad, cols, bias_w,
     below, tri_in, tri_cols, proj_t, gate_t, proj, gate_w,
     grad_out, tri_out, gate_back, bias_w_grad, proj_grad, gate_grad, vecs,
     norm_gain, norm_bias, out_gain, out_bias, bias_scratch, tri_scratch,
 ):
-    zero_first(bias_w_grad, proj_grad, gate_grad, norm_gain, norm_bias, out_gain, out_bias)
+    zero_first(norm_gain, norm_bias, out_gain, out_bias)
     fill_bias_grad(bias_scratch, bias_grad)
     copy_blocks(tri_scratch, tri_in, tri_in.shape[0])
     rows = source.shape[0]
@@ -1246,31 +1321,29 @@
     copy_blocks(tri_out, tri_scratch, tri_out.shape[0])
 
     def finish():
-        vecs[0:1] = lane_sums(norm_gain)
-        vecs[1:2] = lane_sums(norm_bias)
-        vecs[2:3] = lane_sums(out_gain)
-        vecs[3:4] = lane_sums(out_bias)
-
-    on_last(steps, finish)
-
-
-def tri_product_back_kernel(incoming, grad, operands, out):
+        vecs[0:1] += lane_sums(norm_gain)
+        vecs[1:2] += lane_sums(norm_bias)
+        vecs[2:3] += lane_sums(out_gain)
+        vecs[3:4] += lane_sums(out_bias)
+
+    on_last(finish)
+
+
+def tri_product_back_kernel(incoming, grad, operands, first_out, second_out):
     def body(channel):
-        length = operands.shape[-1]
-        first = operands[:, 0, channel].reshape(length, length)
-        second = operands[:, 1, channel].reshape(length, length)
-        tri = grad[:, channel].reshape(length, length)
+        first = whole_rows(operands, 0, channel)
+        second = whole_rows(operands, 1, channel)
+        tri = whole_rows(grad, channel)
         if incoming:
             grad_first = mm_nt(second, tri)
             grad_second = mm(first, tri)
         else:
             grad_first = mm(tri, second)
             grad_second = mm_tn(tri, first)
-        shape = (out.shape[0], out.shape[3], length)
-        out[:, 0, channel] = grad_first.astype(BF16).reshape(shape)
-        out[:, 1, channel] = grad_second.astype(BF16).reshape(shape)
-
-    each_channel(operands.shape[2], body)
+        split_rows(grad_first, (first_out, second_out), 0, channel)
+        split_rows(grad_second, (first_out, second_out), 1, channel)
+
+    each_channel(operands[0].shape[2], body)
 
 
 def tri_pre_back_row(
@@ -1304,12 +1377,12 @@
 
 
 def tri_join_back_kernel(
-    steps, read, info, alive, source, product_grad, gate_in, grad_in, cols, proj_t, proj,
+    read, info, alive, source, product_grad, gate_in, grad_in, cols, proj_t, proj,
     below, tri_in, tri_cols, out_t, gate_t, out_w, gate_w,
     grad_out, tri_out, gate_back, proj_grad, out_grad, gate_grad, vecs,
     norm_gain, norm_bias, out_gain, out_bias, scratch, tri_scratch,
 ):
-    zero_first(proj_grad, out_grad, gate_grad, norm_gain, norm_bias, out_gain, out_bias)
+    zero_first(norm_gain, norm_bias, out_gain, out_bias)
     fill_product_grad(scratch, product_grad)
     copy_blocks(tri_scratch, tri_in, tri_in.shape[0])
     rows = source.shape[0]
@@ -1332,19 +1405,19 @@
     copy_blocks(tri_out, tri_scratch, tri_out.shape[0])
 
     def finish():
-        vecs[0:1] = lane_sums(norm_gain)
-        vecs[1:2] = lane_sums(norm_bias)
-        vecs[2:3] = lane_sums(out_gain)
-        vecs[3:4] = lane_sums(out_bias)
-
-    on_last(steps, finish)
+        vecs[0:1] += lane_sums(norm_gain)
+        vecs[1:2] += lane_sums(norm_bias)
+        vecs[2:3] += lane_sums(out_gain)
+        vecs[3:4] += lane_sums(out_bias)
+
+    on_last(finish)
 
 
 def tri_first_back_kernel(
-    steps, read, order, info, alive, source, product_grad, gate_in, grad_in, cols, proj_t, proj,
+    read, order, info, alive, source, product_grad, gate_in, grad_in, cols, proj_t, proj,
     grad_out, proj_grad, vecs, norm_gain, norm_bias, scratch,
 ):
-    zero_first(proj_grad, norm_gain, norm_bias)
+    zero_first(norm_gain, norm_bias)
     fill_product_grad(scratch, product_grad)
     rows = source.shape[0]
 
@@ -1360,10 +1433,10 @@
     each_group(rows, body)
 
     def finish():
-        vecs[0:1] = lane_sums(norm_gain)
-        vecs[1:2] = lane_sums(norm_bias)
-
-    on_last(steps, finish)
+        vecs[0:1] += lane_sums(norm_gain)
+        vecs[1:2] += lane_sums(norm_bias)
+
+    on_last(finish)
 
 
 RUN = 24
@@ -1761,19 +1834,26 @@
     part = hidden // devices
     steps = rows // 16
     state_shape = (rows, width, length)
+    block = rows // steps
+    half = rows // 2
     flip_shape = (devices, rows, rows, width)
-    product_shape = (devices, 2, part, rows, length)
-    tri_shape = (devices, part, rows, length)
-    block = rows // steps
+    flip_half = (devices, rows, half, width)
+    product_half = (devices, 2, part, half, length)
+    tri_half = (devices, part, half, length)
+    tri_rows = (hidden, half, length)
     channel_block = math.gcd(part, 4)
 
     def products(name, kernel, arrays, out_shape):
         axes = {4: 1, 5: 2}
+        out = (out_shape, BF16, axes[len(out_shape)])
         return run_rows(
             kernel, name, part // channel_block,
-            [(array, axes[array.ndim]) for array in arrays],
-            [(out_shape, BF16, axes[len(out_shape)])], [],
-        )[0]
+            [(Both(halves), axes[halves[0].ndim]) for halves in arrays], [out, out], [], 7,
+        )
+
+    def swap_halves(halves, shape=None):
+        moved = [swap(values, group) for values in halves]
+        return moved if shape is None else [values.reshape(shape) for values in moved]
 
     def cols(prefix):
         return weights[(prefix, COLS)]
@@ -1791,34 +1871,34 @@
     table = ((TA_HEADS, length, length), F32)
     attend_saves = [((rows, TA_HEADS, length), F32, 0), (state_shape, BF16, 0)]
 
-    (product,) = run_rows(
+    (product,) = run_halves(
         functools.partial(tri_pre_first_kernel, devices, read_first), "outgoing_in", steps,
         [
-            (info, "smem"), (alive, None), (pair, 0), (tri_cols(OUTGOING), None),
+            ([info[:half], info[half:]], "smem"), (alive, None), (pair, 0), (tri_cols(OUTGOING), None),
             (turned((OUTGOING, PROJ_GATE)), None),
         ],
-        [(product_shape, BF16, 3)], [product_scratch],
-    )
-    product_one = swap(product, group)
+        [(product_half, BF16, 3)], [product_scratch], 13,
+    )
+    product_one = swap_halves(product)
     tri_one = products(
-        "outgoing_product", functools.partial(tri_product_kernel, False), [product_one], tri_shape
-    )
-    tri_one = swap(tri_one, group).reshape(hidden, rows, length)
-    state_one, product = run_rows(
+        "outgoing_product", functools.partial(tri_product_kernel, False), [product_one], tri_half
+    )
+    tri_one = swap_halves(tri_one, tri_rows)
+    state_one, product = run_halves(
         functools.partial(tri_join_kernel, devices, read_first), "outgoing_out_incoming_in", steps,
         [
-            (info, "smem"), (alive, None), (pair, 0), (tri_one, 1), (tri_cols(OUTGOING), None),
+            ([info[:half], info[half:]], "smem"), (alive, None), (pair, 0), (tri_one, 1), (tri_cols(OUTGOING), None),
             (turned((OUTGOING, PROJ_OUT)), None), (turned((OUTGOING, GATE_OUT)), None),
             (tri_cols(INCOMING), None), (turned((INCOMING, PROJ_GATE)), None),
         ],
-        [(state_shape, F32, 0), (product_shape, BF16, 3)], [tri_scratch, product_scratch],
-    )
-    product_two = swap(product, group)
+        [(state_shape, F32, 0), (product_half, BF16, 3)], [tri_scratch, product_scratch], 22,
+    )
+    product_two = swap_halves(product)
     tri_two = products(
-        "incoming_product", functools.partial(tri_product_kernel, True), [product_two], tri_shape
-    )
-    tri_two = swap(tri_two, group).reshape(hidden, rows, length)
-    state_two, bias = run_rows(
+        "incoming_product", functools.partial(tri_product_kernel, True), [product_two], tri_half
+    )
+    tri_two = swap_halves(tri_two, tri_rows)
+    state_two, bias = run_halves(
         tri_last_kernel, "incoming_out_starting_bias", steps,
         [
             (state_one, 0), (tri_two, 1), (tri_cols(INCOMING), None),
@@ -1831,15 +1911,15 @@
     cotangent = cotangent.reshape(rows, parts, cores, parts, -1, width).transpose(3, 2, 1, 4, 0, 5)
     cotangent = swap(cotangent.reshape(flip_shape), group)
     cotangent = swap(cotangent.reshape((parts, cores) + flip_shape[1:]), "z").reshape(flip_shape)
-    flipped, totals_one, mixed_one = run_rows(
+    flipped, totals_one, mixed_one = run_halves(
         starting_kernel, "starting_attention", steps,
         [
             (alive, None), (state_two, 0), (bias_one, None), (cols(STARTING), None),
             (turned((STARTING, QKVG)), None), (turned((STARTING, OUTPUT)), None),
         ],
-        [(flip_shape, BF16, 2)] + attend_saves, [table, flip_scratch],
-    )
-    state_three = swap(flipped, group)
+        [(flip_half, BF16, 2)] + attend_saves, [table, flip_scratch], 21,
+    )
+    state_three = Both(swap_halves(flipped))
     (bias,) = run_rows(
         flipped_bias_kernel, "ending_bias", steps,
         [(state_three, 1), (cols(ENDING), None), (weights[(ENDING, BIAS_T)], None)],
@@ -1875,7 +1955,7 @@
     single_grad_scores = middle(turn(single_bias).astype(F32))
     grads = {}
     grad_four, grads[(PAIR, UP)], grads[(PAIR, DOWN)], grads[(ATTEND, PAIR_PROJ)], vecs = run_rows(
-        functools.partial(transition_back_kernel, steps, read_last), "pair_transition_back", steps,
+        functools.partial(transition_back_kernel, read_last), "pair_transition_back", steps,
         [
             (state_four, 0), (state_five, 0), (cotangent, 1), (turn(single_grad_scores), 1),
             (pair_cols, None), (turned((PAIR, UP)), None), (weights[(PAIR, UP)], None),
@@ -1886,7 +1966,7 @@
             (weights[(PAIR, DOWN)].shape, F32, None), (weights[(ATTEND, PAIR_PROJ)].shape, F32, None),
             ((8, width), F32, None),
         ],
-        [wide, wide, wide, wide, ((SA_HEADS, block, length), F32)],
+        [wide, wide, wide, wide, ((SA_HEADS, block, length), F32)], 30,
     )
     grads[(PAIR, VECTORS)] = vecs
 
@@ -1895,7 +1975,7 @@
 
     def attention_back(prefix, read, read_grad, source, source_axis, grad, grad_axis, bias, totals, mixed):
         lowered_grad, bias_grad, grads[(prefix, QKVG)], grads[(prefix, OUTPUT)] = run_rows(
-            functools.partial(attention_back_kernel, steps, read, read_grad),
+            functools.partial(attention_back_kernel, read, read_grad),
             "attention_back", steps,
             [
                 (alive, None), (source, source_axis), (grad, grad_axis), (bias, None), (totals, 0),
@@ -1906,7 +1986,7 @@
                 (state_shape, BF16, 0), ((devices, TA_HEADS, rows, length), BF16, None),
                 (weights[(prefix, QKVG)].shape, F32, None), (weights[(prefix, OUTPUT)].shape, F32, None),
             ],
-            [table, table],
+            [table, table], 34,
         )
         return lowered_grad, swap(bias_grad, group)
 
@@ -1916,26 +1996,25 @@
     bias_grad, pair_out = after(bias_grad, pair_out)
     pair_out = pair_out.reshape(parts, cores, rows, parts, -1, width).transpose(2, 3, 1, 0, 4, 5)
     pair_out = pair_out.reshape(rows, length, width)
-    flipped, bias_w_grad, vecs = run_rows(
-        functools.partial(ending_end_kernel, steps), "ending_attention_end", steps,
+    flipped, bias_w_grad, vecs = run_halves(
+        ending_end_kernel, "ending_attention_end", steps,
         [
             (state_three, 1), (grad_four, 0), (lowered_grad, 0), (bias_grad, 2), (cols(ENDING), None),
             (weights[(ENDING, BIAS_W)], None),
         ],
-        [(flip_shape, BF16, 2), ((width, 8), F32, None), ((8, width), F32, None)],
+        [(flip_half, BF16, 2), ((width, 8), F32, None), ((8, width), F32, None)],
         [wide, wide, head_scratch, flip_scratch],
     )
     grads[(ENDING, BIAS_PROJ)], grads[(ENDING, VECTORS)] = bias_w_grad, vecs
-    grad_three = swap(flipped, group)
-    grad_three, *_ = after(grad_three, between(0, grads))
+    grad_three = Both(after(*swap_halves(flipped), between(0, grads))[:2])
     lowered_grad, bias_grad = attention_back(
         STARTING, read_plain, read_flipped, state_two, 0, grad_three, 1, bias_one, totals_one, mixed_one
     )
     square = weights[(INCOMING, GATE_OUT)].shape
     (
         grad_two, grad_tri, gate_back, bias_w_grad, grads[(INCOMING, PROJ_OUT)], grads[(INCOMING, GATE_OUT)], vecs,
-    ) = run_rows(
-        functools.partial(starting_end_kernel, steps), "starting_end_incoming_out_back", steps,
+    ) = run_halves(
+        starting_end_kernel, "starting_end_incoming_out_back", steps,
         [
             (state_two, 0), (grad_three, 1), (lowered_grad, 0), (bias_grad, 2), (cols(STARTING), None),
             (weights[(STARTING, BIAS_W)], None), (state_one, 0), (tri_two, 1), (tri_cols(INCOMING), None),
@@ -1943,53 +2022,51 @@
             (weights[(INCOMING, PROJ_OUT)], None), (weights[(INCOMING, GATE_OUT)], None),
         ],
         [
-            (state_shape, F32, 0), ((hidden, rows, length), BF16, 1), (state_shape, BF16, 0),
+            (state_shape, F32, 0), (tri_rows, BF16, 1), (state_shape, BF16, 0),
             ((width, 8), F32, None), (square, F32, None), (square, F32, None), ((8, width), F32, None),
         ],
-        [wide, wide, wide, wide, head_scratch, tri_scratch],
+        [wide, wide, wide, wide, head_scratch, tri_scratch], 26,
     )
     grads[(STARTING, BIAS_PROJ)], grads[(STARTING, VECTORS)] = bias_w_grad, vecs
-    grad_tri = swap(grad_tri.reshape(tri_shape), group)
-    product_grad = swap(
-        products(
-            "incoming_product_back", functools.partial(tri_product_back_kernel, True),
-            [grad_tri, product_two], product_shape,
-        ),
-        group,
-    )
+    grad_tri = swap_halves([values.reshape(tri_half) for values in grad_tri])
+    grad_tri = after(*grad_tri, between(1, grads))[:2]
+    product_grad = products(
+        "incoming_product_back", functools.partial(tri_product_back_kernel, True),
+        [grad_tri, product_two], product_half,
+    )
+    product_grad = swap_halves(product_grad)
     (
         grad_one, grad_tri, gate_back, grads[(INCOMING, PROJ_GATE)], grads[(OUTGOING, PROJ_OUT)],
         grads[(OUTGOING, GATE_OUT)], vecs,
-    ) = run_rows(
-        functools.partial(tri_join_back_kernel, steps, read_first), "incoming_in_outgoing_out_back", steps,
+    ) = run_halves(
+        functools.partial(tri_join_back_kernel, read_first), "incoming_in_outgoing_out_back", steps,
         [
-            (info, "smem"), (alive, None), (state_one, 0), (product_grad, 3), (gate_back, 0), (grad_two, 0),
+            ([info[:half], info[half:]], "smem"), (alive, None), (state_one, 0), (product_grad, 3), (gate_back, 0), (grad_two, 0),
             (tri_cols(INCOMING), None), (turned((INCOMING, PROJ_GATE)), None),
             (weights[(INCOMING, PROJ_GATE)], None), (pair, 0), (tri_one, 1), (tri_cols(OUTGOING), None),
             (turned((OUTGOING, PROJ_OUT)), None), (turned((OUTGOING, GATE_OUT)), None),
             (weights[(OUTGOING, PROJ_OUT)], None), (weights[(OUTGOING, GATE_OUT)], None),
         ],
         [
-            (state_shape, F32, 0), ((hidden, rows, length), BF16, 1), (state_shape, BF16, 0),
+            (state_shape, F32, 0), (tri_rows, BF16, 1), (state_shape, BF16, 0),
             (weights[(INCOMING, PROJ_GATE)].shape, F32, None), (square, F32, None), (square, F32, None),
             ((8, width), F32, None),
         ],
-        [wide, wide, wide, wide, product_scratch, tri_scratch],
+        [wide, wide, wide, wide, product_scratch, tri_scratch], 37,
     )
     grads[(INCOMING, VECTORS)] = vecs
-    between(1, grads)
-    grad_tri = swap(grad_tri.reshape(tri_shape), group)
-    product_grad = swap(
-        products(
-            "outgoing_product_back", functools.partial(tri_product_back_kernel, False),
-            [grad_tri, product_one], product_shape,
-        ),
-        group,
-    )
-    pair_grad, grads[(OUTGOING, PROJ_GATE)], vecs = run_rows(
-        functools.partial(tri_first_back_kernel, steps, read_first, order_back), "outgoing_in_back", steps,
+    between(2, grads)
+    grad_tri = swap_halves([values.reshape(tri_half) for values in grad_tri])
+    grad_tri = after(*grad_tri, between(3, grads))[:2]
+    product_grad = products(
+        "outgoing_product_back", functools.partial(tri_product_back_kernel, False),
+        [grad_tri, product_one], product_half,
+    )
+    product_grad = swap_halves(product_grad)
+    pair_grad, grads[(OUTGOING, PROJ_GATE)], vecs = run_halves(
+        functools.partial(tri_first_back_kernel, read_first, order_back), "outgoing_in_back", steps,
         [
-            (info, "smem"), (alive, None), (pair, 0), (product_grad, 3), (gate_back, 0), (grad_one, 0),
+            ([info[:half], info[half:]], "smem"), (alive, None), (pair, 0), (product_grad, 3), (gate_back, 0), (grad_one, 0),
             (tri_cols(OUTGOING), None), (turned((OUTGOING, PROJ_GATE)), None),
             (weights[(OUTGOING, PROJ_GATE)], None),
         ],
@@ -1997,7 +2074,7 @@
             ((rows, length, width), BF16, 0), (weights[(OUTGOING, PROJ_GATE)].shape, F32, None),
             ((8, width), F32, None),
         ],
-        [wide, wide, product_scratch],
+        [wide, wide, product_scratch], 20,
     )
     grads[(OUTGOING, VECTORS)] = vecs
     return pair_out, pair_grad, grads
@@ -2041,10 +2118,9 @@
     )
     rows, length, width = pair.shape[1:]
     pair_in = swap(pair[0].reshape(parts, -1, length, width), "crop")
-    pair_in, first_runs, live = after(
-        pair_in, runs[:pair_lanes], swap(jnp.broadcast_to(lengths.astype(F32), (parts, STRIDE)), "crop")
-    )
+    pair_in, first_runs, lengths = after(pair_in, runs[:pair_lanes], lengths)
     pair_in = swap(pair_in, "z").reshape(rows, length, width)
+    live = swap(jnp.broadcast_to(lengths.astype(F32), (parts, STRIDE)), "crop")
     weights = unpack_pair(table, total, lax.all_gather(first_runs, line))
     pair_in, last_runs = after(pair_in, runs[single_lane:])
     weights.update(unpack_single(table, total, single_lane, lax.all_gather(last_runs, line)))
@@ -2097,10 +2173,14 @@
                 + [((ATTEND, PAIR_PROJ), grads[(ATTEND, PAIR_PROJ)])]
                 + [vector_part(grads, (PAIR, VECTORS), ATTEND), (lines_held, lines())],
             )
-            reduced[2] = lax.psum(
-                lax.psum_scatter(sent, line, scatter_dimension=0, tiled=False), "crop"
-            ).astype(F32)
+            reduced[2] = lax.psum_scatter(sent, line, scatter_dimension=0, tiled=False)
             return sent
+        if number == 1:
+            scattered = reduced[2]
+            reduced[2] = lax.psum(scattered, "crop")
+            return scattered
+        if number == 3:
+            return reduced[2]
         taken = -(-(pair_lanes * count - (attend + 2 * S // STRIDE) * STRIDE) // (4 * S))
         first = table[(INCOMING, NORM_GAIN)][0]
         sent = pack(
@@ -2113,7 +2193,7 @@
             + [(lines_held[:2], lines()), ((ATTEND, QKVG), single_grads[(ATTEND, QKVG)][: -(-taken // 8) * 8])],
         )
         reduced[1] = reduce_runs(sent)
-        return sent
+        return None
 
     pair_out, pair_grad, grads = pair_path(
         pair_in, info, alive, orders, weights, pair_cotangent[0], middle, between, group, parts
@@ -2133,7 +2213,7 @@
     reduced[0] = reduce_runs(sent)
     shard, squares = whole_call(
         functools.partial(shard_kernel, shard_size), "gradient_share",
-        [(place, "smem"), (jnp.concatenate([reduced[part] for part in range(3)], axis=0), None)],
+        [(place, "smem"), (jnp.concatenate([reduced[part].astype(F32) for part in range(3)], axis=0), None)],
         [((RUN * STRIDE, STRIDE), F32), ((8, STRIDE), F32)], [],
     )
     shard = shard.reshape(-1)[:shard_size]

time: 1230 us -> 1250 us (1.016)
  starting transfers between devices: 99.5 us -> 138 us
  waiting for transfers between devices: 359 us -> 325 us
  Pallas kernels: 415 us -> 447 us
    all_to_all x23 -> x34, starting transfers between devices: 99.4 us -> 138 us  [swap(): lax.all_to_all(values, group, split_axis=0, concat_axis=0, tiled=True)]
    all_to_all x23 -> x34, waiting for transfers between devices: 278 us -> 246 us  [swap(): lax.all_to_all(values, group, split_axis=0, concat_axis=0, tiled=True)]
    pallas_call x18 -> x26, Pallas kernels: 328 us -> 358 us  [run_rows(): pl.pallas_call(run, grid=(grid,), in_specs=in_specs, out_specs=out_specs,...]
    all_gather x1, blocking collectives: 14.3 us -> 27.1 us  [fast_shards(): clip_norm = jnp.sqrt(jnp.sum(lax.all_gather(squares, line)))]
    psum x1, waiting for transfers between devices: 46.4 us -> 33.7 us  [between(): reduced[2] = lax.psum(scattered, 'crop')]
    all_to_all x7 -> x6, blocking collectives: 145 us -> 145 us  [swap(): lax.all_to_all(values, group, split_axis=0, concat_axis=0, tiled=True)]
  transfers between devices with their start and end apart: 27 -> 38, of which waited for: 16 -> 24; matrix products, arithmetic and copies ran while one was open for 6% -> 4% of each run, Pallas kernels for 23% -> 32%
where the time goes in v2:
time: 1250 us; the launch traced here: 1240 us
  Pallas kernels  447 us (36%)
  waiting for transfers between devices  325 us (26%)
  blocking collectives  225 us (18%)
  starting transfers between devices  138 us (11%)
  local copies, waits for them, and re-layouts  43.1 us (3%)
  matrix products  23.8 us (2%)
  other arithmetic  21.7 us (2%)
  between operations  17.9 us (1%)
    pallas_call x26, Pallas kernels, run_rows(): pl.pallas_call(run, grid=(grid,), in_specs=in_specs, out_specs=out_specs,...  358 us
    all_to_all x34, waiting for transfers between devices, swap(): lax.all_to_all(values, group, split_axis=0, concat_axis=0, tiled=True)  246 us
    all_to_all x6, blocking collectives, swap(): lax.all_to_all(values, group, split_axis=0, concat_axis=0, tiled=True)  145 us
    all_to_all x34, starting transfers between devices, swap(): lax.all_to_all(values, group, split_axis=0, concat_axis=0, tiled=True)  138 us
    pallas_call x7, Pallas kernels, whole_call(): pl.pallas_call(kernel, in_specs=[spec(axis) for array, axis in ins], out_...  88.3 us
    all_gather x1, waiting for transfers between devices, fast_shards(): weights = unpack_pair(table, total, lax.all_gather(first_runs, line))  43.1 us
    psum x1, waiting for transfers between devices, between(): reduced[2] = lax.psum(scattered, 'crop')  33.7 us
    all_gather x1, blocking collectives, fast_shards(): clip_norm = jnp.sqrt(jnp.sum(lax.all_gather(squares, line)))  27.1 us
  transfers between devices with their start and end apart: 38, of which 24 were waited for; matrix products, arithmetic and copies ran while one was open for 4% of the time, Pallas kernels for 32%

profile of v2, /device:TPU:0, one launch (start us, length us, event | category | flops | bytes accessed | tf_op | source)
XLA Modules:
  0.0 1241.3 jit_solution(4732615393959083723)
XLA Ops:
  7.2 5.3 all-to-all-start
  15.1 23.1 %all-to-all-done = bf16[4,8,256,128]{3,2,1,0:T(8,128)(2,1)} async-done(((bf16[4,8,256,128]{3,2,1,0:T(8,128)(2,1)}), bf16[4,8,256,128]{3,2,1,0:T(8,128)(2,1)}, u32[]{:S(2)}, u32[]{:S(2)}) %all-to-all-start) | async-done | bytes 2097184 | tf_op jit(solution)/shard_map/all_to_all | solution.py:1744
  42.0 5.9 parameter_runs.1
  58.3 43.1 %all-gather.10.cloned.1.call-done = bf16[192,24,128]{2,1,0:T(8,128)(2,1)} async-done(((bf16[24,24,128]{2,1,0:T(8,128)(2,1)}), bf16[192,24,128]{2,1,0:T(8,128)(2,1)}) %all-gather.10.cloned.1.call-update) | async-done | bytes 1179664 | tf_op jit(solution)/shard_map/all_gather | solution.py:2124
  101.4 7.9 pair_weights.1
  113.0 7.6 outgoing_in.2
  124.5 7.6 outgoing_in.3
  132.1 19.0 %all-to-all-done.3.refs_0_.refs_2_ = bf16[8,2,16,16,256]{4,3,2,1,0:T(8,128)(2,1)S(1)} async-done(((bf16[8,2,16,16,256]{4,3,2,1,0:T(8,128)(2,1)}), bf16[8,2,16,16,256]{4,3,2,1,0:T(8,128)(2,1)S(1)}, u32[]{:S(2)}, u32[]{:S(2)}) %all-to-all-start.3) | async-done | bytes 2097184 | tf_op jit(solution)/shard_map/all_to_all | solution.py:1744
  157.5 26.0 %all-to-all-done.4.refs_1_.refs_3_ = bf16[8,2,16,16,256]{4,3,2,1,0:T(8,128)(2,1)} async-done(((bf16[8,2,16,16,256]{4,3,2,1,0:T(8,128)(2,1)}), bf16[8,2,16,16,256]{4,3,2,1,0:T(8,128)(2,1)}, u32[]{:S(2)}, u32[]{:S(2)}) %all-to-all-start.4) | async-done | bytes 2097184 | tf_op jit(solution)/shard_map/all_to_all | solution.py:1744
  187.3 6.2 outgoing_product.1
  193.6 19.6 %all_to_all.201 = bf16[8,16,16,256]{3,2,1,0:T(8,128)(2,1)} all-to-all(bf16[8,16,16,256]{3,2,1,0:T(8,128)(2,1)} %get-tuple-element.160), channel_id=1, replica_groups=mesh['crop'=4,'z'=4,'core'=2] {'crop','core'}, dimensions={0} | all-to-all | bytes 2097152 | tf_op jit(solution)/shard_map/all_to_all | solution.py:1744
  216.7 12.4 %outgoing_out_incoming_in.2 = (f32[32,128,256]{2,1,0:T(8,128)}, bf16[8,2,16,16,256]{4,3,2,1,0:T(8,128)(2,1)}) custom-call(s32[16]{0:T(128)} %get-tuple-element.314.refs_0_, f32[8,256]{1,0:T(8,128)} %broadcast_in_dim.17.refs_1_.refs_0_, bf16[32,256,128]{2,1,0:T(8,128)(2,1)} %bitcast.125, bf16[128,16,256]{2,1,0:T(8,128)(2,1)} %bitcast.141, ...), custom_call_target="tpu_custom_call" | custom-call | flops 11000000512 | bytes 33000000 | tf_op jit(solution)/shard_map/outgoing_out_incoming_in/pallas_call | solution.py:762
  236.7 12.4 %outgoing_out_incoming_in.3 = (f32[32,128,256]{2,1,0:T(8,128)}, bf16[8,2,16,16,256]{4,3,2,1,0:T(8,128)(2,1)}) custom-call(s32[16]{0:T(128)} %get-tuple-element.315.refs_0_, f32[8,256]{1,0:T(8,128)} %broadcast_in_dim.17.refs_1_.refs_0_, bf16[32,256,128]{2,1,0:T(8,128)(2,1)} %bitcast.126, ...), custom_call_target="tpu_custom_call", output_to_operand_aliasing={{0}: (9, {})} | custom-call | flops 11000000512 | bytes 33000000 | tf_op jit(solution)/shard_map/outgoing_out_incoming_in/pallas_call | solution.py:762
  249.1 14.2 %all-to-all-done.7.refs_0_.refs_2_ = bf16[8,2,16,16,256]{4,3,2,1,0:T(8,128)(2,1)S(1)} async-done(((bf16[8,2,16,16,256]{4,3,2,1,0:T(8,128)(2,1)}), bf16[8,2,16,16,256]{4,3,2,1,0:T(8,128)(2,1)S(1)}, u32[]{:S(2)}, u32[]{:S(2)}) %all-to-all-start.7) | async-done | bytes 2097184 | tf_op jit(solution)/shard_map/all_to_all | solution.py:1744
  263.2 30.9 %all_to_all.202.refs_1_.refs_3_ = bf16[8,2,16,16,256]{4,3,2,1,0:T(8,128)(2,1)} all-to-all(bf16[8,2,16,16,256]{4,3,2,1,0:T(8,128)(2,1)} %get-tuple-element.164), channel_id=1, replica_groups=mesh['crop'=4,'z'=4,'core'=2] {'crop','core'}, dimensions={0} | all-to-all | bytes 4194304 | tf_op jit(solution)/shard_map/all_to_all | solution.py:1744
  294.2 5.6 all-to-all-start.16
  299.8 6.3 incoming_product.1
  310.5 14.6 %all-to-all-done.9 = bf16[8,16,16,256]{3,2,1,0:T(8,128)(2,1)S(1)} async-done(((bf16[8,16,16,256]{3,2,1,0:T(8,128)(2,1)}), bf16[8,16,16,256]{3,2,1,0:T(8,128)(2,1)S(1)}, u32[]{:S(2)}, u32[]{:S(2)}) %all-to-all-start.9) | async-done | bytes 1048608 | tf_op jit(solution)/shard_map/all_to_all | solution.py:1744
  333.6 11.6 all-to-all-done.10
  349.6 8.3 incoming_out_starting_bias.2
  357.9 8.4 incoming_out_starting_bias.3
  366.3 15.0 %all-gather.1 = bf16[32,32,256]{2,1,0:T(8,128)(2,1)} all-gather(bf16[4,32,256]{2,1,0:T(8,128)(2,1)} %get-tuple-element.174), channel_id=3, replica_groups=mesh['crop'=4,'z'=4,'core'=2] {'crop','core'}, dimensions={0}, use_global_device_ids=true | all-gather | bytes 589824 | tf_op jit(solution)/shard_map/all_gather | solution.py:1910
  381.4 11.9 starting_attention.2
  396.8 11.9 starting_attention.3
  416.7 14.3 %all-to-all-done.12.refs_1_.refs_2_ = bf16[8,32,16,128]{3,2,1,0:T(8,128)(2,1)S(1)} async-done(((bf16[8,32,16,128]{3,2,1,0:T(8,128)(2,1)}), bf16[8,32,16,128]{3,2,1,0:T(8,128)(2,1)S(1)}, u32[]{:S(2)}, u32[]{:S(2)}) %all-to-all-start.12) | async-done | bytes 1048608 | tf_op jit(solution)/shard_map/all_to_all | solution.py:1744
  442.3 10.9 all-gather.2
  453.2 19.3 %ending_attention.1 = (f32[32,128,256]{2,1,0:T(8,128)}, f32[32,4,256]{2,1,0:T(4,128)}, bf16[32,128,256]{2,1,0:T(8,128)(2,1)}) custom-call(f32[8,256]{1,0:T(8,128)} %broadcast_in_dim.17.refs_1_.refs_0_, bf16[8,32,16,128]{3,2,1,0:T(8,128)(2,1)} %copy-done.22, bf16[8,32,16,128]{3,2,1,0:T(8,128)(2,1)} %copy-done.23, bf16[8,4,32,256]{3,2,1,0:T(8,128)(2,1)} %bitcast.155, ...), custom_call_target="tpu_custom_call" | custom-call | flops 15000000512 | bytes 45000000 | tf_op jit(solution)/shard_map/ending_attention/pallas_call | solution.py:762
  472.5 10.0 all-to-all-done.14
  482.5 29.2 %single_weights.1 = (bf16[384,1536]{1,0:T(8,128)(2,1)}, bf16[384,384]{1,0:T(8,128)(2,1)}, bf16[384,3072]{1,0:T(8,128)(2,1)}, bf16[1536,384]{1,0:T(8,128)(2,1)}, ...) custom-call(bf16[8,105,24,128]{3,2,1,0:T(8,128)(2,1)} %bitcast.168), custom_call_target="tpu_custom_call" | custom-call | flops 8000000000 | bytes 24000000 | tf_op jit(solution)/shard_map/single_weights/pallas_call | solution.py:1682
  514.9 15.0 %pair_transition.1 = (f32[32,128,256]{2,1,0:T(8,128)}, bf16[256,32,128]{2,1,0:T(8,128)(2,1)}, bf16[16,32,256]{2,1,0:T(8,128)(2,1)}) custom-call(f32[32,128,256]{2,1,0:T(8,128)} %get-tuple-element.186.refs_0_, f32[128,8]{1,0:T(8,128)} %get-tuple-element.187.refs_1_.refs_4_, bf16[1024,128]{1,0:T(8,128)(2,1)} %get-tuple-element.188.refs_2_.refs_5_, ...), custom_call_target="tpu_custom_call" | custom-call | flops 15000000512 | bytes 45000000 | tf_op jit(solution)/shard_map/pair_transition/pallas_call | solution.py:762
  539.1 10.4 all_gather.53
  596.5 30.8 %pair_transition_back.1 = (f32[32,128,256]{2,1,0:T(8,128)}, f32[128,1024]{1,0:T(8,128)}, f32[512,128]{1,0:T(8,128)}, f32[128,16]{1,0:T(8,128)}, f32[8,128]{1,0:T(8,128)}) custom-call(f32[32,128,256]{2,1,0:T(8,128)} %get-tuple-element.186.refs_0_, f32[32,128,256]{2,1,0:T(8,128)} %get-tuple-element.193.refs_1_, bf16[8,32,32,128]{3,2,1,0:T(8,128)(2,1)} %bitcast.131, ...), custom_call_target="tpu_custom_call" | custom-call | flops 30000001024 | bytes 90000000 | tf_op jit(solution)/shard_map/pair_transition_back/pallas_call | solution.py:762
  627.3 8.0 all-to-all-done.19
  638.8 33.3 %attention_back.2 = (bf16[32,128,256]{2,1,0:T(8,128)(2,1)}, bf16[8,4,32,256]{3,2,1,0:T(8,128)(2,1)}, f32[128,512]{1,0:T(8,128)}, f32[128,128]{1,0:T(8,128)}) custom-call(f32[8,256]{1,0:T(8,128)} %broadcast_in_dim.17.refs_1_.refs_0_, bf16[8,32,16,128]{3,2,1,0:T(8,128)(2,1)} %copy-done.22, bf16[8,32,16,128]{3,2,1,0:T(8,128)(2,1)} %copy-done.23, ...), custom_call_target="tpu_custom_call" | custom-call | flops 33999998976 | bytes 102000000 | tf_op jit(solution)/shard_map/attention_back/pallas_call | solution.py:762
  679.9 6.1 all-to-all-done.20.refs_4_
  695.0 30.2 %single_gradient.1 = bf16[8,104,24,128]{3,2,1,0:T(8,128)(2,1)} custom-call(f32[384,1536]{1,0:T(8,128)} %fusion.21.refs_0_, f32[384,384]{1,0:T(8,128)} %fusion.27.refs_1_, f32[384,3072]{1,0:T(8,128)} %fusion.23.refs_2_, f32[1536,384]{1,0:T(8,128)} %fusion.31.refs_3_, f32[128,16]{1,0:T(8,128)} %get-tuple-element.221.refs_4_, ...), custom_call_target="tpu_custom_call" | custom-call | flops 8000000000 | bytes 24000000 | tf_op jit(solution)/shard_map/single_gradient/pallas_call | solution.py:1682
  725.3 8.2 ending_attention_end.2
  737.7 7.6 ending_attention_end.3
  745.2 7.9 all-to-all-done.25.refs_2_.refs_1_
  753.1 19.6 %all_to_all.203.refs_3_.refs_2_ = bf16[8,32,16,128]{3,2,1,0:T(8,128)(2,1)} all-to-all(bf16[8,32,16,128]{3,2,1,0:T(8,128)(2,1)} %get-tuple-element.220), channel_id=1, replica_groups=mesh['crop'=4,'z'=4,'core'=2] {'crop','core'}, dimensions={0} | all-to-all | bytes 2097152 | tf_op jit(solution)/shard_map/all_to_all | solution.py:1744
  772.7 33.7 %attention_back.3 = (bf16[32,128,256]{2,1,0:T(8,128)(2,1)}, bf16[8,4,32,256]{3,2,1,0:T(8,128)(2,1)}, f32[128,512]{1,0:T(8,128)}, f32[128,128]{1,0:T(8,128)}) custom-call(f32[8,256]{1,0:T(8,128)} %broadcast_in_dim.17.refs_1_.refs_0_, f32[32,128,256]{2,1,0:T(8,128)} %get-tuple-element.173.refs_1_.refs_0_, bf16[8,32,16,128]{3,2,1,0:T(8,128)(2,1)} %copy-done.25, ...), custom_call_target="tpu_custom_call" | custom-call | flops 33999998976 | bytes 102000000 | tf_op jit(solution)/shard_map/attention_back/pallas_call | solution.py:762
  810.1 9.4 all-to-all-done.27.refs_4_
  820.3 15.8 %starting_end_incoming_out_back.2 = (f32[32,128,256]{2,1,0:T(8,128)}, bf16[128,16,256]{2,1,0:T(8,128)(2,1)}, bf16[32,128,256]{2,1,0:T(8,128)(2,1)}, f32[128,8]{1...) custom-call(f32[32,128,256]{2,1,0:T(8,128)} %get-tuple-element.173.refs_1_.refs_0_, ...), custom_call_target="tpu_custom_call" | custom-call | flops 12999999488 | bytes 39000000 | tf_op jit(solution)/shard_map/starting_end_incoming_out_back/pallas_call | solution.py:762
  840.0 16.0 %starting_end_incoming_out_back.3 = (f32[32,128,256]{2,1,0:T(8,128)}, bf16[128,16,256]{2,1,0:T(8,128)(2,1)}, bf16[32,128,256]{2,1,0:T(8,128)(2,1)}, f32[128,8]{1...) custom-call(f32[32,128,256]{2,1,0:T(8,128)} %get-tuple-element.173.r, ...), custom_call_target="tpu_custom_call", output_to_operand_aliasing={{0}: (14, {}), {2}: (15, {}), {3}: (16, {}), {4}: (17, {}),... | custom-call | flops 12999999488 | bytes 39000000 | tf_op jit(solution)/shard_map/starting_end_incoming_out_back/pallas_call | solution.py:762
  861.1 14.4 %all-to-all-done.29.refs_1_ = bf16[8,16,16,256]{3,2,1,0:T(8,128)(2,1)S(1)} async-done(((bf16[8,16,16,256]{3,2,1,0:T(8,128)(2,1)}), bf16[8,16,16,256]{3,2,1,0:T(8,128)(2,1)S(1)}, u32[]{:S(2)}, u32[]{:S(2)}) %all-to-all-start.29) | async-done | bytes 1048608 | tf_op jit(solution)/shard_map/all_to_all | solution.py:1744
  879.6 7.4 incoming_product_back.1
  886.9 30.9 %all_to_all.204.refs_3_ = bf16[8,2,16,16,256]{4,3,2,1,0:T(8,128)(2,1)} all-to-all(bf16[8,2,16,16,256]{4,3,2,1,0:T(8,128)(2,1)} %get-tuple-element.244), channel_id=1, replica_groups=mesh['crop'=4,'z'=4,'core'=2] {'crop','core'}, dimensions={0} | all-to-all | bytes 4194304 | tf_op jit(solution)/shard_map/all_to_all | solution.py:1744
  921.5 21.1 %incoming_in_outgoing_out_back.2 = (f32[32,128,256]{2,1,0:T(8,128)}, bf16[128,16,256]{2,1,0:T(8,128)(2,1)}, bf16[32,128,256]{2,1,0:T(8,128)(2,1)}, f32[128,512]{...) custom-call(s32[16]{0:T(128)} %get-tuple-element.314.refs_0_, ...), custom_call_target="tpu_custom_call" | custom-call | flops 18499999744 | bytes 55500000 | tf_op jit(solution)/shard_map/incoming_in_outgoing_out_back/pallas_call | solution.py:762
  942.6 5.4 all-to-all-done.32.refs_3_
  951.6 21.2 %incoming_in_outgoing_out_back.3 = (f32[32,128,256]{2,1,0:T(8,128)}, bf16[128,16,256]{2,1,0:T(8,128)(2,1)}, bf16[32,128,256]{2,1,0:T(8,128)(2,1)}, f32[128,512]{...) custom-call(s32[16]{0:T(128)} %get-tuple-element.315.refs_0_, ...), custom_call_target="tpu_custom_call", output_to_operand_aliasing={{0}: (16, {}), {2}: (17, {}), {3}: (18, {}), {4}: (19, {}),... | custom-call | flops 18499999744 | bytes 55500000 | tf_op jit(solution)/shard_map/incoming_in_outgoing_out_back/pallas_call | solution.py:762
  977.5 16.6 %all-to-all-done.33.refs_1_ = bf16[8,16,16,256]{3,2,1,0:T(8,128)(2,1)S(1)} async-done(((bf16[8,16,16,256]{3,2,1,0:T(8,128)(2,1)}), bf16[8,16,16,256]{3,2,1,0:T(8,128)(2,1)S(1)}, u32[]{:S(2)}, u32[]{:S(2)}) %all-to-all-start.33) | async-done | bytes 1048608 | tf_op jit(solution)/shard_map/all_to_all | solution.py:1744
  997.4 33.7 %all-reduce.6.cloned.1.call-done = bf16[104,24,128]{2,1,0:T(8,128)(2,1)} async-done(((bf16[104,24,128]{2,1,0:T(8,128)(2,1)}), bf16[104,24,128]{2,1,0:T(8,128)(2,1)}) %all-reduce.6.cloned.1.call-update) | async-done | bytes 638992 | tf_op jit(solution)/shard_map/psum | solution.py:2180
  1031.1 7.2 outgoing_product_back.1
  1038.3 30.9 %all_to_all.205.refs_3_ = bf16[8,2,16,16,256]{4,3,2,1,0:T(8,128)(2,1)} all-to-all(bf16[8,2,16,16,256]{4,3,2,1,0:T(8,128)(2,1)} %get-tuple-element.265), channel_id=1, replica_groups=mesh['crop'=4,'z'=4,'core'=2] {'crop','core'}, dimensions={0} | all-to-all | bytes 4194304 | tf_op jit(solution)/shard_map/all_to_all | solution.py:1744
  1076.2 7.0 pair_gradient.1
  1083.2 11.8 outgoing_in_back.2
  1104.3 11.8 outgoing_in_back.3
  1119.0 9.4 all-to-all-done.39
  1128.5 12.7 %all_to_all.206 = bf16[8,5,24,128]{3,2,1,0:T(8,128)(2,1)S(1)} all-to-all(bf16[8,5,24,128]{3,2,1,0:T(8,128)(2,1)} %outgoing_gradient.1), channel_id=1, replica_groups=mesh['crop'=4,'z'=4,'core'=2] {'z','core'}, dimensions={0} | all-to-all | bytes 491520 | tf_op jit(solution)/shard_map/all_to_all | solution.py:1744
  1149.2 8.9 all-gather.5
  1158.2 8.4 all-gather.4
  1173.1 27.1 %all-gather.6 = f32[64,128]{1,0:T(8,128)S(1)} all-gather(f32[8,128]{1,0:T(8,128)} %get-tuple-element.289), channel_id=8, replica_groups=mesh['crop'=4,'z'=4,'core'=2] {'z','core'}, dimensions={0}, use_global_device_ids=true | all-gather | bytes 36864 | tf_op jit(solution)/shard_map/all_gather | solution.py:2220
  1205.1 7.5 multiply_subtract_fusion
  1212.6 18.1 %all-to-all-done.37 = bf16[4,8,256,128]{3,2,1,0:T(8,128)(2,1)S(1)} async-done(((bf16[4,8,256,128]{3,2,1,0:T(8,128)(2,1)}), bf16[4,8,256,128]{3,2,1,0:T(8,128)(2,1)S(1)}, u32[]{:S(2)}, u32[]{:S(2)}) %all-to-all-start.37) | async-done | bytes 2097184 | tf_op jit(solution)/shard_map/all_to_all | solution.py:1744
  (304 shorter events, 241.2 us)
Async XLA Ops:
  7.2 31.0 %all-to-all-start = ((bf16[4,8,256,128]{3,2,1,0:T(8,128)(2,1)}), bf16[4,8,256,128]{3,2,1,0:T(8,128)(2,1)}, u32[]{:S(2)}, u32[]{:S(2)}) async-start(bf16[4,8,256,128]{3,2,1,0:T(8,128)(2,1)} %bitcast.121), calls=%async_computation | async-start | bytes 4194304 | tf_op jit(solution)/shard_map/all_to_all | solution.py:1744
  38.8 10.7 all-to-all-start.1
  49.5 62.1 %all-to-all-start.2 = ((bf16[4,8,256,128]{3,2,1,0:T(8,128)(2,1)}), bf16[4,8,256,128]{3,2,1,0:T(8,128)(2,1)S(1)}, u32[]{:S(2)}, u32[]{:S(2)}) async-start(bf16[4,8,256,128]{3,2,1,0:T(8,128)(2,1)} %all-to-all-done), calls=%async_computation.2 | async-start | bytes 4194304 | tf_op jit(solution)/shard_map/all_to_all | solution.py:1744
  54.7 46.6 %all-gather.10.cloned.1.call-start = ((), (), s32[]{:S(2)}) async-start(), calls=%async_computation.43 | async-start | bytes 1327104 | tf_op jit(solution)/shard_map/all_gather | solution.py:2124
  120.6 30.5 %all-to-all-start.3 = ((bf16[8,2,16,16,256]{4,3,2,1,0:T(8,128)(2,1)}), bf16[8,2,16,16,256]{4,3,2,1,0:T(8,128)(2,1)S(1)}, u32[]{:S(2)}, u32[]{:S(2)}) async-start(bf16[8,2,16,16,256]{4,3,2,1,0:T(8,128)(2,1)} %outgoing_in.2), calls=%async_computation.3 | async-start | bytes 4194304 | tf_op jit(solution)/shard_map/all_to_all | solution.py:1744
  132.1 24.7 %copy-start.52 = (bf16[1,32,384]{2,1,0:T(8,128)(2,1)S(1)}, bf16[1,32,384]{2,1,0:T(8,128)(2,1)}, u32[]{:S(2)}) copy-start(bf16[1,32,384]{2,1,0:T(8,128)(2,1)} %param.18) | copy-start | bytes 73732
  132.1 24.7 %copy-start.53 = (bf16[1,32,384]{2,1,0:T(8,128)(2,1)S(1)}, bf16[1,32,384]{2,1,0:T(8,128)(2,1)}, u32[]{:S(2)}) copy-start(bf16[1,32,384]{2,1,0:T(8,128)(2,1)} %param.12) | copy-start | bytes 73732
  152.4 31.0 %all-to-all-start.4 = ((bf16[8,2,16,16,256]{4,3,2,1,0:T(8,128)(2,1)}), bf16[8,2,16,16,256]{4,3,2,1,0:T(8,128)(2,1)}, u32[]{:S(2)}, u32[]{:S(2)}) async-start(bf16[8,2,16,16,256]{4,3,2,1,0:T(8,128)(2,1)} %outgoing_in.3), calls=%async_computation.4 | async-start | bytes 4194304 | tf_op jit(solution)/shard_map/all_to_all | solution.py:1744
  183.5 10.1 all-to-all-start.15
  213.2 18.9 %all-to-all-start.5 = ((bf16[8,16,16,256]{3,2,1,0:T(8,128)(2,1)}), bf16[8,16,16,256]{3,2,1,0:T(8,128)(2,1)S(1)}, u32[]{:S(2)}, u32[]{:S(2)}) async-start(bf16[8,16,16,256]{3,2,1,0:T(8,128)(2,1)} %get-tuple-element.155), calls=%async_computation.5 | async-start | bytes 2097152 | tf_op jit(solution)/shard_map/all_to_all | solution.py:1744
  233.0 30.2 %all-to-all-start.7 = ((bf16[8,2,16,16,256]{4,3,2,1,0:T(8,128)(2,1)}), bf16[8,2,16,16,256]{4,3,2,1,0:T(8,128)(2,1)S(1)}, u32[]{:S(2)}, u32[]{:S(2)}) async-start(bf16[8,2,16,16,256]{4,3,2,1,0:T(8,128)(2,1)} %get-tuple-element.163), calls=%async_computation.7 | async-start | bytes 4194304 | tf_op jit(solution)/shard_map/all_to_all | solution.py:1744
  263.2 30.9 %copy-start.9 = (bf16[8,2,16,16,256]{4,3,2,1,0:T(8,128)(2,1)}, bf16[8,2,16,16,256]{4,3,2,1,0:T(8,128)(2,1)S(1)}, u32[]{:S(2)}) copy-start(bf16[8,2,16,16,256]{4,3,2,1,0:T(8,128)(2,1)S(1)} %all-to-all-done.7.refs_0_.refs_2_) | copy-start | bytes 6291460
  294.2 11.9 all-to-all-start.16
  306.1 23.8 %copy-start.6 = (bf16[1,32,256,128]{3,2,1,0:T(8,128)(2,1)S(1)}, bf16[1,32,256,128]{3,2,1,0:T(8,128)(2,1)}, u32[]{:S(2)}) copy-start(bf16[1,32,256,128]{3,2,1,0:T(8,128)(2,1)} %param.17) | copy-start | bytes 6291460
  306.1 19.0 %all-to-all-start.9 = ((bf16[8,16,16,256]{3,2,1,0:T(8,128)(2,1)}), bf16[8,16,16,256]{3,2,1,0:T(8,128)(2,1)S(1)}, u32[]{:S(2)}, u32[]{:S(2)}) async-start(bf16[8,16,16,256]{3,2,1,0:T(8,128)(2,1)} %get-tuple-element.165), calls=%async_computation.9 | async-start | bytes 2097152 | tf_op jit(solution)/shard_map/all_to_all | solution.py:1744
  309.8 172.7 %all-gather.12.cloned.1.call-start = ((), (), s32[]{:S(2)}) async-start(), calls=%async_computation.44 | async-start | bytes 5806080 | tf_op jit(solution)/shard_map/all_gather | solution.py:2126
  325.1 20.1 %all-to-all-start.10 = ((bf16[8,16,16,256]{3,2,1,0:T(8,128)(2,1)}), bf16[8,16,16,256]{3,2,1,0:T(8,128)(2,1)}, u32[]{:S(2)}, u32[]{:S(2)}) async-start(bf16[8,16,16,256]{3,2,1,0:T(8,128)(2,1)} %get-tuple-element.170), calls=%async_computation.10 | async-start | bytes 2097152 | tf_op jit(solution)/shard_map/all_to_all | solution.py:1744
  345.3 48.0 %all-to-all-start.13 = ((bf16[8,32,32,128]{3,2,1,0:T(8,128)(2,1)}), bf16[8,32,32,128]{3,2,1,0:T(8,128)(2,1)}, u32[]{:S(2)}, u32[]{:S(2)}) async-start(bf16[8,32,32,128]{3,2,1,0:T(8,128)(2,1)} %bitcast.15), calls=%async_computation.13 | async-start | bytes 4194304 | tf_op jit(solution)/shard_map/all_to_all | solution.py:1744
  393.2 18.9 %all-to-all-start.11 = ((bf16[8,32,16,128]{3,2,1,0:T(8,128)(2,1)}), bf16[8,32,16,128]{3,2,1,0:T(8,128)(2,1)S(1)}, u32[]{:S(2)}, u32[]{:S(2)}) async-start(bf16[8,32,16,128]{3,2,1,0:T(8,128)(2,1)} %get-tuple-element.177), calls=%async_computation.11 | async-start | bytes 2097152 | tf_op jit(solution)/shard_map/all_to_all | solution.py:1744
  412.1 19.9 %copy-start.22 = (bf16[8,32,16,128]{3,2,1,0:T(8,128)(2,1)}, bf16[8,32,16,128]{3,2,1,0:T(8,128)(2,1)S(1)}, u32[]{:S(2)}) copy-start(bf16[8,32,16,128]{3,2,1,0:T(8,128)(2,1)S(1)} %all-to-all-done.11.refs_0_.refs_1_) | copy-start | bytes 3145732
  412.1 18.9 %all-to-all-start.12 = ((bf16[8,32,16,128]{3,2,1,0:T(8,128)(2,1)}), bf16[8,32,16,128]{3,2,1,0:T(8,128)(2,1)S(1)}, u32[]{:S(2)}, u32[]{:S(2)}) async-start(bf16[8,32,16,128]{3,2,1,0:T(8,128)(2,1)} %get-tuple-element.180), calls=%async_computation.12 | async-start | bytes 2097152 | tf_op jit(solution)/shard_map/all_to_all | solution.py:1744
  416.5 96.1 %copy-start.58 = (f32[32]{0:T(128)}, f32[32]{0:T(128)S(1)}, u32[]{:S(2)}) copy-start(f32[32]{0:T(128)S(1)} %broadcast_multiply_fusion.1) | copy-start | bytes 388
  416.7 20.4 %copy-start.69 = (f32[32]{0:T(128)}, f32[32]{0:T(128)S(1)}, u32[]{:S(2)}) copy-start(f32[32]{0:T(128)S(1)} %multiply_reduce_fusion.6) | copy-start | bytes 388
  432.0 50.4 %all-to-all-start.14 = ((bf16[4,2,32,32,128]{4,3,2,1,0:T(8,128)(2,1)}), bf16[4,2,32,32,128]{4,3,2,1,0:T(8,128)(2,1)S(1)}, u32[]{:S(2)}, u32[]{:S(2)}) async-start(bf16[4,2,32,32,128]{4,3,2,1,0:T(8,128)(2,1)} %bitcast.16), calls=%async_computation.14 | async-start | bytes 4194304 | tf_op jit(solution)/shard_map/all_to_all | solution.py:1744
  437.1 75.4 %copy-start.62 = (f32[32]{0:T(128)}, f32[32]{0:T(128)S(1)}, u32[]{:S(2)}) copy-start(f32[32]{0:T(128)S(1)} %fusion.33) | copy-start | bytes 388
  482.5 29.2 %copy-start.10 = (bf16[4,2,32,32,128]{4,3,2,1,0:T(8,128)(2,1)}, bf16[4,2,32,32,128]{4,3,2,1,0:T(8,128)(2,1)S(1)}, u32[]{:S(2)}) copy-start(bf16[4,2,32,32,128]{4,3,2,1,0:T(8,128)(2,1)S(1)} %all-to-all-done.14) | copy-start | bytes 6291460
  512.5 49.2 %copy-start.54 = (f32[384]{0:T(512)}, f32[384]{0:T(512)S(1)}, u32[]{:S(2)}) copy-start(f32[384]{0:T(512)S(1)} %get-tuple-element.297) | copy-start | bytes 4612
  512.5 52.3 %copy-start.48 = (f32[384]{0:T(512)}, f32[384]{0:T(512)S(1)}, u32[]{:S(2)}) copy-start(f32[384]{0:T(512)S(1)} %get-tuple-element.296) | copy-start | bytes 4612
  533.4 17.0 %all-to-all-start.17 = ((bf16[8,2,8192]{2,1,0:T(2,128)(2,1)}), bf16[8,2,8192]{2,1,0:T(2,128)(2,1)S(1)}, u32[]{:S(2)}, u32[]{:S(2)}) async-start(bf16[8,2,8192]{2,1,0:T(2,128)(2,1)} %reshape.272), calls=%async_computation.17 | async-start | bytes 524288 | tf_op jit(solution)/shard_map/all_to_all | solution.py:1744
  572.4 10.4 all-to-all-start.18
  583.5 51.8 %all-to-all-start.19 = ((bf16[4,64,32,128]{3,2,1,0:T(8,128)(2,1)}), bf16[4,64,32,128]{3,2,1,0:T(8,128)(2,1)S(1)}, u32[]{:S(2)}, u32[]{:S(2)}) async-start(bf16[4,64,32,128]{3,2,1,0:T(8,128)(2,1)} %bitcast.132), calls=%async_computation.19 | async-start | bytes 4194304 | tf_op jit(solution)/shard_map/all_to_all | solution.py:1744
  635.3 36.8 %copy-start.3 = (bf16[4,64,32,128]{3,2,1,0:T(8,128)(2,1)}, bf16[4,64,32,128]{3,2,1,0:T(8,128)(2,1)S(1)}, u32[]{:S(2)}) copy-start(bf16[4,64,32,128]{3,2,1,0:T(8,128)(2,1)S(1)} %all-to-all-done.19) | copy-start | bytes 6291460
  635.3 36.8 %all-to-all-start.22 = ((bf16[8,32,768]{2,1,0:T(8,128)(2,1)}), bf16[8,32,768]{2,1,0:T(8,128)(2,1)S(1)}, u32[]{:S(2)}, u32[]{:S(2)}) async-start(bf16[8,32,768]{2,1,0:T(8,128)(2,1)} %pad_maximum_fusion.1), calls=%async_computation.22 | async-start | bytes 786432 | tf_op jit(solution)/shard_map/all_to_all | solution.py:1744
  638.8 37.5 %copy-start.15 = (bf16[256,384]{0,1:T(8,128)(2,1)S(1)}, bf16[256,384]{0,1:T(8,128)(2,1)}, u32[]{:S(2)}) copy-start(bf16[256,384]{0,1:T(8,128)(2,1)} %copy-done.14) | copy-start | bytes 589828
  638.8 37.8 %copy-start.67 = (f32[384]{0:T(512)S(1)}, f32[384]{0:T(512)}, u32[]{:S(2)}) copy-start(f32[384]{0:T(512)} %get-tuple-element.295) | copy-start | bytes 4612
  638.8 37.8 %copy-start.66 = (f32[384]{0:T(512)S(1)}, f32[384]{0:T(512)}, u32[]{:S(2)}) copy-start(f32[384]{0:T(512)} %get-tuple-element.292) | copy-start | bytes 4612
  638.8 37.8 %copy-start.32 = (f32[32,1536]{1,0:T(8,128)S(1)}, f32[32,1536]{1,0:T(8,128)}, u32[]{:S(2)}) copy-start(f32[32,1536]{1,0:T(8,128)} %copy-done.31) | copy-start | bytes 589828
  638.8 37.8 %copy-start.34 = (f32[32,1536]{1,0:T(8,128)S(1)}, f32[32,1536]{1,0:T(8,128)}, u32[]{:S(2)}) copy-start(f32[32,1536]{1,0:T(8,128)} %copy-done.33) | copy-start | bytes 589828
  638.8 37.8 %copy-start.49 = (f32[384]{0:T(512)S(1)}, f32[384]{0:T(512)}, u32[]{:S(2)}) copy-start(f32[384]{0:T(512)} %copy-done.48) | copy-start | bytes 4612
  638.8 37.8 %copy-start.55 = (f32[384]{0:T(512)S(1)}, f32[384]{0:T(512)}, u32[]{:S(2)}) copy-start(f32[384]{0:T(512)} %copy-done.54) | copy-start | bytes 4612
  638.8 37.8 %copy-start.61 = (f32[32]{0:T(128)S(1)}, f32[32]{0:T(128)}, u32[]{:S(2)}) copy-start(f32[32]{0:T(128)} %copy-done.60) | copy-start | bytes 388
  638.8 37.8 %copy-start.65 = (f32[32]{0:T(128)S(1)}, f32[32]{0:T(128)}, u32[]{:S(2)}) copy-start(f32[32]{0:T(128)} %copy-done.64) | copy-start | bytes 388
  672.2 13.8 %all-to-all-start.20 = ((bf16[8,4,32,256]{3,2,1,0:T(8,128)(2,1)}), bf16[8,4,32,256]{3,2,1,0:T(8,128)(2,1)S(1)}, u32[]{:S(2)}, u32[]{:S(2)}) async-start(bf16[8,4,32,256]{3,2,1,0:T(8,128)(2,1)} %get-tuple-element.211), calls=%async_computation.20 | async-start | bytes 1048576 | tf_op jit(solution)/shard_map/all_to_all | solution.py:1744
  686.8 38.5 %all-to-all-start.21 = ((bf16[8,32,32,128]{3,2,1,0:T(8,128)(2,1)}), bf16[8,32,32,128]{3,2,1,0:T(8,128)(2,1)S(1)}, u32[]{:S(2)}, u32[]{:S(2)}) async-start(bf16[8,32,32,128]{3,2,1,0:T(8,128)(2,1)} %bitcast.117), calls=%async_computation.21 | async-start | bytes 4194304 | tf_op jit(solution)/shard_map/all_to_all | solution.py:1744
  690.4 189.1 %reduce-scatter.2.cloned.1.call-start = ((), (), s32[]{:S(2)}) async-start(), calls=%async_computation.41 | async-start | bytes 5750784 | tf_op jit(solution)/shard_map/reduce_scatter | solution.py:2176
  733.6 19.5 %all-to-all-start.25 = ((bf16[8,32,16,128]{3,2,1,0:T(8,128)(2,1)}), bf16[8,32,16,128]{3,2,1,0:T(8,128)(2,1)S(1)}, u32[]{:S(2)}, u32[]{:S(2)}) async-start(bf16[8,32,16,128]{3,2,1,0:T(8,128)(2,1)} %get-tuple-element.217), calls=%async_computation.25 | async-start | bytes 2097152 | tf_op jit(solution)/shard_map/all_to_all | solution.py:1744
  772.7 37.2 %copy-start.18 = (bf16[1536,384]{1,0:T(8,128)(2,1)S(1)}, bf16[1536,384]{1,0:T(8,128)(2,1)}, u32[]{:S(2)}) copy-start(bf16[1536,384]{1,0:T(8,128)(2,1)} %get-tuple-element.200) | copy-start | bytes 3538948
  772.7 37.2 %copy-start.41 = (bf16[32,1536]{1,0:T(8,128)(2,1)S(1)}, bf16[32,1536]{1,0:T(8,128)(2,1)}, u32[]{:S(2)}) copy-start(bf16[32,1536]{1,0:T(8,128)(2,1)} %get-tuple-element.309) | copy-start | bytes 294916
  806.3 13.2 %all-to-all-start.27 = ((bf16[8,4,32,256]{3,2,1,0:T(8,128)(2,1)}), bf16[8,4,32,256]{3,2,1,0:T(8,128)(2,1)S(1)}, u32[]{:S(2)}, u32[]{:S(2)}) async-start(bf16[8,4,32,256]{3,2,1,0:T(8,128)(2,1)} %get-tuple-element.230), calls=%async_computation.27 | async-start | bytes 1048576 | tf_op jit(solution)/shard_map/all_to_all | solution.py:1744
  836.2 19.8 %all-to-all-start.28 = ((bf16[8,16,16,256]{3,2,1,0:T(8,128)(2,1)}), bf16[8,16,16,256]{3,2,1,0:T(8,128)(2,1)S(1)}, u32[]{:S(2)}, u32[]{:S(2)}) async-start(bf16[8,16,16,256]{3,2,1,0:T(8,128)(2,1)} %bitcast.148), calls=%async_computation.28 | async-start | bytes 2097152 | tf_op jit(solution)/shard_map/all_to_all | solution.py:1744
  856.0 23.6 %copy-start.24 = (bf16[8,16,16,256]{3,2,1,0:T(8,128)(2,1)}, bf16[8,16,16,256]{3,2,1,0:T(8,128)(2,1)S(1)}, u32[]{:S(2)}) copy-start(bf16[8,16,16,256]{3,2,1,0:T(8,128)(2,1)S(1)} %all-to-all-done.28.refs_0_) | copy-start | bytes 3145732
  856.0 19.6 %all-to-all-start.29 = ((bf16[8,16,16,256]{3,2,1,0:T(8,128)(2,1)}), bf16[8,16,16,256]{3,2,1,0:T(8,128)(2,1)S(1)}, u32[]{:S(2)}, u32[]{:S(2)}) async-start(bf16[8,16,16,256]{3,2,1,0:T(8,128)(2,1)} %bitcast.145), calls=%async_computation.29 | async-start | bytes 2097152 | tf_op jit(solution)/shard_map/all_to_all | solution.py:1744
  875.6 11.3 all-to-all-start.23
  917.9 30.2 %all-to-all-start.32 = ((bf16[8,2,16,16,256]{4,3,2,1,0:T(8,128)(2,1)}), bf16[8,2,16,16,256]{4,3,2,1,0:T(8,128)(2,1)S(1)}, u32[]{:S(2)}, u32[]{:S(2)}) async-start(bf16[8,2,16,16,256]{4,3,2,1,0:T(8,128)(2,1)} %get-tuple-element.251), calls=%async_computation.33 | async-start | bytes 4194304 | tf_op jit(solution)/shard_map/all_to_all | solution.py:1744
  948.0 24.8 %all-to-all-start.31 = ((bf16[8,16,16,256]{3,2,1,0:T(8,128)(2,1)}), bf16[8,16,16,256]{3,2,1,0:T(8,128)(2,1)S(1)}, u32[]{:S(2)}, u32[]{:S(2)}) async-start(bf16[8,16,16,256]{3,2,1,0:T(8,128)(2,1)} %bitcast.147), calls=%async_computation.32 | async-start | bytes 2097152 | tf_op jit(solution)/shard_map/all_to_all | solution.py:1744
  972.8 58.3 %copy-start.26 = (bf16[8,16,16,256]{3,2,1,0:T(8,128)(2,1)}, bf16[8,16,16,256]{3,2,1,0:T(8,128)(2,1)S(1)}, u32[]{:S(2)}) copy-start(bf16[8,16,16,256]{3,2,1,0:T(8,128)(2,1)S(1)} %all-to-all-done.31.refs_0_) | copy-start | bytes 3145732
  972.8 21.2 %all-to-all-start.33 = ((bf16[8,16,16,256]{3,2,1,0:T(8,128)(2,1)}), bf16[8,16,16,256]{3,2,1,0:T(8,128)(2,1)S(1)}, u32[]{:S(2)}, u32[]{:S(2)}) async-start(bf16[8,16,16,256]{3,2,1,0:T(8,128)(2,1)} %bitcast.146), calls=%async_computation.34 | async-start | bytes 2097152 | tf_op jit(solution)/shard_map/all_to_all | solution.py:1744
  976.9 54.2 %all-reduce.6.cloned.1.call-start = ((), (), s32[]{:S(2)}) async-start(), calls=%async_computation.42 | async-start | bytes 1277952 | tf_op jit(solution)/shard_map/psum | solution.py:2180
  994.1 37.1 %copy-start.28 = (bf16[8,16,16,256]{3,2,1,0:T(8,128)(2,1)}, bf16[8,16,16,256]{3,2,1,0:T(8,128)(2,1)S(1)}, u32[]{:S(2)}) copy-start(bf16[8,16,16,256]{3,2,1,0:T(8,128)(2,1)S(1)} %all-to-all-done.33.refs_1_) | copy-start | bytes 3145732
  994.1 44.3 %all-to-all-start.24 = ((f32[4,8,768]{2,1,0:T(8,128)}), f32[4,8,768]{2,1,0:T(8,128)S(1)}, u32[]{:S(2)}, u32[]{:S(2)}) async-start(f32[4,8,768]{2,1,0:T(8,128)} %all-to-all-done.23), calls=%async_computation.24 | async-start | bytes 196608 | tf_op jit(solution)/shard_map/all_to_all | solution.py:1744
  1069.3 30.4 %all-to-all-start.34 = ((bf16[8,2,16,16,256]{4,3,2,1,0:T(8,128)(2,1)}), bf16[8,2,16,16,256]{4,3,2,1,0:T(8,128)(2,1)S(1)}, u32[]{:S(2)}, u32[]{:S(2)}) async-start(bf16[8,2,16,16,256]{4,3,2,1,0:T(8,128)(2,1)} %get-tuple-element.261), calls=%async_computation.35 | async-start | bytes 4194304 | tf_op jit(solution)/shard_map/all_to_all | solution.py:1744
  1099.7 28.7 %all-to-all-start.39 = ((bf16[8,19,24,128]{3,2,1,0:T(8,128)(2,1)}), bf16[8,19,24,128]{3,2,1,0:T(8,128)(2,1)S(1)}, u32[]{:S(2)}, u32[]{:S(2)}) async-start(bf16[8,19,24,128]{3,2,1,0:T(8,128)(2,1)} %pair_gradient.1), calls=%async_computation.40 | async-start | bytes 1867776 | tf_op jit(solution)/shard_map/all_to_all | solution.py:1744
  1141.2 60.3 %all-to-all-start.36 = ((bf16[4,8,256,128]{3,2,1,0:T(8,128)(2,1)}), bf16[4,8,256,128]{3,2,1,0:T(8,128)(2,1)}, u32[]{:S(2)}, u32[]{:S(2)}) async-start(bf16[4,8,256,128]{3,2,1,0:T(8,128)(2,1)} %bitcast.134), calls=%async_computation.37 | async-start | bytes 4194304 | tf_op jit(solution)/shard_map/all_to_all | solution.py:1744
  1201.5 29.2 %all-to-all-start.37 = ((bf16[4,8,256,128]{3,2,1,0:T(8,128)(2,1)}), bf16[4,8,256,128]{3,2,1,0:T(8,128)(2,1)S(1)}, u32[]{:S(2)}, u32[]{:S(2)}) async-start(bf16[4,8,256,128]{3,2,1,0:T(8,128)(2,1)} %all-to-all-done.36), calls=%async_computation.38 | async-start | bytes 4194304 | tf_op jit(solution)/shard_map/all_to_all | solution.py:1744
  (46 other events, 237.9 us)
Sparse Core Ops, SparseCore 0:
  57.8 43.5 all-gather.9
  312.3 57.2 all-gather.11
  725.4 58.1 reduce-scatter.1
  980.8 50.2 all-reduce.5

commit v3 on v2

--- a/solution.py
+++ b/solution.py
@@ -907,12 +907,12 @@
         out[(slice(None),) + place] = parts[:, half * part : (half + 1) * part]
 
 
-def tri_product_kernel(incoming, operands, first_out, second_out):
+def tri_product_kernel(incoming, operands, *outs):
     def body(channel):
         first = whole_rows(operands, 0, channel)
         second = whole_rows(operands, 1, channel)
         tri = mm_tn(first, second) if incoming else mm_nt(first, second)
-        split_rows(tri, (first_out, second_out), channel)
+        split_rows(tri, outs, channel)
 
     each_channel(operands[0].shape[2], body)
 
@@ -1329,7 +1329,7 @@
     on_last(finish)
 
 
-def tri_product_back_kernel(incoming, grad, operands, first_out, second_out):
+def tri_product_back_kernel(incoming, grad, operands, *outs):
     def body(channel):
         first = whole_rows(operands, 0, channel)
         second = whole_rows(operands, 1, channel)
@@ -1340,8 +1340,8 @@
         else:
             grad_first = mm(tri, second)
             grad_second = mm_tn(tri, first)
-        split_rows(grad_first, (first_out, second_out), 0, channel)
-        split_rows(grad_second, (first_out, second_out), 1, channel)
+        split_rows(grad_first, outs, 0, channel)
+        split_rows(grad_second, outs, 1, channel)
 
     each_channel(operands[0].shape[2], body)
 
@@ -1744,15 +1744,23 @@
     return lax.all_to_all(values, group, split_axis=0, concat_axis=0, tiled=True)
 
 
-def single_attend(single_state, bias, penalty, weights, group):
+def single_project(single_state, weights, devices):
     gain, shift = norm_pair(weights, ATTEND)
     lowered = layer_norm(single_state, gain, shift).astype(BF16)
+    width = lowered.shape[1]
+    qkvg = matmul(lowered, weights[(ATTEND, QKVG)])
+    both = qkvg[:, width : 3 * width].astype(BF16)
+    both = jnp.broadcast_to(both[None], (devices,) + both.shape)
+    return lowered, qkvg, both
+
+
+def single_attend(single_state, projected, bias, penalty, weights):
+    lowered, qkvg, both = projected
     rows, width = lowered.shape
     size = width // SA_HEADS
-    qkvg = matmul(lowered, weights[(ATTEND, QKVG)])
     query = qkvg[:, :width].astype(BF16).reshape(rows, SA_HEADS, size)
     gate = qkvg[:, 3 * width :]
-    both = lax.all_gather(qkvg[:, width : 3 * width].astype(BF16), group, axis=0, tiled=True)
+    both = both.reshape(-1, 2 * width)
     keys_all = both[:, :width].reshape(-1, SA_HEADS, size)
     values_all = both[:, width:].reshape(-1, SA_HEADS, size)
     scores = jnp.einsum(
@@ -1771,7 +1779,7 @@
     )
 
 
-def single_attend_back(saved, grad_update, weights, grads, group):
+def single_attend_back(saved, grad_update, weights, grads):
     single_state, lowered, query, keys_all, values_all, gate, probs, probs_low, mixed, gated_low = saved
     rows, width = lowered.shape
     size = width // SA_HEADS
@@ -1793,7 +1801,13 @@
     parts = jnp.concatenate(
         [key_part.reshape(-1, rows, width), value_part.reshape(-1, rows, width)], axis=-1
     )
-    grad_both = jnp.sum(swap(parts.astype(BF16), group).astype(F32), axis=0)
+    return grad_scores, (parts.astype(BF16), single_state, lowered, grad_query, grad_gate)
+
+
+def single_attend_end(pending, parts, weights, grads):
+    _, single_state, lowered, grad_query, grad_gate = pending
+    rows, width = lowered.shape
+    grad_both = jnp.sum(parts.astype(F32), axis=0)
     grad_qkvg = jnp.concatenate(
         [grad_query.reshape(rows, width), grad_both, grad_gate], axis=-1
     ).astype(BF16)
@@ -1803,19 +1817,7 @@
     grad_single, grads[(ATTEND, NORM_GAIN)], grads[(ATTEND, NORM_BIAS)] = norm_backward(
         single_state, gain, shift, grad_lowered
     )
-    return grad_single, grad_scores
-
-
-def to_plane(values, parts):
-    shape = values.shape
-    values = swap(values.reshape((parts, -1) + shape[1:]), "crop")
-    return swap(values, "z").reshape(shape)
-
-
-def from_plane(values, parts):
-    shape = values.shape
-    values = swap(values.reshape((parts, -1) + shape[1:]), "z")
-    return swap(values, "crop").reshape(shape)
+    return grad_single
 
 
 def after(values, *others):
@@ -1823,7 +1825,26 @@
     return held
 
 
-def pair_path(pair, info, alive, orders, weights, cotangent, middle, between, group, parts):
+def in_turn():
+    last = []
+
+    def send(values, axes):
+        if last:
+            values = after(values, last.pop())[0]
+        moved = swap(values, axes)
+        last.append(moved)
+        return moved
+
+    return send
+
+
+def to_plane(values, parts, send):
+    shape = values.shape
+    values = send(values.reshape((parts, -1) + shape[1:]), "crop")
+    return send(values, "z").reshape(shape)
+
+
+def pair_path(pair, info, alive, orders, weights, cotangent, middle, between, meet, send, group, parts):
     rows, length, width = pair.shape
     hidden = weights[(OUTGOING, PROJ_OUT)].shape[0]
     devices = length // rows
@@ -1837,10 +1858,10 @@
     block = rows // steps
     half = rows // 2
     flip_shape = (devices, rows, rows, width)
-    flip_half = (devices, rows, half, width)
+    product_shape = (devices, 2, part, rows, length)
     product_half = (devices, 2, part, half, length)
+    tri_shape = (devices, part, rows, length)
     tri_half = (devices, part, half, length)
-    tri_rows = (hidden, half, length)
     channel_block = math.gcd(part, 4)
 
     def products(name, kernel, arrays, out_shape):
@@ -1848,12 +1869,18 @@
         out = (out_shape, BF16, axes[len(out_shape)])
         return run_rows(
             kernel, name, part // channel_block,
-            [(Both(halves), axes[halves[0].ndim]) for halves in arrays], [out, out], [], 7,
-        )
-
-    def swap_halves(halves, shape=None):
-        moved = [swap(values, group) for values in halves]
-        return moved if shape is None else [values.reshape(shape) for values in moved]
+            [(Both(pieces), axes[pieces[0].ndim]) for pieces in arrays],
+            [out] * (rows // out_shape[-2]), [], 7,
+        )
+
+    def swap_all(pieces):
+        return [send(values, group) for values in pieces]
+
+    def by_hidden(pieces):
+        return [values.reshape((hidden,) + values.shape[2:]) for values in pieces]
+
+    def by_device(pieces):
+        return [values.reshape((devices, part) + values.shape[1:]) for values in pieces]
 
     def cols(prefix):
         return weights[(prefix, COLS)]
@@ -1871,19 +1898,21 @@
     table = ((TA_HEADS, length, length), F32)
     attend_saves = [((rows, TA_HEADS, length), F32, 0), (state_shape, BF16, 0)]
 
-    (product,) = run_halves(
+    product = run_rows(
         functools.partial(tri_pre_first_kernel, devices, read_first), "outgoing_in", steps,
         [
-            ([info[:half], info[half:]], "smem"), (alive, None), (pair, 0), (tri_cols(OUTGOING), None),
+            (info, "smem"), (alive, None), (pair, 0), (tri_cols(OUTGOING), None),
             (turned((OUTGOING, PROJ_GATE)), None),
         ],
-        [(product_half, BF16, 3)], [product_scratch], 13,
-    )
-    product_one = swap_halves(product)
+        [(product_shape, BF16, 3)], [product_scratch], 13,
+    )
+    between(0, None)
+    product_one = swap_all(product)
     tri_one = products(
         "outgoing_product", functools.partial(tri_product_kernel, False), [product_one], tri_half
     )
-    tri_one = swap_halves(tri_one, tri_rows)
+    tri_one = by_hidden(swap_all(tri_one))
+    tri_one = [tri_one[0], *meet(0, tri_one[1])]
     state_one, product = run_halves(
         functools.partial(tri_join_kernel, devices, read_first), "outgoing_out_incoming_in", steps,
         [
@@ -1893,12 +1922,16 @@
         ],
         [(state_shape, F32, 0), (product_half, BF16, 3)], [tri_scratch, product_scratch], 22,
     )
-    product_two = swap_halves(product)
+    product_two = list(meet(1, *swap_all(product)))
     tri_two = products(
-        "incoming_product", functools.partial(tri_product_kernel, True), [product_two], tri_half
-    )
-    tri_two = swap_halves(tri_two, tri_rows)
-    state_two, bias = run_halves(
+        "incoming_product", functools.partial(tri_product_kernel, True), [product_two], tri_shape
+    )
+    tri_two = by_hidden(swap_all(tri_two))
+    between(1, None)
+    (tri_two,) = meet(2, *tri_two)
+    cotangent = cotangent.reshape(rows, parts, cores, parts, -1, width).transpose(3, 2, 1, 4, 0, 5)
+    cotangent = send(cotangent.reshape(flip_shape), group)
+    state_two, bias = run_rows(
         tri_last_kernel, "incoming_out_starting_bias", steps,
         [
             (state_one, 0), (tri_two, 1), (tri_cols(INCOMING), None),
@@ -1908,18 +1941,16 @@
         [(state_shape, F32, 0), ((TA_HEADS, rows, length), BF16, 1)], [tri_scratch, head_scratch],
     )
     bias_one = lax.all_gather(bias, group, axis=0, tiled=False)
-    cotangent = cotangent.reshape(rows, parts, cores, parts, -1, width).transpose(3, 2, 1, 4, 0, 5)
-    cotangent = swap(cotangent.reshape(flip_shape), group)
-    cotangent = swap(cotangent.reshape((parts, cores) + flip_shape[1:]), "z").reshape(flip_shape)
-    flipped, totals_one, mixed_one = run_halves(
+    flipped, totals_one, mixed_one = run_rows(
         starting_kernel, "starting_attention", steps,
         [
             (alive, None), (state_two, 0), (bias_one, None), (cols(STARTING), None),
             (turned((STARTING, QKVG)), None), (turned((STARTING, OUTPUT)), None),
         ],
-        [(flip_half, BF16, 2)] + attend_saves, [table, flip_scratch], 21,
-    )
-    state_three = Both(swap_halves(flipped))
+        [(flip_shape, BF16, 2)] + attend_saves, [table, flip_scratch], 21,
+    )
+    state_three = Both([send(flipped, group)])
+    cotangent = send(cotangent.reshape((parts, cores) + flip_shape[1:]), "z").reshape(flip_shape)
     (bias,) = run_rows(
         flipped_bias_kernel, "ending_bias", steps,
         [(state_three, 1), (cols(ENDING), None), (weights[(ENDING, BIAS_T)], None)],
@@ -1945,19 +1976,19 @@
         [(state_shape, F32, 0), ((length, rows, width), BF16, 1), ((SA_HEADS, rows, length), BF16, 1)],
         [flip_scratch, ((SA_HEADS, block, length), F32)],
     )
-    pair_out = swap(pair_out.reshape((parts, -1) + pair_out.shape[1:]), "z")
-
     def turn(values):
         heads = values.shape[0]
         sent = values.reshape(heads, rows, devices, rows).transpose(2, 0, 3, 1)
-        return swap(sent, group).transpose(1, 2, 0, 3).reshape(heads, rows, length)
-
-    single_grad_scores = middle(turn(single_bias).astype(F32))
+        return send(sent, group).transpose(1, 2, 0, 3).reshape(heads, rows, length)
+
+    single_grad_scores = turn(middle(turn(single_bias).astype(F32)))
+    pair_out = send(pair_out.reshape((parts, -1) + pair_out.shape[1:]), "z")
+    between(2, None)
     grads = {}
     grad_four, grads[(PAIR, UP)], grads[(PAIR, DOWN)], grads[(ATTEND, PAIR_PROJ)], vecs = run_rows(
         functools.partial(transition_back_kernel, read_last), "pair_transition_back", steps,
         [
-            (state_four, 0), (state_five, 0), (cotangent, 1), (turn(single_grad_scores), 1),
+            (state_four, 0), (state_five, 0), (cotangent, 1), (single_grad_scores, 1),
             (pair_cols, None), (turned((PAIR, UP)), None), (weights[(PAIR, UP)], None),
             (weights[(PAIR, DOWN)], None), (attend_cols, None), (weights[(ATTEND, PAIR_PROJ)], None),
         ],
@@ -1969,9 +2000,6 @@
         [wide, wide, wide, wide, ((SA_HEADS, block, length), F32)], 30,
     )
     grads[(PAIR, VECTORS)] = vecs
-
-    grad_four, pair_out = after(grad_four, pair_out)
-    pair_out = swap(pair_out.reshape(flip_shape), group)
 
     def attention_back(prefix, read, read_grad, source, source_axis, grad, grad_axis, bias, totals, mixed):
         lowered_grad, bias_grad, grads[(prefix, QKVG)], grads[(prefix, OUTPUT)] = run_rows(
@@ -1988,28 +2016,34 @@
             ],
             [table, table], 34,
         )
-        return lowered_grad, swap(bias_grad, group)
+        return lowered_grad, send(bias_grad, group)
 
     lowered_grad, bias_grad = attention_back(
         ENDING, read_flipped, read_plain, state_three, 1, grad_four, 0, bias_two, totals_two, mixed_two
     )
-    bias_grad, pair_out = after(bias_grad, pair_out)
-    pair_out = pair_out.reshape(parts, cores, rows, parts, -1, width).transpose(2, 3, 1, 0, 4, 5)
-    pair_out = pair_out.reshape(rows, length, width)
-    flipped, bias_w_grad, vecs = run_halves(
+    between(3, grads)
+    flipped, bias_w_grad, vecs = run_rows(
         ending_end_kernel, "ending_attention_end", steps,
         [
             (state_three, 1), (grad_four, 0), (lowered_grad, 0), (bias_grad, 2), (cols(ENDING), None),
             (weights[(ENDING, BIAS_W)], None),
         ],
-        [(flip_half, BF16, 2), ((width, 8), F32, None), ((8, width), F32, None)],
+        [(flip_shape, BF16, 2), ((width, 8), F32, None), ((8, width), F32, None)],
         [wide, wide, head_scratch, flip_scratch],
     )
     grads[(ENDING, BIAS_PROJ)], grads[(ENDING, VECTORS)] = bias_w_grad, vecs
-    grad_three = Both(after(*swap_halves(flipped), between(0, grads))[:2])
+    flipped, held = after(flipped, grads[(ATTEND, PAIR_PROJ)])
+    grads[(ATTEND, PAIR_PROJ)] = held
+    grad_three = send(flipped, group)
+    between(4, grads)
+    grad_three = Both(meet(3, grad_three))
+    pair_out = send(pair_out.reshape(flip_shape), group)
+    pair_out = pair_out.reshape(parts, cores, rows, parts, -1, width).transpose(2, 3, 1, 0, 4, 5)
+    pair_out = pair_out.reshape(rows, length, width)
     lowered_grad, bias_grad = attention_back(
         STARTING, read_plain, read_flipped, state_two, 0, grad_three, 1, bias_one, totals_one, mixed_one
     )
+    between(7, grads)
     square = weights[(INCOMING, GATE_OUT)].shape
     (
         grad_two, grad_tri, gate_back, bias_w_grad, grads[(INCOMING, PROJ_OUT)], grads[(INCOMING, GATE_OUT)], vecs,
@@ -2022,19 +2056,19 @@
             (weights[(INCOMING, PROJ_OUT)], None), (weights[(INCOMING, GATE_OUT)], None),
         ],
         [
-            (state_shape, F32, 0), (tri_rows, BF16, 1), (state_shape, BF16, 0),
+            (state_shape, F32, 0), ((hidden, half, length), BF16, 1), (state_shape, BF16, 0),
             ((width, 8), F32, None), (square, F32, None), (square, F32, None), ((8, width), F32, None),
         ],
         [wide, wide, wide, wide, head_scratch, tri_scratch], 26,
     )
     grads[(STARTING, BIAS_PROJ)], grads[(STARTING, VECTORS)] = bias_w_grad, vecs
-    grad_tri = swap_halves([values.reshape(tri_half) for values in grad_tri])
-    grad_tri = after(*grad_tri, between(1, grads))[:2]
+    grad_tri = swap_all(by_device(grad_tri))
     product_grad = products(
         "incoming_product_back", functools.partial(tri_product_back_kernel, True),
         [grad_tri, product_two], product_half,
     )
-    product_grad = swap_halves(product_grad)
+    product_grad = swap_all(product_grad)
+    product_grad = [*meet(4, product_grad[0]), product_grad[1]]
     (
         grad_one, grad_tri, gate_back, grads[(INCOMING, PROJ_GATE)], grads[(OUTGOING, PROJ_OUT)],
         grads[(OUTGOING, GATE_OUT)], vecs,
@@ -2048,25 +2082,26 @@
             (weights[(OUTGOING, PROJ_OUT)], None), (weights[(OUTGOING, GATE_OUT)], None),
         ],
         [
-            (state_shape, F32, 0), (tri_rows, BF16, 1), (state_shape, BF16, 0),
+            (state_shape, F32, 0), ((hidden, half, length), BF16, 1), (state_shape, BF16, 0),
             (weights[(INCOMING, PROJ_GATE)].shape, F32, None), (square, F32, None), (square, F32, None),
             ((8, width), F32, None),
         ],
         [wide, wide, wide, wide, product_scratch, tri_scratch], 37,
     )
     grads[(INCOMING, VECTORS)] = vecs
-    between(2, grads)
-    grad_tri = swap_halves([values.reshape(tri_half) for values in grad_tri])
-    grad_tri = after(*grad_tri, between(3, grads))[:2]
+    between(5, grads)
+    grad_tri = swap_all(by_device(grad_tri))
+    grad_tri = [grad_tri[0], *meet(6, grad_tri[1])]
     product_grad = products(
         "outgoing_product_back", functools.partial(tri_product_back_kernel, False),
-        [grad_tri, product_one], product_half,
-    )
-    product_grad = swap_halves(product_grad)
-    pair_grad, grads[(OUTGOING, PROJ_GATE)], vecs = run_halves(
+        [grad_tri, product_one], product_shape,
+    )
+    (product_grad,) = meet(5, *swap_all(product_grad))
+    between(6, grads)
+    pair_grad, grads[(OUTGOING, PROJ_GATE)], vecs = run_rows(
         functools.partial(tri_first_back_kernel, read_first, order_back), "outgoing_in_back", steps,
         [
-            ([info[:half], info[half:]], "smem"), (alive, None), (pair, 0), (product_grad, 3), (gate_back, 0), (grad_one, 0),
+            (info, "smem"), (alive, None), (pair, 0), (product_grad, 3), (gate_back, 0), (grad_one, 0),
             (tri_cols(OUTGOING), None), (turned((OUTGOING, PROJ_GATE)), None),
             (weights[(OUTGOING, PROJ_GATE)], None),
         ],
@@ -2117,13 +2152,16 @@
         [((STRIDE, RUN, STRIDE), BF16)], [((STRIDE, RUN, STRIDE), F32)],
     )
     rows, length, width = pair.shape[1:]
-    pair_in = swap(pair[0].reshape(parts, -1, length, width), "crop")
-    pair_in, first_runs, lengths = after(pair_in, runs[:pair_lanes], lengths)
-    pair_in = swap(pair_in, "z").reshape(rows, length, width)
-    live = swap(jnp.broadcast_to(lengths.astype(F32), (parts, STRIDE)), "crop")
-    weights = unpack_pair(table, total, lax.all_gather(first_runs, line))
+    send = in_turn()
+    pair_in = send(pair[0].reshape(parts, -1, length, width), "crop")
+    first_runs = lax.all_gather(runs[:pair_lanes], line)
+    pair_in, _, lengths = after(pair_in, runs, lengths)
+    live = lax.all_gather(jnp.broadcast_to(lengths.astype(F32), (8, STRIDE)), "crop")
+    pair_in = send(pair_in, "z").reshape(rows, length, width)
+    weights = unpack_pair(table, total, first_runs)
     pair_in, last_runs = after(pair_in, runs[single_lane:])
-    weights.update(unpack_single(table, total, single_lane, lax.all_gather(last_runs, line)))
+    last_runs = lax.all_gather(last_runs, line)
+    weights.update(unpack_single(table, total, single_lane, last_runs))
     for index, name in enumerate(SINGLE_VECTORS):
         weights[name] = weights[(SINGLE, VECTORS)][index]
     size = rows // parts
@@ -2131,30 +2169,45 @@
     order = blocks.transpose(2, 1, 0).reshape(-1)
     orders = (order.tolist(), np.argsort(order).tolist())
     tokens = (order[:, None] * size + np.arange(size)).reshape(-1)
-    live = live[lax.axis_index("z"), 0]
+    live = live[lax.axis_index("z"), 0, 0]
     width = single.shape[2]
-    both = to_plane(jnp.concatenate([single[0], single_cotangent[0]], axis=1), parts).astype(F32)
-    single_state, single_back = both[:, :width], both[:, width:]
     mask = (tokens.astype(np.float32) < live).astype(F32)
     info = lax.dynamic_slice_in_dim(mask, lax.axis_index(group) * rows, rows).astype(jnp.int32)
     alive = jnp.broadcast_to(mask, (8, length))
     penalty = (mask - 1.0) * MASKED
-    results = {}
+    held = {}
     single_grads = {}
 
     def middle(bias):
-        update, saved = single_attend(single_state, bias, penalty, weights, group)
-        single_mid = single_state + update
+        update, saved = single_attend(held["state"], held["projected"], bias, penalty, weights)
+        single_mid = held["state"] + update
         update, saved_last = transition_forward(single_mid, weights, SINGLE)
-        results[SINGLE] = single_mid + update
-        grad = single_back
-        grad = grad + transition_backward(saved_last, grad, weights, SINGLE, single_grads)
-        more, grad_scores = single_attend_back(saved, grad, weights, single_grads, group)
-        results["single_grad"] = grad + more
+        held["out"] = single_mid + update
+        grad = held["back"] + transition_backward(saved_last, held["back"], weights, SINGLE, single_grads)
+        held["grad"] = grad
+        grad_scores, held["pending"] = single_attend_back(saved, grad, weights, single_grads)
         return grad_scores
 
+    def meet(number, *values):
+        if number == 0:
+            others = [last_runs]
+        elif number == 1:
+            others = [weights[(SINGLE, UP)]]
+        elif number == 2:
+            others = [held["projected"][1]]
+        elif number == 3:
+            others = [reduced[3]]
+        elif number == 4:
+            others = [reduced[2]]
+            reduced[2] = lax.psum(reduced[2], "crop")
+        elif number == 5:
+            others = [reduced[2]]
+        else:
+            others = [reduced[1]]
+        return after(*values, *others)[: len(values)]
+
     def reduce_runs(sent):
-        part = jnp.sum(swap(sent, line).astype(F32), axis=0).astype(BF16)
+        part = jnp.sum(send(sent, line).astype(F32), axis=0).astype(BF16)
         return jnp.sum(lax.all_gather(part, "crop").astype(F32), axis=0)
 
     reduced = {}
@@ -2167,20 +2220,40 @@
 
     def between(number, grads):
         if number == 0:
+            both = jnp.concatenate([single[0], single_cotangent[0]], axis=1)
+            both = to_plane(both, parts, send).astype(F32)
+            held["state"], held["back"] = both[:, :width], both[:, width:]
+            return
+        if number == 1:
+            lowered, qkvg, both = single_project(held["state"], weights, devices)
+            held["projected"] = lowered, qkvg, send(both, group)
+            return
+        if number == 2:
+            pending = held["pending"]
+            moved = send(pending[0], group)
+            grad = held["grad"] + single_attend_end(pending, moved, weights, single_grads)
+            held["both"] = jnp.concatenate([held["out"], grad], axis=1).reshape(parts, -1, 2 * width)
+            return
+        if number == 3:
+            held["both"] = send(held["both"], "z")
+            return
+        if number == 7:
+            both = send(held["both"], "crop").reshape(rows, 2 * width)
+            held[SINGLE] = both[:, :width].astype(BF16), both[:, width:]
+            return
+        if number == 6:
+            reduced[1] = reduce_runs(reduced[1])
+            return
+        if number == 4:
             sent = pack(
                 "single_gradient", table, total, devices, (pair_lanes, STRIDE), attend,
                 [(name, single_grads[name]) for name in SINGLE_MATRICES]
                 + [((ATTEND, PAIR_PROJ), grads[(ATTEND, PAIR_PROJ)])]
                 + [vector_part(grads, (PAIR, VECTORS), ATTEND), (lines_held, lines())],
             )
+            reduced[3] = sent
             reduced[2] = lax.psum_scatter(sent, line, scatter_dimension=0, tiled=False)
-            return sent
-        if number == 1:
-            scattered = reduced[2]
-            reduced[2] = lax.psum(scattered, "crop")
-            return scattered
-        if number == 3:
-            return reduced[2]
+            return
         taken = -(-(pair_lanes * count - (attend + 2 * S // STRIDE) * STRIDE) // (4 * S))
         first = table[(INCOMING, NORM_GAIN)][0]
         sent = pack(
@@ -2192,15 +2265,11 @@
             + [vector_part(grads, (PAIR, VECTORS), PAIR)]
             + [(lines_held[:2], lines()), ((ATTEND, QKVG), single_grads[(ATTEND, QKVG)][: -(-taken // 8) * 8])],
         )
-        reduced[1] = reduce_runs(sent)
-        return None
+        reduced[1] = sent
 
     pair_out, pair_grad, grads = pair_path(
-        pair_in, info, alive, orders, weights, pair_cotangent[0], middle, between, group, parts
-    )
-    pair_grad = from_plane(pair_grad, parts).astype(F32)
-    both = from_plane(jnp.concatenate([results[SINGLE], results["single_grad"]], axis=1), parts)
-    single_out, single_grad = both[:, :width].astype(BF16), both[:, width:]
+        pair_in, info, alive, orders, weights, pair_cotangent[0], middle, between, meet, send, group, parts
+    )
     first = table[(INCOMING, NORM_GAIN)][0]
     taken = -(-(late_lanes * count - (first + 2) * STRIDE) // (4 * H))
     sent = pack(
@@ -2211,6 +2280,9 @@
         + [((INCOMING, PROJ_GATE), grads[(INCOMING, PROJ_GATE)][: -(-taken // 8) * 8])],
     )
     reduced[0] = reduce_runs(sent)
+    pair_grad = send(pair_grad.reshape(parts, -1, length, pair_grad.shape[2]), "z")
+    pair_grad = send(pair_grad, "crop").reshape(rows, length, -1).astype(F32)
+    single_out, single_grad = held[SINGLE]
     shard, squares = whole_call(
         functools.partial(shard_kernel, shard_size), "gradient_share",
         [(place, "smem"), (jnp.concatenate([reduced[part].astype(F32) for part in range(3)], axis=0), None)],

time: 1250 us -> 1160 us (0.928)
  waiting for transfers between devices: 325 us -> 257 us
  starting transfers between devices: 138 us -> 119 us
  Pallas kernels: 447 us -> 431 us
  blocking collectives: 225 us -> 239 us
    all_gather x2, waiting for transfers between devices: 43.1 us -> 0.04 us  [the longest x1 0.02 us: fast_shards(): last_runs = lax.all_gather(last_runs, line)]
    all_to_all x34 -> x29, starting transfers between devices: 138 us -> 119 us  [swap(): lax.all_to_all(values, group, split_axis=0, concat_axis=0, tiled=True)]
    psum x1, waiting for transfers between devices: 33.7 us -> 15.7 us  [meet(): reduced[2] = lax.psum(reduced[2], 'crop')]
    all_to_all x6, blocking collectives: 145 us -> 162 us  [swap(): lax.all_to_all(values, group, split_axis=0, concat_axis=0, tiled=True)]
    pallas_call x26 -> x21, Pallas kernels: 358 us -> 343 us  [run_rows(): pl.pallas_call(run, grid=(grid,), in_specs=in_specs, out_specs=out_specs,...]
    all_to_all x34 -> x29, waiting for transfers between devices: 246 us -> 240 us  [swap(): lax.all_to_all(values, group, split_axis=0, concat_axis=0, tiled=True)]
  transfers between devices with their start and end apart: 38 -> 33, of which waited for: 24 -> 18; matrix products, arithmetic and copies ran while one was open for 4% -> 4% of each run, Pallas kernels for 32% -> 35%
where the time goes in v3:
time: 1160 us; the launch traced here: 1150 us
  Pallas kernels  431 us (37%)
  waiting for transfers between devices  257 us (22%)
  blocking collectives  239 us (21%)
  starting transfers between devices  119 us (10%)
  local copies, waits for them, and re-layouts  38.4 us (3%)
  other arithmetic  24 us (2%)
  matrix products  23.6 us (2%)
  between operations  17.5 us (2%)
    pallas_call x21, Pallas kernels, run_rows(): pl.pallas_call(run, grid=(grid,), in_specs=in_specs, out_specs=out_specs,...  343 us
    all_to_all x29, waiting for transfers between devices, swap(): lax.all_to_all(values, group, split_axis=0, concat_axis=0, tiled=True)  240 us
    all_to_all x6, blocking collectives, swap(): lax.all_to_all(values, group, split_axis=0, concat_axis=0, tiled=True)  162 us
    all_to_all x29, starting transfers between devices, swap(): lax.all_to_all(values, group, split_axis=0, concat_axis=0, tiled=True)  119 us
    pallas_call x7, Pallas kernels, whole_call(): pl.pallas_call(kernel, in_specs=[spec(axis) for array, axis in ins], out_...  87.6 us
    all_gather x1, blocking collectives, fast_shards(): clip_norm = jnp.sqrt(jnp.sum(lax.all_gather(squares, line)))  26.8 us
  transfers between devices with their start and end apart: 33, of which 18 were waited for; matrix products, arithmetic and copies ran while one was open for 4% of the time, Pallas kernels for 35%

profile of v3, /device:TPU:0, one launch (start us, length us, event | category | flops | bytes accessed | tf_op | source)
XLA Modules:
  0.0 1149.0 jit_solution(13814048794620541080)
XLA Ops:
  7.2 5.3 all-to-all-start
  14.3 5.9 parameter_runs.1
  20.3 17.9 %all-to-all-done = bf16[4,8,256,128]{3,2,1,0:T(8,128)(2,1)} async-done(((bf16[4,8,256,128]{3,2,1,0:T(8,128)(2,1)}), bf16[4,8,256,128]{3,2,1,0:T(8,128)(2,1)}, u32[]{:S(2)}, u32[]{:S(2)}) %all-to-all-start) | async-done | bytes 2097184 | tf_op jit(solution)/shard_map/all_to_all | solution.py:1744
  38.2 5.1 all-to-all-start.1
  46.0 8.9 all-reduce.4
  58.3 41.9 %all-to-all-done.1 = bf16[4,8,256,128]{3,2,1,0:T(8,128)(2,1)S(1)} async-done(((bf16[4,8,256,128]{3,2,1,0:T(8,128)(2,1)}), bf16[4,8,256,128]{3,2,1,0:T(8,128)(2,1)S(1)}, u32[]{:S(2)}, u32[]{:S(2)}) %all-to-all-start.1) | async-done | bytes 2097184 | tf_op jit(solution)/shard_map/all_to_all | solution.py:1744
  104.9 8.0 pair_weights.1
  116.8 12.7 %outgoing_in.1 = bf16[8,2,16,32,256]{4,3,2,1,0:T(8,128)(2,1)} custom-call(s32[32]{0:T(128)} %dynamic-slice_convert_fusion.refs_0_, f32[8,256]{1,0:T(8,128)} %broadcast_in_dim.16.refs_1_.refs_0_, bf16[32,256,128]{2,1,0:T(8,128)(2,1)} %bitcast.119, f32[128,8]{1,0:T(8,128)} %get-tuple-element.169.refs_3_.refs_4_.refs_11_.refs_6_, ...), custom_call_target="tpu_custom_call" | custom-call | flops 12999999488 | bytes 39000000 | tf_op jit(solution)/shard_map/outgoing_in/pallas_call | solution.py:762
  129.5 53.6 %all_to_all.175.refs_0_.refs_2_ = bf16[8,2,16,32,256]{4,3,2,1,0:T(8,128)(2,1)} all-to-all(bf16[8,2,16,32,256]{4,3,2,1,0:T(8,128)(2,1)} %outgoing_in.1), channel_id=1, replica_groups=mesh['crop'=4,'z'=4,'core'=2] {'crop','core'}, dimensions={0} | all-to-all | bytes 8388608 | tf_op jit(solution)/shard_map/all_to_all | solution.py:1744
  183.1 6.2 outgoing_product.1
  193.6 14.7 %all-to-all-done.5 = bf16[8,16,16,256]{3,2,1,0:T(8,128)(2,1)S(1)} async-done(((bf16[8,16,16,256]{3,2,1,0:T(8,128)(2,1)}), bf16[8,16,16,256]{3,2,1,0:T(8,128)(2,1)S(1)}, u32[]{:S(2)}, u32[]{:S(2)}) %all-to-all-start.5) | async-done | bytes 1048608 | tf_op jit(solution)/shard_map/all_to_all | solution.py:1744
  212.0 12.4 %outgoing_out_incoming_in.2 = (f32[32,128,256]{2,1,0:T(8,128)}, bf16[8,2,16,16,256]{4,3,2,1,0:T(8,128)(2,1)}) custom-call(s32[16]{0:T(128)} %get-tuple-element.346.refs_0_, f32[8,256]{1,0:T(8,128)} %broadcast_in_dim.16.refs_1_.refs_0_, bf16[32,256,128]{2,1,0:T(8,128)(2,1)} %bitcast.120, bf16[128,16,256]{2,1,0:T(8,128)(2,1)} %bitcast.136, ...), custom_call_target="tpu_custom_call" | custom-call | flops 11000000512 | bytes 33000000 | tf_op jit(solution)/shard_map/outgoing_out_incoming_in/pallas_call | solution.py:762
  231.9 12.5 %outgoing_out_incoming_in.3 = (f32[32,128,256]{2,1,0:T(8,128)}, bf16[8,2,16,16,256]{4,3,2,1,0:T(8,128)(2,1)}) custom-call(s32[16]{0:T(128)} %get-tuple-element.347.refs_0_, f32[8,256]{1,0:T(8,128)} %broadcast_in_dim.16.refs_1_.refs_0_, bf16[32,256,128]{2,1,0:T(8,128)(2,1)} %bitcast.121, ...), custom_call_target="tpu_custom_call", output_to_operand_aliasing={{0}: (9, {})} | custom-call | flops 11000000512 | bytes 33000000 | tf_op jit(solution)/shard_map/outgoing_out_incoming_in/pallas_call | solution.py:762
  244.4 14.1 %all-to-all-done.7.refs_0_.refs_2_ = bf16[8,2,16,16,256]{4,3,2,1,0:T(8,128)(2,1)S(1)} async-done(((bf16[8,2,16,16,256]{4,3,2,1,0:T(8,128)(2,1)}), bf16[8,2,16,16,256]{4,3,2,1,0:T(8,128)(2,1)S(1)}, u32[]{:S(2)}, u32[]{:S(2)}) %all-to-all-start.7) | async-done | bytes 2097184 | tf_op jit(solution)/shard_map/all_to_all | solution.py:1744
  259.8 4.4 all-to-all-start.8
  264.2 28.3 %single_weights.1 = (bf16[384,1536]{1,0:T(8,128)(2,1)}, bf16[384,384]{1,0:T(8,128)(2,1)}, bf16[384,3072]{1,0:T(8,128)(2,1)}, bf16[1536,384]{1,0:T(8,128)(2,1)}, ...) custom-call(bf16[8,105,24,128]{3,2,1,0:T(8,128)(2,1)} %bitcast.160), custom_call_target="tpu_custom_call" | custom-call | flops 8000000000 | bytes 24000000 | tf_op jit(solution)/shard_map/single_weights/pallas_call | solution.py:1682
  292.5 6.3 incoming_product.1
  298.8 4.7 all-to-all-start.9
  308.8 21.4 %all-to-all-done.9 = bf16[8,16,32,256]{3,2,1,0:T(8,128)(2,1)} async-done(((bf16[8,16,32,256]{3,2,1,0:T(8,128)(2,1)}), bf16[8,16,32,256]{3,2,1,0:T(8,128)(2,1)}, u32[]{:S(2)}, u32[]{:S(2)}) %all-to-all-start.9) | async-done | bytes 2097184 | tf_op jit(solution)/shard_map/all_to_all | solution.py:1744
  334.4 13.9 %incoming_out_starting_bias.1 = (f32[32,128,256]{2,1,0:T(8,128)}, bf16[4,32,256]{2,1,0:T(8,128)(2,1)}) custom-call(f32[32,128,256]{2,1,0:T(8,128)} %get-tuple-element.184.refs_0_.refs_6_.refs_2_, bf16[128,32,256]{2,1,0:T(8,128)(2,1)} %bitcast.12.refs_1_.refs_7_, f32[128,8]{1,0:T(8,128)} %get-tuple-element.181.refs_7_.refs_2_.refs_8_.refs_6_, ...), custom_call_target="tpu_custom_call" | custom-call | flops 15000000512 | bytes 45000000 | tf_op jit(solution)/shard_map/incoming_out_starting_bias/pallas_call | solution.py:762
  348.3 12.2 %all-gather.3 = bf16[32,32,256]{2,1,0:T(8,128)(2,1)} all-gather(bf16[4,32,256]{2,1,0:T(8,128)(2,1)} %get-tuple-element.201), channel_id=6, replica_groups=mesh['crop'=4,'z'=4,'core'=2] {'crop','core'}, dimensions={0}, use_global_device_ids=true | all-gather | bytes 589824 | tf_op jit(solution)/shard_map/all_gather | solution.py:1943
  364.8 20.5 %starting_attention.1 = (bf16[8,32,32,128]{3,2,1,0:T(8,128)(2,1)}, f32[32,4,256]{2,1,0:T(4,128)}, bf16[32,128,256]{2,1,0:T(8,128)(2,1)}) custom-call(f32[8,256]{1,0:T(8,128)} %broadcast_in_dim.16.refs_1_.refs_0_, f32[32,128,256]{2,1,0:T(8,128)} %get-tuple-element.200.refs_1_.refs_0_, bf16[8,4,32,256]{3,2,1,0:T(8,128)(2,1)} %bitcast.145, ...), custom_call_target="tpu_custom_call" | custom-call | flops 20999999488 | bytes 63000000 | tf_op jit(solution)/shard_map/starting_attention/pallas_call | solution.py:762
  385.3 6.2 all-to-all-done.11
  391.5 30.9 %all_to_all.176.refs_0_.refs_1_ = bf16[8,32,32,128]{3,2,1,0:T(8,128)(2,1)} all-to-all(bf16[8,32,32,128]{3,2,1,0:T(8,128)(2,1)} %get-tuple-element.207), channel_id=1, replica_groups=mesh['crop'=4,'z'=4,'core'=2] {'crop','core'}, dimensions={0} | all-to-all | bytes 4194304 | tf_op jit(solution)/shard_map/all_to_all | solution.py:1744
  422.4 5.1 all-to-all-start.13
  428.3 5.2 ending_bias.1
  433.4 10.8 all-gather.4
  444.2 19.2 %ending_attention.1 = (f32[32,128,256]{2,1,0:T(8,128)}, f32[32,4,256]{2,1,0:T(4,128)}, bf16[32,128,256]{2,1,0:T(8,128)(2,1)}) custom-call(f32[8,256]{1,0:T(8,128)} %broadcast_in_dim.16.refs_1_.refs_0_, bf16[8,32,32,128]{3,2,1,0:T(8,128)(2,1)} %all_to_all.176.refs_0_.refs_1_, bf16[8,4,32,256]{3,2,1,0:T(8,128)(2,1)} %bitcast.147, ...), custom_call_target="tpu_custom_call" | custom-call | flops 15000000512 | bytes 45000000 | tf_op jit(solution)/shard_map/ending_attention/pallas_call | solution.py:762
  463.4 11.7 %all-to-all-done.13 = bf16[4,2,32,32,128]{4,3,2,1,0:T(8,128)(2,1)S(1)} async-done(((bf16[4,2,32,32,128]{4,3,2,1,0:T(8,128)(2,1)}), bf16[4,2,32,32,128]{4,3,2,1,0:T(8,128)(2,1)S(1)}, u32[]{:S(2)}, u32[]{:S(2)}) %all-to-all-start.13) | async-done | bytes 2097184 | tf_op jit(solution)/shard_map/all_to_all | solution.py:1744
  475.0 15.7 %pair_transition.1 = (f32[32,128,256]{2,1,0:T(8,128)}, bf16[256,32,128]{2,1,0:T(8,128)(2,1)}, bf16[16,32,256]{2,1,0:T(8,128)(2,1)}) custom-call(f32[32,128,256]{2,1,0:T(8,128)} %get-tuple-element.214.refs_0_, f32[128,8]{1,0:T(8,128)} %get-tuple-element.215.refs_1_.refs_4_, bf16[1024,128]{1,0:T(8,128)(2,1)} %get-tuple-element.216.refs_2_.refs_5_, ...), custom_call_target="tpu_custom_call" | custom-call | flops 15000000512 | bytes 45000000 | tf_op jit(solution)/shard_map/pair_transition/pallas_call | solution.py:762
  499.8 5.1 all-to-all-done.14
  552.3 31.0 %pair_transition_back.1 = (f32[32,128,256]{2,1,0:T(8,128)}, f32[128,1024]{1,0:T(8,128)}, f32[512,128]{1,0:T(8,128)}, f32[128,16]{1,0:T(8,128)}, f32[8,128]{1,0:T(8,128)}) custom-call(f32[32,128,256]{2,1,0:T(8,128)} %get-tuple-element.214.refs_0_, f32[32,128,256]{2,1,0:T(8,128)} %get-tuple-element.227.refs_1_, bf16[8,32,32,128]{3,2,1,0:T(8,128)(2,1)} %bitcast.125, ...), custom_call_target="tpu_custom_call" | custom-call | flops 30000001024 | bytes 90000000 | tf_op jit(solution)/shard_map/pair_transition_back/pallas_call | solution.py:762
  583.2 8.4 all-to-all-done.16
  595.8 33.1 %attention_back.2 = (bf16[32,128,256]{2,1,0:T(8,128)(2,1)}, bf16[8,4,32,256]{3,2,1,0:T(8,128)(2,1)}, f32[128,512]{1,0:T(8,128)}, f32[128,128]{1,0:T(8,128)}) custom-call(f32[8,256]{1,0:T(8,128)} %broadcast_in_dim.16.refs_1_.refs_0_, bf16[8,32,32,128]{3,2,1,0:T(8,128)(2,1)} %all_to_all.176.refs_0_.refs_1_, ...), custom_call_target="tpu_custom_call" | custom-call | flops 33999998976 | bytes 102000000 | tf_op jit(solution)/shard_map/attention_back/pallas_call | solution.py:762
  636.2 8.8 all-to-all-done.18.refs_3_
  649.0 12.1 %ending_attention_end.1 = (bf16[8,32,32,128]{3,2,1,0:T(8,128)(2,1)}, f32[128,8]{1,0:T(8,128)}, f32[8,128]{1,0:T(8,128)}) custom-call(bf16[8,32,32,128]{3,2,1,0:T(8,128)(2,1)} %all_to_all.176.refs_0_.refs_1_, f32[32,128,256]{2,1,0:T(8,128)} %get-tuple-element.232.refs_2_.refs_1_, bf16[32,128,256]{2,1,0:T(8,128)(2,1)} %get-tuple-element.237.refs_2_, ...), custom_call_target="tpu_custom_call" | custom-call | flops 15000000512 | bytes 45000000 | tf_op jit(solution)/shard_map/ending_attention_end/pallas_call | solution.py:762
  668.8 30.3 %single_gradient.1 = bf16[8,104,24,128]{3,2,1,0:T(8,128)(2,1)} custom-call(f32[384,1536]{1,0:T(8,128)} %fusion.21.refs_0_, f32[384,384]{1,0:T(8,128)} %fusion.27.refs_1_, f32[384,3072]{1,0:T(8,128)} %fusion.23.refs_2_, f32[1536,384]{1,0:T(8,128)} %fusion.31.refs_3_, f32[128,16]{1,0:T(8,128)} %get-tuple-element.248.refs_4_, ...), custom_call_target="tpu_custom_call" | custom-call | flops 8000000000 | bytes 24000000 | tf_op jit(solution)/shard_map/single_gradient/pallas_call | solution.py:1682
  704.5 33.6 %attention_back.3 = (bf16[32,128,256]{2,1,0:T(8,128)(2,1)}, bf16[8,4,32,256]{3,2,1,0:T(8,128)(2,1)}, f32[128,512]{1,0:T(8,128)}, f32[128,128]{1,0:T(8,128)}) custom-call(f32[8,256]{1,0:T(8,128)} %broadcast_in_dim.16.refs_1_.refs_0_, f32[32,128,256]{2,1,0:T(8,128)} %get-tuple-element.200.refs_1_.refs_0_, bf16[8,32,32,128]{3,2,1,0:T(8,128)(2,1)} %copy-done.9, ...), custom_call_target="tpu_custom_call" | custom-call | flops 33999998976 | bytes 102000000 | tf_op jit(solution)/shard_map/attention_back/pallas_call | solution.py:762
  738.1 14.3 %all_to_all.177.refs_3_ = bf16[8,4,32,256]{3,2,1,0:T(8,128)(2,1)} all-to-all(bf16[8,4,32,256]{3,2,1,0:T(8,128)(2,1)} %get-tuple-element.256), channel_id=1, replica_groups=mesh['crop'=4,'z'=4,'core'=2] {'crop','core'}, dimensions={0} | all-to-all | bytes 1048576 | tf_op jit(solution)/shard_map/all_to_all | solution.py:1744
  755.6 15.9 %starting_end_incoming_out_back.2 = (f32[32,128,256]{2,1,0:T(8,128)}, bf16[128,16,256]{2,1,0:T(8,128)(2,1)}, bf16[32,128,256]{2,1,0:T(8,128)(2,1)}, f32[128,8]{1...) custom-call(f32[32,128,256]{2,1,0:T(8,128)} %get-tuple-element.200.refs_1_.refs_0_, ...), custom_call_target="tpu_custom_call" | custom-call | flops 12999999488 | bytes 39000000 | tf_op jit(solution)/shard_map/starting_end_incoming_out_back/pallas_call | solution.py:762
  775.7 15.9 %starting_end_incoming_out_back.3 = (f32[32,128,256]{2,1,0:T(8,128)}, bf16[128,16,256]{2,1,0:T(8,128)(2,1)}, bf16[32,128,256]{2,1,0:T(8,128)(2,1)}, f32[128,8]{1...) custom-call(f32[32,128,256]{2,1,0:T(8,128)} %get-tuple-element.200.r, ...), custom_call_target="tpu_custom_call", output_to_operand_aliasing={{0}: (13, {}), {2}: (14, {}), {3}: (15, {}), {4}: (16, {}),... | custom-call | flops 12999999488 | bytes 39000000 | tf_op jit(solution)/shard_map/starting_end_incoming_out_back/pallas_call | solution.py:762
  791.6 19.7 %all_to_all.178.refs_1_ = bf16[8,16,16,256]{3,2,1,0:T(8,128)(2,1)} all-to-all(bf16[8,16,16,256]{3,2,1,0:T(8,128)(2,1)} %bitcast.141), channel_id=1, replica_groups=mesh['crop'=4,'z'=4,'core'=2] {'crop','core'}, dimensions={0} | all-to-all | bytes 2097152 | tf_op jit(solution)/shard_map/all_to_all | solution.py:1744
  811.3 7.4 incoming_product_back.1
  818.7 30.9 %all_to_all.179.refs_3_ = bf16[8,2,16,16,256]{4,3,2,1,0:T(8,128)(2,1)} all-to-all(bf16[8,2,16,16,256]{4,3,2,1,0:T(8,128)(2,1)} %get-tuple-element.273), channel_id=1, replica_groups=mesh['crop'=4,'z'=4,'core'=2] {'crop','core'}, dimensions={0} | all-to-all | bytes 4194304 | tf_op jit(solution)/shard_map/all_to_all | solution.py:1744
  849.6 4.8 all-to-all-start.27
  854.4 21.2 %incoming_in_outgoing_out_back.2 = (f32[32,128,256]{2,1,0:T(8,128)}, bf16[128,16,256]{2,1,0:T(8,128)(2,1)}, bf16[32,128,256]{2,1,0:T(8,128)(2,1)}, f32[128,512]{...) custom-call(s32[16]{0:T(128)} %get-tuple-element.346.refs_0_, ...), custom_call_target="tpu_custom_call" | custom-call | flops 18499999744 | bytes 55500000 | tf_op jit(solution)/shard_map/incoming_in_outgoing_out_back/pallas_call | solution.py:762
  875.6 5.5 all-to-all-done.27.refs_3_
  884.6 21.2 %incoming_in_outgoing_out_back.3 = (f32[32,128,256]{2,1,0:T(8,128)}, bf16[128,16,256]{2,1,0:T(8,128)(2,1)}, bf16[32,128,256]{2,1,0:T(8,128)(2,1)}, f32[128,512]{...) custom-call(s32[16]{0:T(128)} %get-tuple-element.347.refs_0_, ...), custom_call_target="tpu_custom_call", output_to_operand_aliasing={{0}: (16, {}), {2}: (17, {}), {3}: (18, {}), {4}: (19, {}),... | custom-call | flops 18499999744 | bytes 55500000 | tf_op jit(solution)/shard_map/incoming_in_outgoing_out_back/pallas_call | solution.py:762
  911.6 7.0 pair_gradient.1
  918.6 6.9 all-to-all-done.29.refs_1_
  925.5 7.3 outgoing_product_back.1
  932.8 4.6 all-to-all-start.30
  939.5 52.2 %all-to-all-done.30.refs_3_ = bf16[8,2,16,32,256]{4,3,2,1,0:T(8,128)(2,1)} async-done(((bf16[8,2,16,32,256]{4,3,2,1,0:T(8,128)(2,1)}), bf16[8,2,16,32,256]{4,3,2,1,0:T(8,128)(2,1)}, u32[]{:S(2)}, u32[]{:S(2)}) %all-to-all-start.30) | async-done | bytes 4194336 | tf_op jit(solution)/shard_map/all_to_all | solution.py:1744
  991.7 15.7 %all-reduce.7.cloned.1.call-done = bf16[104,24,128]{2,1,0:T(8,128)(2,1)} async-done(((bf16[104,24,128]{2,1,0:T(8,128)(2,1)}), bf16[104,24,128]{2,1,0:T(8,128)(2,1)}) %all-reduce.7.cloned.1.call-update) | async-done | bytes 638992 | tf_op jit(solution)/shard_map/psum | solution.py:2202
  1007.4 4.6 all-to-all-start.31
  1012.0 19.9 %outgoing_in_back.1 = (bf16[32,256,128]{2,1,0:T(8,128)(2,1)}, f32[128,512]{1,0:T(8,128)}, f32[8,128]{1,0:T(8,128)}) custom-call(s32[32]{0:T(128)} %dynamic-slice_convert_fusion.refs_0_, f32[8,256]{1,0:T(8,128)} %broadcast_in_dim.16.refs_1_.refs_0_, bf16[32,256,128]{2,1,0:T(8,128)(2,1)} %bitcast.124, bf16[8,2,16,32,256]{4,3,2,1,0:T(8,128)(2,1)} %all-to-all-done.30.refs_3_, ...), custom_call_target="tpu_custom_call" | custom-call | flops 20000000000 | bytes 60000000 | tf_op jit(solution)/shard_map/outgoing_in_back/pallas_call | solution.py:762
  1036.2 13.1 %all_to_all.180 = bf16[8,5,24,128]{3,2,1,0:T(8,128)(2,1)S(1)} all-to-all(bf16[8,5,24,128]{3,2,1,0:T(8,128)(2,1)} %outgoing_gradient.1), channel_id=1, replica_groups=mesh['crop'=4,'z'=4,'core'=2] {'z','core'}, dimensions={0} | all-to-all | bytes 491520 | tf_op jit(solution)/shard_map/all_to_all | solution.py:1744
  1049.3 4.5 all-to-all-start.33
  1057.1 9.8 all-gather.6
  1067.0 7.8 all-gather.5
  1076.1 5.2 gradient_share.1
  1081.3 26.8 %all-gather.7 = f32[64,128]{1,0:T(8,128)S(1)} all-gather(f32[8,128]{1,0:T(8,128)} %get-tuple-element.321), channel_id=10, replica_groups=mesh['crop'=4,'z'=4,'core'=2] {'z','core'}, dimensions={0}, use_global_device_ids=true | all-gather | bytes 36864 | tf_op jit(solution)/shard_map/all_gather | solution.py:2292
  1113.1 7.5 multiply_subtract_fusion
  1120.6 18.1 %all-to-all-done.34 = bf16[4,8,256,128]{3,2,1,0:T(8,128)(2,1)S(1)} async-done(((bf16[4,8,256,128]{3,2,1,0:T(8,128)(2,1)}), bf16[4,8,256,128]{3,2,1,0:T(8,128)(2,1)S(1)}, u32[]{:S(2)}, u32[]{:S(2)}) %all-to-all-start.34) | async-done | bytes 2097184 | tf_op jit(solution)/shard_map/all_to_all | solution.py:1744
  (252 shorter events, 166.2 us)
Async XLA Ops:
  7.2 5.9 copy-start.2
  7.2 31.0 %all-to-all-start = ((bf16[4,8,256,128]{3,2,1,0:T(8,128)(2,1)}), bf16[4,8,256,128]{3,2,1,0:T(8,128)(2,1)}, u32[]{:S(2)}, u32[]{:S(2)}) async-start(bf16[4,8,256,128]{3,2,1,0:T(8,128)(2,1)} %bitcast.117), calls=%async_computation | async-start | bytes 4194304 | tf_op jit(solution)/shard_map/all_to_all | solution.py:1744
  20.2 23.1 %copy-start.19 = (bf16[128,24,128]{2,1,0:T(8,128)(2,1)S(1)}, bf16[128,24,128]{2,1,0:T(8,128)(2,1)}, u32[]{:S(2)}) copy-start(bf16[128,24,128]{2,1,0:T(8,128)(2,1)} %parameter_runs.1) | copy-start | bytes 2359300
  20.2 24.4 %copy-start.51 = (u32[32]{0:T(128)S(1)}, u32[32]{0:T(128)}, u32[]{:S(2)}) copy-start(u32[32]{0:T(128)} %constant.132) | copy-start | bytes 388
  20.2 36.2 %copy-start.46 = (f32[256]{0:T(256)S(1)}, f32[256]{0:T(256)}, u32[]{:S(2)}) copy-start(f32[256]{0:T(256)} %constant.113.clone) | copy-start | bytes 3076
  20.2 37.5 %copy-start.33 = (bf16[1,32,384]{2,1,0:T(8,128)(2,1)S(1)}, bf16[1,32,384]{2,1,0:T(8,128)(2,1)}, u32[]{:S(2)}) copy-start(bf16[1,32,384]{2,1,0:T(8,128)(2,1)} %param.18) | copy-start | bytes 73732
  20.2 37.5 %copy-start.34 = (bf16[1,32,384]{2,1,0:T(8,128)(2,1)S(1)}, bf16[1,32,384]{2,1,0:T(8,128)(2,1)}, u32[]{:S(2)}) copy-start(bf16[1,32,384]{2,1,0:T(8,128)(2,1)} %param.12) | copy-start | bytes 73732
  38.2 62.0 %all-to-all-start.1 = ((bf16[4,8,256,128]{3,2,1,0:T(8,128)(2,1)}), bf16[4,8,256,128]{3,2,1,0:T(8,128)(2,1)S(1)}, u32[]{:S(2)}, u32[]{:S(2)}) async-start(bf16[4,8,256,128]{3,2,1,0:T(8,128)(2,1)} %all-to-all-done), calls=%async_computation.1 | async-start | bytes 4194304 | tf_op jit(solution)/shard_map/all_to_all | solution.py:1744
  43.3 61.6 %all-gather.11.cloned.1.call-start = ((), (), s32[]{:S(2)}) async-start(), calls=%async_computation.38 | async-start | bytes 1327104 | tf_op jit(solution)/shard_map/all_gather | solution.py:2157
  100.2 12.7 %copy-start.6 = (bf16[4,8,256,128]{3,2,1,0:T(8,128)(2,1)}, bf16[4,8,256,128]{3,2,1,0:T(8,128)(2,1)S(1)}, u32[]{:S(2)}) copy-start(bf16[4,8,256,128]{3,2,1,0:T(8,128)(2,1)S(1)} %all-to-all-done.1) | copy-start | bytes 6291460
  100.2 12.7 %all-to-all-start.2 = ((bf16[4,8,768]{2,1,0:T(8,128)(2,1)}), bf16[4,8,768]{2,1,0:T(8,128)(2,1)}, u32[]{:S(2)}, u32[]{:S(2)}) async-start(bf16[4,8,768]{2,1,0:T(8,128)(2,1)} %pad_maximum_fusion.3), calls=%async_computation.2 | async-start | bytes 98304 | tf_op jit(solution)/shard_map/all_to_all | solution.py:1744
  104.1 127.8 %all-gather.13.cloned.1.call-start = ((), (), s32[]{:S(2)}) async-start(), calls=%async_computation.39 | async-start | bytes 5806080 | tf_op jit(solution)/shard_map/all_gather | solution.py:2163
  112.9 16.6 %all-to-all-start.3 = ((bf16[4,8,768]{2,1,0:T(8,128)(2,1)}), bf16[4,8,768]{2,1,0:T(8,128)(2,1)S(1)}, u32[]{:S(2)}, u32[]{:S(2)}) async-start(bf16[4,8,768]{2,1,0:T(8,128)(2,1)} %all-to-all-done.2), calls=%async_computation.3 | async-start | bytes 98304 | tf_op jit(solution)/shard_map/all_to_all | solution.py:1744
  189.3 19.0 %all-to-all-start.5 = ((bf16[8,16,16,256]{3,2,1,0:T(8,128)(2,1)}), bf16[8,16,16,256]{3,2,1,0:T(8,128)(2,1)S(1)}, u32[]{:S(2)}, u32[]{:S(2)}) async-start(bf16[8,16,16,256]{3,2,1,0:T(8,128)(2,1)} %get-tuple-element.175), calls=%async_computation.5 | async-start | bytes 2097152 | tf_op jit(solution)/shard_map/all_to_all | solution.py:1744
  208.4 18.9 %all-to-all-start.6 = ((bf16[8,16,16,256]{3,2,1,0:T(8,128)(2,1)}), bf16[8,16,16,256]{3,2,1,0:T(8,128)(2,1)S(1)}, u32[]{:S(2)}, u32[]{:S(2)}) async-start(bf16[8,16,16,256]{3,2,1,0:T(8,128)(2,1)} %get-tuple-element.176), calls=%async_computation.6 | async-start | bytes 2097152 | tf_op jit(solution)/shard_map/all_to_all | solution.py:1744
  228.3 30.2 %all-to-all-start.7 = ((bf16[8,2,16,16,256]{4,3,2,1,0:T(8,128)(2,1)}), bf16[8,2,16,16,256]{4,3,2,1,0:T(8,128)(2,1)S(1)}, u32[]{:S(2)}, u32[]{:S(2)}) async-start(bf16[8,2,16,16,256]{4,3,2,1,0:T(8,128)(2,1)} %get-tuple-element.186), calls=%async_computation.7 | async-start | bytes 4194304 | tf_op jit(solution)/shard_map/all_to_all | solution.py:1744
  259.8 32.7 %all-to-all-start.8 = ((bf16[8,2,16,16,256]{4,3,2,1,0:T(8,128)(2,1)}), bf16[8,2,16,16,256]{4,3,2,1,0:T(8,128)(2,1)}, u32[]{:S(2)}, u32[]{:S(2)}) async-start(bf16[8,2,16,16,256]{4,3,2,1,0:T(8,128)(2,1)} %get-tuple-element.188), calls=%async_computation.8 | async-start | bytes 4194304 | tf_op jit(solution)/shard_map/all_to_all | solution.py:1744
  298.8 31.3 %all-to-all-start.9 = ((bf16[8,16,32,256]{3,2,1,0:T(8,128)(2,1)}), bf16[8,16,32,256]{3,2,1,0:T(8,128)(2,1)}, u32[]{:S(2)}, u32[]{:S(2)}) async-start(bf16[8,16,32,256]{3,2,1,0:T(8,128)(2,1)} %incoming_product.1), calls=%async_computation.9 | async-start | bytes 4194304 | tf_op jit(solution)/shard_map/all_to_all | solution.py:1744
  307.4 40.8 %copy-start.37 = (f32[32]{0:T(128)}, f32[32]{0:T(128)S(1)}, u32[]{:S(2)}) copy-start(f32[32]{0:T(128)S(1)} %broadcast_multiply_fusion.1) | copy-start | bytes 388
  307.6 40.7 %copy-start.49 = (f32[32]{0:T(128)}, f32[32]{0:T(128)S(1)}, u32[]{:S(2)}) copy-start(f32[32]{0:T(128)S(1)} %multiply_reduce_fusion.6) | copy-start | bytes 388
  307.7 40.6 %copy-start.39 = (f32[32]{0:T(128)}, f32[32]{0:T(128)S(1)}, u32[]{:S(2)}) copy-start(f32[32]{0:T(128)S(1)} %fusion.33) | copy-start | bytes 388
  307.7 40.6 %copy-start.31 = (f32[384]{0:T(512)}, f32[384]{0:T(512)S(1)}, u32[]{:S(2)}) copy-start(f32[384]{0:T(512)S(1)} %get-tuple-element.331) | copy-start | bytes 4612
  307.7 40.6 %copy-start.35 = (f32[384]{0:T(512)}, f32[384]{0:T(512)S(1)}, u32[]{:S(2)}) copy-start(f32[384]{0:T(512)S(1)} %get-tuple-element.330) | copy-start | bytes 4612
  330.9 29.5 %all-to-all-start.10 = ((bf16[8,32,768]{2,1,0:T(8,128)(2,1)}), bf16[8,32,768]{2,1,0:T(8,128)(2,1)S(1)}, u32[]{:S(2)}, u32[]{:S(2)}) async-start(bf16[8,32,768]{2,1,0:T(8,128)(2,1)} %broadcast_in_dim.17), calls=%async_computation.10 | async-start | bytes 786432 | tf_op jit(solution)/shard_map/all_to_all | solution.py:1744
  360.5 31.0 %all-to-all-start.11 = ((bf16[8,32,32,128]{3,2,1,0:T(8,128)(2,1)}), bf16[8,32,32,128]{3,2,1,0:T(8,128)(2,1)}, u32[]{:S(2)}, u32[]{:S(2)}) async-start(bf16[8,32,32,128]{3,2,1,0:T(8,128)(2,1)} %bitcast.17), calls=%async_computation.11 | async-start | bytes 4194304 | tf_op jit(solution)/shard_map/all_to_all | solution.py:1744
  422.4 52.6 %all-to-all-start.13 = ((bf16[4,2,32,32,128]{4,3,2,1,0:T(8,128)(2,1)}), bf16[4,2,32,32,128]{4,3,2,1,0:T(8,128)(2,1)S(1)}, u32[]{:S(2)}, u32[]{:S(2)}) async-start(bf16[4,2,32,32,128]{4,3,2,1,0:T(8,128)(2,1)} %bitcast.19), calls=%async_computation.13 | async-start | bytes 4194304 | tf_op jit(solution)/shard_map/all_to_all | solution.py:1744
  475.0 15.7 %copy-start.8 = (bf16[4,2,32,32,128]{4,3,2,1,0:T(8,128)(2,1)}, bf16[4,2,32,32,128]{4,3,2,1,0:T(8,128)(2,1)S(1)}, u32[]{:S(2)}) copy-start(bf16[4,2,32,32,128]{4,3,2,1,0:T(8,128)(2,1)S(1)} %all-to-all-done.13) | copy-start | bytes 6291460
  494.3 10.7 all-to-all-start.14
  510.9 5.3 copy-start
  517.9 5.1 copy-start.20
  526.6 6.1 copy-start.24
  529.1 6.3 copy-start.14
  529.1 10.4 all-to-all-start.15
  540.1 51.6 %all-to-all-start.16 = ((bf16[4,64,32,128]{3,2,1,0:T(8,128)(2,1)}), bf16[4,64,32,128]{3,2,1,0:T(8,128)(2,1)S(1)}, u32[]{:S(2)}, u32[]{:S(2)}) async-start(bf16[4,64,32,128]{3,2,1,0:T(8,128)(2,1)} %bitcast.126), calls=%async_computation.16 | async-start | bytes 4194304 | tf_op jit(solution)/shard_map/all_to_all | solution.py:1744
  591.6 37.3 %copy-start.1 = (bf16[4,64,32,128]{3,2,1,0:T(8,128)(2,1)}, bf16[4,64,32,128]{3,2,1,0:T(8,128)(2,1)S(1)}, u32[]{:S(2)}) copy-start(bf16[4,64,32,128]{3,2,1,0:T(8,128)(2,1)S(1)} %all-to-all-done.16) | copy-start | bytes 6291460
  591.6 37.3 %all-to-all-start.17 = ((bf16[8,32,768]{2,1,0:T(8,128)(2,1)}), bf16[8,32,768]{2,1,0:T(8,128)(2,1)}, u32[]{:S(2)}, u32[]{:S(2)}) async-start(bf16[8,32,768]{2,1,0:T(8,128)(2,1)} %pad_maximum_fusion.1), calls=%async_computation.17 | async-start | bytes 786432 | tf_op jit(solution)/shard_map/all_to_all | solution.py:1744
  595.7 34.3 %copy-start.4 = (bf16[384,1536]{1,0:T(8,128)(2,1)S(1)}, bf16[384,1536]{1,0:T(8,128)(2,1)}, u32[]{:S(2)}) copy-start(bf16[384,1536]{1,0:T(8,128)(2,1)} %get-tuple-element.194) | copy-start | bytes 3538948
  595.8 34.3 %copy-start.25 = (bf16[32,384]{1,0:T(8,128)(2,1)S(1)}, bf16[32,384]{1,0:T(8,128)(2,1)}, u32[]{:S(2)}) copy-start(bf16[32,384]{1,0:T(8,128)(2,1)} %get-tuple-element.344) | copy-start | bytes 73732
  595.8 34.3 %copy-start.32 = (f32[384]{0:T(512)S(1)}, f32[384]{0:T(512)}, u32[]{:S(2)}) copy-start(f32[384]{0:T(512)} %copy-done.31) | copy-start | bytes 4612
  595.8 34.3 %copy-start.38 = (f32[32]{0:T(128)S(1)}, f32[32]{0:T(128)}, u32[]{:S(2)}) copy-start(f32[32]{0:T(128)} %copy-done.37) | copy-start | bytes 388
  595.8 34.3 %copy-start.40 = (f32[32]{0:T(128)S(1)}, f32[32]{0:T(128)}, u32[]{:S(2)}) copy-start(f32[32]{0:T(128)} %copy-done.39) | copy-start | bytes 388
  595.8 35.4 %copy-start.50 = (f32[32]{0:T(128)S(1)}, f32[32]{0:T(128)}, u32[]{:S(2)}) copy-start(f32[32]{0:T(128)} %copy-done.49) | copy-start | bytes 388
  628.9 6.6 copy-start.28
  631.2 13.8 %all-to-all-start.18 = ((bf16[8,4,32,256]{3,2,1,0:T(8,128)(2,1)}), bf16[8,4,32,256]{3,2,1,0:T(8,128)(2,1)S(1)}, u32[]{:S(2)}, u32[]{:S(2)}) async-start(bf16[8,4,32,256]{3,2,1,0:T(8,128)(2,1)} %get-tuple-element.240), calls=%async_computation.18 | async-start | bytes 1048576 | tf_op jit(solution)/shard_map/all_to_all | solution.py:1744
  645.0 16.1 %all-to-all-start.19 = ((f32[4,8,768]{2,1,0:T(8,128)}), f32[4,8,768]{2,1,0:T(8,128)}, u32[]{:S(2)}, u32[]{:S(2)}) async-start(f32[4,8,768]{2,1,0:T(8,128)} %maximum_bitcast_fusion), calls=%async_computation.19 | async-start | bytes 196608 | tf_op jit(solution)/shard_map/all_to_all | solution.py:1744
  661.1 5.0 copy-start.43
  661.1 5.1 copy-start.44
  661.1 5.7 copy-start.36
  661.2 5.7 copy-start.41
  661.2 37.9 %all-to-all-start.20 = ((bf16[8,32,32,128]{3,2,1,0:T(8,128)(2,1)}), bf16[8,32,32,128]{3,2,1,0:T(8,128)(2,1)S(1)}, u32[]{:S(2)}, u32[]{:S(2)}) async-start(bf16[8,32,32,128]{3,2,1,0:T(8,128)(2,1)} %get-tuple-element.246), calls=%async_computation.20 | async-start | bytes 4194304 | tf_op jit(solution)/shard_map/all_to_all | solution.py:1744
  664.8 189.6 %reduce-scatter.2.cloned.1.call-start = ((), (), s32[]{:S(2)}) async-start(), calls=%async_computation.36 | async-start | bytes 5750784 | tf_op jit(solution)/shard_map/reduce_scatter | solution.py:2255
  700.4 37.7 %all-to-all-start.21 = ((bf16[8,32,32,128]{3,2,1,0:T(8,128)(2,1)}), bf16[8,32,32,128]{3,2,1,0:T(8,128)(2,1)S(1)}, u32[]{:S(2)}, u32[]{:S(2)}) async-start(bf16[8,32,32,128]{3,2,1,0:T(8,128)(2,1)} %bitcast.113), calls=%async_computation.21 | async-start | bytes 4194304 | tf_op jit(solution)/shard_map/all_to_all | solution.py:1744
  752.3 19.2 %all-to-all-start.23 = ((f32[4,8,768]{2,1,0:T(8,128)}), f32[4,8,768]{2,1,0:T(8,128)S(1)}, u32[]{:S(2)}, u32[]{:S(2)}) async-start(f32[4,8,768]{2,1,0:T(8,128)} %all-to-all-done.19), calls=%async_computation.23 | async-start | bytes 196608 | tf_op jit(solution)/shard_map/all_to_all | solution.py:1744
  771.6 20.0 %all-to-all-start.24 = ((bf16[8,16,16,256]{3,2,1,0:T(8,128)(2,1)}), bf16[8,16,16,256]{3,2,1,0:T(8,128)(2,1)S(1)}, u32[]{:S(2)}, u32[]{:S(2)}) async-start(bf16[8,16,16,256]{3,2,1,0:T(8,128)(2,1)} %bitcast.140), calls=%async_computation.24 | async-start | bytes 2097152 | tf_op jit(solution)/shard_map/all_to_all | solution.py:1744
  791.6 19.7 %copy-start.18 = (bf16[8,16,16,256]{3,2,1,0:T(8,128)(2,1)}, bf16[8,16,16,256]{3,2,1,0:T(8,128)(2,1)S(1)}, u32[]{:S(2)}) copy-start(bf16[8,16,16,256]{3,2,1,0:T(8,128)(2,1)S(1)} %all-to-all-done.24.refs_0_) | copy-start | bytes 3145732
  849.6 31.4 %all-to-all-start.27 = ((bf16[8,2,16,16,256]{4,3,2,1,0:T(8,128)(2,1)}), bf16[8,2,16,16,256]{4,3,2,1,0:T(8,128)(2,1)}, u32[]{:S(2)}, u32[]{:S(2)}) async-start(bf16[8,2,16,16,256]{4,3,2,1,0:T(8,128)(2,1)} %get-tuple-element.282), calls=%async_computation.28 | async-start | bytes 4194304 | tf_op jit(solution)/shard_map/all_to_all | solution.py:1744
  881.0 24.8 %all-to-all-start.28 = ((bf16[8,16,16,256]{3,2,1,0:T(8,128)(2,1)}), bf16[8,16,16,256]{3,2,1,0:T(8,128)(2,1)S(1)}, u32[]{:S(2)}, u32[]{:S(2)}) async-start(bf16[8,16,16,256]{3,2,1,0:T(8,128)(2,1)} %bitcast.139), calls=%async_computation.29 | async-start | bytes 2097152 | tf_op jit(solution)/shard_map/all_to_all | solution.py:1744
  905.8 12.8 %copy-start.17 = (bf16[8,16,16,256]{3,2,1,0:T(8,128)(2,1)}, bf16[8,16,16,256]{3,2,1,0:T(8,128)(2,1)S(1)}, u32[]{:S(2)}) copy-start(bf16[8,16,16,256]{3,2,1,0:T(8,128)(2,1)S(1)} %all-to-all-done.28.refs_0_) | copy-start | bytes 3145732
  905.8 19.7 %all-to-all-start.29 = ((bf16[8,16,16,256]{3,2,1,0:T(8,128)(2,1)}), bf16[8,16,16,256]{3,2,1,0:T(8,128)(2,1)}, u32[]{:S(2)}, u32[]{:S(2)}) async-start(bf16[8,16,16,256]{3,2,1,0:T(8,128)(2,1)} %bitcast.138), calls=%async_computation.30 | async-start | bytes 2097152 | tf_op jit(solution)/shard_map/all_to_all | solution.py:1744
  932.8 58.9 %all-to-all-start.30 = ((bf16[8,2,16,32,256]{4,3,2,1,0:T(8,128)(2,1)}), bf16[8,2,16,32,256]{4,3,2,1,0:T(8,128)(2,1)}, u32[]{:S(2)}, u32[]{:S(2)}) async-start(bf16[8,2,16,32,256]{4,3,2,1,0:T(8,128)(2,1)} %outgoing_product_back.1), calls=%async_computation.31 | async-start | bytes 8388608 | tf_op jit(solution)/shard_map/all_to_all | solution.py:1744
  937.4 70.0 %all-reduce.7.cloned.1.call-start = ((), (), s32[]{:S(2)}) async-start(), calls=%async_computation.37 | async-start | bytes 1277952 | tf_op jit(solution)/shard_map/psum | solution.py:2202
  1007.4 28.7 %all-to-all-start.31 = ((bf16[8,19,24,128]{3,2,1,0:T(8,128)(2,1)}), bf16[8,19,24,128]{3,2,1,0:T(8,128)(2,1)S(1)}, u32[]{:S(2)}, u32[]{:S(2)}) async-start(bf16[8,19,24,128]{3,2,1,0:T(8,128)(2,1)} %pair_gradient.1), calls=%async_computation.32 | async-start | bytes 1867776 | tf_op jit(solution)/shard_map/all_to_all | solution.py:1744
  1049.3 60.2 %all-to-all-start.33 = ((bf16[4,8,256,128]{3,2,1,0:T(8,128)(2,1)}), bf16[4,8,256,128]{3,2,1,0:T(8,128)(2,1)}, u32[]{:S(2)}, u32[]{:S(2)}) async-start(bf16[4,8,256,128]{3,2,1,0:T(8,128)(2,1)} %bitcast.127), calls=%async_computation.34 | async-start | bytes 4194304 | tf_op jit(solution)/shard_map/all_to_all | solution.py:1744
  1109.5 29.2 %all-to-all-start.34 = ((bf16[4,8,256,128]{3,2,1,0:T(8,128)(2,1)}), bf16[4,8,256,128]{3,2,1,0:T(8,128)(2,1)S(1)}, u32[]{:S(2)}, u32[]{:S(2)}) async-start(bf16[4,8,256,128]{3,2,1,0:T(8,128)(2,1)} %all-to-all-done.33), calls=%async_computation.35 | async-start | bytes 4194304 | tf_op jit(solution)/shard_map/all_to_all | solution.py:1744
  (21 other events, 66.2 us)
Sparse Core Ops, SparseCore 0:
  46.3 32.0 all-gather.10
  106.6 55.8 all-gather.12
  699.2 60.4 reduce-scatter.1
  941.2 66.1 all-reduce.6

commit v4 on v3

--- a/solution.py
+++ b/solution.py
@@ -1657,8 +1657,22 @@
     runs_from_rows(rows, out, first_lane, base, total)
 
 
-def shard_kernel(whole, info, runs, out, squares):
+def shard_kernel(whole, info, summed, others, out, squares, runs):
     half = STRIDE // 2
+    crops, first, part = summed.shape[0], summed.shape[1], others.shape[1]
+
+    def add(lane, carry):
+        runs[lane] = sum(summed[crop, lane].astype(F32) for crop in range(crops))
+        return carry
+
+    lax.fori_loop(0, first, add, 0)
+    for crop in range(crops):
+
+        def move(lane, carry, crop=crop):
+            runs[first + crop * part + lane] = others[crop, lane].astype(F32)
+            return carry
+
+        lax.fori_loop(0, part, move, 0)
     squares[...] = jnp.zeros(squares.shape, F32)
 
     def one(block, carry):
@@ -1838,12 +1852,6 @@
     return send
 
 
-def to_plane(values, parts, send):
-    shape = values.shape
-    values = send(values.reshape((parts, -1) + shape[1:]), "crop")
-    return send(values, "z").reshape(shape)
-
-
 def pair_path(pair, info, alive, orders, weights, cotangent, middle, between, meet, send, group, parts):
     rows, length, width = pair.shape
     hidden = weights[(OUTGOING, PROJ_OUT)].shape[0]
@@ -1908,6 +1916,7 @@
     )
     between(0, None)
     product_one = swap_all(product)
+    between(9, None)
     tri_one = products(
         "outgoing_product", functools.partial(tri_product_kernel, False), [product_one], tri_half
     )
@@ -2091,12 +2100,13 @@
     grads[(INCOMING, VECTORS)] = vecs
     between(5, grads)
     grad_tri = swap_all(by_device(grad_tri))
-    grad_tri = [grad_tri[0], *meet(6, grad_tri[1])]
+    grad_tri = [grad_tri[0], *meet(5, grad_tri[1])]
+    between(8, grads)
     product_grad = products(
         "outgoing_product_back", functools.partial(tri_product_back_kernel, False),
         [grad_tri, product_one], product_shape,
     )
-    (product_grad,) = meet(5, *swap_all(product_grad))
+    (product_grad,) = swap_all(product_grad)
     between(6, grads)
     pair_grad, grads[(OUTGOING, PROJ_GATE)], vecs = run_rows(
         functools.partial(tri_first_back_kernel, read_first, order_back), "outgoing_in_back", steps,
@@ -2159,7 +2169,7 @@
     live = lax.all_gather(jnp.broadcast_to(lengths.astype(F32), (8, STRIDE)), "crop")
     pair_in = send(pair_in, "z").reshape(rows, length, width)
     weights = unpack_pair(table, total, first_runs)
-    pair_in, last_runs = after(pair_in, runs[single_lane:])
+    last_runs = after(runs[single_lane:], weights[(OUTGOING, COLS)])[0]
     last_runs = lax.all_gather(last_runs, line)
     weights.update(unpack_single(table, total, single_lane, last_runs))
     for index, name in enumerate(SINGLE_VECTORS):
@@ -2199,16 +2209,12 @@
             others = [reduced[3]]
         elif number == 4:
             others = [reduced[2]]
-            reduced[2] = lax.psum(reduced[2], "crop")
-        elif number == 5:
-            others = [reduced[2]]
         else:
             others = [reduced[1]]
         return after(*values, *others)[: len(values)]
 
     def reduce_runs(sent):
-        part = jnp.sum(send(sent, line).astype(F32), axis=0).astype(BF16)
-        return jnp.sum(lax.all_gather(part, "crop").astype(F32), axis=0)
+        return jnp.sum(send(sent, line).astype(F32), axis=0).astype(BF16)
 
     reduced = {}
     lines_held = list(enumerate(SINGLE_VECTORS))
@@ -2221,8 +2227,15 @@
     def between(number, grads):
         if number == 0:
             both = jnp.concatenate([single[0], single_cotangent[0]], axis=1)
-            both = to_plane(both, parts, send).astype(F32)
+            both = after(both, weights[(OUTGOING, COLS)])[0]
+            held["both"] = send(both.reshape(parts, -1, 2 * width), "crop")
+            return
+        if number == 9:
+            both = send(held["both"], "z").reshape(rows, 2 * width).astype(F32)
             held["state"], held["back"] = both[:, :width], both[:, width:]
+            return
+        if number == 8:
+            reduced[1] = reduce_runs(reduced[1])
             return
         if number == 1:
             lowered, qkvg, both = single_project(held["state"], weights, devices)
@@ -2242,7 +2255,8 @@
             held[SINGLE] = both[:, :width].astype(BF16), both[:, width:]
             return
         if number == 6:
-            reduced[1] = reduce_runs(reduced[1])
+            part = send(reduced[2].reshape((parts, -1) + reduced[2].shape[1:]), "crop")
+            reduced[2] = jnp.sum(part.astype(F32), axis=0).astype(BF16)
             return
         if number == 4:
             sent = pack(
@@ -2283,10 +2297,12 @@
     pair_grad = send(pair_grad.reshape(parts, -1, length, pair_grad.shape[2]), "z")
     pair_grad = send(pair_grad, "crop").reshape(rows, length, -1).astype(F32)
     single_out, single_grad = held[SINGLE]
+    summed = lax.all_gather(jnp.concatenate([reduced[0], reduced[1]], axis=0), "crop")
+    others = lax.all_gather(reduced[2], "crop")
     shard, squares = whole_call(
         functools.partial(shard_kernel, shard_size), "gradient_share",
-        [(place, "smem"), (jnp.concatenate([reduced[part].astype(F32) for part in range(3)], axis=0), None)],
-        [((RUN * STRIDE, STRIDE), F32), ((8, STRIDE), F32)], [],
+        [(place, "smem"), (summed, None), (others, None)],
+        [((RUN * STRIDE, STRIDE), F32), ((8, STRIDE), F32)], [((STRIDE, RUN, STRIDE), F32)],
     )
     shard = shard.reshape(-1)[:shard_size]
     clip_norm = jnp.sqrt(jnp.sum(lax.all_gather(squares, line)))
@@ -2315,8 +2331,10 @@
 
 def solution(mesh):
     crops, devices = mesh.devices.shape
-    count = table_of(layout(C, H, S, TA_HEADS, SA_HEADS))[1] // STRIDE
-    fast = devices == 2 * crops and LENGTH % (devices * 16) == 0 and count // devices + 2 <= RUN * STRIDE
+    table, total = table_of(layout(C, H, S, TA_HEADS, SA_HEADS))
+    count = total // STRIDE
+    lanes = STRIDE + -table[(ATTEND, NORM_GAIN)][0] * STRIDE // count
+    fast = devices == 2 * crops and LENGTH % (devices * 16) == 0 and count // devices + 2 <= RUN * STRIDE and lanes % crops == 0
     row = "row"
     if fast:
         mesh = jax.sharding.Mesh(mesh.devices.reshape(crops, crops, 2), ("crop", "z", "core"))

time: 1160 us -> 1180 us (1.017)
  waiting for transfers between devices: 257 us -> 289 us
  blocking collectives: 239 us -> 208 us
    all_to_all x29 -> x31, waiting for transfers between devices: 240 us -> 286 us  [swap(): lax.all_to_all(values, group, split_axis=0, concat_axis=0, tiled=True)]
    all_to_all x6 -> x5, blocking collectives: 162 us -> 131 us  [swap(): lax.all_to_all(values, group, split_axis=0, concat_axis=0, tiled=True)]
    psum x1 -> x0, waiting for transfers between devices: 15.7 us -> none  [meet(): reduced[2] = lax.psum(reduced[2], 'crop')]
    all_to_all x29 -> x31, starting transfers between devices: 119 us -> 129 us  [swap(): lax.all_to_all(values, group, split_axis=0, concat_axis=0, tiled=True)]
  transfers between devices with their start and end apart: 33 -> 34, of which waited for: 18 -> 19; matrix products, arithmetic and copies ran while one was open for 4% -> 5% of each run, Pallas kernels for 35% -> 34%
where the time goes in v4:
time: 1180 us; the launch traced here: 1170 us
  Pallas kernels  431 us (37%)
  waiting for transfers between devices  289 us (24%)
  blocking collectives  208 us (18%)
  starting transfers between devices  130 us (11%)
  local copies, waits for them, and re-layouts  41 us (3%)
  other arithmetic  25.5 us (2%)
  matrix products  25.1 us (2%)
  between operations  17.7 us (2%)
    pallas_call x21, Pallas kernels, run_rows(): pl.pallas_call(run, grid=(grid,), in_specs=in_specs, out_specs=out_specs,...  343 us
    all_to_all x31, waiting for transfers between devices, swap(): lax.all_to_all(values, group, split_axis=0, concat_axis=0, tiled=True)  286 us
    all_to_all x5, blocking collectives, swap(): lax.all_to_all(values, group, split_axis=0, concat_axis=0, tiled=True)  131 us
    all_to_all x31, starting transfers between devices, swap(): lax.all_to_all(values, group, split_axis=0, concat_axis=0, tiled=True)  129 us
    pallas_call x7, Pallas kernels, whole_call(): pl.pallas_call(kernel, in_specs=[spec(axis) for array, axis in ins], out_...  88.3 us
  transfers between devices with their start and end apart: 34, of which 19 were waited for; matrix products, arithmetic and copies ran while one was open for 5% of the time, Pallas kernels for 34%

profile of v4, /device:TPU:0, one launch (start us, length us, event | category | flops | bytes accessed | tf_op | source)
XLA Modules:
  0.0 1167.4 jit_solution(9989225000808545998)
XLA Ops:
  7.2 5.3 all-to-all-start
  14.3 5.9 parameter_runs.1
  21.8 16.3 %all-to-all-done = bf16[4,8,256,128]{3,2,1,0:T(8,128)(2,1)} async-done(((bf16[4,8,256,128]{3,2,1,0:T(8,128)(2,1)}), bf16[4,8,256,128]{3,2,1,0:T(8,128)(2,1)}, u32[]{:S(2)}, u32[]{:S(2)}) %all-to-all-start) | async-done | bytes 2097184 | tf_op jit(solution)/shard_map/all_to_all | solution.py:1758
  38.2 5.1 all-to-all-start.1
  47.2 8.1 pair_weights.1
  57.3 10.3 all-reduce.4
  70.1 51.2 %all-to-all-done.1 = bf16[4,8,256,128]{3,2,1,0:T(8,128)(2,1)S(1)} async-done(((bf16[4,8,256,128]{3,2,1,0:T(8,128)(2,1)}), bf16[4,8,256,128]{3,2,1,0:T(8,128)(2,1)S(1)}, u32[]{:S(2)}, u32[]{:S(2)}) %all-to-all-start.1) | async-done | bytes 2097184 | tf_op jit(solution)/shard_map/all_to_all | solution.py:1758
  125.8 12.8 %outgoing_in.1 = bf16[8,2,16,32,256]{4,3,2,1,0:T(8,128)(2,1)} custom-call(s32[32]{0:T(128)} %dynamic-slice_convert_fusion.refs_0_, f32[8,256]{1,0:T(8,128)} %broadcast_in_dim.16.refs_1_.refs_0_, bf16[32,256,128]{2,1,0:T(8,128)(2,1)} %bitcast.118, f32[128,8]{1,0:T(8,128)} %get-tuple-element.168.refs_3_.refs_4_.refs_11_.refs_6_, ...), custom_call_target="tpu_custom_call" | custom-call | flops 12999999488 | bytes 39000000 | tf_op jit(solution)/shard_map/outgoing_in/pallas_call | solution.py:762
  138.6 53.5 %all_to_all.180.refs_0_.refs_2_ = bf16[8,2,16,32,256]{4,3,2,1,0:T(8,128)(2,1)} all-to-all(bf16[8,2,16,32,256]{4,3,2,1,0:T(8,128)(2,1)} %outgoing_in.1), channel_id=1, replica_groups=mesh['crop'=4,'z'=4,'core'=2] {'crop','core'}, dimensions={0} | all-to-all | bytes 8388608 | tf_op jit(solution)/shard_map/all_to_all | solution.py:1758
  196.4 6.2 outgoing_product.1
  206.8 14.7 %all-to-all-done.5 = bf16[8,16,16,256]{3,2,1,0:T(8,128)(2,1)S(1)} async-done(((bf16[8,16,16,256]{3,2,1,0:T(8,128)(2,1)}), bf16[8,16,16,256]{3,2,1,0:T(8,128)(2,1)S(1)}, u32[]{:S(2)}, u32[]{:S(2)}) %all-to-all-start.5) | async-done | bytes 1048608 | tf_op jit(solution)/shard_map/all_to_all | solution.py:1758
  225.1 12.4 %outgoing_out_incoming_in.2 = (f32[32,128,256]{2,1,0:T(8,128)}, bf16[8,2,16,16,256]{4,3,2,1,0:T(8,128)(2,1)}) custom-call(s32[16]{0:T(128)} %get-tuple-element.346.refs_0_, f32[8,256]{1,0:T(8,128)} %broadcast_in_dim.16.refs_1_.refs_0_, bf16[32,256,128]{2,1,0:T(8,128)(2,1)} %bitcast.119, bf16[128,16,256]{2,1,0:T(8,128)(2,1)} %bitcast.134, ...), custom_call_target="tpu_custom_call" | custom-call | flops 11000000512 | bytes 33000000 | tf_op jit(solution)/shard_map/outgoing_out_incoming_in/pallas_call | solution.py:762
  245.1 12.4 %outgoing_out_incoming_in.3 = (f32[32,128,256]{2,1,0:T(8,128)}, bf16[8,2,16,16,256]{4,3,2,1,0:T(8,128)(2,1)}) custom-call(s32[16]{0:T(128)} %get-tuple-element.347.refs_0_, f32[8,256]{1,0:T(8,128)} %broadcast_in_dim.16.refs_1_.refs_0_, bf16[32,256,128]{2,1,0:T(8,128)(2,1)} %bitcast.120, ...), custom_call_target="tpu_custom_call", output_to_operand_aliasing={{0}: (9, {})} | custom-call | flops 11000000512 | bytes 33000000 | tf_op jit(solution)/shard_map/outgoing_out_incoming_in/pallas_call | solution.py:762
  257.5 14.1 %all-to-all-done.7.refs_0_.refs_2_ = bf16[8,2,16,16,256]{4,3,2,1,0:T(8,128)(2,1)S(1)} async-done(((bf16[8,2,16,16,256]{4,3,2,1,0:T(8,128)(2,1)}), bf16[8,2,16,16,256]{4,3,2,1,0:T(8,128)(2,1)S(1)}, u32[]{:S(2)}, u32[]{:S(2)}) %all-to-all-start.7) | async-done | bytes 2097184 | tf_op jit(solution)/shard_map/all_to_all | solution.py:1758
  277.4 28.4 %single_weights.1 = (bf16[384,1536]{1,0:T(8,128)(2,1)}, bf16[384,384]{1,0:T(8,128)(2,1)}, bf16[384,3072]{1,0:T(8,128)(2,1)}, bf16[1536,384]{1,0:T(8,128)(2,1)}, ...) custom-call(bf16[8,105,24,128]{3,2,1,0:T(8,128)(2,1)} %bitcast.159), custom_call_target="tpu_custom_call" | custom-call | flops 8000000000 | bytes 24000000 | tf_op jit(solution)/shard_map/single_weights/pallas_call | solution.py:1696
  305.8 6.3 incoming_product.1
  312.0 4.7 all-to-all-start.9
  322.6 20.8 %all-to-all-done.9 = bf16[8,16,32,256]{3,2,1,0:T(8,128)(2,1)} async-done(((bf16[8,16,32,256]{3,2,1,0:T(8,128)(2,1)}), bf16[8,16,32,256]{3,2,1,0:T(8,128)(2,1)}, u32[]{:S(2)}, u32[]{:S(2)}) %all-to-all-start.9) | async-done | bytes 2097184 | tf_op jit(solution)/shard_map/all_to_all | solution.py:1758
  347.6 13.9 %incoming_out_starting_bias.1 = (f32[32,128,256]{2,1,0:T(8,128)}, bf16[4,32,256]{2,1,0:T(8,128)(2,1)}) custom-call(f32[32,128,256]{2,1,0:T(8,128)} %get-tuple-element.185.refs_0_.refs_6_.refs_2_, bf16[128,32,256]{2,1,0:T(8,128)(2,1)} %bitcast.13.refs_1_.refs_7_, f32[128,8]{1,0:T(8,128)} %get-tuple-element.182.refs_7_.refs_2_.refs_8_.refs_6_, ...), custom_call_target="tpu_custom_call" | custom-call | flops 15000000512 | bytes 45000000 | tf_op jit(solution)/shard_map/incoming_out_starting_bias/pallas_call | solution.py:762
  361.6 12.2 %all-gather.3 = bf16[32,32,256]{2,1,0:T(8,128)(2,1)} all-gather(bf16[4,32,256]{2,1,0:T(8,128)(2,1)} %get-tuple-element.202), channel_id=6, replica_groups=mesh['crop'=4,'z'=4,'core'=2] {'crop','core'}, dimensions={0}, use_global_device_ids=true | all-gather | bytes 589824 | tf_op jit(solution)/shard_map/all_gather | solution.py:1952
  378.1 20.4 %starting_attention.1 = (bf16[8,32,32,128]{3,2,1,0:T(8,128)(2,1)}, f32[32,4,256]{2,1,0:T(4,128)}, bf16[32,128,256]{2,1,0:T(8,128)(2,1)}) custom-call(f32[8,256]{1,0:T(8,128)} %broadcast_in_dim.16.refs_1_.refs_0_, f32[32,128,256]{2,1,0:T(8,128)} %get-tuple-element.201.refs_1_.refs_0_, bf16[8,4,32,256]{3,2,1,0:T(8,128)(2,1)} %bitcast.145, ...), custom_call_target="tpu_custom_call" | custom-call | flops 20999999488 | bytes 63000000 | tf_op jit(solution)/shard_map/starting_attention/pallas_call | solution.py:762
  398.5 6.2 all-to-all-done.11
  404.8 30.9 %all_to_all.181.refs_0_.refs_1_ = bf16[8,32,32,128]{3,2,1,0:T(8,128)(2,1)} all-to-all(bf16[8,32,32,128]{3,2,1,0:T(8,128)(2,1)} %get-tuple-element.208), channel_id=1, replica_groups=mesh['crop'=4,'z'=4,'core'=2] {'crop','core'}, dimensions={0} | all-to-all | bytes 4194304 | tf_op jit(solution)/shard_map/all_to_all | solution.py:1758
  435.7 5.1 all-to-all-start.13
  441.6 5.2 ending_bias.1
  446.7 10.8 all-gather.4
  457.5 19.2 %ending_attention.1 = (f32[32,128,256]{2,1,0:T(8,128)}, f32[32,4,256]{2,1,0:T(4,128)}, bf16[32,128,256]{2,1,0:T(8,128)(2,1)}) custom-call(f32[8,256]{1,0:T(8,128)} %broadcast_in_dim.16.refs_1_.refs_0_, bf16[8,32,32,128]{3,2,1,0:T(8,128)(2,1)} %all_to_all.181.refs_0_.refs_1_, bf16[8,4,32,256]{3,2,1,0:T(8,128)(2,1)} %bitcast.147, ...), custom_call_target="tpu_custom_call" | custom-call | flops 15000000512 | bytes 45000000 | tf_op jit(solution)/shard_map/ending_attention/pallas_call | solution.py:762
  476.7 11.6 all-to-all-done.13
  488.3 15.9 %pair_transition.1 = (f32[32,128,256]{2,1,0:T(8,128)}, bf16[256,32,128]{2,1,0:T(8,128)(2,1)}, bf16[16,32,256]{2,1,0:T(8,128)(2,1)}) custom-call(f32[32,128,256]{2,1,0:T(8,128)} %get-tuple-element.215.refs_0_, f32[128,8]{1,0:T(8,128)} %get-tuple-element.216.refs_1_.refs_4_, bf16[1024,128]{1,0:T(8,128)(2,1)} %get-tuple-element.217.refs_2_.refs_5_, ...), custom_call_target="tpu_custom_call" | custom-call | flops 15000000512 | bytes 45000000 | tf_op jit(solution)/shard_map/pair_transition/pallas_call | solution.py:762
  513.0 5.2 all-to-all-done.14
  564.7 30.9 %pair_transition_back.1 = (f32[32,128,256]{2,1,0:T(8,128)}, f32[128,1024]{1,0:T(8,128)}, f32[512,128]{1,0:T(8,128)}, f32[128,16]{1,0:T(8,128)}, f32[8,128]{1,0:T(8,128)}) custom-call(f32[32,128,256]{2,1,0:T(8,128)} %get-tuple-element.215.refs_0_, f32[32,128,256]{2,1,0:T(8,128)} %get-tuple-element.228.refs_1_, bf16[8,32,32,128]{3,2,1,0:T(8,128)(2,1)} %bitcast.124, ...), custom_call_target="tpu_custom_call" | custom-call | flops 30000001024 | bytes 90000000 | tf_op jit(solution)/shard_map/pair_transition_back/pallas_call | solution.py:762
  595.6 8.7 all-to-all-done.16
  608.4 33.1 %attention_back.2 = (bf16[32,128,256]{2,1,0:T(8,128)(2,1)}, bf16[8,4,32,256]{3,2,1,0:T(8,128)(2,1)}, f32[128,512]{1,0:T(8,128)}, f32[128,128]{1,0:T(8,128)}) custom-call(f32[8,256]{1,0:T(8,128)} %broadcast_in_dim.16.refs_1_.refs_0_, bf16[8,32,32,128]{3,2,1,0:T(8,128)(2,1)} %all_to_all.181.refs_0_.refs_1_, ...), custom_call_target="tpu_custom_call" | custom-call | flops 33999998976 | bytes 102000000 | tf_op jit(solution)/shard_map/attention_back/pallas_call | solution.py:762
  650.2 8.8 all-to-all-done.18.refs_3_
  662.9 12.0 %ending_attention_end.1 = (bf16[8,32,32,128]{3,2,1,0:T(8,128)(2,1)}, f32[128,8]{1,0:T(8,128)}, f32[8,128]{1,0:T(8,128)}) custom-call(bf16[8,32,32,128]{3,2,1,0:T(8,128)(2,1)} %all_to_all.181.refs_0_.refs_1_, f32[32,128,256]{2,1,0:T(8,128)} %get-tuple-element.233.refs_2_.refs_1_, bf16[32,128,256]{2,1,0:T(8,128)(2,1)} %get-tuple-element.238.refs_2_, ...), custom_call_target="tpu_custom_call" | custom-call | flops 15000000512 | bytes 45000000 | tf_op jit(solution)/shard_map/ending_attention_end/pallas_call | solution.py:762
  687.9 30.3 %single_gradient.1 = bf16[8,104,24,128]{3,2,1,0:T(8,128)(2,1)} custom-call(f32[384,1536]{1,0:T(8,128)} %fusion.21.refs_0_, f32[384,384]{1,0:T(8,128)} %fusion.27.refs_1_, f32[384,3072]{1,0:T(8,128)} %fusion.23.refs_2_, f32[1536,384]{1,0:T(8,128)} %fusion.31.refs_3_, f32[128,16]{1,0:T(8,128)} %get-tuple-element.249.refs_4_, ...), custom_call_target="tpu_custom_call" | custom-call | flops 8000000000 | bytes 24000000 | tf_op jit(solution)/shard_map/single_gradient/pallas_call | solution.py:1696
  723.7 33.5 %attention_back.3 = (bf16[32,128,256]{2,1,0:T(8,128)(2,1)}, bf16[8,4,32,256]{3,2,1,0:T(8,128)(2,1)}, f32[128,512]{1,0:T(8,128)}, f32[128,128]{1,0:T(8,128)}) custom-call(f32[8,256]{1,0:T(8,128)} %broadcast_in_dim.16.refs_1_.refs_0_, f32[32,128,256]{2,1,0:T(8,128)} %get-tuple-element.201.refs_1_.refs_0_, bf16[8,32,32,128]{3,2,1,0:T(8,128)(2,1)} %copy-done.9, ...), custom_call_target="tpu_custom_call" | custom-call | flops 33999998976 | bytes 102000000 | tf_op jit(solution)/shard_map/attention_back/pallas_call | solution.py:762
  757.2 14.0 %all_to_all.182.refs_3_ = bf16[8,4,32,256]{3,2,1,0:T(8,128)(2,1)} all-to-all(bf16[8,4,32,256]{3,2,1,0:T(8,128)(2,1)} %get-tuple-element.257), channel_id=1, replica_groups=mesh['crop'=4,'z'=4,'core'=2] {'crop','core'}, dimensions={0} | all-to-all | bytes 1048576 | tf_op jit(solution)/shard_map/all_to_all | solution.py:1758
  774.6 15.8 %starting_end_incoming_out_back.2 = (f32[32,128,256]{2,1,0:T(8,128)}, bf16[128,16,256]{2,1,0:T(8,128)(2,1)}, bf16[32,128,256]{2,1,0:T(8,128)(2,1)}, f32[128,8]{1...) custom-call(f32[32,128,256]{2,1,0:T(8,128)} %get-tuple-element.201.refs_1_.refs_0_, ...), custom_call_target="tpu_custom_call" | custom-call | flops 12999999488 | bytes 39000000 | tf_op jit(solution)/shard_map/starting_end_incoming_out_back/pallas_call | solution.py:762
  790.4 4.4 all-to-all-start.24
  794.8 15.9 %starting_end_incoming_out_back.3 = (f32[32,128,256]{2,1,0:T(8,128)}, bf16[128,16,256]{2,1,0:T(8,128)(2,1)}, bf16[32,128,256]{2,1,0:T(8,128)(2,1)}, f32[128,8]{1...) custom-call(f32[32,128,256]{2,1,0:T(8,128)} %get-tuple-element.201.r, ...), custom_call_target="tpu_custom_call", output_to_operand_aliasing={{0}: (13, {}), {2}: (14, {}), {3}: (15, {}), {4}: (16, {}),... | custom-call | flops 12999999488 | bytes 39000000 | tf_op jit(solution)/shard_map/starting_end_incoming_out_back/pallas_call | solution.py:762
  810.7 19.7 %all_to_all.183.refs_1_ = bf16[8,16,16,256]{3,2,1,0:T(8,128)(2,1)} all-to-all(bf16[8,16,16,256]{3,2,1,0:T(8,128)(2,1)} %bitcast.139), channel_id=1, replica_groups=mesh['crop'=4,'z'=4,'core'=2] {'crop','core'}, dimensions={0} | all-to-all | bytes 2097152 | tf_op jit(solution)/shard_map/all_to_all | solution.py:1758
  830.4 7.4 incoming_product_back.1
  842.9 25.9 %all-to-all-done.26.refs_3_ = bf16[8,2,16,16,256]{4,3,2,1,0:T(8,128)(2,1)} async-done(((bf16[8,2,16,16,256]{4,3,2,1,0:T(8,128)(2,1)}), bf16[8,2,16,16,256]{4,3,2,1,0:T(8,128)(2,1)}, u32[]{:S(2)}, u32[]{:S(2)}) %all-to-all-start.26) | async-done | bytes 2097184 | tf_op jit(solution)/shard_map/all_to_all | solution.py:1758
  873.2 21.2 %incoming_in_outgoing_out_back.2 = (f32[32,128,256]{2,1,0:T(8,128)}, bf16[128,16,256]{2,1,0:T(8,128)(2,1)}, bf16[32,128,256]{2,1,0:T(8,128)(2,1)}, f32[128,512]{...) custom-call(s32[16]{0:T(128)} %get-tuple-element.346.refs_0_, ...), custom_call_target="tpu_custom_call" | custom-call | flops 18499999744 | bytes 55500000 | tf_op jit(solution)/shard_map/incoming_in_outgoing_out_back/pallas_call | solution.py:762
  894.4 5.5 all-to-all-done.27.refs_3_
  903.4 21.2 %incoming_in_outgoing_out_back.3 = (f32[32,128,256]{2,1,0:T(8,128)}, bf16[128,16,256]{2,1,0:T(8,128)(2,1)}, bf16[32,128,256]{2,1,0:T(8,128)(2,1)}, f32[128,512]{...) custom-call(s32[16]{0:T(128)} %get-tuple-element.347.refs_0_, ...), custom_call_target="tpu_custom_call", output_to_operand_aliasing={{0}: (16, {}), {2}: (17, {}), {3}: (18, {}), {4}: (19, {}),... | custom-call | flops 18499999744 | bytes 55500000 | tf_op jit(solution)/shard_map/incoming_in_outgoing_out_back/pallas_call | solution.py:762
  930.5 7.0 pair_gradient.1
  937.4 6.9 all-to-all-done.29.refs_1_
  944.3 4.9 all-to-all-start.30
  949.3 7.3 outgoing_product_back.1
  956.6 16.8 %all-to-all-done.30 = bf16[8,19,24,128]{3,2,1,0:T(8,128)(2,1)S(1)} async-done(((bf16[8,19,24,128]{3,2,1,0:T(8,128)(2,1)}), bf16[8,19,24,128]{3,2,1,0:T(8,128)(2,1)S(1)}, u32[]{:S(2)}, u32[]{:S(2)}) %all-to-all-start.30) | async-done | bytes 933920 | tf_op jit(solution)/shard_map/all_to_all | solution.py:1758
  973.4 4.6 all-to-all-start.31
  979.6 47.6 %all-to-all-done.31.refs_3_ = bf16[8,2,16,32,256]{4,3,2,1,0:T(8,128)(2,1)} async-done(((bf16[8,2,16,32,256]{4,3,2,1,0:T(8,128)(2,1)}), bf16[8,2,16,32,256]{4,3,2,1,0:T(8,128)(2,1)}, u32[]{:S(2)}, u32[]{:S(2)}) %all-to-all-start.31) | async-done | bytes 4194336 | tf_op jit(solution)/shard_map/all_to_all | solution.py:1758
  1027.1 4.4 all-to-all-start.32
  1031.6 19.9 %outgoing_in_back.1 = (bf16[32,256,128]{2,1,0:T(8,128)(2,1)}, f32[128,512]{1,0:T(8,128)}, f32[8,128]{1,0:T(8,128)}) custom-call(s32[32]{0:T(128)} %dynamic-slice_convert_fusion.refs_0_, f32[8,256]{1,0:T(8,128)} %broadcast_in_dim.16.refs_1_.refs_0_, bf16[32,256,128]{2,1,0:T(8,128)(2,1)} %bitcast.123, bf16[8,2,16,32,256]{4,3,2,1,0:T(8,128)(2,1)} %all-to-all-done.31.refs_3_, ...), custom_call_target="tpu_custom_call" | custom-call | flops 20000000000 | bytes 60000000 | tf_op jit(solution)/shard_map/outgoing_in_back/pallas_call | solution.py:762
  1054.3 12.7 %all_to_all.184 = bf16[8,5,24,128]{3,2,1,0:T(8,128)(2,1)S(1)} all-to-all(bf16[8,5,24,128]{3,2,1,0:T(8,128)(2,1)} %outgoing_gradient.1), channel_id=1, replica_groups=mesh['crop'=4,'z'=4,'core'=2] {'z','core'}, dimensions={0} | all-to-all | bytes 491520 | tf_op jit(solution)/shard_map/all_to_all | solution.py:1758
  1067.0 4.5 all-to-all-start.34
  1076.0 11.8 %all-gather.6 = bf16[104,24,128]{2,1,0:T(8,128)(2,1)} all-gather(bf16[26,24,128]{2,1,0:T(8,128)(2,1)S(1)} %reduce_sum.211), channel_id=9, replica_groups=mesh['crop'=4,'z'=4,'core'=2] {'crop'}, dimensions={0}, use_global_device_ids=true | all-gather | bytes 798720 | tf_op jit(solution)/shard_map/all_gather | solution.py:2301
  1087.8 11.5 all-gather.5
  1099.4 5.9 gradient_share.1
  1105.3 20.6 %all-gather.7 = f32[64,128]{1,0:T(8,128)S(1)} all-gather(f32[8,128]{1,0:T(8,128)} %get-tuple-element.321), channel_id=10, replica_groups=mesh['crop'=4,'z'=4,'core'=2] {'z','core'}, dimensions={0}, use_global_device_ids=true | all-gather | bytes 36864 | tf_op jit(solution)/shard_map/all_gather | solution.py:2308
  1131.4 7.5 multiply_subtract_fusion
  1138.9 17.8 %all-to-all-done.35 = bf16[4,8,256,128]{3,2,1,0:T(8,128)(2,1)S(1)} async-done(((bf16[4,8,256,128]{3,2,1,0:T(8,128)(2,1)}), bf16[4,8,256,128]{3,2,1,0:T(8,128)(2,1)S(1)}, u32[]{:S(2)}, u32[]{:S(2)}) %all-to-all-start.35) | async-done | bytes 2097184 | tf_op jit(solution)/shard_map/all_to_all | solution.py:1758
  (260 shorter events, 184.4 us)
Async XLA Ops:
  7.2 5.9 copy-start.2
  7.2 31.0 %all-to-all-start = ((bf16[4,8,256,128]{3,2,1,0:T(8,128)(2,1)}), bf16[4,8,256,128]{3,2,1,0:T(8,128)(2,1)}, u32[]{:S(2)}, u32[]{:S(2)}) async-start(bf16[4,8,256,128]{3,2,1,0:T(8,128)(2,1)} %bitcast.116), calls=%async_computation | async-start | bytes 4194304 | tf_op jit(solution)/shard_map/all_to_all | solution.py:1758
  12.5 34.7 %all-gather.11.cloned.1.call-start = ((), (), s32[]{:S(2)}) async-start(), calls=%async_computation.38 | async-start | bytes 1327104 | tf_op jit(solution)/shard_map/all_gather | solution.py:2167
  21.8 21.5 %copy-start.18 = (bf16[128,24,128]{2,1,0:T(8,128)(2,1)S(1)}, bf16[128,24,128]{2,1,0:T(8,128)(2,1)}, u32[]{:S(2)}) copy-start(bf16[128,24,128]{2,1,0:T(8,128)(2,1)} %parameter_runs.1) | copy-start | bytes 2359300
  38.2 83.1 %all-to-all-start.1 = ((bf16[4,8,256,128]{3,2,1,0:T(8,128)(2,1)}), bf16[4,8,256,128]{3,2,1,0:T(8,128)(2,1)S(1)}, u32[]{:S(2)}, u32[]{:S(2)}) async-start(bf16[4,8,256,128]{3,2,1,0:T(8,128)(2,1)} %all-to-all-done), calls=%async_computation.1 | async-start | bytes 4194304 | tf_op jit(solution)/shard_map/all_to_all | solution.py:1758
  43.3 201.7 %all-gather.13.cloned.1.call-start = ((), (), s32[]{:S(2)}) async-start(), calls=%async_computation.39 | async-start | bytes 5806080 | tf_op jit(solution)/shard_map/all_gather | solution.py:2173
  47.2 8.8 copy-start.56
  47.2 21.0 %copy-start.52 = (f32[256]{0:T(256)S(1)}, f32[256]{0:T(256)}, u32[]{:S(2)}) copy-start(f32[256]{0:T(256)} %constant.114.clone) | copy-start | bytes 3076
  47.2 22.3 %copy-start.32 = (bf16[1,32,384]{2,1,0:T(8,128)(2,1)S(1)}, bf16[1,32,384]{2,1,0:T(8,128)(2,1)}, u32[]{:S(2)}) copy-start(bf16[1,32,384]{2,1,0:T(8,128)(2,1)} %param.18) | copy-start | bytes 73732
  47.2 22.3 %copy-start.33 = (bf16[1,32,384]{2,1,0:T(8,128)(2,1)S(1)}, bf16[1,32,384]{2,1,0:T(8,128)(2,1)}, u32[]{:S(2)}) copy-start(bf16[1,32,384]{2,1,0:T(8,128)(2,1)} %param.12) | copy-start | bytes 73732
  121.3 4.5 copy-start.6
  121.3 17.3 %all-to-all-start.2 = ((bf16[4,8,768]{2,1,0:T(8,128)(2,1)}), bf16[4,8,768]{2,1,0:T(8,128)(2,1)}, u32[]{:S(2)}, u32[]{:S(2)}) async-start(bf16[4,8,768]{2,1,0:T(8,128)(2,1)} %bitcast.9), calls=%async_computation.2 | async-start | bytes 98304 | tf_op jit(solution)/shard_map/all_to_all | solution.py:1758
  192.1 10.5 all-to-all-start.4
  202.6 18.9 %all-to-all-start.5 = ((bf16[8,16,16,256]{3,2,1,0:T(8,128)(2,1)}), bf16[8,16,16,256]{3,2,1,0:T(8,128)(2,1)S(1)}, u32[]{:S(2)}, u32[]{:S(2)}) async-start(bf16[8,16,16,256]{3,2,1,0:T(8,128)(2,1)} %get-tuple-element.176), calls=%async_computation.5 | async-start | bytes 2097152 | tf_op jit(solution)/shard_map/all_to_all | solution.py:1758
  221.5 18.9 %all-to-all-start.6 = ((bf16[8,16,16,256]{3,2,1,0:T(8,128)(2,1)}), bf16[8,16,16,256]{3,2,1,0:T(8,128)(2,1)S(1)}, u32[]{:S(2)}, u32[]{:S(2)}) async-start(bf16[8,16,16,256]{3,2,1,0:T(8,128)(2,1)} %get-tuple-element.177), calls=%async_computation.6 | async-start | bytes 2097152 | tf_op jit(solution)/shard_map/all_to_all | solution.py:1758
  241.4 30.2 %all-to-all-start.7 = ((bf16[8,2,16,16,256]{4,3,2,1,0:T(8,128)(2,1)}), bf16[8,2,16,16,256]{4,3,2,1,0:T(8,128)(2,1)S(1)}, u32[]{:S(2)}, u32[]{:S(2)}) async-start(bf16[8,2,16,16,256]{4,3,2,1,0:T(8,128)(2,1)} %get-tuple-element.187), calls=%async_computation.7 | async-start | bytes 4194304 | tf_op jit(solution)/shard_map/all_to_all | solution.py:1758
  273.0 32.7 %all-to-all-start.8 = ((bf16[8,2,16,16,256]{4,3,2,1,0:T(8,128)(2,1)}), bf16[8,2,16,16,256]{4,3,2,1,0:T(8,128)(2,1)}, u32[]{:S(2)}, u32[]{:S(2)}) async-start(bf16[8,2,16,16,256]{4,3,2,1,0:T(8,128)(2,1)} %get-tuple-element.189), calls=%async_computation.8 | async-start | bytes 4194304 | tf_op jit(solution)/shard_map/all_to_all | solution.py:1758
  312.0 4.7 copy-start.5
  312.0 31.3 %all-to-all-start.9 = ((bf16[8,16,32,256]{3,2,1,0:T(8,128)(2,1)}), bf16[8,16,32,256]{3,2,1,0:T(8,128)(2,1)}, u32[]{:S(2)}, u32[]{:S(2)}) async-start(bf16[8,16,32,256]{3,2,1,0:T(8,128)(2,1)} %incoming_product.1), calls=%async_computation.9 | async-start | bytes 4194304 | tf_op jit(solution)/shard_map/all_to_all | solution.py:1758
  316.7 4.7 copy-start.53
  316.7 4.8 copy-start.3
  320.7 40.9 %copy-start.38 = (f32[32]{0:T(128)}, f32[32]{0:T(128)S(1)}, u32[]{:S(2)}) copy-start(f32[32]{0:T(128)S(1)} %broadcast_multiply_fusion.1) | copy-start | bytes 388
  321.4 40.1 %copy-start.43 = (f32[32]{0:T(128)}, f32[32]{0:T(128)S(1)}, u32[]{:S(2)}) copy-start(f32[32]{0:T(128)S(1)} %fusion.33) | copy-start | bytes 388
  321.5 40.1 %copy-start.30 = (f32[384]{0:T(512)}, f32[384]{0:T(512)S(1)}, u32[]{:S(2)}) copy-start(f32[384]{0:T(512)S(1)} %get-tuple-element.331) | copy-start | bytes 4612
  321.5 40.1 %copy-start.36 = (f32[384]{0:T(512)}, f32[384]{0:T(512)S(1)}, u32[]{:S(2)}) copy-start(f32[384]{0:T(512)S(1)} %get-tuple-element.330) | copy-start | bytes 4612
  321.5 208.1 %copy-start.34 = (f32[384]{0:T(512)}, f32[384]{0:T(512)S(1)}, u32[]{:S(2)}) copy-start(f32[384]{0:T(512)S(1)} %get-tuple-element.329) | copy-start | bytes 4612
  344.2 29.6 %all-to-all-start.10 = ((bf16[8,32,768]{2,1,0:T(8,128)(2,1)}), bf16[8,32,768]{2,1,0:T(8,128)(2,1)S(1)}, u32[]{:S(2)}, u32[]{:S(2)}) async-start(bf16[8,32,768]{2,1,0:T(8,128)(2,1)} %broadcast_in_dim.17), calls=%async_computation.10 | async-start | bytes 786432 | tf_op jit(solution)/shard_map/all_to_all | solution.py:1758
  373.7 31.0 %all-to-all-start.11 = ((bf16[8,32,32,128]{3,2,1,0:T(8,128)(2,1)}), bf16[8,32,32,128]{3,2,1,0:T(8,128)(2,1)}, u32[]{:S(2)}, u32[]{:S(2)}) async-start(bf16[8,32,32,128]{3,2,1,0:T(8,128)(2,1)} %bitcast.18), calls=%async_computation.11 | async-start | bytes 4194304 | tf_op jit(solution)/shard_map/all_to_all | solution.py:1758
  435.7 52.6 %all-to-all-start.13 = ((bf16[4,2,32,32,128]{4,3,2,1,0:T(8,128)(2,1)}), bf16[4,2,32,32,128]{4,3,2,1,0:T(8,128)(2,1)S(1)}, u32[]{:S(2)}, u32[]{:S(2)}) async-start(bf16[4,2,32,32,128]{4,3,2,1,0:T(8,128)(2,1)} %bitcast.20), calls=%async_computation.13 | async-start | bytes 4194304 | tf_op jit(solution)/shard_map/all_to_all | solution.py:1758
  488.3 15.9 %copy-start.8 = (bf16[4,2,32,32,128]{4,3,2,1,0:T(8,128)(2,1)}, bf16[4,2,32,32,128]{4,3,2,1,0:T(8,128)(2,1)S(1)}, u32[]{:S(2)}) copy-start(bf16[4,2,32,32,128]{4,3,2,1,0:T(8,128)(2,1)S(1)} %all-to-all-done.13) | copy-start | bytes 6291460
  507.7 10.5 all-to-all-start.14
  524.2 5.4 copy-start
  531.2 5.0 copy-start.19
  541.5 10.3 all-to-all-start.15
  552.3 6.0 copy-start.24
  552.3 51.9 %all-to-all-start.16 = ((bf16[4,64,32,128]{3,2,1,0:T(8,128)(2,1)}), bf16[4,64,32,128]{3,2,1,0:T(8,128)(2,1)S(1)}, u32[]{:S(2)}, u32[]{:S(2)}) async-start(bf16[4,64,32,128]{3,2,1,0:T(8,128)(2,1)} %bitcast.125), calls=%async_computation.16 | async-start | bytes 4194304 | tf_op jit(solution)/shard_map/all_to_all | solution.py:1758
  604.2 37.3 %copy-start.1 = (bf16[4,64,32,128]{3,2,1,0:T(8,128)(2,1)}, bf16[4,64,32,128]{3,2,1,0:T(8,128)(2,1)S(1)}, u32[]{:S(2)}) copy-start(bf16[4,64,32,128]{3,2,1,0:T(8,128)(2,1)S(1)} %all-to-all-done.16) | copy-start | bytes 6291460
  604.2 37.3 %all-to-all-start.17 = ((bf16[8,32,768]{2,1,0:T(8,128)(2,1)}), bf16[8,32,768]{2,1,0:T(8,128)(2,1)}, u32[]{:S(2)}, u32[]{:S(2)}) async-start(bf16[8,32,768]{2,1,0:T(8,128)(2,1)} %pad_maximum_fusion), calls=%async_computation.17 | async-start | bytes 786432 | tf_op jit(solution)/shard_map/all_to_all | solution.py:1758
  608.3 34.3 %copy-start.4 = (bf16[384,1536]{1,0:T(8,128)(2,1)S(1)}, bf16[384,1536]{1,0:T(8,128)(2,1)}, u32[]{:S(2)}) copy-start(bf16[384,1536]{1,0:T(8,128)(2,1)} %get-tuple-element.195) | copy-start | bytes 3538948
  608.3 34.3 %copy-start.31 = (f32[384]{0:T(512)S(1)}, f32[384]{0:T(512)}, u32[]{:S(2)}) copy-start(f32[384]{0:T(512)} %copy-done.30) | copy-start | bytes 4612
  641.5 7.7 copy-start.39
  641.5 7.7 copy-start.44
  641.5 8.0 copy-start.29
  645.2 13.8 %all-to-all-start.18 = ((bf16[8,4,32,256]{3,2,1,0:T(8,128)(2,1)}), bf16[8,4,32,256]{3,2,1,0:T(8,128)(2,1)S(1)}, u32[]{:S(2)}, u32[]{:S(2)}) async-start(bf16[8,4,32,256]{3,2,1,0:T(8,128)(2,1)} %get-tuple-element.241), calls=%async_computation.18 | async-start | bytes 1048576 | tf_op jit(solution)/shard_map/all_to_all | solution.py:1758
  659.0 16.0 %all-to-all-start.19 = ((f32[4,8,768]{2,1,0:T(8,128)}), f32[4,8,768]{2,1,0:T(8,128)}, u32[]{:S(2)}, u32[]{:S(2)}) async-start(f32[4,8,768]{2,1,0:T(8,128)} %maximum_bitcast_fusion), calls=%async_computation.19 | async-start | bytes 196608 | tf_op jit(solution)/shard_map/all_to_all | solution.py:1758
  675.0 5.1 copy-start.49
  675.0 5.1 copy-start.48
  675.0 5.1 copy-start.25
  675.0 43.2 %all-to-all-start.20 = ((bf16[8,32,32,128]{3,2,1,0:T(8,128)(2,1)}), bf16[8,32,32,128]{3,2,1,0:T(8,128)(2,1)S(1)}, u32[]{:S(2)}, u32[]{:S(2)}) async-start(bf16[8,32,32,128]{3,2,1,0:T(8,128)(2,1)} %get-tuple-element.247), calls=%async_computation.20 | async-start | bytes 4194304 | tf_op jit(solution)/shard_map/all_to_all | solution.py:1758
  719.5 37.7 %all-to-all-start.21 = ((bf16[8,32,32,128]{3,2,1,0:T(8,128)(2,1)}), bf16[8,32,32,128]{3,2,1,0:T(8,128)(2,1)S(1)}, u32[]{:S(2)}, u32[]{:S(2)}) async-start(bf16[8,32,32,128]{3,2,1,0:T(8,128)(2,1)} %bitcast.112), calls=%async_computation.21 | async-start | bytes 4194304 | tf_op jit(solution)/shard_map/all_to_all | solution.py:1758
  771.3 19.1 %all-to-all-start.23 = ((f32[4,8,768]{2,1,0:T(8,128)}), f32[4,8,768]{2,1,0:T(8,128)S(1)}, u32[]{:S(2)}, u32[]{:S(2)}) async-start(f32[4,8,768]{2,1,0:T(8,128)} %all-to-all-done.19), calls=%async_computation.23 | async-start | bytes 196608 | tf_op jit(solution)/shard_map/all_to_all | solution.py:1758
  790.4 20.3 %all-to-all-start.24 = ((bf16[8,16,16,256]{3,2,1,0:T(8,128)(2,1)}), bf16[8,16,16,256]{3,2,1,0:T(8,128)(2,1)S(1)}, u32[]{:S(2)}, u32[]{:S(2)}) async-start(bf16[8,16,16,256]{3,2,1,0:T(8,128)(2,1)} %bitcast.138), calls=%async_computation.24 | async-start | bytes 2097152 | tf_op jit(solution)/shard_map/all_to_all | solution.py:1758
  810.7 19.7 %copy-start.17 = (bf16[8,16,16,256]{3,2,1,0:T(8,128)(2,1)}, bf16[8,16,16,256]{3,2,1,0:T(8,128)(2,1)S(1)}, u32[]{:S(2)}) copy-start(bf16[8,16,16,256]{3,2,1,0:T(8,128)(2,1)S(1)} %all-to-all-done.24.refs_0_) | copy-start | bytes 3145732
  837.8 31.0 %all-to-all-start.26 = ((bf16[8,2,16,16,256]{4,3,2,1,0:T(8,128)(2,1)}), bf16[8,2,16,16,256]{4,3,2,1,0:T(8,128)(2,1)}, u32[]{:S(2)}, u32[]{:S(2)}) async-start(bf16[8,2,16,16,256]{4,3,2,1,0:T(8,128)(2,1)} %get-tuple-element.274), calls=%async_computation.26 | async-start | bytes 4194304 | tf_op jit(solution)/shard_map/all_to_all | solution.py:1758
  842.2 137.4 %reduce-scatter.2.cloned.1.call-start = ((), (), s32[]{:S(2)}) async-start(), calls=%async_computation.37 | async-start | bytes 5750784 | tf_op jit(solution)/shard_map/reduce_scatter | solution.py:2269
  868.8 31.0 %all-to-all-start.27 = ((bf16[8,2,16,16,256]{4,3,2,1,0:T(8,128)(2,1)}), bf16[8,2,16,16,256]{4,3,2,1,0:T(8,128)(2,1)}, u32[]{:S(2)}, u32[]{:S(2)}) async-start(bf16[8,2,16,16,256]{4,3,2,1,0:T(8,128)(2,1)} %get-tuple-element.282), calls=%async_computation.27 | async-start | bytes 4194304 | tf_op jit(solution)/shard_map/all_to_all | solution.py:1758
  899.8 24.8 %all-to-all-start.28 = ((bf16[8,16,16,256]{3,2,1,0:T(8,128)(2,1)}), bf16[8,16,16,256]{3,2,1,0:T(8,128)(2,1)S(1)}, u32[]{:S(2)}, u32[]{:S(2)}) async-start(bf16[8,16,16,256]{3,2,1,0:T(8,128)(2,1)} %bitcast.137), calls=%async_computation.28 | async-start | bytes 2097152 | tf_op jit(solution)/shard_map/all_to_all | solution.py:1758
  924.6 12.8 %copy-start.16 = (bf16[8,16,16,256]{3,2,1,0:T(8,128)(2,1)}, bf16[8,16,16,256]{3,2,1,0:T(8,128)(2,1)S(1)}, u32[]{:S(2)}) copy-start(bf16[8,16,16,256]{3,2,1,0:T(8,128)(2,1)S(1)} %all-to-all-done.28.refs_0_) | copy-start | bytes 3145732
  924.6 19.7 %all-to-all-start.29 = ((bf16[8,16,16,256]{3,2,1,0:T(8,128)(2,1)}), bf16[8,16,16,256]{3,2,1,0:T(8,128)(2,1)}, u32[]{:S(2)}, u32[]{:S(2)}) async-start(bf16[8,16,16,256]{3,2,1,0:T(8,128)(2,1)} %bitcast.136), calls=%async_computation.29 | async-start | bytes 2097152 | tf_op jit(solution)/shard_map/all_to_all | solution.py:1758
  944.3 29.1 %all-to-all-start.30 = ((bf16[8,19,24,128]{3,2,1,0:T(8,128)(2,1)}), bf16[8,19,24,128]{3,2,1,0:T(8,128)(2,1)S(1)}, u32[]{:S(2)}, u32[]{:S(2)}) async-start(bf16[8,19,24,128]{3,2,1,0:T(8,128)(2,1)} %pair_gradient.1), calls=%async_computation.30 | async-start | bytes 1867776 | tf_op jit(solution)/shard_map/all_to_all | solution.py:1758
  973.4 53.7 %all-to-all-start.31 = ((bf16[8,2,16,32,256]{4,3,2,1,0:T(8,128)(2,1)}), bf16[8,2,16,32,256]{4,3,2,1,0:T(8,128)(2,1)}, u32[]{:S(2)}, u32[]{:S(2)}) async-start(bf16[8,2,16,32,256]{4,3,2,1,0:T(8,128)(2,1)} %outgoing_product_back.1), calls=%async_computation.31 | async-start | bytes 8388608 | tf_op jit(solution)/shard_map/all_to_all | solution.py:1758
  1027.1 27.2 %all-to-all-start.32 = ((bf16[4,26,24,128]{3,2,1,0:T(8,128)(2,1)}), bf16[4,26,24,128]{3,2,1,0:T(8,128)(2,1)}, u32[]{:S(2)}, u32[]{:S(2)}) async-start(bf16[4,26,24,128]{3,2,1,0:T(8,128)(2,1)} %bitcast.142), calls=%async_computation.33 | async-start | bytes 1277952 | tf_op jit(solution)/shard_map/all_to_all | solution.py:1758
  1067.0 60.2 %all-to-all-start.34 = ((bf16[4,8,256,128]{3,2,1,0:T(8,128)(2,1)}), bf16[4,8,256,128]{3,2,1,0:T(8,128)(2,1)}, u32[]{:S(2)}, u32[]{:S(2)}) async-start(bf16[4,8,256,128]{3,2,1,0:T(8,128)(2,1)} %bitcast.126), calls=%async_computation.35 | async-start | bytes 4194304 | tf_op jit(solution)/shard_map/all_to_all | solution.py:1758
  1127.2 29.5 %all-to-all-start.35 = ((bf16[4,8,256,128]{3,2,1,0:T(8,128)(2,1)}), bf16[4,8,256,128]{3,2,1,0:T(8,128)(2,1)S(1)}, u32[]{:S(2)}, u32[]{:S(2)}) async-start(bf16[4,8,256,128]{3,2,1,0:T(8,128)(2,1)} %all-to-all-done.34), calls=%async_computation.36 | async-start | bytes 4194304 | tf_op jit(solution)/shard_map/all_to_all | solution.py:1758
  (27 other events, 81.1 us)
Sparse Core Ops, SparseCore 0:
  21.9 25.2 all-gather.10
  55.4 78.5 all-gather.12
  845.3 60.4 reduce-scatter.1

commit v5 on v4

--- a/solution.py
+++ b/solution.py
@@ -1104,7 +1104,7 @@
     size = pair_out.shape[0] // len(order)
     for place, held in enumerate(order):
         pair_out[place * size : (place + 1) * size] = scratch[held * size : (held + 1) * size].astype(BF16)
-    bias_out[...] = bias_scratch[...].astype(BF16)
+    bias_to_lanes(bias_out, bias_scratch)
 
 
 def transition_back_kernel(
@@ -1113,7 +1113,7 @@
 ):
     zero_first(norm_gain, norm_bias, pair_gain, pair_bias)
     rows = mid.shape[0]
-    bias_scratch[...] = bias_grad[...].astype(F32)
+    lanes_to_bias(bias_scratch, bias_grad)
 
     def body(row):
         grad = join(read, cotangent, row)
@@ -1754,6 +1754,164 @@
     )[0]
 
 
+def bias_to_lanes(out, scratch):
+    heads, devices = scratch.shape[0], out.shape[0]
+    part = scratch.shape[2] // devices
+    per = STRIDE // part
+    lane = lax.broadcasted_iota(jnp.int32, (scratch.shape[1], STRIDE), 1)
+    for device in range(devices):
+        block, place = device // per, device % per
+        for first in range(0, heads, per):
+            total = None
+            for index in range(per):
+                values = scratch[first + index, :, block * STRIDE : (block + 1) * STRIDE]
+                values = pltpu.roll(values, (index - place) * part % STRIDE, 1)
+                total = values if index == 0 else jnp.where(lane < index * part, total, values)
+            out[device, :, first * part : first * part + STRIDE] = total.astype(out.dtype)
+
+
+def lanes_to_bias(scratch, sent):
+    heads, devices = scratch.shape[0], sent.shape[0]
+    part = scratch.shape[2] // devices
+    per = STRIDE // part
+    lane = lax.broadcasted_iota(jnp.int32, (scratch.shape[1], STRIDE), 1)
+    for head in range(heads):
+        first, index = head // per * per, head % per
+        for block in range(devices // per):
+            total = None
+            for place in range(per):
+                values = sent[block * per + place, :, first * part : first * part + STRIDE].astype(F32)
+                values = pltpu.roll(values, (place - index) * part % STRIDE, 1)
+                total = values if place == 0 else jnp.where(lane < place * part, total, values)
+            scratch[head, :, block * STRIDE : (block + 1) * STRIDE] = total
+
+
+def standardize_lanes(values):
+    centred = values - jnp.mean(values, axis=1, keepdims=True)
+    inverse = lax.rsqrt(jnp.mean(centred * centred, axis=1, keepdims=True) + EPSILON)
+    return centred * inverse, inverse
+
+
+def single_kernel(
+    state_in, back_in, project, kv, bias, alive, vectors, output_w, up, down,
+    final_out, grad_out, score_grad, kv_grad, query_grad, gate_grad, output_grad, up_grad, down_grad, vecs,
+):
+    state = state_in[...]
+    rows, width = state.shape
+    size = width // SA_HEADS
+    per = STRIDE // rows
+    groups = SA_HEADS // per
+    scale = size**-0.5
+    tokens = kv.shape[0] * rows
+    both = kv[...].reshape(tokens, 2 * width)
+    keys, values = both[:, :width], both[:, width:]
+    penalty = ((alive[...] - 1.0) * (MASKED * LOG2E)).T[:, 0:1]
+
+    channel = lax.broadcasted_iota(jnp.int32, (width, STRIDE), 0)
+    lane = lax.broadcasted_iota(jnp.int32, (width, STRIDE), 1)
+    own = [lax.div(channel, size) == group * per + lax.div(lane, rows) for group in range(groups)]
+    channel_b = lax.broadcasted_iota(jnp.int32, (STRIDE, width), 1)
+    row_b = lax.broadcasted_iota(jnp.int32, (STRIDE, width), 0)
+    own_b = [lax.div(channel_b, size) == group * per + lax.div(row_b, rows) for group in range(groups)]
+
+    def spread_rows(matrix):
+        turned = jnp.concatenate([matrix] * per, axis=0).T
+        return [jnp.where(mask, turned, 0.0).astype(BF16) for mask in own]
+
+    def collect(blocks):
+        total = sum(jnp.where(mask, block, 0.0) for mask, block in zip(own_b, blocks))
+        return sum(total[index * rows : (index + 1) * rows] for index in range(per))
+
+    queries = spread_rows(project[:, :width] * (scale * LOG2E))
+    gate = sigmoid(project[:, 3 * width :])
+    scores = [
+        mm(keys, queries[group])
+        + bias[:, :, group * STRIDE : (group + 1) * STRIDE].reshape(tokens, STRIDE).astype(F32) * LOG2E
+        + penalty
+        for group in range(groups)
+    ]
+    shifted = [jnp.exp2(block - jnp.max(block, axis=0, keepdims=True)) for block in scores]
+    probs = [block / jnp.sum(block, axis=0, keepdims=True) for block in shifted]
+    probs_low = [block.astype(BF16) for block in probs]
+    mixed = collect([mm_tn(block, values) for block in probs_low])
+    gated = mixed * gate
+    gated_low = gated.astype(BF16)
+    state = state + mm(gated_low, output_w[...])
+
+    unit, inverse = standardize_lanes(state)
+    gain = vectors[2:3]
+    lowered = (unit * gain + vectors[3:4]).astype(BF16)
+    hidden = mm(lowered, up[...])
+    half = hidden.shape[1] // 2
+    first, second = hidden[:, :half], hidden[:, half:]
+    slope = sigmoid(first)
+    silu = first * slope
+    swish = (silu * second).astype(BF16)
+    final_out[...] = state + mm(swish, down[...])
+
+    grad = back_in[...]
+    grad_low = grad.astype(BF16)
+    grad_mixed = mm_nt(grad_low, down[...])
+    down_grad[...] = mm_tn(swish, grad_low)
+    grad_hidden = jnp.concatenate(
+        [
+            (grad_mixed * second * (slope + silu * (1.0 - slope))).astype(BF16),
+            (grad_mixed * silu).astype(BF16),
+        ],
+        axis=1,
+    )
+    grad_lowered = mm_nt(grad_hidden, up[...])
+    vecs[...] = jnp.zeros(vecs.shape, F32)
+    vecs[0:1] = jnp.sum(grad_lowered * unit, axis=0, keepdims=True)
+    vecs[1:2] = jnp.sum(grad_lowered, axis=0, keepdims=True)
+    grad_unit = grad_lowered * gain
+    grad = grad + inverse * (
+        grad_unit
+        - jnp.mean(grad_unit, axis=1, keepdims=True)
+        - unit * jnp.mean(grad_unit * unit, axis=1, keepdims=True)
+    )
+    grad_out[...] = grad
+
+    grad_low = grad.astype(BF16)
+    grad_gated = mm_nt(grad_low, output_w[...])
+    gate_grad[...] = grad_gated * gated * (1.0 - gate)
+    grads = spread_rows(grad_gated * gate)
+    grad_probs = [mm(values, block) for block in grads]
+    grad_scores = []
+    for block, grad_block in zip(probs, grad_probs):
+        delta = jnp.sum(block * grad_block, axis=0, keepdims=True)
+        grad_scores.append((block * (grad_block - delta)).astype(BF16))
+    for group, block in enumerate(grad_scores):
+        score_grad[:, :, group * STRIDE : (group + 1) * STRIDE] = block.reshape(kv.shape[0], rows, STRIDE)
+    query_grad[...] = collect([mm_tn(block, keys) for block in grad_scores]) * scale
+    key_part = sum(mm_nt(block, query) for block, query in zip(grad_scores, queries)) * (1.0 / LOG2E)
+    value_part = sum(mm_nt(block, grad_block) for block, grad_block in zip(probs_low, grads))
+    kv_grad[:, :, :width] = key_part.astype(BF16).reshape(kv.shape[0], rows, width)
+    kv_grad[:, :, width:] = value_part.astype(BF16).reshape(kv.shape[0], rows, width)
+    output_grad[...] = mm_tn(gated_low, grad_low)
+    up_grad[...] = mm_tn(lowered, grad_hidden)
+
+
+def single_middle(state, back, projected, bias, alive, weights):
+    lowered, project, kv = projected
+    rows, width = state.shape
+    devices = kv.shape[0]
+    names = ((ATTEND, OUTPUT), (SINGLE, UP), (SINGLE, DOWN))
+    matrices = [weights[name] for name in names]
+    square = (rows, width)
+    outs = [
+        (square, F32), (square, F32), ((devices, rows, SA_HEADS * rows), BF16),
+        ((devices, rows, 2 * width), BF16), (square, F32), (square, F32),
+    ] + [(matrix.shape, F32) for matrix in matrices] + [((8, width), F32)]
+    ins = [state, back, project, kv, bias, alive, weights[(SINGLE, VECTORS)]] + matrices
+    final, grad, score_grad, kv_grad, query_grad, gate_grad, *found, vecs = whole_call(
+        single_kernel, "single_path", [(array, None) for array in ins], outs, [], 15
+    )
+    grads = dict(zip(names, found))
+    grads[(SINGLE, NORM_GAIN)], grads[(SINGLE, NORM_BIAS)] = vecs[0], vecs[1]
+    return final, grad, score_grad, grads, (kv_grad, state, lowered, query_grad, gate_grad)
+
+
 def swap(values, group):
     return lax.all_to_all(values, group, split_axis=0, concat_axis=0, tiled=True)
 
@@ -1766,56 +1924,6 @@
     both = qkvg[:, width : 3 * width].astype(BF16)
     both = jnp.broadcast_to(both[None], (devices,) + both.shape)
     return lowered, qkvg, both
-
-
-def single_attend(single_state, projected, bias, penalty, weights):
-    lowered, qkvg, both = projected
-    rows, width = lowered.shape
-    size = width // SA_HEADS
-    query = qkvg[:, :width].astype(BF16).reshape(rows, SA_HEADS, size)
-    gate = qkvg[:, 3 * width :]
-    both = both.reshape(-1, 2 * width)
-    keys_all = both[:, :width].reshape(-1, SA_HEADS, size)
-    values_all = both[:, width:].reshape(-1, SA_HEADS, size)
-    scores = jnp.einsum(
-        "ihd,jhd->hij", query, keys_all, preferred_element_type=F32
-    ) * size ** (-0.5)
-    scores = scores + bias + penalty[None, None, :]
-    probs = jax.nn.softmax(scores, axis=-1)
-    probs_low = probs.astype(BF16)
-    mixed = jnp.einsum("hij,jhd->ihd", probs_low, values_all, preferred_element_type=F32)
-    mixed = mixed.reshape(rows, width)
-    gated_low = gated_output(mixed, gate).astype(BF16)
-    update = matmul(gated_low, weights[(ATTEND, OUTPUT)])
-    return (
-        update,
-        (single_state, lowered, query, keys_all, values_all, gate, probs, probs_low, mixed, gated_low),
-    )
-
-
-def single_attend_back(saved, grad_update, weights, grads):
-    single_state, lowered, query, keys_all, values_all, gate, probs, probs_low, mixed, gated_low = saved
-    rows, width = lowered.shape
-    size = width // SA_HEADS
-    scale = size ** (-0.5)
-    grad_low = grad_update.astype(BF16)
-    grads[(ATTEND, OUTPUT)] = outer_sum(gated_low, grad_low)
-    grad_gated = matmul(grad_low, weights[(ATTEND, OUTPUT)].T)
-    _, pullback = jax.vjp(gated_output, mixed, gate)
-    grad_mixed, grad_gate = pullback(grad_gated)
-    grad_mixed = grad_mixed.astype(BF16).reshape(rows, SA_HEADS, size)
-    grad_probs = jnp.einsum("ihd,jhd->hij", grad_mixed, values_all, preferred_element_type=F32)
-    delta = jnp.sum(probs * grad_probs, axis=-1, keepdims=True)
-    grad_scores = (probs * (grad_probs - delta)).astype(BF16)
-    grad_query = (
-        jnp.einsum("hij,jhd->ihd", grad_scores, keys_all, preferred_element_type=F32) * scale
-    )
-    key_part = jnp.einsum("hij,ihd->jhd", grad_scores, query, preferred_element_type=F32) * scale
-    value_part = jnp.einsum("hij,ihd->jhd", probs_low, grad_mixed, preferred_element_type=F32)
-    parts = jnp.concatenate(
-        [key_part.reshape(-1, rows, width), value_part.reshape(-1, rows, width)], axis=-1
-    )
-    return grad_scores, (parts.astype(BF16), single_state, lowered, grad_query, grad_gate)
 
 
 def single_attend_end(pending, parts, weights, grads):
@@ -1914,7 +2022,7 @@
         ],
         [(product_shape, BF16, 3)], [product_scratch], 13,
     )
-    between(0, None)
+    between(0, product[0])
     product_one = swap_all(product)
     between(9, None)
     tri_one = products(
@@ -1982,15 +2090,10 @@
             (state_four, 0), (pair_cols, None), (turned((PAIR, UP)), None), (turned((PAIR, DOWN)), None),
             (attend_cols, None), (turned((ATTEND, PAIR_PROJ)), None),
         ],
-        [(state_shape, F32, 0), ((length, rows, width), BF16, 1), ((SA_HEADS, rows, length), BF16, 1)],
+        [(state_shape, F32, 0), ((length, rows, width), BF16, 1), ((devices, rows, SA_HEADS * rows), BF16, 1)],
         [flip_scratch, ((SA_HEADS, block, length), F32)],
     )
-    def turn(values):
-        heads = values.shape[0]
-        sent = values.reshape(heads, rows, devices, rows).transpose(2, 0, 3, 1)
-        return send(sent, group).transpose(1, 2, 0, 3).reshape(heads, rows, length)
-
-    single_grad_scores = turn(middle(turn(single_bias).astype(F32)))
+    single_grad_scores = send(middle(send(single_bias, group)), group)
     pair_out = send(pair_out.reshape((parts, -1) + pair_out.shape[1:]), "z")
     between(2, None)
     grads = {}
@@ -2101,7 +2204,6 @@
     between(5, grads)
     grad_tri = swap_all(by_device(grad_tri))
     grad_tri = [grad_tri[0], *meet(5, grad_tri[1])]
-    between(8, grads)
     product_grad = products(
         "outgoing_product_back", functools.partial(tri_product_back_kernel, False),
         [grad_tri, product_one], product_shape,
@@ -2138,8 +2240,10 @@
 }
 
 
-def vector_part(grads, name, prefix):
-    pairs = [(row, held) for row, held in enumerate(HELD[name]) if prefix in (None, held[0])]
+def vector_part(grads, table, name, first, last):
+    pairs = [
+        (row, held) for row, held in enumerate(HELD[name]) if first <= table[held][0] < last
+    ]
     return (pairs, grads[name])
 
 
@@ -2169,11 +2273,6 @@
     live = lax.all_gather(jnp.broadcast_to(lengths.astype(F32), (8, STRIDE)), "crop")
     pair_in = send(pair_in, "z").reshape(rows, length, width)
     weights = unpack_pair(table, total, first_runs)
-    last_runs = after(runs[single_lane:], weights[(OUTGOING, COLS)])[0]
-    last_runs = lax.all_gather(last_runs, line)
-    weights.update(unpack_single(table, total, single_lane, last_runs))
-    for index, name in enumerate(SINGLE_VECTORS):
-        weights[name] = weights[(SINGLE, VECTORS)][index]
     size = rows // parts
     blocks = np.arange(length // size).reshape(parts, cores, parts)
     order = blocks.transpose(2, 1, 0).reshape(-1)
@@ -2184,23 +2283,18 @@
     mask = (tokens.astype(np.float32) < live).astype(F32)
     info = lax.dynamic_slice_in_dim(mask, lax.axis_index(group) * rows, rows).astype(jnp.int32)
     alive = jnp.broadcast_to(mask, (8, length))
-    penalty = (mask - 1.0) * MASKED
     held = {}
     single_grads = {}
 
     def middle(bias):
-        update, saved = single_attend(held["state"], held["projected"], bias, penalty, weights)
-        single_mid = held["state"] + update
-        update, saved_last = transition_forward(single_mid, weights, SINGLE)
-        held["out"] = single_mid + update
-        grad = held["back"] + transition_backward(saved_last, held["back"], weights, SINGLE, single_grads)
-        held["grad"] = grad
-        grad_scores, held["pending"] = single_attend_back(saved, grad, weights, single_grads)
+        found = single_middle(held["state"], held["back"], held["projected"], bias, alive, weights)
+        held["out"], held["grad"], grad_scores, grads, held["pending"] = found
+        single_grads.update(grads)
         return grad_scores
 
     def meet(number, *values):
         if number == 0:
-            others = [last_runs]
+            others = [held["runs"]]
         elif number == 1:
             others = [weights[(SINGLE, UP)]]
         elif number == 2:
@@ -2208,7 +2302,8 @@
         elif number == 3:
             others = [reduced[3]]
         elif number == 4:
-            others = [reduced[2]]
+            values, reduced[2] = after(*values, reduced[2])
+            return [values]
         else:
             others = [reduced[1]]
         return after(*values, *others)[: len(values)]
@@ -2218,7 +2313,9 @@
 
     reduced = {}
     lines_held = list(enumerate(SINGLE_VECTORS))
-    late_lanes = -(-table[(INCOMING, NORM_GAIN)][0] * STRIDE // count)
+    late_lanes = -(-table[(OUTGOING, OUT_GAIN)][0] * STRIDE // count)
+    late_end = table[(OUTGOING, GATE_OUT)][0]
+    early = table[(OUTGOING, PROJ_OUT)][0]
 
     def lines():
         values = jnp.concatenate([single_grads[name].reshape(1, S) for name in SINGLE_VECTORS], axis=0)
@@ -2226,16 +2323,17 @@
 
     def between(number, grads):
         if number == 0:
+            last_runs = after(runs[single_lane:], pair_in, weights[(OUTGOING, COLS)], live)[0]
+            held["runs"] = lax.all_gather(last_runs, line)
+            weights.update(unpack_single(table, total, single_lane, held["runs"]))
+            for index, name in enumerate(SINGLE_VECTORS):
+                weights[name] = weights[(SINGLE, VECTORS)][index]
             both = jnp.concatenate([single[0], single_cotangent[0]], axis=1)
-            both = after(both, weights[(OUTGOING, COLS)])[0]
             held["both"] = send(both.reshape(parts, -1, 2 * width), "crop")
             return
         if number == 9:
             both = send(held["both"], "z").reshape(rows, 2 * width).astype(F32)
             held["state"], held["back"] = both[:, :width], both[:, width:]
-            return
-        if number == 8:
-            reduced[1] = reduce_runs(reduced[1])
             return
         if number == 1:
             lowered, qkvg, both = single_project(held["state"], weights, devices)
@@ -2255,28 +2353,25 @@
             held[SINGLE] = both[:, :width].astype(BF16), both[:, width:]
             return
         if number == 6:
-            part = send(reduced[2].reshape((parts, -1) + reduced[2].shape[1:]), "crop")
-            reduced[2] = jnp.sum(part.astype(F32), axis=0).astype(BF16)
+            reduced[1] = reduce_runs(reduced[1])
             return
         if number == 4:
             sent = pack(
                 "single_gradient", table, total, devices, (pair_lanes, STRIDE), attend,
                 [(name, single_grads[name]) for name in SINGLE_MATRICES]
                 + [((ATTEND, PAIR_PROJ), grads[(ATTEND, PAIR_PROJ)])]
-                + [vector_part(grads, (PAIR, VECTORS), ATTEND), (lines_held, lines())],
+                + [vector_part(grads, table, (PAIR, VECTORS), attend, total), (lines_held, lines())],
             )
             reduced[3] = sent
-            reduced[2] = lax.psum_scatter(sent, line, scatter_dimension=0, tiled=False)
+            sent = sent.reshape((devices * parts, -1) + sent.shape[2:])
+            reduced[2] = lax.psum_scatter(sent, line + ("crop",), scatter_dimension=0, tiled=False)
             return
         taken = -(-(pair_lanes * count - (attend + 2 * S // STRIDE) * STRIDE) // (4 * S))
-        first = table[(INCOMING, NORM_GAIN)][0]
         sent = pack(
-            "pair_gradient", table, total, devices, (late_lanes, pair_lanes), first,
-            [(name, grads[name]) for name in PAIR_MATRICES if table[name][0] >= first]
+            "pair_gradient", table, total, devices, (late_lanes, pair_lanes), early,
+            [(name, grads[name]) for name in PAIR_MATRICES if table[name][0] >= early]
             + [(name, grads[name]) for name in ((STARTING, BIAS_PROJ), (ENDING, BIAS_PROJ))]
-            + [vector_part(grads, name, None) for name in ((ENDING, VECTORS), (STARTING, VECTORS))]
-            + [vector_part(grads, (INCOMING, VECTORS), INCOMING)]
-            + [vector_part(grads, (PAIR, VECTORS), PAIR)]
+            + [vector_part(grads, table, name, early, attend) for name in HELD if name in grads]
             + [(lines_held[:2], lines()), ((ATTEND, QKVG), single_grads[(ATTEND, QKVG)][: -(-taken // 8) * 8])],
         )
         reduced[1] = sent
@@ -2284,14 +2379,10 @@
     pair_out, pair_grad, grads = pair_path(
         pair_in, info, alive, orders, weights, pair_cotangent[0], middle, between, meet, send, group, parts
     )
-    first = table[(INCOMING, NORM_GAIN)][0]
-    taken = -(-(late_lanes * count - (first + 2) * STRIDE) // (4 * H))
     sent = pack(
         "outgoing_gradient", table, total, devices, (0, late_lanes), 0,
-        [(name, grads[name]) for name in PAIR_MATRICES if table[name][0] < first]
-        + [vector_part(grads, (OUTGOING, VECTORS), None)]
-        + [vector_part(grads, (INCOMING, VECTORS), None)]
-        + [((INCOMING, PROJ_GATE), grads[(INCOMING, PROJ_GATE)][: -(-taken // 8) * 8])],
+        [(name, grads[name]) for name in PAIR_MATRICES if table[name][0] < late_end]
+        + [vector_part(grads, table, name, 0, late_end) for name in ((OUTGOING, VECTORS), (INCOMING, VECTORS))],
     )
     reduced[0] = reduce_runs(sent)
     pair_grad = send(pair_grad.reshape(parts, -1, length, pair_grad.shape[2]), "z")

time: 1180 us -> 1120 us (0.949)
  blocking collectives: 208 us -> 313 us
  waiting for transfers between devices: 289 us -> 184 us
  matrix products: 25.1 us -> 2.97 us
  starting transfers between devices: 130 us -> 110 us
  local copies, waits for them, and re-layouts: 41 us -> 21.2 us
  Pallas kernels: 431 us -> 443 us
    all_to_all x31 -> x26, waiting for transfers between devices: 286 us -> 162 us  [swap(): lax.all_to_all(values, group, split_axis=0, concat_axis=0, tiled=True)]
    all_to_all x5 -> x9, blocking collectives: 131 us -> 236 us  [swap(): lax.all_to_all(values, group, split_axis=0, concat_axis=0, tiled=True)]
    all_to_all x31 -> x26, starting transfers between devices: 129 us -> 110 us  [swap(): lax.all_to_all(values, group, split_axis=0, concat_axis=0, tiled=True)]
    all_gather x1, waiting for transfers between devices: 2.95 us -> 22 us  [fast_shards(): first_runs = lax.all_gather(runs[:pair_lanes], line)]
    pallas_call x7 -> x8, Pallas kernels: 88.3 us -> 99 us  [whole_call(): pl.pallas_call(kernel, in_specs=[spec(axis) for array, axis in ins], out_...]
  transfers between devices with their start and end apart: 34 -> 29, of which waited for: 19 -> 16; matrix products, arithmetic and copies ran while one was open for 5% -> 3% of each run, Pallas kernels for 34% -> 36%
where the time goes in v5:
time: 1120 us; the launch traced here: 1110 us
  Pallas kernels  443 us (40%)
  blocking collectives  313 us (28%)
  waiting for transfers between devices  184 us (16%)
  starting transfers between devices  110 us (10%)
  local copies, waits for them, and re-layouts  21.2 us (2%)
  other arithmetic  17.7 us (2%)
  between operations  17.4 us (2%)
    pallas_call x21, Pallas kernels, run_rows(): pl.pallas_call(run, grid=(grid,), in_specs=in_specs, out_specs=out_specs,...  344 us
    all_to_all x9, blocking collectives, swap(): lax.all_to_all(values, group, split_axis=0, concat_axis=0, tiled=True)  236 us
    all_to_all x26, waiting for transfers between devices, swap(): lax.all_to_all(values, group, split_axis=0, concat_axis=0, tiled=True)  162 us
    all_to_all x26, starting transfers between devices, swap(): lax.all_to_all(values, group, split_axis=0, concat_axis=0, tiled=True)  110 us
    pallas_call x8, Pallas kernels, whole_call(): pl.pallas_call(kernel, in_specs=[spec(axis) for array, axis in ins], out_...  99 us
    all_gather x1, blocking collectives, fast_shards(): clip_norm = jnp.sqrt(jnp.sum(lax.all_gather(squares, line)))  23.1 us
  transfers between devices with their start and end apart: 29, of which 16 were waited for; matrix products, arithmetic and copies ran while one was open for 3% of the time, Pallas kernels for 36%

profile of v5, /device:TPU:0, one launch (start us, length us, event | category | flops | bytes accessed | tf_op | source)
XLA Modules:
  0.0 1108.7 jit_solution(3690223623387933219)
XLA Ops:
  7.2 5.3 all-to-all-start
  14.4 5.9 parameter_runs.1
  20.3 17.9 %all-to-all-done = bf16[4,8,256,128]{3,2,1,0:T(8,128)(2,1)} async-done(((bf16[4,8,256,128]{3,2,1,0:T(8,128)(2,1)}), bf16[4,8,256,128]{3,2,1,0:T(8,128)(2,1)}, u32[]{:S(2)}, u32[]{:S(2)}) %all-to-all-start) | async-done | bytes 2097184 | tf_op jit(solution)/shard_map/all_to_all | solution.py:1916
  38.2 5.1 all-to-all-start.1
  46.1 8.9 all-reduce.2
  56.5 22.0 %all-gather.11.cloned.1.call-done = bf16[192,24,128]{2,1,0:T(8,128)(2,1)} async-done(((bf16[24,24,128]{2,1,0:T(8,128)(2,1)}), bf16[192,24,128]{2,1,0:T(8,128)(2,1)}) %all-gather.11.cloned.1.call-update) | async-done | bytes 1179664 | tf_op jit(solution)/shard_map/all_gather | solution.py:2271
  78.4 8.0 pair_weights.1
  86.5 13.7 %all-to-all-done.1 = bf16[4,8,256,128]{3,2,1,0:T(8,128)(2,1)S(1)} async-done(((bf16[4,8,256,128]{3,2,1,0:T(8,128)(2,1)}), bf16[4,8,256,128]{3,2,1,0:T(8,128)(2,1)S(1)}, u32[]{:S(2)}, u32[]{:S(2)}) %all-to-all-start.1) | async-done | bytes 2097184 | tf_op jit(solution)/shard_map/all_to_all | solution.py:1916
  106.7 12.8 %outgoing_in.1 = bf16[8,2,16,32,256]{4,3,2,1,0:T(8,128)(2,1)} custom-call(s32[32]{0:T(128)} %dynamic-slice_convert_fusion.refs_0_, f32[8,256]{1,0:T(8,128)} %broadcast_in_dim.12.refs_1_.refs_0_.alive, bf16[32,256,128]{2,1,0:T(8,128)(2,1)} %bitcast.60, f32[128,8]{1,0:T(8,128)} %get-tuple-element.178.refs_3_.refs_4_.refs_11_.refs_6_, ...), custom_call_target="tpu_custom_call" | custom-call | flops 12999999488 | bytes 39000000 | tf_op jit(solution)/shard_map/outgoing_in/pallas_call | solution.py:762
  119.5 53.5 %all_to_all.175.refs_0_.refs_2_ = bf16[8,2,16,32,256]{4,3,2,1,0:T(8,128)(2,1)} all-to-all(bf16[8,2,16,32,256]{4,3,2,1,0:T(8,128)(2,1)} %outgoing_in.1), channel_id=1, replica_groups=mesh['crop'=4,'z'=4,'core'=2] {'crop','core'}, dimensions={0} | all-to-all | bytes 8388608 | tf_op jit(solution)/shard_map/all_to_all | solution.py:1916
  173.0 5.3 all-to-all-start.4
  178.3 6.2 outgoing_product.1
  188.8 14.7 %all-to-all-done.5 = bf16[8,16,16,256]{3,2,1,0:T(8,128)(2,1)S(1)} async-done(((bf16[8,16,16,256]{3,2,1,0:T(8,128)(2,1)}), bf16[8,16,16,256]{3,2,1,0:T(8,128)(2,1)S(1)}, u32[]{:S(2)}, u32[]{:S(2)}) %all-to-all-start.5) | async-done | bytes 1048608 | tf_op jit(solution)/shard_map/all_to_all | solution.py:1916
  207.2 12.4 %outgoing_out_incoming_in.2 = (f32[32,128,256]{2,1,0:T(8,128)}, bf16[8,2,16,16,256]{4,3,2,1,0:T(8,128)(2,1)}) custom-call(s32[16]{0:T(128)} %get-tuple-element.355.refs_0_, f32[8,256]{1,0:T(8,128)} %broadcast_in_dim.12.refs_1_.refs_0_.alive, bf16[32,256,128]{2,1,0:T(8,128)(2,1)} %bitcast.61, bf16[128,16,256]{2,1,0:T(8,128)(2,1)} %bitcast.73, ...), custom_call_target="tpu_custom_call" | custom-call | flops 11000000512 | bytes 33000000 | tf_op jit(solution)/shard_map/outgoing_out_incoming_in/pallas_call | solution.py:762
  227.1 12.4 %outgoing_out_incoming_in.3 = (f32[32,128,256]{2,1,0:T(8,128)}, bf16[8,2,16,16,256]{4,3,2,1,0:T(8,128)(2,1)}) custom-call(s32[16]{0:T(128)} %get-tuple-element.356.refs_0_, f32[8,256]{1,0:T(8,128)} %broadcast_in_dim.12.refs_1_.refs_0_.alive, bf16[32,256,128]{2,1,0:T(8,128)(2,1)} %bitcast.62, ...), custom_call_target="tpu_custom_call", output_to_operand_aliasing={{0}: (9, {})} | custom-call | flops 11000000512 | bytes 33000000 | tf_op jit(solution)/shard_map/outgoing_out_incoming_in/pallas_call | solution.py:762
  239.5 14.1 %all-to-all-done.7.refs_0_.refs_2_ = bf16[8,2,16,16,256]{4,3,2,1,0:T(8,128)(2,1)S(1)} async-done(((bf16[8,2,16,16,256]{4,3,2,1,0:T(8,128)(2,1)}), bf16[8,2,16,16,256]{4,3,2,1,0:T(8,128)(2,1)S(1)}, u32[]{:S(2)}, u32[]{:S(2)}) %all-to-all-start.7) | async-done | bytes 2097184 | tf_op jit(solution)/shard_map/all_to_all | solution.py:1916
  259.3 28.4 %single_weights.1 = (bf16[384,1536]{1,0:T(8,128)(2,1)}, bf16[384,384]{1,0:T(8,128)(2,1)}, bf16[384,3072]{1,0:T(8,128)(2,1)}, bf16[1536,384]{1,0:T(8,128)(2,1)}, ...) custom-call(bf16[8,105,24,128]{3,2,1,0:T(8,128)(2,1)} %bitcast.90), custom_call_target="tpu_custom_call" | custom-call | flops 8000000000 | bytes 24000000 | tf_op jit(solution)/shard_map/single_weights/pallas_call | solution.py:1696
  287.7 6.3 incoming_product.1
  293.9 4.7 all-to-all-start.9
  305.4 19.9 %all-to-all-done.9 = bf16[8,16,32,256]{3,2,1,0:T(8,128)(2,1)} async-done(((bf16[8,16,32,256]{3,2,1,0:T(8,128)(2,1)}), bf16[8,16,32,256]{3,2,1,0:T(8,128)(2,1)}, u32[]{:S(2)}, u32[]{:S(2)}) %all-to-all-start.9) | async-done | bytes 2097184 | tf_op jit(solution)/shard_map/all_to_all | solution.py:1916
  329.5 13.9 %incoming_out_starting_bias.1 = (f32[32,128,256]{2,1,0:T(8,128)}, bf16[4,32,256]{2,1,0:T(8,128)(2,1)}) custom-call(f32[32,128,256]{2,1,0:T(8,128)} %get-tuple-element.194.refs_0_.refs_6_.refs_2_, bf16[128,32,256]{2,1,0:T(8,128)(2,1)} %bitcast.12.refs_1_.refs_7_, f32[128,8]{1,0:T(8,128)} %get-tuple-element.191.refs_7_.refs_2_.refs_8_.refs_6_, ...), custom_call_target="tpu_custom_call" | custom-call | flops 15000000512 | bytes 45000000 | tf_op jit(solution)/shard_map/incoming_out_starting_bias/pallas_call | solution.py:762
  343.4 12.1 %all-gather.3 = bf16[32,32,256]{2,1,0:T(8,128)(2,1)} all-gather(bf16[4,32,256]{2,1,0:T(8,128)(2,1)} %get-tuple-element.211), channel_id=6, replica_groups=mesh['crop'=4,'z'=4,'core'=2] {'crop','core'}, dimensions={0}, use_global_device_ids=true | all-gather | bytes 589824 | tf_op jit(solution)/shard_map/all_gather | solution.py:2060
  360.7 20.5 %starting_attention.1 = (bf16[8,32,32,128]{3,2,1,0:T(8,128)(2,1)}, f32[32,4,256]{2,1,0:T(4,128)}, bf16[32,128,256]{2,1,0:T(8,128)(2,1)}) custom-call(f32[8,256]{1,0:T(8,128)} %broadcast_in_dim.12.refs_1_.refs_0_.alive, f32[32,128,256]{2,1,0:T(8,128)} %get-tuple-element.210.refs_1_.refs_0_, bf16[8,4,32,256]{3,2,1,0:T(8,128)(2,1)} %bitcast.81, ...), custom_call_target="tpu_custom_call" | custom-call | flops 20999999488 | bytes 63000000 | tf_op jit(solution)/shard_map/starting_attention/pallas_call | solution.py:762
  381.1 6.2 all-to-all-done.11
  387.3 30.9 %all_to_all.176.refs_0_.refs_1_ = bf16[8,32,32,128]{3,2,1,0:T(8,128)(2,1)} all-to-all(bf16[8,32,32,128]{3,2,1,0:T(8,128)(2,1)} %get-tuple-element.217), channel_id=1, replica_groups=mesh['crop'=4,'z'=4,'core'=2] {'crop','core'}, dimensions={0} | all-to-all | bytes 4194304 | tf_op jit(solution)/shard_map/all_to_all | solution.py:1916
  418.3 5.1 all-to-all-start.13
  423.4 5.1 ending_bias.1
  428.5 11.2 %all-gather.4 = bf16[32,32,256]{2,1,0:T(8,128)(2,1)} all-gather(bf16[4,32,256]{2,1,0:T(8,128)(2,1)} %ending_bias.1), channel_id=7, replica_groups=mesh['crop'=4,'z'=4,'core'=2] {'crop','core'}, dimensions={0}, use_global_device_ids=true | all-gather | bytes 589824 | tf_op jit(solution)/shard_map/all_gather | solution.py:2076
  439.7 19.1 %ending_attention.1 = (f32[32,128,256]{2,1,0:T(8,128)}, f32[32,4,256]{2,1,0:T(4,128)}, bf16[32,128,256]{2,1,0:T(8,128)(2,1)}) custom-call(f32[8,256]{1,0:T(8,128)} %broadcast_in_dim.12.refs_1_.refs_0_.alive, bf16[8,32,32,128]{3,2,1,0:T(8,128)(2,1)} %all_to_all.176.refs_0_.refs_1_, bf16[8,4,32,256]{3,2,1,0:T(8,128)(2,1)} %bitcast.83, ...), custom_call_target="tpu_custom_call" | custom-call | flops 15000000512 | bytes 45000000 | tf_op jit(solution)/shard_map/ending_attention/pallas_call | solution.py:762
  458.8 12.1 %all-to-all-done.13 = bf16[4,2,32,32,128]{4,3,2,1,0:T(8,128)(2,1)S(1)} async-done(((bf16[4,2,32,32,128]{4,3,2,1,0:T(8,128)(2,1)}), bf16[4,2,32,32,128]{4,3,2,1,0:T(8,128)(2,1)S(1)}, u32[]{:S(2)}, u32[]{:S(2)}) %all-to-all-start.13) | async-done | bytes 2097184 | tf_op jit(solution)/shard_map/all_to_all | solution.py:1916
  470.9 15.8 %pair_transition.1 = (f32[32,128,256]{2,1,0:T(8,128)}, bf16[256,32,128]{2,1,0:T(8,128)(2,1)}, bf16[8,32,512]{2,1,0:T(8,128)(2,1)}) custom-call(f32[32,128,256]{2,1,0:T(8,128)} %get-tuple-element.224.refs_0_, f32[128,8]{1,0:T(8,128)} %get-tuple-element.225.refs_1_.refs_4_, bf16[1024,128]{1,0:T(8,128)(2,1)} %get-tuple-element.226.refs_2_.refs_5_, ...), custom_call_target="tpu_custom_call" | custom-call | flops 15000000512 | bytes 45000000 | tf_op jit(solution)/shard_map/pair_transition/pallas_call | solution.py:762
  486.8 11.0 all_to_all.177.bias
  497.7 10.7 single_path.1
  508.4 11.0 all_to_all.178.refs_3_
  523.3 31.3 %pair_transition_back.1 = (f32[32,128,256]{2,1,0:T(8,128)}, f32[128,1024]{1,0:T(8,128)}, f32[512,128]{1,0:T(8,128)}, f32[128,16]{1,0:T(8,128)}, f32[8,128]{1,0:T(8,128)}) custom-call(f32[32,128,256]{2,1,0:T(8,128)} %get-tuple-element.224.refs_0_, f32[32,128,256]{2,1,0:T(8,128)} %get-tuple-element.238.refs_1_, bf16[8,32,32,128]{3,2,1,0:T(8,128)(2,1)} %bitcast.66, ...), custom_call_target="tpu_custom_call" | custom-call | flops 30000001024 | bytes 90000000 | tf_op jit(solution)/shard_map/pair_transition_back/pallas_call | solution.py:762
  554.6 16.5 %all-to-all-done.16 = bf16[4,64,32,128]{3,2,1,0:T(8,128)(2,1)S(1)} async-done(((bf16[4,64,32,128]{3,2,1,0:T(8,128)(2,1)}), bf16[4,64,32,128]{3,2,1,0:T(8,128)(2,1)S(1)}, u32[]{:S(2)}, u32[]{:S(2)}) %all-to-all-start.16) | async-done | bytes 2097184 | tf_op jit(solution)/shard_map/all_to_all | solution.py:1916
  575.2 33.1 %attention_back.2 = (bf16[32,128,256]{2,1,0:T(8,128)(2,1)}, bf16[8,4,32,256]{3,2,1,0:T(8,128)(2,1)}, f32[128,512]{1,0:T(8,128)}, f32[128,128]{1,0:T(8,128)}) custom-call(f32[8,256]{1,0:T(8,128)} %broadcast_in_dim.12.refs_1_.refs_0_.alive, bf16[8,32,32,128]{3,2,1,0:T(8,128)(2,1)} %all_to_all.176.refs_0_.refs_1_, ...), custom_call_target="tpu_custom_call" | custom-call | flops 33999998976 | bytes 102000000 | tf_op jit(solution)/shard_map/attention_back/pallas_call | solution.py:762
  615.3 7.1 all-to-all-done.18.refs_3_
  626.3 12.1 %ending_attention_end.1 = (bf16[8,32,32,128]{3,2,1,0:T(8,128)(2,1)}, f32[128,8]{1,0:T(8,128)}, f32[8,128]{1,0:T(8,128)}) custom-call(bf16[8,32,32,128]{3,2,1,0:T(8,128)(2,1)} %all_to_all.176.refs_0_.refs_1_, f32[32,128,256]{2,1,0:T(8,128)} %get-tuple-element.243.refs_2_.refs_1_, bf16[32,128,256]{2,1,0:T(8,128)(2,1)} %get-tuple-element.248.refs_2_, ...), custom_call_target="tpu_custom_call" | custom-call | flops 15000000512 | bytes 45000000 | tf_op jit(solution)/shard_map/ending_attention_end/pallas_call | solution.py:762
  645.5 30.3 %single_gradient.1 = bf16[8,104,24,128]{3,2,1,0:T(8,128)(2,1)} custom-call(f32[384,1536]{1,0:T(8,128)} %fusion.1.refs_0_, f32[384,384]{1,0:T(8,128)} %get-tuple-element.264.refs_1_, f32[384,3072]{1,0:T(8,128)} %get-tuple-element.265.refs_2_, f32[1536,384]{1,0:T(8,128)} %get-tuple-element.266.refs_3_, f32[128,16]{1,0:T(8,128)} %get-tuple-element.267.refs_4_, ...), custom_call_target="tpu_custom_call" | custom-call | flops 8000000000 | bytes 24000000 | tf_op jit(solution)/shard_map/single_gradient/pallas_call | solution.py:1696
  681.5 33.6 %attention_back.3 = (bf16[32,128,256]{2,1,0:T(8,128)(2,1)}, bf16[8,4,32,256]{3,2,1,0:T(8,128)(2,1)}, f32[128,512]{1,0:T(8,128)}, f32[128,128]{1,0:T(8,128)}) custom-call(f32[8,256]{1,0:T(8,128)} %broadcast_in_dim.12.refs_1_.refs_0_.alive, f32[32,128,256]{2,1,0:T(8,128)} %get-tuple-element.210.refs_1_.refs_0_, bf16[8,32,32,128]{3,2,1,0:T(8,128)(2,1)} %copy-done.7, ...), custom_call_target="tpu_custom_call" | custom-call | flops 33999998976 | bytes 102000000 | tf_op jit(solution)/shard_map/attention_back/pallas_call | solution.py:762
  715.1 14.1 %all_to_all.179.refs_3_ = bf16[8,4,32,256]{3,2,1,0:T(8,128)(2,1)} all-to-all(bf16[8,4,32,256]{3,2,1,0:T(8,128)(2,1)} %get-tuple-element.276), channel_id=1, replica_groups=mesh['crop'=4,'z'=4,'core'=2] {'crop','core'}, dimensions={0} | all-to-all | bytes 1048576 | tf_op jit(solution)/shard_map/all_to_all | solution.py:1916
  732.5 15.9 %starting_end_incoming_out_back.2 = (f32[32,128,256]{2,1,0:T(8,128)}, bf16[128,16,256]{2,1,0:T(8,128)(2,1)}, bf16[32,128,256]{2,1,0:T(8,128)(2,1)}, f32[128,8]{1...) custom-call(f32[32,128,256]{2,1,0:T(8,128)} %get-tuple-element.210.refs_1_.refs_0_, ...), custom_call_target="tpu_custom_call" | custom-call | flops 12999999488 | bytes 39000000 | tf_op jit(solution)/shard_map/starting_end_incoming_out_back/pallas_call | solution.py:762
  752.5 16.1 %starting_end_incoming_out_back.3 = (f32[32,128,256]{2,1,0:T(8,128)}, bf16[128,16,256]{2,1,0:T(8,128)(2,1)}, bf16[32,128,256]{2,1,0:T(8,128)(2,1)}, f32[128,8]{1...) custom-call(f32[32,128,256]{2,1,0:T(8,128)} %get-tuple-element.210.r, ...), custom_call_target="tpu_custom_call", output_to_operand_aliasing={{0}: (13, {}), {2}: (14, {}), {3}: (15, {}), {4}: (16, {}),... | custom-call | flops 12999999488 | bytes 39000000 | tf_op jit(solution)/shard_map/starting_end_incoming_out_back/pallas_call | solution.py:762
  771.5 20.7 %all_to_all.180.refs_1_ = bf16[8,16,16,256]{3,2,1,0:T(8,128)(2,1)} all-to-all(bf16[8,16,16,256]{3,2,1,0:T(8,128)(2,1)} %bitcast.78), channel_id=1, replica_groups=mesh['crop'=4,'z'=4,'core'=2] {'crop','core'}, dimensions={0} | all-to-all | bytes 2097152 | tf_op jit(solution)/shard_map/all_to_all | solution.py:1916
  792.3 7.4 incoming_product_back.1
  799.6 30.9 %all_to_all.181.refs_3_ = bf16[8,2,16,16,256]{4,3,2,1,0:T(8,128)(2,1)} all-to-all(bf16[8,2,16,16,256]{4,3,2,1,0:T(8,128)(2,1)} %get-tuple-element.293), channel_id=1, replica_groups=mesh['crop'=4,'z'=4,'core'=2] {'crop','core'}, dimensions={0} | all-to-all | bytes 4194304 | tf_op jit(solution)/shard_map/all_to_all | solution.py:1916
  830.6 4.6 all-to-all-start.27
  835.2 21.1 %incoming_in_outgoing_out_back.2 = (f32[32,128,256]{2,1,0:T(8,128)}, bf16[128,16,256]{2,1,0:T(8,128)(2,1)}, bf16[32,128,256]{2,1,0:T(8,128)(2,1)}, f32[128,512]{...) custom-call(s32[16]{0:T(128)} %get-tuple-element.355.refs_0_, ...), custom_call_target="tpu_custom_call" | custom-call | flops 18499999744 | bytes 55500000 | tf_op jit(solution)/shard_map/incoming_in_outgoing_out_back/pallas_call | solution.py:762
  856.3 5.5 all-to-all-done.27.refs_3_
  865.4 21.3 %incoming_in_outgoing_out_back.3 = (f32[32,128,256]{2,1,0:T(8,128)}, bf16[128,16,256]{2,1,0:T(8,128)(2,1)}, bf16[32,128,256]{2,1,0:T(8,128)(2,1)}, f32[128,512]{...) custom-call(s32[16]{0:T(128)} %get-tuple-element.356.refs_0_, ...), custom_call_target="tpu_custom_call", output_to_operand_aliasing={{0}: (16, {}), {2}: (17, {}), {3}: (18, {}), {4}: (19, {}),... | custom-call | flops 18499999744 | bytes 55500000 | tf_op jit(solution)/shard_map/incoming_in_outgoing_out_back/pallas_call | solution.py:762
  892.5 7.5 pair_gradient.1
  900.0 6.4 all-to-all-done.29.refs_1_
  906.4 7.3 outgoing_product_back.1
  913.6 53.6 %all_to_all.182.refs_3_ = bf16[8,2,16,32,256]{4,3,2,1,0:T(8,128)(2,1)} all-to-all(bf16[8,2,16,32,256]{4,3,2,1,0:T(8,128)(2,1)} %outgoing_product_back.1), channel_id=1, replica_groups=mesh['crop'=4,'z'=4,'core'=2] {'crop','core'}, dimensions={0} | all-to-all | bytes 8388608 | tf_op jit(solution)/shard_map/all_to_all | solution.py:1916
  967.2 5.1 all-to-all-start.31
  972.3 19.9 %outgoing_in_back.1 = (bf16[32,256,128]{2,1,0:T(8,128)(2,1)}, f32[128,512]{1,0:T(8,128)}, f32[8,128]{1,0:T(8,128)}) custom-call(s32[32]{0:T(128)} %dynamic-slice_convert_fusion.refs_0_, f32[8,256]{1,0:T(8,128)} %broadcast_in_dim.12.refs_1_.refs_0_.alive, bf16[32,256,128]{2,1,0:T(8,128)(2,1)} %bitcast.65, bf16[8,2,16,32,256]{4,3,2,1,0:T(8,128)(2,1)} %all_to_all.182.refs_3_, ...), custom_call_target="tpu_custom_call" | custom-call | flops 20000000000 | bytes 60000000 | tf_op jit(solution)/shard_map/outgoing_in_back/pallas_call | solution.py:762
  998.5 10.3 all_to_all.183
  1016.5 10.3 all-gather.6
  1027.0 11.6 %all-gather.5 = bf16[96,24,128]{2,1,0:T(8,128)(2,1)} all-gather(bf16[24,24,128]{2,1,0:T(8,128)(2,1)S(1)} %pad_maximum_fusion), channel_id=8, replica_groups=mesh['crop'=4,'z'=4,'core'=2] {'crop'}, dimensions={0}, use_global_device_ids=true | all-gather | bytes 737280 | tf_op jit(solution)/shard_map/all_gather | solution.py:2391
  1038.6 5.9 gradient_share.1
  1044.5 23.1 %all-gather.7 = f32[64,128]{1,0:T(8,128)S(1)} all-gather(f32[8,128]{1,0:T(8,128)} %get-tuple-element.341), channel_id=10, replica_groups=mesh['crop'=4,'z'=4,'core'=2] {'z','core'}, dimensions={0}, use_global_device_ids=true | all-gather | bytes 36864 | tf_op jit(solution)/shard_map/all_gather | solution.py:2399
  1072.6 7.5 multiply_subtract_fusion
  1080.1 18.1 %all-to-all-done.34 = bf16[4,8,256,128]{3,2,1,0:T(8,128)(2,1)S(1)} async-done(((bf16[4,8,256,128]{3,2,1,0:T(8,128)(2,1)}), bf16[4,8,256,128]{3,2,1,0:T(8,128)(2,1)S(1)}, u32[]{:S(2)}, u32[]{:S(2)}) %all-to-all-start.34) | async-done | bytes 2097184 | tf_op jit(solution)/shard_map/all_to_all | solution.py:1916
  (166 shorter events, 121.0 us)
Async XLA Ops:
  7.2 6.0 copy-start.1
  7.2 31.0 %all-to-all-start = ((bf16[4,8,256,128]{3,2,1,0:T(8,128)(2,1)}), bf16[4,8,256,128]{3,2,1,0:T(8,128)(2,1)}, u32[]{:S(2)}, u32[]{:S(2)}) async-start(bf16[4,8,256,128]{3,2,1,0:T(8,128)(2,1)} %bitcast.58), calls=%async_computation | async-start | bytes 4194304 | tf_op jit(solution)/shard_map/all_to_all | solution.py:1916
  20.3 23.0 %copy-start.15 = (bf16[128,24,128]{2,1,0:T(8,128)(2,1)S(1)}, bf16[128,24,128]{2,1,0:T(8,128)(2,1)}, u32[]{:S(2)}) copy-start(bf16[128,24,128]{2,1,0:T(8,128)(2,1)} %parameter_runs.1) | copy-start | bytes 2359300
  20.3 24.4 %copy-start.38 = (u32[32]{0:T(128)S(1)}, u32[32]{0:T(128)}, u32[]{:S(2)}) copy-start(u32[32]{0:T(128)} %constant.107) | copy-start | bytes 388
  38.2 62.0 %all-to-all-start.1 = ((bf16[4,8,256,128]{3,2,1,0:T(8,128)(2,1)}), bf16[4,8,256,128]{3,2,1,0:T(8,128)(2,1)S(1)}, u32[]{:S(2)}, u32[]{:S(2)}) async-start(bf16[4,8,256,128]{3,2,1,0:T(8,128)(2,1)} %all-to-all-done), calls=%async_computation.1 | async-start | bytes 4194304 | tf_op jit(solution)/shard_map/all_to_all | solution.py:1916
  43.3 35.1 %all-gather.11.cloned.1.call-start = ((), (), s32[]{:S(2)}) async-start(), calls=%async_computation.37 | async-start | bytes 1327104 | tf_op jit(solution)/shard_map/all_gather | solution.py:2271
  44.0 183.1 %all-gather.13.cloned.1.call-start = ((), (), s32[]{:S(2)}) async-start(), calls=%async_computation.38 | async-start | bytes 5806080 | tf_op jit(solution)/shard_map/all_gather | solution.py:2327
  78.4 21.8 %copy-start.35 = (f32[256]{0:T(256)S(1)}, f32[256]{0:T(256)}, u32[]{:S(2)}) copy-start(f32[256]{0:T(256)} %constant.92.clone) | copy-start | bytes 3076
  78.4 23.1 %copy-start.26 = (bf16[1,32,384]{2,1,0:T(8,128)(2,1)S(1)}, bf16[1,32,384]{2,1,0:T(8,128)(2,1)}, u32[]{:S(2)}) copy-start(bf16[1,32,384]{2,1,0:T(8,128)(2,1)} %param.18) | copy-start | bytes 73732
  78.4 23.1 %copy-start.27 = (bf16[1,32,384]{2,1,0:T(8,128)(2,1)S(1)}, bf16[1,32,384]{2,1,0:T(8,128)(2,1)}, u32[]{:S(2)}) copy-start(bf16[1,32,384]{2,1,0:T(8,128)(2,1)} %param.12) | copy-start | bytes 73732
  100.2 6.5 copy-start.5
  102.2 17.3 %all-to-all-start.2 = ((bf16[4,8,768]{2,1,0:T(8,128)(2,1)}), bf16[4,8,768]{2,1,0:T(8,128)(2,1)}, u32[]{:S(2)}, u32[]{:S(2)}) async-start(bf16[4,8,768]{2,1,0:T(8,128)(2,1)} %pad_maximum_fusion.2), calls=%async_computation.2 | async-start | bytes 98304 | tf_op jit(solution)/shard_map/all_to_all | solution.py:1916
  173.0 11.5 %all-to-all-start.4 = ((bf16[4,8,768]{2,1,0:T(8,128)(2,1)}), bf16[4,8,768]{2,1,0:T(8,128)(2,1)S(1)}, u32[]{:S(2)}, u32[]{:S(2)}) async-start(bf16[4,8,768]{2,1,0:T(8,128)(2,1)} %all-to-all-done.2), calls=%async_computation.4 | async-start | bytes 98304 | tf_op jit(solution)/shard_map/all_to_all | solution.py:1916
  184.5 3.7 copy-start.34
  184.5 19.0 %all-to-all-start.5 = ((bf16[8,16,16,256]{3,2,1,0:T(8,128)(2,1)}), bf16[8,16,16,256]{3,2,1,0:T(8,128)(2,1)S(1)}, u32[]{:S(2)}, u32[]{:S(2)}) async-start(bf16[8,16,16,256]{3,2,1,0:T(8,128)(2,1)} %get-tuple-element.185), calls=%async_computation.5 | async-start | bytes 2097152 | tf_op jit(solution)/shard_map/all_to_all | solution.py:1916
  203.6 3.6 copy-start.12
  203.6 18.9 %all-to-all-start.6 = ((bf16[8,16,16,256]{3,2,1,0:T(8,128)(2,1)}), bf16[8,16,16,256]{3,2,1,0:T(8,128)(2,1)S(1)}, u32[]{:S(2)}, u32[]{:S(2)}) async-start(bf16[8,16,16,256]{3,2,1,0:T(8,128)(2,1)} %get-tuple-element.186), calls=%async_computation.6 | async-start | bytes 2097152 | tf_op jit(solution)/shard_map/all_to_all | solution.py:1916
  222.5 1.0 copy-start.11
  223.5 30.2 %all-to-all-start.7 = ((bf16[8,2,16,16,256]{4,3,2,1,0:T(8,128)(2,1)}), bf16[8,2,16,16,256]{4,3,2,1,0:T(8,128)(2,1)S(1)}, u32[]{:S(2)}, u32[]{:S(2)}) async-start(bf16[8,2,16,16,256]{4,3,2,1,0:T(8,128)(2,1)} %get-tuple-element.196), calls=%async_computation.7 | async-start | bytes 4194304 | tf_op jit(solution)/shard_map/all_to_all | solution.py:1916
  253.6 1.3 copy-start.6
  254.9 32.7 %all-to-all-start.8 = ((bf16[8,2,16,16,256]{4,3,2,1,0:T(8,128)(2,1)}), bf16[8,2,16,16,256]{4,3,2,1,0:T(8,128)(2,1)}, u32[]{:S(2)}, u32[]{:S(2)}) async-start(bf16[8,2,16,16,256]{4,3,2,1,0:T(8,128)(2,1)} %get-tuple-element.198), calls=%async_computation.8 | async-start | bytes 4194304 | tf_op jit(solution)/shard_map/all_to_all | solution.py:1916
  293.9 4.7 copy-start.4
  293.9 31.4 %all-to-all-start.9 = ((bf16[8,16,32,256]{3,2,1,0:T(8,128)(2,1)}), bf16[8,16,32,256]{3,2,1,0:T(8,128)(2,1)}, u32[]{:S(2)}, u32[]{:S(2)}) async-start(bf16[8,16,32,256]{3,2,1,0:T(8,128)(2,1)} %incoming_product.1), calls=%async_computation.9 | async-start | bytes 4194304 | tf_op jit(solution)/shard_map/all_to_all | solution.py:1916
  298.6 6.1 copy-start.2
  302.4 2.7 copy-start.9
  303.2 1.9 copy-start.30
  304.0 1.2 copy-start.32
  305.3 38.1 %copy-start.18 = (f32[32,1536]{1,0:T(8,128)}, f32[32,1536]{1,0:T(8,128)S(1)}, u32[]{:S(2)}) copy-start(f32[32,1536]{1,0:T(8,128)S(1)} %fusion.7.project) | copy-start | bytes 589828
  326.1 29.5 %all-to-all-start.10 = ((bf16[8,32,768]{2,1,0:T(8,128)(2,1)}), bf16[8,32,768]{2,1,0:T(8,128)(2,1)S(1)}, u32[]{:S(2)}, u32[]{:S(2)}) async-start(bf16[8,32,768]{2,1,0:T(8,128)(2,1)} %broadcast_in_dim.13), calls=%async_computation.10 | async-start | bytes 786432 | tf_op jit(solution)/shard_map/all_to_all | solution.py:1916
  356.3 31.0 %all-to-all-start.11 = ((bf16[8,32,32,128]{3,2,1,0:T(8,128)(2,1)}), bf16[8,32,32,128]{3,2,1,0:T(8,128)(2,1)}, u32[]{:S(2)}, u32[]{:S(2)}) async-start(bf16[8,32,32,128]{3,2,1,0:T(8,128)(2,1)} %bitcast.17), calls=%async_computation.11 | async-start | bytes 4194304 | tf_op jit(solution)/shard_map/all_to_all | solution.py:1916
  418.3 52.6 %all-to-all-start.13 = ((bf16[4,2,32,32,128]{4,3,2,1,0:T(8,128)(2,1)}), bf16[4,2,32,32,128]{4,3,2,1,0:T(8,128)(2,1)S(1)}, u32[]{:S(2)}, u32[]{:S(2)}) async-start(bf16[4,2,32,32,128]{4,3,2,1,0:T(8,128)(2,1)} %bitcast.19), calls=%async_computation.13 | async-start | bytes 4194304 | tf_op jit(solution)/shard_map/all_to_all | solution.py:1916
  470.9 15.9 %copy-start.8 = (bf16[4,2,32,32,128]{4,3,2,1,0:T(8,128)(2,1)}, bf16[4,2,32,32,128]{4,3,2,1,0:T(8,128)(2,1)S(1)}, u32[]{:S(2)}) copy-start(bf16[4,2,32,32,128]{4,3,2,1,0:T(8,128)(2,1)S(1)} %all-to-all-done.13) | copy-start | bytes 6291460
  519.4 3.9 copy-start.23
  519.4 3.9 copy-start.22
  519.4 51.7 %all-to-all-start.16 = ((bf16[4,64,32,128]{3,2,1,0:T(8,128)(2,1)}), bf16[4,64,32,128]{3,2,1,0:T(8,128)(2,1)S(1)}, u32[]{:S(2)}, u32[]{:S(2)}) async-start(bf16[4,64,32,128]{3,2,1,0:T(8,128)(2,1)} %bitcast.69), calls=%async_computation.16 | async-start | bytes 4194304 | tf_op jit(solution)/shard_map/all_to_all | solution.py:1916
  571.1 37.3 %copy-start = (bf16[4,64,32,128]{3,2,1,0:T(8,128)(2,1)}, bf16[4,64,32,128]{3,2,1,0:T(8,128)(2,1)S(1)}, u32[]{:S(2)}) copy-start(bf16[4,64,32,128]{3,2,1,0:T(8,128)(2,1)S(1)} %all-to-all-done.16) | copy-start | bytes 6291460
  571.1 37.3 %all-to-all-start.17 = ((bf16[8,32,768]{2,1,0:T(8,128)(2,1)}), bf16[8,32,768]{2,1,0:T(8,128)(2,1)}, u32[]{:S(2)}, u32[]{:S(2)}) async-start(bf16[8,32,768]{2,1,0:T(8,128)(2,1)} %get-tuple-element.251), calls=%async_computation.17 | async-start | bytes 786432 | tf_op jit(solution)/shard_map/all_to_all | solution.py:1916
  575.2 38.5 %copy-start.3 = (bf16[384,1536]{1,0:T(8,128)(2,1)S(1)}, bf16[384,1536]{1,0:T(8,128)(2,1)}, u32[]{:S(2)}) copy-start(bf16[384,1536]{1,0:T(8,128)(2,1)} %get-tuple-element.204) | copy-start | bytes 3538948
  575.2 38.5 %copy-start.10 = (f32[32,768]{1,0:T(8,128)S(1)}, f32[32,768]{1,0:T(8,128)}, u32[]{:S(2)}) copy-start(f32[32,768]{1,0:T(8,128)} %copy-done.9) | copy-start | bytes 294916
  575.2 38.5 %copy-start.21 = (f32[384]{0:T(512)S(1)}, f32[384]{0:T(512)}, u32[]{:S(2)}) copy-start(f32[384]{0:T(512)} %copy-done.20) | copy-start | bytes 4612
  575.2 38.5 %copy-start.31 = (f32[32]{0:T(128)S(1)}, f32[32]{0:T(128)}, u32[]{:S(2)}) copy-start(f32[32]{0:T(128)} %copy-done.30) | copy-start | bytes 388
  575.2 38.5 %copy-start.33 = (f32[32]{0:T(128)S(1)}, f32[32]{0:T(128)}, u32[]{:S(2)}) copy-start(f32[32]{0:T(128)} %copy-done.32) | copy-start | bytes 388
  608.4 6.0 copy-start.37
  608.4 6.3 copy-start.24
  608.4 6.2 copy-start.25
  608.4 14.0 %all-to-all-start.18 = ((bf16[8,4,32,256]{3,2,1,0:T(8,128)(2,1)}), bf16[8,4,32,256]{3,2,1,0:T(8,128)(2,1)S(1)}, u32[]{:S(2)}, u32[]{:S(2)}) async-start(bf16[8,4,32,256]{3,2,1,0:T(8,128)(2,1)} %get-tuple-element.252), calls=%async_computation.18 | async-start | bytes 1048576 | tf_op jit(solution)/shard_map/all_to_all | solution.py:1916
  622.4 3.9 copy-start.16
  622.4 16.1 %all-to-all-start.19 = ((f32[4,8,768]{2,1,0:T(8,128)}), f32[4,8,768]{2,1,0:T(8,128)}, u32[]{:S(2)}, u32[]{:S(2)}) async-start(f32[4,8,768]{2,1,0:T(8,128)} %maximum_bitcast_fusion), calls=%async_computation.19 | async-start | bytes 196608 | tf_op jit(solution)/shard_map/all_to_all | solution.py:1916
  638.5 5.0 copy-start.29
  638.5 37.3 %all-to-all-start.20 = ((bf16[8,32,32,128]{3,2,1,0:T(8,128)(2,1)}), bf16[8,32,32,128]{3,2,1,0:T(8,128)(2,1)S(1)}, u32[]{:S(2)}, u32[]{:S(2)}) async-start(bf16[8,32,32,128]{3,2,1,0:T(8,128)(2,1)} %get-tuple-element.262), calls=%async_computation.20 | async-start | bytes 4194304 | tf_op jit(solution)/shard_map/all_to_all | solution.py:1916
  642.1 193.1 %reduce-scatter.2.cloned.1.call-start = ((), (), s32[]{:S(2)}) async-start(), calls=%async_computation.36 | async-start | bytes 5271552 | tf_op jit(solution)/shard_map/reduce_scatter | solution.py:2367
  675.8 1.3 copy-start.7
  677.1 38.0 %all-to-all-start.21 = ((bf16[8,32,32,128]{3,2,1,0:T(8,128)(2,1)}), bf16[8,32,32,128]{3,2,1,0:T(8,128)(2,1)S(1)}, u32[]{:S(2)}, u32[]{:S(2)}) async-start(bf16[8,32,32,128]{3,2,1,0:T(8,128)(2,1)} %bitcast.56), calls=%async_computation.21 | async-start | bytes 4194304 | tf_op jit(solution)/shard_map/all_to_all | solution.py:1916
  729.2 19.2 %all-to-all-start.23 = ((f32[4,8,768]{2,1,0:T(8,128)}), f32[4,8,768]{2,1,0:T(8,128)S(1)}, u32[]{:S(2)}, u32[]{:S(2)}) async-start(f32[4,8,768]{2,1,0:T(8,128)} %all-to-all-done.19), calls=%async_computation.23 | async-start | bytes 196608 | tf_op jit(solution)/shard_map/all_to_all | solution.py:1916
  748.3 23.2 %all-to-all-start.24 = ((bf16[8,16,16,256]{3,2,1,0:T(8,128)(2,1)}), bf16[8,16,16,256]{3,2,1,0:T(8,128)(2,1)S(1)}, u32[]{:S(2)}, u32[]{:S(2)}) async-start(bf16[8,16,16,256]{3,2,1,0:T(8,128)(2,1)} %bitcast.77), calls=%async_computation.24 | async-start | bytes 2097152 | tf_op jit(solution)/shard_map/all_to_all | solution.py:1916
  771.5 20.7 %copy-start.14 = (bf16[8,16,16,256]{3,2,1,0:T(8,128)(2,1)}, bf16[8,16,16,256]{3,2,1,0:T(8,128)(2,1)S(1)}, u32[]{:S(2)}) copy-start(bf16[8,16,16,256]{3,2,1,0:T(8,128)(2,1)S(1)} %all-to-all-done.24.refs_0_) | copy-start | bytes 3145732
  830.6 31.3 %all-to-all-start.27 = ((bf16[8,2,16,16,256]{4,3,2,1,0:T(8,128)(2,1)}), bf16[8,2,16,16,256]{4,3,2,1,0:T(8,128)(2,1)}, u32[]{:S(2)}, u32[]{:S(2)}) async-start(bf16[8,2,16,16,256]{4,3,2,1,0:T(8,128)(2,1)} %get-tuple-element.302), calls=%async_computation.28 | async-start | bytes 4194304 | tf_op jit(solution)/shard_map/all_to_all | solution.py:1916
  861.8 24.8 %all-to-all-start.28 = ((bf16[8,16,16,256]{3,2,1,0:T(8,128)(2,1)}), bf16[8,16,16,256]{3,2,1,0:T(8,128)(2,1)S(1)}, u32[]{:S(2)}, u32[]{:S(2)}) async-start(bf16[8,16,16,256]{3,2,1,0:T(8,128)(2,1)} %bitcast.76), calls=%async_computation.29 | async-start | bytes 2097152 | tf_op jit(solution)/shard_map/all_to_all | solution.py:1916
  886.7 13.3 %copy-start.13 = (bf16[8,16,16,256]{3,2,1,0:T(8,128)(2,1)}, bf16[8,16,16,256]{3,2,1,0:T(8,128)(2,1)S(1)}, u32[]{:S(2)}) copy-start(bf16[8,16,16,256]{3,2,1,0:T(8,128)(2,1)S(1)} %all-to-all-done.28.refs_0_) | copy-start | bytes 3145732
  886.7 19.7 %all-to-all-start.29 = ((bf16[8,16,16,256]{3,2,1,0:T(8,128)(2,1)}), bf16[8,16,16,256]{3,2,1,0:T(8,128)(2,1)}, u32[]{:S(2)}, u32[]{:S(2)}) async-start(bf16[8,16,16,256]{3,2,1,0:T(8,128)(2,1)} %bitcast.75), calls=%async_computation.30 | async-start | bytes 2097152 | tf_op jit(solution)/shard_map/all_to_all | solution.py:1916
  967.2 31.3 %all-to-all-start.31 = ((bf16[8,21,24,128]{3,2,1,0:T(8,128)(2,1)}), bf16[8,21,24,128]{3,2,1,0:T(8,128)(2,1)S(1)}, u32[]{:S(2)}, u32[]{:S(2)}) async-start(bf16[8,21,24,128]{3,2,1,0:T(8,128)(2,1)} %pair_gradient.1), calls=%async_computation.32 | async-start | bytes 2064384 | tf_op jit(solution)/shard_map/all_to_all | solution.py:1916
  1008.8 60.1 %all-to-all-start.33 = ((bf16[4,8,256,128]{3,2,1,0:T(8,128)(2,1)}), bf16[4,8,256,128]{3,2,1,0:T(8,128)(2,1)}, u32[]{:S(2)}, u32[]{:S(2)}) async-start(bf16[4,8,256,128]{3,2,1,0:T(8,128)(2,1)} %bitcast.68), calls=%async_computation.34 | async-start | bytes 4194304 | tf_op jit(solution)/shard_map/all_to_all | solution.py:1916
  1013.3 3.2 copy-start.19
  1068.9 29.2 %all-to-all-start.34 = ((bf16[4,8,256,128]{3,2,1,0:T(8,128)(2,1)}), bf16[4,8,256,128]{3,2,1,0:T(8,128)(2,1)S(1)}, u32[]{:S(2)}, u32[]{:S(2)}) async-start(bf16[4,8,256,128]{3,2,1,0:T(8,128)(2,1)} %all-to-all-done.33), calls=%async_computation.35 | async-start | bytes 4194304 | tf_op jit(solution)/shard_map/all_to_all | solution.py:1916
  (4 other events, 2.5 us)
Sparse Core Ops, SparseCore 0:
  46.3 32.0 all-gather.10
  100.3 56.4 all-gather.12
  675.9 123.0 reduce-scatter.1

commit v6 on v5

--- a/solution.py
+++ b/solution.py
@@ -1721,7 +1721,7 @@
     height = row_height(0, 0, runs.shape[1], total)
     values = whole_call(
         functools.partial(unpack_pair_kernel, table, total), "pair_weights", [(runs, None)], outs,
-        [((height, STRIDE), F32)],
+        [((height, STRIDE), F32)], 20,
     )
     return dict(zip(names, values))
 
@@ -1794,7 +1794,7 @@
 
 def single_kernel(
     state_in, back_in, project, kv, bias, alive, vectors, output_w, up, down,
-    final_out, grad_out, score_grad, kv_grad, query_grad, gate_grad, output_grad, up_grad, down_grad, vecs,
+    final_out, grad_out, sent, query_grad, gate_grad, output_grad, up_grad, down_grad, vecs,
 ):
     state = state_in[...]
     rows, width = state.shape
@@ -1882,12 +1882,13 @@
         delta = jnp.sum(block * grad_block, axis=0, keepdims=True)
         grad_scores.append((block * (grad_block - delta)).astype(BF16))
     for group, block in enumerate(grad_scores):
-        score_grad[:, :, group * STRIDE : (group + 1) * STRIDE] = block.reshape(kv.shape[0], rows, STRIDE)
+        sent[:, :, group * STRIDE : (group + 1) * STRIDE] = block.reshape(kv.shape[0], rows, STRIDE)
     query_grad[...] = collect([mm_tn(block, keys) for block in grad_scores]) * scale
     key_part = sum(mm_nt(block, query) for block, query in zip(grad_scores, queries)) * (1.0 / LOG2E)
     value_part = sum(mm_nt(block, grad_block) for block, grad_block in zip(probs_low, grads))
-    kv_grad[:, :, :width] = key_part.astype(BF16).reshape(kv.shape[0], rows, width)
-    kv_grad[:, :, width:] = value_part.astype(BF16).reshape(kv.shape[0], rows, width)
+    first = groups * STRIDE
+    sent[:, :, first : first + width] = key_part.astype(BF16).reshape(kv.shape[0], rows, width)
+    sent[:, :, first + width :] = value_part.astype(BF16).reshape(kv.shape[0], rows, width)
     output_grad[...] = mm_tn(gated_low, grad_low)
     up_grad[...] = mm_tn(lowered, grad_hidden)
 
@@ -1900,16 +1901,16 @@
     matrices = [weights[name] for name in names]
     square = (rows, width)
     outs = [
-        (square, F32), (square, F32), ((devices, rows, SA_HEADS * rows), BF16),
-        ((devices, rows, 2 * width), BF16), (square, F32), (square, F32),
+        (square, F32), (square, F32), ((devices, rows, SA_HEADS * rows + 2 * width), BF16),
+        (square, F32), (square, F32),
     ] + [(matrix.shape, F32) for matrix in matrices] + [((8, width), F32)]
     ins = [state, back, project, kv, bias, alive, weights[(SINGLE, VECTORS)]] + matrices
-    final, grad, score_grad, kv_grad, query_grad, gate_grad, *found, vecs = whole_call(
+    final, grad, sent, query_grad, gate_grad, *found, vecs = whole_call(
         single_kernel, "single_path", [(array, None) for array in ins], outs, [], 15
     )
     grads = dict(zip(names, found))
     grads[(SINGLE, NORM_GAIN)], grads[(SINGLE, NORM_BIAS)] = vecs[0], vecs[1]
-    return final, grad, score_grad, grads, (kv_grad, state, lowered, query_grad, gate_grad)
+    return final, grad, sent, grads, (state, lowered, query_grad, gate_grad)
 
 
 def swap(values, group):
@@ -1927,7 +1928,7 @@
 
 
 def single_attend_end(pending, parts, weights, grads):
-    _, single_state, lowered, grad_query, grad_gate = pending
+    single_state, lowered, grad_query, grad_gate = pending
     rows, width = lowered.shape
     grad_both = jnp.sum(parts.astype(F32), axis=0)
     grad_qkvg = jnp.concatenate(
@@ -2024,7 +2025,6 @@
     )
     between(0, product[0])
     product_one = swap_all(product)
-    between(9, None)
     tri_one = products(
         "outgoing_product", functools.partial(tri_product_kernel, False), [product_one], tri_half
     )
@@ -2083,7 +2083,6 @@
         [(state_shape, F32, 0)] + attend_saves, [table],
     )
     pair_cols, attend_cols = cols(PAIR), cols(ATTEND)
-    state_four, cotangent = after(state_four, cotangent)
     state_five, pair_out, single_bias = run_rows(
         functools.partial(transition_kernel, order_back), "pair_transition", steps,
         [
@@ -2093,14 +2092,14 @@
         [(state_shape, F32, 0), ((length, rows, width), BF16, 1), ((devices, rows, SA_HEADS * rows), BF16, 1)],
         [flip_scratch, ((SA_HEADS, block, length), F32)],
     )
-    single_grad_scores = send(middle(send(single_bias, group)), group)
+    single_sent = send(middle(send(single_bias, group)), group)
+    between(2, single_sent)
     pair_out = send(pair_out.reshape((parts, -1) + pair_out.shape[1:]), "z")
-    between(2, None)
     grads = {}
     grad_four, grads[(PAIR, UP)], grads[(PAIR, DOWN)], grads[(ATTEND, PAIR_PROJ)], vecs = run_rows(
         functools.partial(transition_back_kernel, read_last), "pair_transition_back", steps,
         [
-            (state_four, 0), (state_five, 0), (cotangent, 1), (single_grad_scores, 1),
+            (state_four, 0), (state_five, 0), (cotangent, 1), (single_sent, 1),
             (pair_cols, None), (turned((PAIR, UP)), None), (weights[(PAIR, UP)], None),
             (weights[(PAIR, DOWN)], None), (attend_cols, None), (weights[(ATTEND, PAIR_PROJ)], None),
         ],
@@ -2133,7 +2132,6 @@
     lowered_grad, bias_grad = attention_back(
         ENDING, read_flipped, read_plain, state_three, 1, grad_four, 0, bias_two, totals_two, mixed_two
     )
-    between(3, grads)
     flipped, bias_w_grad, vecs = run_rows(
         ending_end_kernel, "ending_attention_end", steps,
         [
@@ -2155,7 +2153,6 @@
     lowered_grad, bias_grad = attention_back(
         STARTING, read_plain, read_flipped, state_two, 0, grad_three, 1, bias_one, totals_one, mixed_one
     )
-    between(7, grads)
     square = weights[(INCOMING, GATE_OUT)].shape
     (
         grad_two, grad_tri, gate_back, bias_w_grad, grads[(INCOMING, PROJ_OUT)], grads[(INCOMING, GATE_OUT)], vecs,
@@ -2296,7 +2293,7 @@
         if number == 0:
             others = [held["runs"]]
         elif number == 1:
-            others = [weights[(SINGLE, UP)]]
+            others = [weights[(SINGLE, UP)], held["state"]]
         elif number == 2:
             others = [held["projected"][1]]
         elif number == 3:
@@ -2305,7 +2302,8 @@
             values, reduced[2] = after(*values, reduced[2])
             return [values]
         else:
-            others = [reduced[1]]
+            values, held["both"], reduced[1] = after(*values, held["both"], reduced[1])
+            return [values]
         return after(*values, *others)[: len(values)]
 
     def reduce_runs(sent):
@@ -2329,10 +2327,10 @@
             for index, name in enumerate(SINGLE_VECTORS):
                 weights[name] = weights[(SINGLE, VECTORS)][index]
             both = jnp.concatenate([single[0], single_cotangent[0]], axis=1)
-            held["both"] = send(both.reshape(parts, -1, 2 * width), "crop")
-            return
-        if number == 9:
-            both = send(held["both"], "z").reshape(rows, 2 * width).astype(F32)
+            both = lax.all_gather(both, ("crop",) + line)
+            both = both.reshape(parts, parts, cores, parts, -1, 2 * width)
+            here = lax.axis_index("z"), lax.axis_index("core"), lax.axis_index("crop")
+            both = both[here[0], :, here[1], here[2]].reshape(rows, 2 * width).astype(F32)
             held["state"], held["back"] = both[:, :width], both[:, width:]
             return
         if number == 1:
@@ -2340,17 +2338,10 @@
             held["projected"] = lowered, qkvg, send(both, group)
             return
         if number == 2:
-            pending = held["pending"]
-            moved = send(pending[0], group)
-            grad = held["grad"] + single_attend_end(pending, moved, weights, single_grads)
-            held["both"] = jnp.concatenate([held["out"], grad], axis=1).reshape(parts, -1, 2 * width)
-            return
-        if number == 3:
-            held["both"] = send(held["both"], "z")
-            return
-        if number == 7:
-            both = send(held["both"], "crop").reshape(rows, 2 * width)
-            held[SINGLE] = both[:, :width].astype(BF16), both[:, width:]
+            parts_held = grads[:, :, SA_HEADS * rows :]
+            grad = held["grad"] + single_attend_end(held["pending"], parts_held, weights, single_grads)
+            both = jnp.concatenate([held["out"], grad], axis=1).astype(BF16)
+            held["both"] = lax.all_gather(both, ("crop",) + line)
             return
         if number == 6:
             reduced[1] = reduce_runs(reduced[1])
@@ -2386,8 +2377,11 @@
     )
     reduced[0] = reduce_runs(sent)
     pair_grad = send(pair_grad.reshape(parts, -1, length, pair_grad.shape[2]), "z")
-    pair_grad = send(pair_grad, "crop").reshape(rows, length, -1).astype(F32)
-    single_out, single_grad = held[SINGLE]
+    pair_grad, held["z"] = send(pair_grad, "crop").reshape(rows, length, -1).astype(F32), pair_grad
+    both = held["both"].reshape(parts, parts, cores, parts, -1, 2 * width)
+    both = both[:, lax.axis_index("crop"), lax.axis_index("core"), lax.axis_index("z")]
+    both = both.reshape(rows, 2 * width)
+    single_out, single_grad = both[:, :width], both[:, width:].astype(F32)
     summed = lax.all_gather(jnp.concatenate([reduced[0], reduced[1]], axis=0), "crop")
     others = lax.all_gather(reduced[2], "crop")
     shard, squares = whole_call(
@@ -2396,6 +2390,7 @@
         [((RUN * STRIDE, STRIDE), F32), ((8, STRIDE), F32)], [((STRIDE, RUN, STRIDE), F32)],
     )
     shard = shard.reshape(-1)[:shard_size]
+    squares = after(squares, held["z"])[0]
     clip_norm = jnp.sqrt(jnp.sum(lax.all_gather(squares, line)))
     clipped = shard * (CLIP / jnp.maximum(clip_norm, CLIP))
     new_first = BETA_ONE * moment_one + (1.0 - BETA_ONE) * clipped

time: 1120 us -> 1060 us (0.946)
  starting transfers between devices: 110 us -> 88.8 us
  blocking collectives: 313 us -> 292 us
  waiting for transfers between devices: 184 us -> 167 us
    all_gather x1, waiting for transfers between devices: 22 us -> 0.01 us  [fast_shards(): first_runs = lax.all_gather(runs[:pair_lanes], line)]
    all_to_all x26 -> x21, starting transfers between devices: 110 us -> 88.4 us  [swap(): lax.all_to_all(values, group, split_axis=0, concat_axis=0, tiled=True)]
    all_to_all x9, blocking collectives: 236 us -> 223 us  [swap(): lax.all_to_all(values, group, split_axis=0, concat_axis=0, tiled=True)]
    all_to_all x26 -> x21, waiting for transfers between devices: 162 us -> 167 us  [swap(): lax.all_to_all(values, group, split_axis=0, concat_axis=0, tiled=True)]
  transfers between devices with their start and end apart: 29 -> 26, of which waited for: 16 -> 15; matrix products, arithmetic and copies ran while one was open for 3% -> 3% of each run, Pallas kernels for 36% -> 39%
where the time goes in v6:
time: 1060 us; the launch traced here: 1050 us
  Pallas kernels  441 us (42%)
  blocking collectives  292 us (28%)
  waiting for transfers between devices  167 us (16%)
  starting transfers between devices  88.8 us (8%)
  local copies, waits for them, and re-layouts  21.6 us (2%)
  other arithmetic  19.1 us (2%)
  between operations  17.5 us (2%)
    pallas_call x21, Pallas kernels, run_rows(): pl.pallas_call(run, grid=(grid,), in_specs=in_specs, out_specs=out_specs,...  342 us
    all_to_all x9, blocking collectives, swap(): lax.all_to_all(values, group, split_axis=0, concat_axis=0, tiled=True)  223 us
    all_to_all x21, waiting for transfers between devices, swap(): lax.all_to_all(values, group, split_axis=0, concat_axis=0, tiled=True)  167 us
    pallas_call x8, Pallas kernels, whole_call(): pl.pallas_call(kernel, in_specs=[spec(axis) for array, axis in ins], out_...  98.2 us
    all_to_all x21, starting transfers between devices, swap(): lax.all_to_all(values, group, split_axis=0, concat_axis=0, tiled=True)  88.4 us
  transfers between devices with their start and end apart: 26, of which 15 were waited for; matrix products, arithmetic and copies ran while one was open for 3% of the time, Pallas kernels for 39%

profile of v6, /device:TPU:0, one launch (start us, length us, event | category | flops | bytes accessed | tf_op | source)
XLA Modules:
  0.0 1049.5 jit_solution(2024025499750767934)
XLA Ops:
  7.2 5.3 all-to-all-start
  14.4 5.9 parameter_runs.1
  21.9 16.3 %all-to-all-done = bf16[4,8,256,128]{3,2,1,0:T(8,128)(2,1)} async-done(((bf16[4,8,256,128]{3,2,1,0:T(8,128)(2,1)}), bf16[4,8,256,128]{3,2,1,0:T(8,128)(2,1)}, u32[]{:S(2)}, u32[]{:S(2)}) %all-to-all-start) | async-done | bytes 2097184 | tf_op jit(solution)/shard_map/all_to_all | solution.py:1917
  38.2 5.1 all-to-all-start.1
  45.3 8.9 all-reduce.2
  55.7 8.0 pair_weights.1
  63.7 27.2 %all-to-all-done.1 = bf16[4,8,256,128]{3,2,1,0:T(8,128)(2,1)S(1)} async-done(((bf16[4,8,256,128]{3,2,1,0:T(8,128)(2,1)}), bf16[4,8,256,128]{3,2,1,0:T(8,128)(2,1)S(1)}, u32[]{:S(2)}, u32[]{:S(2)}) %all-to-all-start.1) | async-done | bytes 2097184 | tf_op jit(solution)/shard_map/all_to_all | solution.py:1917
  92.9 12.8 %outgoing_in.1 = bf16[8,2,16,32,256]{4,3,2,1,0:T(8,128)(2,1)} custom-call(s32[32]{0:T(128)} %dynamic-slice_convert_fusion.refs_0_, f32[8,256]{1,0:T(8,128)} %broadcast_in_dim.29.refs_1_.refs_0_.alive, bf16[32,256,128]{2,1,0:T(8,128)(2,1)} %bitcast.70, f32[128,8]{1,0:T(8,128)} %get-tuple-element.174.refs_3_.refs_4_.refs_11_.refs_6_, ...), custom_call_target="tpu_custom_call" | custom-call | flops 12999999488 | bytes 39000000 | tf_op jit(solution)/shard_map/outgoing_in/pallas_call | solution.py:762
  105.6 53.5 %all_to_all.150.refs_0_.refs_2_ = bf16[8,2,16,32,256]{4,3,2,1,0:T(8,128)(2,1)} all-to-all(bf16[8,2,16,32,256]{4,3,2,1,0:T(8,128)(2,1)} %outgoing_in.1), channel_id=1, replica_groups=mesh['crop'=4,'z'=4,'core'=2] {'crop','core'}, dimensions={0} | all-to-all | bytes 8388608 | tf_op jit(solution)/shard_map/all_to_all | solution.py:1917
  159.2 6.2 outgoing_product.1
  170.5 13.9 %all-to-all-done.3 = bf16[8,16,16,256]{3,2,1,0:T(8,128)(2,1)S(1)} async-done(((bf16[8,16,16,256]{3,2,1,0:T(8,128)(2,1)}), bf16[8,16,16,256]{3,2,1,0:T(8,128)(2,1)S(1)}, u32[]{:S(2)}, u32[]{:S(2)}) %all-to-all-start.3) | async-done | bytes 1048608 | tf_op jit(solution)/shard_map/all_to_all | solution.py:1917
  188.0 12.4 %outgoing_out_incoming_in.2 = (f32[32,128,256]{2,1,0:T(8,128)}, bf16[8,2,16,16,256]{4,3,2,1,0:T(8,128)(2,1)}) custom-call(s32[16]{0:T(128)} %get-tuple-element.349.refs_0_, f32[8,256]{1,0:T(8,128)} %broadcast_in_dim.29.refs_1_.refs_0_.alive, bf16[32,256,128]{2,1,0:T(8,128)(2,1)} %bitcast.71, bf16[128,16,256]{2,1,0:T(8,128)(2,1)} %bitcast.83, ...), custom_call_target="tpu_custom_call" | custom-call | flops 11000000512 | bytes 33000000 | tf_op jit(solution)/shard_map/outgoing_out_incoming_in/pallas_call | solution.py:762
  209.4 12.4 %outgoing_out_incoming_in.3 = (f32[32,128,256]{2,1,0:T(8,128)}, bf16[8,2,16,16,256]{4,3,2,1,0:T(8,128)(2,1)}) custom-call(s32[16]{0:T(128)} %get-tuple-element.350.refs_0_, f32[8,256]{1,0:T(8,128)} %broadcast_in_dim.29.refs_1_.refs_0_.alive, bf16[32,256,128]{2,1,0:T(8,128)(2,1)} %bitcast.72, ...), custom_call_target="tpu_custom_call", output_to_operand_aliasing={{0}: (9, {})} | custom-call | flops 11000000512 | bytes 33000000 | tf_op jit(solution)/shard_map/outgoing_out_incoming_in/pallas_call | solution.py:762
  221.8 16.9 %all-to-all-done.5.refs_0_.refs_2_ = bf16[8,2,16,16,256]{4,3,2,1,0:T(8,128)(2,1)S(1)} async-done(((bf16[8,2,16,16,256]{4,3,2,1,0:T(8,128)(2,1)}), bf16[8,2,16,16,256]{4,3,2,1,0:T(8,128)(2,1)S(1)}, u32[]{:S(2)}, u32[]{:S(2)}) %all-to-all-start.5) | async-done | bytes 2097184 | tf_op jit(solution)/shard_map/all_to_all | solution.py:1917
  240.0 4.3 all-to-all-start.6
  245.9 28.4 %single_weights.1 = (bf16[384,1536]{1,0:T(8,128)(2,1)}, bf16[384,384]{1,0:T(8,128)(2,1)}, bf16[384,3072]{1,0:T(8,128)(2,1)}, bf16[1536,384]{1,0:T(8,128)(2,1)}, ...) custom-call(bf16[8,105,24,128]{3,2,1,0:T(8,128)(2,1)} %bitcast.100), custom_call_target="tpu_custom_call" | custom-call | flops 8000000000 | bytes 24000000 | tf_op jit(solution)/shard_map/single_weights/pallas_call | solution.py:1696
  274.3 6.3 incoming_product.1
  280.6 4.7 all-to-all-start.7
  291.0 20.9 %all-to-all-done.7 = bf16[8,16,32,256]{3,2,1,0:T(8,128)(2,1)} async-done(((bf16[8,16,32,256]{3,2,1,0:T(8,128)(2,1)}), bf16[8,16,32,256]{3,2,1,0:T(8,128)(2,1)}, u32[]{:S(2)}, u32[]{:S(2)}) %all-to-all-start.7) | async-done | bytes 2097184 | tf_op jit(solution)/shard_map/all_to_all | solution.py:1917
  316.2 13.9 %incoming_out_starting_bias.1 = (f32[32,128,256]{2,1,0:T(8,128)}, bf16[4,32,256]{2,1,0:T(8,128)(2,1)}) custom-call(f32[32,128,256]{2,1,0:T(8,128)} %get-tuple-element.188.refs_0_.refs_6_.refs_2_, bf16[128,32,256]{2,1,0:T(8,128)(2,1)} %bitcast.14.refs_1_.refs_7_, f32[128,8]{1,0:T(8,128)} %get-tuple-element.185.refs_7_.refs_2_.refs_8_.refs_6_, ...), custom_call_target="tpu_custom_call" | custom-call | flops 15000000512 | bytes 45000000 | tf_op jit(solution)/shard_map/incoming_out_starting_bias/pallas_call | solution.py:762
  330.1 12.2 %all-gather.4 = bf16[32,32,256]{2,1,0:T(8,128)(2,1)} all-gather(bf16[4,32,256]{2,1,0:T(8,128)(2,1)} %get-tuple-element.205), channel_id=7, replica_groups=mesh['crop'=4,'z'=4,'core'=2] {'crop','core'}, dimensions={0}, use_global_device_ids=true | all-gather | bytes 589824 | tf_op jit(solution)/shard_map/all_gather | solution.py:2060
  343.0 4.4 all-to-all-start.9
  347.4 20.4 %starting_attention.1 = (bf16[8,32,32,128]{3,2,1,0:T(8,128)(2,1)}, f32[32,4,256]{2,1,0:T(4,128)}, bf16[32,128,256]{2,1,0:T(8,128)(2,1)}) custom-call(f32[8,256]{1,0:T(8,128)} %broadcast_in_dim.29.refs_1_.refs_0_.alive, f32[32,128,256]{2,1,0:T(8,128)} %get-tuple-element.204.refs_1_.refs_0_, bf16[8,4,32,256]{3,2,1,0:T(8,128)(2,1)} %bitcast.91, ...), custom_call_target="tpu_custom_call" | custom-call | flops 20999999488 | bytes 63000000 | tf_op jit(solution)/shard_map/starting_attention/pallas_call | solution.py:762
  367.7 6.3 all-to-all-done.9
  374.0 30.9 %all_to_all.151.refs_0_.refs_1_ = bf16[8,32,32,128]{3,2,1,0:T(8,128)(2,1)} all-to-all(bf16[8,32,32,128]{3,2,1,0:T(8,128)(2,1)} %get-tuple-element.211), channel_id=1, replica_groups=mesh['crop'=4,'z'=4,'core'=2] {'crop','core'}, dimensions={0} | all-to-all | bytes 4194304 | tf_op jit(solution)/shard_map/all_to_all | solution.py:1917
  408.6 5.2 ending_bias.1
  413.7 11.2 %all-gather.5 = bf16[32,32,256]{2,1,0:T(8,128)(2,1)} all-gather(bf16[4,32,256]{2,1,0:T(8,128)(2,1)} %ending_bias.1), channel_id=8, replica_groups=mesh['crop'=4,'z'=4,'core'=2] {'crop','core'}, dimensions={0}, use_global_device_ids=true | all-gather | bytes 589824 | tf_op jit(solution)/shard_map/all_gather | solution.py:2076
  424.9 19.2 %ending_attention.1 = (f32[32,128,256]{2,1,0:T(8,128)}, f32[32,4,256]{2,1,0:T(4,128)}, bf16[32,128,256]{2,1,0:T(8,128)(2,1)}) custom-call(f32[8,256]{1,0:T(8,128)} %broadcast_in_dim.29.refs_1_.refs_0_.alive, bf16[8,32,32,128]{3,2,1,0:T(8,128)(2,1)} %all_to_all.151.refs_0_.refs_1_, bf16[8,4,32,256]{3,2,1,0:T(8,128)(2,1)} %bitcast.93, ...), custom_call_target="tpu_custom_call" | custom-call | flops 15000000512 | bytes 45000000 | tf_op jit(solution)/shard_map/ending_attention/pallas_call | solution.py:762
  444.0 15.1 %pair_transition.1 = (f32[32,128,256]{2,1,0:T(8,128)}, bf16[256,32,128]{2,1,0:T(8,128)(2,1)}, bf16[8,32,512]{2,1,0:T(8,128)(2,1)}) custom-call(f32[32,128,256]{2,1,0:T(8,128)} %get-tuple-element.216.refs_0_, f32[128,8]{1,0:T(8,128)} %get-tuple-element.217.refs_1_.refs_4_, bf16[1024,128]{1,0:T(8,128)(2,1)} %get-tuple-element.218.refs_2_.refs_5_, ...), custom_call_target="tpu_custom_call" | custom-call | flops 15000000512 | bytes 45000000 | tf_op jit(solution)/shard_map/pair_transition/pallas_call | solution.py:762
  459.1 11.0 %all_to_all.152.bias = bf16[8,32,512]{2,1,0:T(8,128)(2,1)} all-to-all(bf16[8,32,512]{2,1,0:T(8,128)(2,1)} %get-tuple-element.225), channel_id=1, replica_groups=mesh['crop'=4,'z'=4,'core'=2] {'crop','core'}, dimensions={0} | all-to-all | bytes 524288 | tf_op jit(solution)/shard_map/all_to_all | solution.py:1917
  470.1 10.0 single_path.1
  480.1 15.4 %all_to_all.153.refs_3_ = bf16[8,32,1280]{2,1,0:T(8,128)(2,1)} all-to-all(bf16[8,32,1280]{2,1,0:T(8,128)(2,1)} %get-tuple-element.229), channel_id=1, replica_groups=mesh['crop'=4,'z'=4,'core'=2] {'crop','core'}, dimensions={0} | all-to-all | bytes 1310720 | tf_op jit(solution)/shard_map/all_to_all | solution.py:1917
  495.5 5.2 all-to-all-start.14
  500.7 31.3 %pair_transition_back.1 = (f32[32,128,256]{2,1,0:T(8,128)}, f32[128,1024]{1,0:T(8,128)}, f32[512,128]{1,0:T(8,128)}, f32[128,16]{1,0:T(8,128)}, f32[8,128]{1,0:T(8,128)}) custom-call(f32[32,128,256]{2,1,0:T(8,128)} %get-tuple-element.216.refs_0_, f32[32,128,256]{2,1,0:T(8,128)} %get-tuple-element.231.refs_1_, bf16[8,32,32,128]{3,2,1,0:T(8,128)(2,1)} %bitcast.77, ...), custom_call_target="tpu_custom_call" | custom-call | flops 30000001024 | bytes 90000000 | tf_op jit(solution)/shard_map/pair_transition_back/pallas_call | solution.py:762
  532.0 33.0 %attention_back.2 = (bf16[32,128,256]{2,1,0:T(8,128)(2,1)}, bf16[8,4,32,256]{3,2,1,0:T(8,128)(2,1)}, f32[128,512]{1,0:T(8,128)}, f32[128,128]{1,0:T(8,128)}) custom-call(f32[8,256]{1,0:T(8,128)} %broadcast_in_dim.29.refs_1_.refs_0_.alive, bf16[8,32,32,128]{3,2,1,0:T(8,128)(2,1)} %all_to_all.151.refs_0_.refs_1_, ...), custom_call_target="tpu_custom_call" | custom-call | flops 33999998976 | bytes 102000000 | tf_op jit(solution)/shard_map/attention_back/pallas_call | solution.py:762
  565.1 13.9 %all_to_all.154.refs_3_ = bf16[8,4,32,256]{3,2,1,0:T(8,128)(2,1)} all-to-all(bf16[8,4,32,256]{3,2,1,0:T(8,128)(2,1)} %get-tuple-element.242), channel_id=1, replica_groups=mesh['crop'=4,'z'=4,'core'=2] {'crop','core'}, dimensions={0} | all-to-all | bytes 1048576 | tf_op jit(solution)/shard_map/all_to_all | solution.py:1917
  578.9 12.0 %ending_attention_end.1 = (bf16[8,32,32,128]{3,2,1,0:T(8,128)(2,1)}, f32[128,8]{1,0:T(8,128)}, f32[8,128]{1,0:T(8,128)}) custom-call(bf16[8,32,32,128]{3,2,1,0:T(8,128)(2,1)} %all_to_all.151.refs_0_.refs_1_, f32[32,128,256]{2,1,0:T(8,128)} %get-tuple-element.235.refs_2_.refs_1_, bf16[32,128,256]{2,1,0:T(8,128)(2,1)} %get-tuple-element.240.refs_2_, ...), custom_call_target="tpu_custom_call" | custom-call | flops 15000000512 | bytes 45000000 | tf_op jit(solution)/shard_map/ending_attention_end/pallas_call | solution.py:762
  600.0 30.3 %single_gradient.1 = bf16[8,104,24,128]{3,2,1,0:T(8,128)(2,1)} custom-call(f32[384,1536]{1,0:T(8,128)} %fusion.2.refs_0_, f32[384,384]{1,0:T(8,128)} %get-tuple-element.251.refs_1_, f32[384,3072]{1,0:T(8,128)} %get-tuple-element.252.refs_2_, f32[1536,384]{1,0:T(8,128)} %get-tuple-element.253.refs_3_, f32[128,16]{1,0:T(8,128)} %get-tuple-element.254.refs_4_, ...), custom_call_target="tpu_custom_call" | custom-call | flops 8000000000 | bytes 24000000 | tf_op jit(solution)/shard_map/single_gradient/pallas_call | solution.py:1696
  635.9 33.7 %attention_back.3 = (bf16[32,128,256]{2,1,0:T(8,128)(2,1)}, bf16[8,4,32,256]{3,2,1,0:T(8,128)(2,1)}, f32[128,512]{1,0:T(8,128)}, f32[128,128]{1,0:T(8,128)}) custom-call(f32[8,256]{1,0:T(8,128)} %broadcast_in_dim.29.refs_1_.refs_0_.alive, f32[32,128,256]{2,1,0:T(8,128)} %get-tuple-element.204.refs_1_.refs_0_, bf16[8,32,32,128]{3,2,1,0:T(8,128)(2,1)} %copy-done.7, ...), custom_call_target="tpu_custom_call" | custom-call | flops 33999998976 | bytes 102000000 | tf_op jit(solution)/shard_map/attention_back/pallas_call | solution.py:762
  669.6 14.0 %all_to_all.155.refs_3_ = bf16[8,4,32,256]{3,2,1,0:T(8,128)(2,1)} all-to-all(bf16[8,4,32,256]{3,2,1,0:T(8,128)(2,1)} %get-tuple-element.264), channel_id=1, replica_groups=mesh['crop'=4,'z'=4,'core'=2] {'crop','core'}, dimensions={0} | all-to-all | bytes 1048576 | tf_op jit(solution)/shard_map/all_to_all | solution.py:1917
  683.6 15.8 %starting_end_incoming_out_back.2 = (f32[32,128,256]{2,1,0:T(8,128)}, bf16[128,16,256]{2,1,0:T(8,128)(2,1)}, bf16[32,128,256]{2,1,0:T(8,128)(2,1)}, f32[128,8]{1...) custom-call(f32[32,128,256]{2,1,0:T(8,128)} %get-tuple-element.204.refs_1_.refs_0_, ...), custom_call_target="tpu_custom_call" | custom-call | flops 12999999488 | bytes 39000000 | tf_op jit(solution)/shard_map/starting_end_incoming_out_back/pallas_call | solution.py:762
  703.1 15.8 %starting_end_incoming_out_back.3 = (f32[32,128,256]{2,1,0:T(8,128)}, bf16[128,16,256]{2,1,0:T(8,128)(2,1)}, bf16[32,128,256]{2,1,0:T(8,128)(2,1)}, f32[128,8]{1...) custom-call(f32[32,128,256]{2,1,0:T(8,128)} %get-tuple-element.204.r, ...), custom_call_target="tpu_custom_call", output_to_operand_aliasing={{0}: (13, {}), {2}: (14, {}), {3}: (15, {}), {4}: (16, {}),... | custom-call | flops 12999999488 | bytes 39000000 | tf_op jit(solution)/shard_map/starting_end_incoming_out_back/pallas_call | solution.py:762
  720.7 20.7 %all_to_all.156.refs_1_ = bf16[8,16,16,256]{3,2,1,0:T(8,128)(2,1)} all-to-all(bf16[8,16,16,256]{3,2,1,0:T(8,128)(2,1)} %bitcast.88), channel_id=1, replica_groups=mesh['crop'=4,'z'=4,'core'=2] {'crop','core'}, dimensions={0} | all-to-all | bytes 2097152 | tf_op jit(solution)/shard_map/all_to_all | solution.py:1917
  741.5 7.3 incoming_product_back.1
  748.8 4.5 all-to-all-start.21
  753.6 26.3 %all-to-all-done.21.refs_3_ = bf16[8,2,16,16,256]{4,3,2,1,0:T(8,128)(2,1)} async-done(((bf16[8,2,16,16,256]{4,3,2,1,0:T(8,128)(2,1)}), bf16[8,2,16,16,256]{4,3,2,1,0:T(8,128)(2,1)}, u32[]{:S(2)}, u32[]{:S(2)}) %all-to-all-start.21) | async-done | bytes 2097184 | tf_op jit(solution)/shard_map/all_to_all | solution.py:1917
  780.0 4.4 all-to-all-start.22
  785.3 21.1 %incoming_in_outgoing_out_back.2 = (f32[32,128,256]{2,1,0:T(8,128)}, bf16[128,16,256]{2,1,0:T(8,128)(2,1)}, bf16[32,128,256]{2,1,0:T(8,128)(2,1)}, f32[128,512]{...) custom-call(s32[16]{0:T(128)} %get-tuple-element.349.refs_0_, ...), custom_call_target="tpu_custom_call" | custom-call | flops 18499999744 | bytes 55500000 | tf_op jit(solution)/shard_map/incoming_in_outgoing_out_back/pallas_call | solution.py:762
  806.4 4.9 all-to-all-done.22.refs_3_
  814.9 21.2 %incoming_in_outgoing_out_back.3 = (f32[32,128,256]{2,1,0:T(8,128)}, bf16[128,16,256]{2,1,0:T(8,128)(2,1)}, bf16[32,128,256]{2,1,0:T(8,128)(2,1)}, f32[128,512]{...) custom-call(s32[16]{0:T(128)} %get-tuple-element.350.refs_0_, ...), custom_call_target="tpu_custom_call", output_to_operand_aliasing={{0}: (16, {}), {2}: (17, {}), {3}: (18, {}), {4}: (19, {}),... | custom-call | flops 18499999744 | bytes 55500000 | tf_op jit(solution)/shard_map/incoming_in_outgoing_out_back/pallas_call | solution.py:762
  842.0 7.5 pair_gradient.1
  849.6 6.2 all-to-all-done.24.refs_1_
  855.8 7.3 outgoing_product_back.1
  863.1 53.6 %all_to_all.157.refs_3_ = bf16[8,2,16,32,256]{4,3,2,1,0:T(8,128)(2,1)} all-to-all(bf16[8,2,16,32,256]{4,3,2,1,0:T(8,128)(2,1)} %outgoing_product_back.1), channel_id=1, replica_groups=mesh['crop'=4,'z'=4,'core'=2] {'crop','core'}, dimensions={0} | all-to-all | bytes 8388608 | tf_op jit(solution)/shard_map/all_to_all | solution.py:1917
  916.7 5.2 all-to-all-start.26
  921.8 19.9 %outgoing_in_back.1 = (bf16[32,256,128]{2,1,0:T(8,128)(2,1)}, f32[128,512]{1,0:T(8,128)}, f32[8,128]{1,0:T(8,128)}) custom-call(s32[32]{0:T(128)} %dynamic-slice_convert_fusion.refs_0_, f32[8,256]{1,0:T(8,128)} %broadcast_in_dim.29.refs_1_.refs_0_.alive, bf16[32,256,128]{2,1,0:T(8,128)(2,1)} %bitcast.75, bf16[8,2,16,32,256]{4,3,2,1,0:T(8,128)(2,1)} %all_to_all.157.refs_3_, ...), custom_call_target="tpu_custom_call" | custom-call | flops 20000000000 | bytes 60000000 | tf_op jit(solution)/shard_map/outgoing_in_back/pallas_call | solution.py:762
  948.1 10.3 all_to_all.158
  958.4 4.5 all-to-all-start.28
  964.8 10.3 all-gather.7
  976.7 11.6 %all-gather.6 = bf16[96,24,128]{2,1,0:T(8,128)(2,1)} all-gather(bf16[24,24,128]{2,1,0:T(8,128)(2,1)S(1)} %pad_maximum_fusion), channel_id=9, replica_groups=mesh['crop'=4,'z'=4,'core'=2] {'crop'}, dimensions={0}, use_global_device_ids=true | all-gather | bytes 737280 | tf_op jit(solution)/shard_map/all_gather | solution.py:2385
  988.3 5.9 gradient_share.1
  994.3 16.7 %all-to-all-done.28 = bf16[4,8,256,128]{3,2,1,0:T(8,128)(2,1)} async-done(((bf16[4,8,256,128]{3,2,1,0:T(8,128)(2,1)}), bf16[4,8,256,128]{3,2,1,0:T(8,128)(2,1)}, u32[]{:S(2)}, u32[]{:S(2)}) %all-to-all-start.28) | async-done | bytes 2097184 | tf_op jit(solution)/shard_map/all_to_all | solution.py:1917
  1014.6 14.3 %all-gather.8 = f32[64,128]{1,0:T(8,128)S(1)} all-gather(f32[8,128]{1,0:T(8,128)S(1)} %copy-done.33), channel_id=11, replica_groups=mesh['crop'=4,'z'=4,'core'=2] {'z','core'}, dimensions={0}, use_global_device_ids=true | all-gather | bytes 36864 | tf_op jit(solution)/shard_map/all_gather | solution.py:2394
  1030.2 7.5 multiply_subtract_fusion
  (162 shorter events, 91.5 us)
Async XLA Ops:
  7.2 5.3 copy-start.1
  7.2 31.0 %all-to-all-start = ((bf16[4,8,256,128]{3,2,1,0:T(8,128)(2,1)}), bf16[4,8,256,128]{3,2,1,0:T(8,128)(2,1)}, u32[]{:S(2)}, u32[]{:S(2)}) async-start(bf16[4,8,256,128]{3,2,1,0:T(8,128)(2,1)} %bitcast.68), calls=%async_computation | async-start | bytes 4194304 | tf_op jit(solution)/shard_map/all_to_all | solution.py:1917
  12.5 43.3 %all-gather.16.cloned.1.call-start = ((), (), s32[]{:S(2)}) async-start(), calls=%async_computation.33 | async-start | bytes 1327104 | tf_op jit(solution)/shard_map/all_gather | solution.py:2268
  21.9 22.1 %copy-start.38 = (u32[32]{0:T(128)S(1)}, u32[32]{0:T(128)}, u32[]{:S(2)}) copy-start(u32[32]{0:T(128)} %constant.107) | copy-start | bytes 388
  21.9 32.3 %copy-start.15 = (bf16[128,24,128]{2,1,0:T(8,128)(2,1)S(1)}, bf16[128,24,128]{2,1,0:T(8,128)(2,1)}, u32[]{:S(2)}) copy-start(bf16[128,24,128]{2,1,0:T(8,128)(2,1)} %parameter_runs.1) | copy-start | bytes 2359300
  38.2 52.7 %all-to-all-start.1 = ((bf16[4,8,256,128]{3,2,1,0:T(8,128)(2,1)}), bf16[4,8,256,128]{3,2,1,0:T(8,128)(2,1)S(1)}, u32[]{:S(2)}, u32[]{:S(2)}) async-start(bf16[4,8,256,128]{3,2,1,0:T(8,128)(2,1)} %all-to-all-done), calls=%async_computation.1 | async-start | bytes 4194304 | tf_op jit(solution)/shard_map/all_to_all | solution.py:1917
  43.3 166.0 %all-gather.18.cloned.1.call-start = ((), (), s32[]{:S(2)}) async-start(), calls=%async_computation.34 | async-start | bytes 5806080 | tf_op jit(solution)/shard_map/all_gather | solution.py:2325
  55.7 35.2 %copy-start.35 = (f32[256]{0:T(256)S(1)}, f32[256]{0:T(256)}, u32[]{:S(2)}) copy-start(f32[256]{0:T(256)} %constant.92.clone) | copy-start | bytes 3076
  90.9 1.9 copy-start.5
  165.4 3.8 copy-start.25
  165.4 3.8 copy-start.26
  165.4 4.5 copy-start.34
  165.4 19.0 %all-to-all-start.3 = ((bf16[8,16,16,256]{3,2,1,0:T(8,128)(2,1)}), bf16[8,16,16,256]{3,2,1,0:T(8,128)(2,1)S(1)}, u32[]{:S(2)}, u32[]{:S(2)}) async-start(bf16[8,16,16,256]{3,2,1,0:T(8,128)(2,1)} %get-tuple-element.179), calls=%async_computation.3 | async-start | bytes 2097152 | tf_op jit(solution)/shard_map/all_to_all | solution.py:1917
  169.1 75.2 %all-gather.20.cloned.1.call-start = ((), (), s32[]{:S(2)}) async-start(), calls=%async_computation.35 | async-start | bytes 1622016 | tf_op jit(solution)/shard_map/all_gather | solution.py:2330
  184.4 3.6 copy-start.12
  184.4 20.3 %all-to-all-start.4 = ((bf16[8,16,16,256]{3,2,1,0:T(8,128)(2,1)}), bf16[8,16,16,256]{3,2,1,0:T(8,128)(2,1)S(1)}, u32[]{:S(2)}, u32[]{:S(2)}) async-start(bf16[8,16,16,256]{3,2,1,0:T(8,128)(2,1)} %get-tuple-element.180), calls=%async_computation.4 | async-start | bytes 2097152 | tf_op jit(solution)/shard_map/all_to_all | solution.py:1917
  204.8 1.0 copy-start.11
  205.7 32.9 %all-to-all-start.5 = ((bf16[8,2,16,16,256]{4,3,2,1,0:T(8,128)(2,1)}), bf16[8,2,16,16,256]{4,3,2,1,0:T(8,128)(2,1)S(1)}, u32[]{:S(2)}, u32[]{:S(2)}) async-start(bf16[8,2,16,16,256]{4,3,2,1,0:T(8,128)(2,1)} %get-tuple-element.190), calls=%async_computation.5 | async-start | bytes 4194304 | tf_op jit(solution)/shard_map/all_to_all | solution.py:1917
  238.7 1.3 copy-start.6
  240.0 34.3 %all-to-all-start.6 = ((bf16[8,2,16,16,256]{4,3,2,1,0:T(8,128)(2,1)}), bf16[8,2,16,16,256]{4,3,2,1,0:T(8,128)(2,1)}, u32[]{:S(2)}, u32[]{:S(2)}) async-start(bf16[8,2,16,16,256]{4,3,2,1,0:T(8,128)(2,1)} %get-tuple-element.192), calls=%async_computation.6 | async-start | bytes 4194304 | tf_op jit(solution)/shard_map/all_to_all | solution.py:1917
  245.2 45.5 %copy-start.9 = (f32[32,768]{1,0:T(8,128)}, f32[32,768]{1,0:T(8,128)S(1)}, u32[]{:S(2)}) copy-start(f32[32,768]{1,0:T(8,128)S(1)} %bitcast_convert_fusion.1) | copy-start | bytes 294916
  280.6 4.7 copy-start.4
  280.6 31.4 %all-to-all-start.7 = ((bf16[8,16,32,256]{3,2,1,0:T(8,128)(2,1)}), bf16[8,16,32,256]{3,2,1,0:T(8,128)(2,1)}, u32[]{:S(2)}, u32[]{:S(2)}) async-start(bf16[8,16,32,256]{3,2,1,0:T(8,128)(2,1)} %incoming_product.1), calls=%async_computation.7 | async-start | bytes 4194304 | tf_op jit(solution)/shard_map/all_to_all | solution.py:1917
  285.3 5.4 copy-start.2
  289.1 23.6 %copy-start.29 = (f32[32]{0:T(128)}, f32[32]{0:T(128)S(1)}, u32[]{:S(2)}) copy-start(f32[32]{0:T(128)S(1)} %broadcast_multiply_fusion) | copy-start | bytes 388
  289.8 22.9 %copy-start.31 = (f32[32]{0:T(128)}, f32[32]{0:T(128)S(1)}, u32[]{:S(2)}) copy-start(f32[32]{0:T(128)S(1)} %fusion.5) | copy-start | bytes 388
  290.6 22.1 %copy-start.19 = (f32[384]{0:T(512)}, f32[384]{0:T(512)S(1)}, u32[]{:S(2)}) copy-start(f32[384]{0:T(512)S(1)} %get-tuple-element.337) | copy-start | bytes 4612
  290.6 22.1 %copy-start.27 = (f32[384]{0:T(512)}, f32[384]{0:T(512)S(1)}, u32[]{:S(2)}) copy-start(f32[384]{0:T(512)S(1)} %get-tuple-element.338) | copy-start | bytes 4612
  291.0 39.1 %copy-start.17 = (f32[32,1536]{1,0:T(8,128)}, f32[32,1536]{1,0:T(8,128)S(1)}, u32[]{:S(2)}) copy-start(f32[32,1536]{1,0:T(8,128)S(1)} %fusion.8.project) | copy-start | bytes 589828
  312.7 29.5 %all-to-all-start.8 = ((bf16[8,32,768]{2,1,0:T(8,128)(2,1)}), bf16[8,32,768]{2,1,0:T(8,128)(2,1)S(1)}, u32[]{:S(2)}, u32[]{:S(2)}) async-start(bf16[8,32,768]{2,1,0:T(8,128)(2,1)} %broadcast_in_dim.30), calls=%async_computation.8 | async-start | bytes 786432 | tf_op jit(solution)/shard_map/all_to_all | solution.py:1917
  342.2 0.7 copy-start.16
  343.0 31.0 %all-to-all-start.9 = ((bf16[8,32,32,128]{3,2,1,0:T(8,128)(2,1)}), bf16[8,32,32,128]{3,2,1,0:T(8,128)(2,1)}, u32[]{:S(2)}, u32[]{:S(2)}) async-start(bf16[8,32,32,128]{3,2,1,0:T(8,128)(2,1)} %bitcast.18), calls=%async_computation.9 | async-start | bytes 4194304 | tf_op jit(solution)/shard_map/all_to_all | solution.py:1917
  404.9 54.2 %all-to-all-start.11 = ((bf16[4,2,32,32,128]{4,3,2,1,0:T(8,128)(2,1)}), bf16[4,2,32,32,128]{4,3,2,1,0:T(8,128)(2,1)S(1)}, u32[]{:S(2)}, u32[]{:S(2)}) async-start(bf16[4,2,32,32,128]{4,3,2,1,0:T(8,128)(2,1)} %bitcast.22), calls=%async_computation.11 | async-start | bytes 4194304 | tf_op jit(solution)/shard_map/all_to_all | solution.py:1917
  459.1 21.0 %copy-start.8 = (bf16[4,2,32,32,128]{4,3,2,1,0:T(8,128)(2,1)}, bf16[4,2,32,32,128]{4,3,2,1,0:T(8,128)(2,1)S(1)}, u32[]{:S(2)}) copy-start(bf16[4,2,32,32,128]{4,3,2,1,0:T(8,128)(2,1)S(1)} %all-to-all-done.11) | copy-start | bytes 6291460
  495.5 69.6 %all-to-all-start.14 = ((bf16[4,64,32,128]{3,2,1,0:T(8,128)(2,1)}), bf16[4,64,32,128]{3,2,1,0:T(8,128)(2,1)S(1)}, u32[]{:S(2)}, u32[]{:S(2)}) async-start(bf16[4,64,32,128]{3,2,1,0:T(8,128)(2,1)} %bitcast.78), calls=%async_computation.14 | async-start | bytes 4194304 | tf_op jit(solution)/shard_map/all_to_all | solution.py:1917
  565.1 25.9 %copy-start = (bf16[4,64,32,128]{3,2,1,0:T(8,128)(2,1)}, bf16[4,64,32,128]{3,2,1,0:T(8,128)(2,1)S(1)}, u32[]{:S(2)}) copy-start(bf16[4,64,32,128]{3,2,1,0:T(8,128)(2,1)S(1)} %all-to-all-done.14) | copy-start | bytes 6291460
  591.0 4.6 copy-start.22
  591.0 4.6 copy-start.21
  591.0 5.7 copy-start.3
  591.0 5.7 copy-start.10
  591.0 5.7 copy-start.20
  591.1 5.7 copy-start.30
  591.1 5.7 copy-start.32
  591.1 6.9 copy-start.28
  591.1 39.2 %all-to-all-start.16 = ((bf16[8,32,32,128]{3,2,1,0:T(8,128)(2,1)}), bf16[8,32,32,128]{3,2,1,0:T(8,128)(2,1)S(1)}, u32[]{:S(2)}, u32[]{:S(2)}) async-start(bf16[8,32,32,128]{3,2,1,0:T(8,128)(2,1)} %get-tuple-element.247), calls=%async_computation.16 | async-start | bytes 4194304 | tf_op jit(solution)/shard_map/all_to_all | solution.py:1917
  594.8 190.5 %reduce-scatter.2.cloned.1.call-start = ((), (), s32[]{:S(2)}) async-start(), calls=%async_computation.31 | async-start | bytes 5271552 | tf_op jit(solution)/shard_map/reduce_scatter | solution.py:2358
  630.3 1.3 copy-start.7
  631.6 38.0 %all-to-all-start.17 = ((bf16[8,32,32,128]{3,2,1,0:T(8,128)(2,1)}), bf16[8,32,32,128]{3,2,1,0:T(8,128)(2,1)S(1)}, u32[]{:S(2)}, u32[]{:S(2)}) async-start(bf16[8,32,32,128]{3,2,1,0:T(8,128)(2,1)} %bitcast.66), calls=%async_computation.17 | async-start | bytes 4194304 | tf_op jit(solution)/shard_map/all_to_all | solution.py:1917
  699.5 21.3 %all-to-all-start.19 = ((bf16[8,16,16,256]{3,2,1,0:T(8,128)(2,1)}), bf16[8,16,16,256]{3,2,1,0:T(8,128)(2,1)S(1)}, u32[]{:S(2)}, u32[]{:S(2)}) async-start(bf16[8,16,16,256]{3,2,1,0:T(8,128)(2,1)} %bitcast.87), calls=%async_computation.19 | async-start | bytes 2097152 | tf_op jit(solution)/shard_map/all_to_all | solution.py:1917
  720.7 20.7 %copy-start.14 = (bf16[8,16,16,256]{3,2,1,0:T(8,128)(2,1)}, bf16[8,16,16,256]{3,2,1,0:T(8,128)(2,1)S(1)}, u32[]{:S(2)}) copy-start(bf16[8,16,16,256]{3,2,1,0:T(8,128)(2,1)S(1)} %all-to-all-done.19.refs_0_) | copy-start | bytes 3145732
  748.8 4.5 copy-start.37
  748.8 4.7 copy-start.23
  748.8 4.7 copy-start.24
  748.8 31.1 %all-to-all-start.21 = ((bf16[8,2,16,16,256]{4,3,2,1,0:T(8,128)(2,1)}), bf16[8,2,16,16,256]{4,3,2,1,0:T(8,128)(2,1)}, u32[]{:S(2)}, u32[]{:S(2)}) async-start(bf16[8,2,16,16,256]{4,3,2,1,0:T(8,128)(2,1)} %get-tuple-element.280), calls=%async_computation.21 | async-start | bytes 4194304 | tf_op jit(solution)/shard_map/all_to_all | solution.py:1917
  780.0 31.4 %all-to-all-start.22 = ((bf16[8,2,16,16,256]{4,3,2,1,0:T(8,128)(2,1)}), bf16[8,2,16,16,256]{4,3,2,1,0:T(8,128)(2,1)}, u32[]{:S(2)}, u32[]{:S(2)}) async-start(bf16[8,2,16,16,256]{4,3,2,1,0:T(8,128)(2,1)} %get-tuple-element.281), calls=%async_computation.22 | async-start | bytes 4194304 | tf_op jit(solution)/shard_map/all_to_all | solution.py:1917
  784.3 65.3 %all-gather.14.cloned.1.call-start = ((), (), s32[]{:S(2)}) async-start(), calls=%async_computation.32 | async-start | bytes 1622016 | tf_op jit(solution)/shard_map/all_gather | solution.py:2344
  811.3 24.8 %all-to-all-start.23 = ((bf16[8,16,16,256]{3,2,1,0:T(8,128)(2,1)}), bf16[8,16,16,256]{3,2,1,0:T(8,128)(2,1)S(1)}, u32[]{:S(2)}, u32[]{:S(2)}) async-start(bf16[8,16,16,256]{3,2,1,0:T(8,128)(2,1)} %bitcast.86), calls=%async_computation.24 | async-start | bytes 2097152 | tf_op jit(solution)/shard_map/all_to_all | solution.py:1917
  836.1 13.3 %copy-start.13 = (bf16[8,16,16,256]{3,2,1,0:T(8,128)(2,1)}, bf16[8,16,16,256]{3,2,1,0:T(8,128)(2,1)S(1)}, u32[]{:S(2)}) copy-start(bf16[8,16,16,256]{3,2,1,0:T(8,128)(2,1)S(1)} %all-to-all-done.23.refs_0_) | copy-start | bytes 3145732
  836.2 19.7 %all-to-all-start.24 = ((bf16[8,16,16,256]{3,2,1,0:T(8,128)(2,1)}), bf16[8,16,16,256]{3,2,1,0:T(8,128)(2,1)}, u32[]{:S(2)}, u32[]{:S(2)}) async-start(bf16[8,16,16,256]{3,2,1,0:T(8,128)(2,1)} %bitcast.85), calls=%async_computation.25 | async-start | bytes 2097152 | tf_op jit(solution)/shard_map/all_to_all | solution.py:1917
  916.7 31.4 %all-to-all-start.26 = ((bf16[8,21,24,128]{3,2,1,0:T(8,128)(2,1)}), bf16[8,21,24,128]{3,2,1,0:T(8,128)(2,1)S(1)}, u32[]{:S(2)}, u32[]{:S(2)}) async-start(bf16[8,21,24,128]{3,2,1,0:T(8,128)(2,1)} %pair_gradient.1), calls=%async_computation.27 | async-start | bytes 2064384 | tf_op jit(solution)/shard_map/all_to_all | solution.py:1917
  958.4 52.6 %all-to-all-start.28 = ((bf16[4,8,256,128]{3,2,1,0:T(8,128)(2,1)}), bf16[4,8,256,128]{3,2,1,0:T(8,128)(2,1)}, u32[]{:S(2)}, u32[]{:S(2)}) async-start(bf16[4,8,256,128]{3,2,1,0:T(8,128)(2,1)} %bitcast.79), calls=%async_computation.29 | async-start | bytes 4194304 | tf_op jit(solution)/shard_map/all_to_all | solution.py:1917
  962.8 1.9 copy-start.18
  994.3 20.3 %copy-start.33 = (f32[8,128]{1,0:T(8,128)S(1)}, f32[8,128]{1,0:T(8,128)}, u32[]{:S(2)}) copy-start(f32[8,128]{1,0:T(8,128)} %get-tuple-element.333) | copy-start | bytes 12292
  1010.9 27.9 %all-to-all-start.29 = ((bf16[4,8,256,128]{3,2,1,0:T(8,128)(2,1)}), bf16[4,8,256,128]{3,2,1,0:T(8,128)(2,1)S(1)}, u32[]{:S(2)}, u32[]{:S(2)}) async-start(bf16[4,8,256,128]{3,2,1,0:T(8,128)(2,1)} %all-to-all-done.28), calls=%async_computation.30 | async-start | bytes 4194304 | tf_op jit(solution)/shard_map/all_to_all | solution.py:1917
  (1 other events, 0.5 us)
Sparse Core Ops, SparseCore 0:
  22.0 25.2 all-gather.15
  91.1 54.5 all-gather.17
  173.5 62.7 all-gather.19
  630.4 119.3 reduce-scatter.1
  788.9 60.6 all-gather.13

commit v7 on v6

--- a/solution.py
+++ b/solution.py
@@ -629,7 +629,7 @@
     )
 
 
-GROUP = 4
+GROUP = 8
 LAG = 4
 
 
@@ -638,7 +638,7 @@
         body(index * GROUP)
         return carry
 
-    lax.fori_loop(0, count // GROUP, step, 0)
+    lax.fori_loop(0, count // GROUP, step, 0, unroll=2)
 
 
 def each_channel(count, body):
@@ -957,26 +957,17 @@
     bias_out[...] = scratch[: bias_out.shape[0]].astype(BF16)
 
 
-def flipped_bias_kernel(source, cols, bias_t, bias_out, scratch):
-    rows = source[0].shape[1]
-
-    def body(row):
-        unit, inverse = standardize(join(read_flipped, source, row))
-        lowered = (unit * column(cols, 0) + column(cols, 1)).astype(BF16)
-        put_inner(scratch, row, mm(bias_t[...], lowered))
-
-    each_group(rows, body)
-    bias_out[...] = scratch[: bias_out.shape[0]].astype(BF16)
-
-
-def fill_bias(alive, bias_in, table):
+def fill_bias(alive, bias_in, table, turned):
     @pl.when(pl.program_id(0) == 0)
     def _():
         length = table.shape[1]
-        penalty = (alive[0:1] - 1.0) * (MASKED * LOG2E)
+        penalty = (alive[...] - 1.0) * (MASKED * LOG2E)
         for head in range(table.shape[0]):
-            values = bias_in[:, head].reshape(length, length).astype(F32)
-            table[head] = (values * LOG2E + penalty).T
+            values = bias_in[:, head].reshape(length, length).astype(F32) * LOG2E
+            if turned:
+                table[head] = values + penalty.T[:, 0:1]
+            else:
+                table[head] = (values + penalty[0:1]).T
 
 
 def attention_row(state, cols, proj_t):
@@ -1052,9 +1043,10 @@
 
 
 def starting_kernel(
-    alive, source, bias_in, cols, proj_t, output_t, out, totals, mixed, table, scratch
+    alive, source, bias_in, cols, proj_t, output_t, next_cols, bias_t, out, totals, mixed, bias_out,
+    table, scratch, bias_scratch,
 ):
-    fill_bias(alive, bias_in, table)
+    fill_bias(alive, bias_in, table, False)
     rows = source.shape[0]
 
     def body(row):
@@ -1062,13 +1054,17 @@
             join(read_plain, source, row), row, cols, proj_t, output_t, table, totals, mixed
         )
         put_turned(scratch, row, state)
+        unit, inverse = standardize(state)
+        lowered = (unit * column(next_cols, 0) + column(next_cols, 1)).astype(BF16)
+        put_inner(bias_scratch, row, mm(bias_t[...], lowered))
 
     each_group(rows, body)
     store_flipped(out, scratch)
+    bias_out[...] = bias_scratch[: bias_out.shape[0]].astype(BF16)
 
 
 def ending_kernel(alive, source, bias_in, cols, proj_t, output_t, out, totals, mixed, table):
-    fill_bias(alive, bias_in, table)
+    fill_bias(alive, bias_in, table, True)
     rows = source[0].shape[1]
 
     def body(row):
@@ -1162,10 +1158,10 @@
 
 
 def attention_back_kernel(
-    read, read_grad, alive, source, grad_in, bias_in, totals, mixed_in, cols, proj_t, proj, output,
+    turned, read, read_grad, alive, source, grad_in, bias_in, totals, mixed_in, cols, proj_t, proj, output,
     grad_out, bias_out, proj_grad, output_grad, table, grad_table,
 ):
-    fill_bias(alive, bias_in, table)
+    fill_bias(alive, bias_in, table, turned)
     zero_first(grad_table)
     rows = grad_out.shape[0]
 
@@ -2057,23 +2053,22 @@
         ],
         [(state_shape, F32, 0), ((TA_HEADS, rows, length), BF16, 1)], [tri_scratch, head_scratch],
     )
+    (bias,) = meet(7, bias)
     bias_one = lax.all_gather(bias, group, axis=0, tiled=False)
-    flipped, totals_one, mixed_one = run_rows(
+    flipped, totals_one, mixed_one, bias = run_rows(
         starting_kernel, "starting_attention", steps,
         [
             (alive, None), (state_two, 0), (bias_one, None), (cols(STARTING), None),
-            (turned((STARTING, QKVG)), None), (turned((STARTING, OUTPUT)), None),
+            (turned((STARTING, QKVG)), None), (turned((STARTING, OUTPUT)), None), (cols(ENDING), None),
+            (weights[(ENDING, BIAS_T)], None),
         ],
-        [(flip_shape, BF16, 2)] + attend_saves, [table, flip_scratch], 21,
+        [(flip_shape, BF16, 2)] + attend_saves + [((TA_HEADS, rows, length), BF16, 1)],
+        [table, flip_scratch, head_scratch], 21,
     )
     state_three = Both([send(flipped, group)])
+    bias_two = lax.all_gather(bias, group, axis=0, tiled=False)
+    cotangent, bias_two = after(cotangent, bias_two)
     cotangent = send(cotangent.reshape((parts, cores) + flip_shape[1:]), "z").reshape(flip_shape)
-    (bias,) = run_rows(
-        flipped_bias_kernel, "ending_bias", steps,
-        [(state_three, 1), (cols(ENDING), None), (weights[(ENDING, BIAS_T)], None)],
-        [((TA_HEADS, rows, length), BF16, 1)], [head_scratch],
-    )
-    bias_two = lax.all_gather(bias, group, axis=0, tiled=False)
     state_four, totals_two, mixed_two = run_rows(
         ending_kernel, "ending_attention", steps,
         [
@@ -2114,7 +2109,7 @@
 
     def attention_back(prefix, read, read_grad, source, source_axis, grad, grad_axis, bias, totals, mixed):
         lowered_grad, bias_grad, grads[(prefix, QKVG)], grads[(prefix, OUTPUT)] = run_rows(
-            functools.partial(attention_back_kernel, read, read_grad),
+            functools.partial(attention_back_kernel, prefix == ENDING, read, read_grad),
             "attention_back", steps,
             [
                 (alive, None), (source, source_axis), (grad, grad_axis), (bias, None), (totals, 0),
@@ -2132,6 +2127,7 @@
     lowered_grad, bias_grad = attention_back(
         ENDING, read_flipped, read_plain, state_three, 1, grad_four, 0, bias_two, totals_two, mixed_two
     )
+    (bias_grad,) = meet(8, bias_grad)
     flipped, bias_w_grad, vecs = run_rows(
         ending_end_kernel, "ending_attention_end", steps,
         [
@@ -2298,6 +2294,10 @@
             others = [held["projected"][1]]
         elif number == 3:
             others = [reduced[3]]
+        elif number == 7:
+            others = [held["projected"][2]]
+        elif number == 8:
+            others = [single_grads[(ATTEND, QKVG)]]
         elif number == 4:
             values, reduced[2] = after(*values, reduced[2])
             return [values]

time: 1060 us -> 1060 us (level)
  Pallas kernels: 441 us -> 412 us
  waiting for transfers between devices: 167 us -> 194 us
    all_to_all x9 -> x7, blocking collectives: 223 us -> 178 us  [swap(): lax.all_to_all(values, group, split_axis=0, concat_axis=0, tiled=True)]
    pallas_call x21 -> x20, Pallas kernels: 342 us -> 314 us  [run_rows(): pl.pallas_call(run, grid=(grid,), in_specs=in_specs, out_specs=out_specs,...]
    all_to_all x21 -> x23, waiting for transfers between devices: 167 us -> 192 us  [swap(): lax.all_to_all(values, group, split_axis=0, concat_axis=0, tiled=True)]
    all_gather x1, blocking collectives: 11.2 us -> 31.7 us  [pair_path(): bias_two = lax.all_gather(bias, group, axis=0, tiled=False)]
    all_gather x1, blocking collectives: 12.2 us -> 31.7 us  [pair_path(): bias_one = lax.all_gather(bias, group, axis=0, tiled=False)]
    all_to_all x21 -> x23, starting transfers between devices: 88.4 us -> 96.6 us  [swap(): lax.all_to_all(values, group, split_axis=0, concat_axis=0, tiled=True)]
  transfers between devices with their start and end apart: 26 -> 28, of which waited for: 15 -> 16; matrix products, arithmetic and copies ran while one was open for 3% -> 3% of each run, Pallas kernels for 39% -> 36%
where the time goes in v7:
time: 1060 us; the launch traced here: 1050 us
  Pallas kernels  412 us (39%)
  blocking collectives  287 us (27%)
  waiting for transfers between devices  194 us (18%)
  starting transfers between devices  96.7 us (9%)
  local copies, waits for them, and re-layouts  23.6 us (2%)
  other arithmetic  18 us (2%)
  between operations  17.3 us (2%)
    pallas_call x20, Pallas kernels, run_rows(): pl.pallas_call(run, grid=(grid,), in_specs=in_specs, out_specs=out_specs,...  314 us
    all_to_all x23, waiting for transfers between devices, swap(): lax.all_to_all(values, group, split_axis=0, concat_axis=0, tiled=True)  192 us
    all_to_all x7, blocking collectives, swap(): lax.all_to_all(values, group, split_axis=0, concat_axis=0, tiled=True)  178 us
    pallas_call x8, Pallas kernels, whole_call(): pl.pallas_call(kernel, in_specs=[spec(axis) for array, axis in ins], out_...  98.2 us
    all_to_all x23, starting transfers between devices, swap(): lax.all_to_all(values, group, split_axis=0, concat_axis=0, tiled=True)  96.6 us
    all_gather x1, blocking collectives, pair_path(): bias_two = lax.all_gather(bias, group, axis=0, tiled=False)  31.7 us
    all_gather x1, blocking collectives, pair_path(): bias_one = lax.all_gather(bias, group, axis=0, tiled=False)  31.7 us
  transfers between devices with their start and end apart: 28, of which 16 were waited for; matrix products, arithmetic and copies ran while one was open for 3% of the time, Pallas kernels for 36%

profile of v7, /device:TPU:0, one launch (start us, length us, event | category | flops | bytes accessed | tf_op | source)
XLA Modules:
  0.0 1051.2 jit_solution(7559044221618096243)
XLA Ops:
  7.2 5.3 all-to-all-start
  14.3 5.9 parameter_runs.1
  21.9 16.3 %all-to-all-done = bf16[4,8,256,128]{3,2,1,0:T(8,128)(2,1)} async-done(((bf16[4,8,256,128]{3,2,1,0:T(8,128)(2,1)}), bf16[4,8,256,128]{3,2,1,0:T(8,128)(2,1)}, u32[]{:S(2)}, u32[]{:S(2)}) %all-to-all-start) | async-done | bytes 2097184 | tf_op jit(solution)/shard_map/all_to_all | solution.py:1913
  38.2 5.1 all-to-all-start.1
  45.3 8.9 all-reduce.2
  55.7 8.0 pair_weights.1
  63.7 27.3 %all-to-all-done.1 = bf16[4,8,256,128]{3,2,1,0:T(8,128)(2,1)S(1)} async-done(((bf16[4,8,256,128]{3,2,1,0:T(8,128)(2,1)}), bf16[4,8,256,128]{3,2,1,0:T(8,128)(2,1)S(1)}, u32[]{:S(2)}, u32[]{:S(2)}) %all-to-all-start.1) | async-done | bytes 2097184 | tf_op jit(solution)/shard_map/all_to_all | solution.py:1913
  92.9 10.2 outgoing_in.1
  103.1 53.5 %all_to_all.150.refs_0_.refs_2_ = bf16[8,2,16,32,256]{4,3,2,1,0:T(8,128)(2,1)} all-to-all(bf16[8,2,16,32,256]{4,3,2,1,0:T(8,128)(2,1)} %outgoing_in.1), channel_id=1, replica_groups=mesh['crop'=4,'z'=4,'core'=2] {'crop','core'}, dimensions={0} | all-to-all | bytes 8388608 | tf_op jit(solution)/shard_map/all_to_all | solution.py:1913
  156.6 6.2 outgoing_product.1
  167.9 14.0 %all-to-all-done.3 = bf16[8,16,16,256]{3,2,1,0:T(8,128)(2,1)S(1)} async-done(((bf16[8,16,16,256]{3,2,1,0:T(8,128)(2,1)}), bf16[8,16,16,256]{3,2,1,0:T(8,128)(2,1)S(1)}, u32[]{:S(2)}, u32[]{:S(2)}) %all-to-all-start.3) | async-done | bytes 1048608 | tf_op jit(solution)/shard_map/all_to_all | solution.py:1913
  185.9 11.1 %outgoing_out_incoming_in.2 = (f32[32,128,256]{2,1,0:T(8,128)}, bf16[8,2,16,16,256]{4,3,2,1,0:T(8,128)(2,1)}) custom-call(s32[16]{0:T(128)} %get-tuple-element.359.refs_0_, f32[8,256]{1,0:T(8,128)} %broadcast_in_dim.29.refs_1_.refs_0_.alive, bf16[32,256,128]{2,1,0:T(8,128)(2,1)} %bitcast.71, bf16[128,16,256]{2,1,0:T(8,128)(2,1)} %bitcast.82, ...), custom_call_target="tpu_custom_call" | custom-call | flops 11000000512 | bytes 33000000 | tf_op jit(solution)/shard_map/outgoing_out_incoming_in/pallas_call | solution.py:762
  197.1 5.6 all-to-all-done.4
  207.4 11.1 %outgoing_out_incoming_in.3 = (f32[32,128,256]{2,1,0:T(8,128)}, bf16[8,2,16,16,256]{4,3,2,1,0:T(8,128)(2,1)}) custom-call(s32[16]{0:T(128)} %get-tuple-element.360.refs_0_, f32[8,256]{1,0:T(8,128)} %broadcast_in_dim.29.refs_1_.refs_0_.alive, bf16[32,256,128]{2,1,0:T(8,128)(2,1)} %bitcast.72, ...), custom_call_target="tpu_custom_call", output_to_operand_aliasing={{0}: (9, {})} | custom-call | flops 11000000512 | bytes 33000000 | tf_op jit(solution)/shard_map/outgoing_out_incoming_in/pallas_call | solution.py:762
  218.5 18.2 %all-to-all-done.5.refs_0_.refs_2_ = bf16[8,2,16,16,256]{4,3,2,1,0:T(8,128)(2,1)S(1)} async-done(((bf16[8,2,16,16,256]{4,3,2,1,0:T(8,128)(2,1)}), bf16[8,2,16,16,256]{4,3,2,1,0:T(8,128)(2,1)S(1)}, u32[]{:S(2)}, u32[]{:S(2)}) %all-to-all-start.5) | async-done | bytes 2097184 | tf_op jit(solution)/shard_map/all_to_all | solution.py:1913
  238.0 4.3 all-to-all-start.6
  244.0 28.3 %single_weights.1 = (bf16[384,1536]{1,0:T(8,128)(2,1)}, bf16[384,384]{1,0:T(8,128)(2,1)}, bf16[384,3072]{1,0:T(8,128)(2,1)}, bf16[1536,384]{1,0:T(8,128)(2,1)}, ...) custom-call(bf16[8,105,24,128]{3,2,1,0:T(8,128)(2,1)} %bitcast.99), custom_call_target="tpu_custom_call" | custom-call | flops 8000000000 | bytes 24000000 | tf_op jit(solution)/shard_map/single_weights/pallas_call | solution.py:1692
  272.4 6.3 incoming_product.1
  278.6 4.5 all-to-all-start.7
  288.9 20.9 %all-to-all-done.7 = bf16[8,16,32,256]{3,2,1,0:T(8,128)(2,1)} async-done(((bf16[8,16,32,256]{3,2,1,0:T(8,128)(2,1)}), bf16[8,16,32,256]{3,2,1,0:T(8,128)(2,1)}, u32[]{:S(2)}, u32[]{:S(2)}) %all-to-all-start.7) | async-done | bytes 2097184 | tf_op jit(solution)/shard_map/all_to_all | solution.py:1913
  314.2 12.1 %incoming_out_starting_bias.1 = (f32[32,128,256]{2,1,0:T(8,128)}, bf16[4,32,256]{2,1,0:T(8,128)(2,1)}) custom-call(f32[32,128,256]{2,1,0:T(8,128)} %get-tuple-element.193.refs_0_.refs_6_.refs_2_, bf16[128,32,256]{2,1,0:T(8,128)(2,1)} %bitcast.14.refs_1_.refs_7_, f32[128,8]{1,0:T(8,128)} %get-tuple-element.190.refs_7_.refs_2_.refs_8_.refs_6_, ...), custom_call_target="tpu_custom_call" | custom-call | flops 15000000512 | bytes 45000000 | tf_op jit(solution)/shard_map/incoming_out_starting_bias/pallas_call | solution.py:762
  331.5 31.7 %all-gather.4 = bf16[32,32,256]{2,1,0:T(8,128)(2,1)} all-gather(bf16[4,32,256]{2,1,0:T(8,128)(2,1)S(1)} %copy-done.22), channel_id=7, replica_groups=mesh['crop'=4,'z'=4,'core'=2] {'crop','core'}, dimensions={0}, use_global_device_ids=true | all-gather | bytes 589824 | tf_op jit(solution)/shard_map/all_gather | solution.py:2057
  363.2 20.1 %starting_attention.1 = (bf16[8,32,32,128]{3,2,1,0:T(8,128)(2,1)}, f32[32,4,256]{2,1,0:T(4,128)}, bf16[32,128,256]{2,1,0:T(8,128)(2,1)}, bf16[4,32,256]{2,1,0:T(8,128)(2,1)}) custom-call(f32[8,256]{1,0:T(8,128)} %broadcast_in_dim.29.refs_1_.refs_0_.alive, f32[32,128,256]{2,1,0:T(8,128)} %get-tuple-element.209.refs_1_.refs_0_, ...), custom_call_target="tpu_custom_call" | custom-call | flops 20999999488 | bytes 63000000 | tf_op jit(solution)/shard_map/starting_attention/pallas_call | solution.py:762
  387.0 31.7 %all-gather.5 = bf16[32,32,256]{2,1,0:T(8,128)(2,1)} all-gather(bf16[4,32,256]{2,1,0:T(8,128)(2,1)S(1)} %copy-done.21), channel_id=8, replica_groups=mesh['crop'=4,'z'=4,'core'=2] {'crop','core'}, dimensions={0}, use_global_device_ids=true | all-gather | bytes 589824 | tf_op jit(solution)/shard_map/all_gather | solution.py:2069
  420.1 4.8 all-to-all-start.11
  424.9 16.6 %ending_attention.1 = (f32[32,128,256]{2,1,0:T(8,128)}, f32[32,4,256]{2,1,0:T(4,128)}, bf16[32,128,256]{2,1,0:T(8,128)(2,1)}) custom-call(f32[8,256]{1,0:T(8,128)} %broadcast_in_dim.29.refs_1_.refs_0_.alive, bf16[8,32,32,128]{3,2,1,0:T(8,128)(2,1)} %copy-done.7, bf16[8,4,32,256]{3,2,1,0:T(8,128)(2,1)} %bitcast.92, ...), custom_call_target="tpu_custom_call" | custom-call | flops 15000000512 | bytes 45000000 | tf_op jit(solution)/shard_map/ending_attention/pallas_call | solution.py:762
  441.5 14.7 %pair_transition.1 = (f32[32,128,256]{2,1,0:T(8,128)}, bf16[256,32,128]{2,1,0:T(8,128)(2,1)}, bf16[8,32,512]{2,1,0:T(8,128)(2,1)}) custom-call(f32[32,128,256]{2,1,0:T(8,128)} %get-tuple-element.224.refs_0_, f32[128,8]{1,0:T(8,128)} %get-tuple-element.225.refs_1_.refs_4_, bf16[1024,128]{1,0:T(8,128)(2,1)} %get-tuple-element.226.refs_2_.refs_5_, ...), custom_call_target="tpu_custom_call" | custom-call | flops 15000000512 | bytes 45000000 | tf_op jit(solution)/shard_map/pair_transition/pallas_call | solution.py:762
  456.2 17.8 %all-to-all-done.11 = bf16[4,2,32,32,128]{4,3,2,1,0:T(8,128)(2,1)} async-done(((bf16[4,2,32,32,128]{4,3,2,1,0:T(8,128)(2,1)}), bf16[4,2,32,32,128]{4,3,2,1,0:T(8,128)(2,1)}, u32[]{:S(2)}, u32[]{:S(2)}) %all-to-all-start.11) | async-done | bytes 2097184 | tf_op jit(solution)/shard_map/all_to_all | solution.py:1913
  474.0 11.0 %all_to_all.151.bias = bf16[8,32,512]{2,1,0:T(8,128)(2,1)} all-to-all(bf16[8,32,512]{2,1,0:T(8,128)(2,1)} %get-tuple-element.234), channel_id=1, replica_groups=mesh['crop'=4,'z'=4,'core'=2] {'crop','core'}, dimensions={0} | all-to-all | bytes 524288 | tf_op jit(solution)/shard_map/all_to_all | solution.py:1913
  484.9 10.0 single_path.1
  494.9 15.3 %all_to_all.152.refs_3_ = bf16[8,32,1280]{2,1,0:T(8,128)(2,1)} all-to-all(bf16[8,32,1280]{2,1,0:T(8,128)(2,1)} %get-tuple-element.238), channel_id=1, replica_groups=mesh['crop'=4,'z'=4,'core'=2] {'crop','core'}, dimensions={0} | all-to-all | bytes 1310720 | tf_op jit(solution)/shard_map/all_to_all | solution.py:1913
  514.1 28.8 %pair_transition_back.1 = (f32[32,128,256]{2,1,0:T(8,128)}, f32[128,1024]{1,0:T(8,128)}, f32[512,128]{1,0:T(8,128)}, f32[128,16]{1,0:T(8,128)}, f32[8,128]{1,0:T(8,128)}) custom-call(f32[32,128,256]{2,1,0:T(8,128)} %get-tuple-element.224.refs_0_, f32[32,128,256]{2,1,0:T(8,128)} %get-tuple-element.240.refs_1_, bf16[8,32,32,128]{3,2,1,0:T(8,128)(2,1)} %bitcast.24.refs_2_, ...), custom_call_target="tpu_custom_call" | custom-call | flops 30000001024 | bytes 90000000 | tf_op jit(solution)/shard_map/pair_transition_back/pallas_call | solution.py:762
  543.0 31.5 %attention_back.2 = (bf16[32,128,256]{2,1,0:T(8,128)(2,1)}, bf16[8,4,32,256]{3,2,1,0:T(8,128)(2,1)}, f32[128,512]{1,0:T(8,128)}, f32[128,128]{1,0:T(8,128)}) custom-call(f32[8,256]{1,0:T(8,128)} %broadcast_in_dim.29.refs_1_.refs_0_.alive, bf16[8,32,32,128]{3,2,1,0:T(8,128)(2,1)} %copy-done.7, f32[32,128,256]{2,1,0:T(8,128)} %get-tuple-element.244.refs_2_.refs_1_, ...), custom_call_target="tpu_custom_call" | custom-call | flops 33999998976 | bytes 102000000 | tf_op jit(solution)/shard_map/attention_back/pallas_call | solution.py:762
  580.2 7.5 all-to-all-done.15.refs_3_
  588.5 10.7 %ending_attention_end.1 = (bf16[8,32,32,128]{3,2,1,0:T(8,128)(2,1)}, f32[128,8]{1,0:T(8,128)}, f32[8,128]{1,0:T(8,128)}) custom-call(bf16[8,32,32,128]{3,2,1,0:T(8,128)(2,1)} %copy-done.7, f32[32,128,256]{2,1,0:T(8,128)} %get-tuple-element.244.refs_2_.refs_1_, bf16[32,128,256]{2,1,0:T(8,128)(2,1)} %get-tuple-element.249.refs_2_, ...), custom_call_target="tpu_custom_call" | custom-call | flops 15000000512 | bytes 45000000 | tf_op jit(solution)/shard_map/ending_attention_end/pallas_call | solution.py:762
  605.0 30.3 %single_gradient.1 = bf16[8,104,24,128]{3,2,1,0:T(8,128)(2,1)} custom-call(f32[384,1536]{1,0:T(8,128)} %fusion.2.refs_0_, f32[384,384]{1,0:T(8,128)} %get-tuple-element.261.refs_1_, f32[384,3072]{1,0:T(8,128)} %get-tuple-element.262.refs_2_, f32[1536,384]{1,0:T(8,128)} %get-tuple-element.263.refs_3_, f32[128,16]{1,0:T(8,128)} %get-tuple-element.264.refs_4_, ...), custom_call_target="tpu_custom_call" | custom-call | flops 8000000000 | bytes 24000000 | tf_op jit(solution)/shard_map/single_gradient/pallas_call | solution.py:1692
  640.7 32.0 %attention_back.3 = (bf16[32,128,256]{2,1,0:T(8,128)(2,1)}, bf16[8,4,32,256]{3,2,1,0:T(8,128)(2,1)}, f32[128,512]{1,0:T(8,128)}, f32[128,128]{1,0:T(8,128)}) custom-call(f32[8,256]{1,0:T(8,128)} %broadcast_in_dim.29.refs_1_.refs_0_.alive, f32[32,128,256]{2,1,0:T(8,128)} %get-tuple-element.209.refs_1_.refs_0_, bf16[8,32,32,128]{3,2,1,0:T(8,128)(2,1)} %copy-done.8, ...), custom_call_target="tpu_custom_call" | custom-call | flops 33999998976 | bytes 102000000 | tf_op jit(solution)/shard_map/attention_back/pallas_call | solution.py:762
  672.8 14.1 %all_to_all.153.refs_3_ = bf16[8,4,32,256]{3,2,1,0:T(8,128)(2,1)} all-to-all(bf16[8,4,32,256]{3,2,1,0:T(8,128)(2,1)} %get-tuple-element.274), channel_id=1, replica_groups=mesh['crop'=4,'z'=4,'core'=2] {'crop','core'}, dimensions={0} | all-to-all | bytes 1048576 | tf_op jit(solution)/shard_map/all_to_all | solution.py:1913
  686.8 15.3 %starting_end_incoming_out_back.2 = (f32[32,128,256]{2,1,0:T(8,128)}, bf16[128,16,256]{2,1,0:T(8,128)(2,1)}, bf16[32,128,256]{2,1,0:T(8,128)(2,1)}, f32[128,8]{1...) custom-call(f32[32,128,256]{2,1,0:T(8,128)} %get-tuple-element.209.refs_1_.refs_0_, ...), custom_call_target="tpu_custom_call" | custom-call | flops 12999999488 | bytes 39000000 | tf_op jit(solution)/shard_map/starting_end_incoming_out_back/pallas_call | solution.py:762
  705.8 15.3 %starting_end_incoming_out_back.3 = (f32[32,128,256]{2,1,0:T(8,128)}, bf16[128,16,256]{2,1,0:T(8,128)(2,1)}, bf16[32,128,256]{2,1,0:T(8,128)(2,1)}, f32[128,8]{1...) custom-call(f32[32,128,256]{2,1,0:T(8,128)} %get-tuple-element.209.r, ...), custom_call_target="tpu_custom_call", output_to_operand_aliasing={{0}: (13, {}), {2}: (14, {}), {3}: (15, {}), {4}: (16, {}),... | custom-call | flops 12999999488 | bytes 39000000 | tf_op jit(solution)/shard_map/starting_end_incoming_out_back/pallas_call | solution.py:762
  723.6 20.7 %all_to_all.154.refs_1_ = bf16[8,16,16,256]{3,2,1,0:T(8,128)(2,1)} all-to-all(bf16[8,16,16,256]{3,2,1,0:T(8,128)(2,1)} %bitcast.87), channel_id=1, replica_groups=mesh['crop'=4,'z'=4,'core'=2] {'crop','core'}, dimensions={0} | all-to-all | bytes 2097152 | tf_op jit(solution)/shard_map/all_to_all | solution.py:1913
  744.3 7.4 incoming_product_back.1
  751.7 4.5 all-to-all-start.21
  756.5 26.3 %all-to-all-done.21.refs_3_ = bf16[8,2,16,16,256]{4,3,2,1,0:T(8,128)(2,1)} async-done(((bf16[8,2,16,16,256]{4,3,2,1,0:T(8,128)(2,1)}), bf16[8,2,16,16,256]{4,3,2,1,0:T(8,128)(2,1)}, u32[]{:S(2)}, u32[]{:S(2)}) %all-to-all-start.21) | async-done | bytes 2097184 | tf_op jit(solution)/shard_map/all_to_all | solution.py:1913
  782.8 4.4 all-to-all-start.22
  787.9 20.0 %incoming_in_outgoing_out_back.2 = (f32[32,128,256]{2,1,0:T(8,128)}, bf16[128,16,256]{2,1,0:T(8,128)(2,1)}, bf16[32,128,256]{2,1,0:T(8,128)(2,1)}, f32[128,512]{...) custom-call(s32[16]{0:T(128)} %get-tuple-element.359.refs_0_, ...), custom_call_target="tpu_custom_call" | custom-call | flops 18499999744 | bytes 55500000 | tf_op jit(solution)/shard_map/incoming_in_outgoing_out_back/pallas_call | solution.py:762
  807.9 6.3 all-to-all-done.22.refs_3_
  818.2 19.9 %incoming_in_outgoing_out_back.3 = (f32[32,128,256]{2,1,0:T(8,128)}, bf16[128,16,256]{2,1,0:T(8,128)(2,1)}, bf16[32,128,256]{2,1,0:T(8,128)(2,1)}, f32[128,512]{...) custom-call(s32[16]{0:T(128)} %get-tuple-element.360.refs_0_, ...), custom_call_target="tpu_custom_call", output_to_operand_aliasing={{0}: (16, {}), {2}: (17, {}), {3}: (18, {}), {4}: (19, {}),... | custom-call | flops 18499999744 | bytes 55500000 | tf_op jit(solution)/shard_map/incoming_in_outgoing_out_back/pallas_call | solution.py:762
  838.0 4.4 all-to-all-start.24
  844.0 7.5 pair_gradient.1
  852.7 5.3 all-to-all-done.24.refs_1_
  857.9 7.3 outgoing_product_back.1
  865.2 53.5 %all_to_all.155.refs_3_ = bf16[8,2,16,32,256]{4,3,2,1,0:T(8,128)(2,1)} all-to-all(bf16[8,2,16,32,256]{4,3,2,1,0:T(8,128)(2,1)} %outgoing_product_back.1), channel_id=1, replica_groups=mesh['crop'=4,'z'=4,'core'=2] {'crop','core'}, dimensions={0} | all-to-all | bytes 8388608 | tf_op jit(solution)/shard_map/all_to_all | solution.py:1913
  918.8 5.0 all-to-all-start.26
  923.8 17.7 %outgoing_in_back.1 = (bf16[32,256,128]{2,1,0:T(8,128)(2,1)}, f32[128,512]{1,0:T(8,128)}, f32[8,128]{1,0:T(8,128)}) custom-call(s32[32]{0:T(128)} %dynamic-slice_convert_fusion.refs_0_, f32[8,256]{1,0:T(8,128)} %broadcast_in_dim.29.refs_1_.refs_0_.alive, bf16[32,256,128]{2,1,0:T(8,128)(2,1)} %bitcast.75, bf16[8,2,16,32,256]{4,3,2,1,0:T(8,128)(2,1)} %all_to_all.155.refs_3_, ...), custom_call_target="tpu_custom_call" | custom-call | flops 20000000000 | bytes 60000000 | tf_op jit(solution)/shard_map/outgoing_in_back/pallas_call | solution.py:762
  943.8 6.3 all-to-all-done.26
  950.0 10.3 all_to_all.156
  960.3 4.5 all-to-all-start.28
  966.7 10.3 all-gather.7
  978.7 11.6 %all-gather.6 = bf16[96,24,128]{2,1,0:T(8,128)(2,1)} all-gather(bf16[24,24,128]{2,1,0:T(8,128)(2,1)S(1)} %pad_maximum_fusion), channel_id=9, replica_groups=mesh['crop'=4,'z'=4,'core'=2] {'crop'}, dimensions={0}, use_global_device_ids=true | all-gather | bytes 737280 | tf_op jit(solution)/shard_map/all_gather | solution.py:2385
  990.3 5.9 gradient_share.1
  996.2 16.7 %all-to-all-done.28 = bf16[4,8,256,128]{3,2,1,0:T(8,128)(2,1)} async-done(((bf16[4,8,256,128]{3,2,1,0:T(8,128)(2,1)}), bf16[4,8,256,128]{3,2,1,0:T(8,128)(2,1)}, u32[]{:S(2)}, u32[]{:S(2)}) %all-to-all-start.28) | async-done | bytes 2097184 | tf_op jit(solution)/shard_map/all_to_all | solution.py:1913
  1016.5 14.0 %all-gather.8 = f32[64,128]{1,0:T(8,128)S(1)} all-gather(f32[8,128]{1,0:T(8,128)S(1)} %copy-done.37), channel_id=11, replica_groups=mesh['crop'=4,'z'=4,'core'=2] {'z','core'}, dimensions={0}, use_global_device_ids=true | all-gather | bytes 36864 | tf_op jit(solution)/shard_map/all_gather | solution.py:2394
  1031.9 7.5 multiply_subtract_fusion
  (171 shorter events, 94.5 us)
Async XLA Ops:
  7.2 5.3 copy-start.1
  7.2 31.0 %all-to-all-start = ((bf16[4,8,256,128]{3,2,1,0:T(8,128)(2,1)}), bf16[4,8,256,128]{3,2,1,0:T(8,128)(2,1)}, u32[]{:S(2)}, u32[]{:S(2)}) async-start(bf16[4,8,256,128]{3,2,1,0:T(8,128)(2,1)} %bitcast.68), calls=%async_computation | async-start | bytes 4194304 | tf_op jit(solution)/shard_map/all_to_all | solution.py:1913
  12.5 43.2 %all-gather.16.cloned.1.call-start = ((), (), s32[]{:S(2)}) async-start(), calls=%async_computation.33 | async-start | bytes 1327104 | tf_op jit(solution)/shard_map/all_gather | solution.py:2264
  21.8 22.1 %copy-start.42 = (u32[32]{0:T(128)S(1)}, u32[32]{0:T(128)}, u32[]{:S(2)}) copy-start(u32[32]{0:T(128)} %constant.107) | copy-start | bytes 388
  21.8 32.3 %copy-start.16 = (bf16[128,24,128]{2,1,0:T(8,128)(2,1)S(1)}, bf16[128,24,128]{2,1,0:T(8,128)(2,1)}, u32[]{:S(2)}) copy-start(bf16[128,24,128]{2,1,0:T(8,128)(2,1)} %parameter_runs.1) | copy-start | bytes 2359300
  38.2 52.7 %all-to-all-start.1 = ((bf16[4,8,256,128]{3,2,1,0:T(8,128)(2,1)}), bf16[4,8,256,128]{3,2,1,0:T(8,128)(2,1)S(1)}, u32[]{:S(2)}, u32[]{:S(2)}) async-start(bf16[4,8,256,128]{3,2,1,0:T(8,128)(2,1)} %all-to-all-done), calls=%async_computation.1 | async-start | bytes 4194304 | tf_op jit(solution)/shard_map/all_to_all | solution.py:1913
  43.3 164.1 %all-gather.18.cloned.1.call-start = ((), (), s32[]{:S(2)}) async-start(), calls=%async_computation.34 | async-start | bytes 5806080 | tf_op jit(solution)/shard_map/all_gather | solution.py:2325
  55.7 35.3 %copy-start.39 = (f32[256]{0:T(256)S(1)}, f32[256]{0:T(256)}, u32[]{:S(2)}) copy-start(f32[256]{0:T(256)} %constant.92.clone) | copy-start | bytes 3076
  90.9 1.9 copy-start.5
  162.8 3.8 copy-start.29
  162.8 3.8 copy-start.30
  162.8 4.5 copy-start.38
  162.8 19.0 %all-to-all-start.3 = ((bf16[8,16,16,256]{3,2,1,0:T(8,128)(2,1)}), bf16[8,16,16,256]{3,2,1,0:T(8,128)(2,1)S(1)}, u32[]{:S(2)}, u32[]{:S(2)}) async-start(bf16[8,16,16,256]{3,2,1,0:T(8,128)(2,1)} %get-tuple-element.184), calls=%async_computation.3 | async-start | bytes 2097152 | tf_op jit(solution)/shard_map/all_to_all | solution.py:1913
  166.5 75.9 %all-gather.20.cloned.1.call-start = ((), (), s32[]{:S(2)}) async-start(), calls=%async_computation.35 | async-start | bytes 1622016 | tf_op jit(solution)/shard_map/all_gather | solution.py:2330
  181.9 4.0 copy-start.13
  181.9 20.8 %all-to-all-start.4 = ((bf16[8,16,16,256]{3,2,1,0:T(8,128)(2,1)}), bf16[8,16,16,256]{3,2,1,0:T(8,128)(2,1)S(1)}, u32[]{:S(2)}, u32[]{:S(2)}) async-start(bf16[8,16,16,256]{3,2,1,0:T(8,128)(2,1)} %get-tuple-element.185), calls=%async_computation.4 | async-start | bytes 2097152 | tf_op jit(solution)/shard_map/all_to_all | solution.py:1913
  203.6 33.1 %all-to-all-start.5 = ((bf16[8,2,16,16,256]{4,3,2,1,0:T(8,128)(2,1)}), bf16[8,2,16,16,256]{4,3,2,1,0:T(8,128)(2,1)S(1)}, u32[]{:S(2)}, u32[]{:S(2)}) async-start(bf16[8,2,16,16,256]{4,3,2,1,0:T(8,128)(2,1)} %get-tuple-element.195), calls=%async_computation.5 | async-start | bytes 4194304 | tf_op jit(solution)/shard_map/all_to_all | solution.py:1913
  238.0 34.3 %all-to-all-start.6 = ((bf16[8,2,16,16,256]{4,3,2,1,0:T(8,128)(2,1)}), bf16[8,2,16,16,256]{4,3,2,1,0:T(8,128)(2,1)}, u32[]{:S(2)}, u32[]{:S(2)}) async-start(bf16[8,2,16,16,256]{4,3,2,1,0:T(8,128)(2,1)} %get-tuple-element.197), calls=%async_computation.6 | async-start | bytes 4194304 | tf_op jit(solution)/shard_map/all_to_all | solution.py:1913
  243.2 45.2 %copy-start.9 = (f32[32,768]{1,0:T(8,128)}, f32[32,768]{1,0:T(8,128)S(1)}, u32[]{:S(2)}) copy-start(f32[32,768]{1,0:T(8,128)S(1)} %bitcast_convert_fusion.1) | copy-start | bytes 294916
  278.6 4.5 copy-start.4
  278.6 31.1 %all-to-all-start.7 = ((bf16[8,16,32,256]{3,2,1,0:T(8,128)(2,1)}), bf16[8,16,32,256]{3,2,1,0:T(8,128)(2,1)}, u32[]{:S(2)}, u32[]{:S(2)}) async-start(bf16[8,16,32,256]{3,2,1,0:T(8,128)(2,1)} %incoming_product.1), calls=%async_computation.7 | async-start | bytes 4194304 | tf_op jit(solution)/shard_map/all_to_all | solution.py:1913
  283.1 5.4 copy-start.2
  286.9 23.6 %copy-start.33 = (f32[32]{0:T(128)}, f32[32]{0:T(128)S(1)}, u32[]{:S(2)}) copy-start(f32[32]{0:T(128)S(1)} %broadcast_multiply_fusion) | copy-start | bytes 388
  287.7 22.9 %copy-start.35 = (f32[32]{0:T(128)}, f32[32]{0:T(128)S(1)}, u32[]{:S(2)}) copy-start(f32[32]{0:T(128)S(1)} %fusion.5) | copy-start | bytes 388
  288.5 22.1 %copy-start.23 = (f32[384]{0:T(512)}, f32[384]{0:T(512)S(1)}, u32[]{:S(2)}) copy-start(f32[384]{0:T(512)S(1)} %get-tuple-element.347) | copy-start | bytes 4612
  288.5 22.1 %copy-start.31 = (f32[384]{0:T(512)}, f32[384]{0:T(512)S(1)}, u32[]{:S(2)}) copy-start(f32[384]{0:T(512)S(1)} %get-tuple-element.348) | copy-start | bytes 4612
  288.9 37.5 %copy-start.19 = (f32[32,1536]{1,0:T(8,128)}, f32[32,1536]{1,0:T(8,128)S(1)}, u32[]{:S(2)}) copy-start(f32[32,1536]{1,0:T(8,128)S(1)} %fusion.8.project) | copy-start | bytes 589828
  310.6 15.8 %all-to-all-start.8 = ((bf16[8,32,768]{2,1,0:T(8,128)(2,1)}), bf16[8,32,768]{2,1,0:T(8,128)(2,1)S(1)}, u32[]{:S(2)}, u32[]{:S(2)}) async-start(bf16[8,32,768]{2,1,0:T(8,128)(2,1)} %broadcast_in_dim.30), calls=%async_computation.8 | async-start | bytes 786432 | tf_op jit(solution)/shard_map/all_to_all | solution.py:1913
  326.4 5.1 copy-start.22
  327.1 56.1 %all-to-all-start.9 = ((bf16[8,32,32,128]{3,2,1,0:T(8,128)(2,1)}), bf16[8,32,32,128]{3,2,1,0:T(8,128)(2,1)}, u32[]{:S(2)}, u32[]{:S(2)}) async-start(bf16[8,32,32,128]{3,2,1,0:T(8,128)(2,1)} %bitcast.18), calls=%async_computation.9 | async-start | bytes 4194304 | tf_op jit(solution)/shard_map/all_to_all | solution.py:1913
  383.3 3.8 copy-start.21
  383.3 35.5 %all-to-all-start.10 = ((bf16[8,32,32,128]{3,2,1,0:T(8,128)(2,1)}), bf16[8,32,32,128]{3,2,1,0:T(8,128)(2,1)S(1)}, u32[]{:S(2)}, u32[]{:S(2)}) async-start(bf16[8,32,32,128]{3,2,1,0:T(8,128)(2,1)} %get-tuple-element.219), calls=%async_computation.10 | async-start | bytes 4194304 | tf_op jit(solution)/shard_map/all_to_all | solution.py:1913
  420.1 53.9 %all-to-all-start.11 = ((bf16[4,2,32,32,128]{4,3,2,1,0:T(8,128)(2,1)}), bf16[4,2,32,32,128]{4,3,2,1,0:T(8,128)(2,1)}, u32[]{:S(2)}, u32[]{:S(2)}) async-start(bf16[4,2,32,32,128]{4,3,2,1,0:T(8,128)(2,1)} %bitcast.22), calls=%async_computation.11 | async-start | bytes 4194304 | tf_op jit(solution)/shard_map/all_to_all | solution.py:1913
  510.2 64.3 %all-to-all-start.14 = ((bf16[4,64,32,128]{3,2,1,0:T(8,128)(2,1)}), bf16[4,64,32,128]{3,2,1,0:T(8,128)(2,1)S(1)}, u32[]{:S(2)}, u32[]{:S(2)}) async-start(bf16[4,64,32,128]{3,2,1,0:T(8,128)(2,1)} %bitcast.77), calls=%async_computation.14 | async-start | bytes 4194304 | tf_op jit(solution)/shard_map/all_to_all | solution.py:1913
  542.9 35.1 %copy-start.26 = (f32[32,384]{1,0:T(8,128)S(1)}, f32[32,384]{1,0:T(8,128)}, u32[]{:S(2)}) copy-start(f32[32,384]{1,0:T(8,128)} %get-tuple-element.252) | copy-start | bytes 147460
  542.9 35.1 %copy-start.25 = (f32[32,384]{1,0:T(8,128)S(1)}, f32[32,384]{1,0:T(8,128)}, u32[]{:S(2)}) copy-start(f32[32,384]{1,0:T(8,128)} %get-tuple-element.253) | copy-start | bytes 147460
  542.9 35.2 %copy-start.11 = (bf16[8,32,1280]{2,1,0:T(8,128)(2,1)S(1)}, bf16[8,32,1280]{2,1,0:T(8,128)(2,1)}, u32[]{:S(2)}) copy-start(bf16[8,32,1280]{2,1,0:T(8,128)(2,1)} %all_to_all.152.refs_3_) | copy-start | bytes 1966084
  543.0 35.2 %copy-start.10 = (f32[32,768]{1,0:T(8,128)S(1)}, f32[32,768]{1,0:T(8,128)}, u32[]{:S(2)}) copy-start(f32[32,768]{1,0:T(8,128)} %copy-done.9) | copy-start | bytes 294916
  543.0 35.2 %copy-start.24 = (f32[384]{0:T(512)S(1)}, f32[384]{0:T(512)}, u32[]{:S(2)}) copy-start(f32[384]{0:T(512)} %copy-done.23) | copy-start | bytes 4612
  543.0 35.2 %copy-start.32 = (f32[384]{0:T(512)S(1)}, f32[384]{0:T(512)}, u32[]{:S(2)}) copy-start(f32[384]{0:T(512)} %copy-done.31) | copy-start | bytes 4612
  543.0 35.2 %copy-start.34 = (f32[32]{0:T(128)S(1)}, f32[32]{0:T(128)}, u32[]{:S(2)}) copy-start(f32[32]{0:T(128)} %copy-done.33) | copy-start | bytes 388
  543.0 35.2 %copy-start.36 = (f32[32]{0:T(128)S(1)}, f32[32]{0:T(128)}, u32[]{:S(2)}) copy-start(f32[32]{0:T(128)} %copy-done.35) | copy-start | bytes 388
  574.5 24.7 %copy-start = (bf16[4,64,32,128]{3,2,1,0:T(8,128)(2,1)}, bf16[4,64,32,128]{3,2,1,0:T(8,128)(2,1)S(1)}, u32[]{:S(2)}) copy-start(bf16[4,64,32,128]{3,2,1,0:T(8,128)(2,1)S(1)} %all-to-all-done.14) | copy-start | bytes 6291460
  574.5 13.2 %all-to-all-start.15 = ((bf16[8,4,32,256]{3,2,1,0:T(8,128)(2,1)}), bf16[8,4,32,256]{3,2,1,0:T(8,128)(2,1)S(1)}, u32[]{:S(2)}, u32[]{:S(2)}) async-start(bf16[8,4,32,256]{3,2,1,0:T(8,128)(2,1)} %get-tuple-element.251), calls=%async_computation.15 | async-start | bytes 1048576 | tf_op jit(solution)/shard_map/all_to_all | solution.py:1913
  599.3 4.5 copy-start.3
  599.3 36.0 %all-to-all-start.16 = ((bf16[8,32,32,128]{3,2,1,0:T(8,128)(2,1)}), bf16[8,32,32,128]{3,2,1,0:T(8,128)(2,1)S(1)}, u32[]{:S(2)}, u32[]{:S(2)}) async-start(bf16[8,32,32,128]{3,2,1,0:T(8,128)(2,1)} %get-tuple-element.259), calls=%async_computation.16 | async-start | bytes 4194304 | tf_op jit(solution)/shard_map/all_to_all | solution.py:1913
  603.0 184.9 %reduce-scatter.2.cloned.1.call-start = ((), (), s32[]{:S(2)}) async-start(), calls=%async_computation.31 | async-start | bytes 5271552 | tf_op jit(solution)/shard_map/reduce_scatter | solution.py:2358
  636.6 36.1 %all-to-all-start.17 = ((bf16[8,32,32,128]{3,2,1,0:T(8,128)(2,1)}), bf16[8,32,32,128]{3,2,1,0:T(8,128)(2,1)S(1)}, u32[]{:S(2)}, u32[]{:S(2)}) async-start(bf16[8,32,32,128]{3,2,1,0:T(8,128)(2,1)} %bitcast.66), calls=%async_computation.17 | async-start | bytes 4194304 | tf_op jit(solution)/shard_map/all_to_all | solution.py:1913
  702.1 21.5 %all-to-all-start.19 = ((bf16[8,16,16,256]{3,2,1,0:T(8,128)(2,1)}), bf16[8,16,16,256]{3,2,1,0:T(8,128)(2,1)S(1)}, u32[]{:S(2)}, u32[]{:S(2)}) async-start(bf16[8,16,16,256]{3,2,1,0:T(8,128)(2,1)} %bitcast.86), calls=%async_computation.19 | async-start | bytes 2097152 | tf_op jit(solution)/shard_map/all_to_all | solution.py:1913
  723.6 20.7 %copy-start.15 = (bf16[8,16,16,256]{3,2,1,0:T(8,128)(2,1)}, bf16[8,16,16,256]{3,2,1,0:T(8,128)(2,1)S(1)}, u32[]{:S(2)}) copy-start(bf16[8,16,16,256]{3,2,1,0:T(8,128)(2,1)S(1)} %all-to-all-done.19.refs_0_) | copy-start | bytes 3145732
  751.7 4.5 copy-start.41
  751.7 4.7 copy-start.27
  751.7 4.7 copy-start.28
  751.7 31.1 %all-to-all-start.21 = ((bf16[8,2,16,16,256]{4,3,2,1,0:T(8,128)(2,1)}), bf16[8,2,16,16,256]{4,3,2,1,0:T(8,128)(2,1)}, u32[]{:S(2)}, u32[]{:S(2)}) async-start(bf16[8,2,16,16,256]{4,3,2,1,0:T(8,128)(2,1)} %get-tuple-element.290), calls=%async_computation.21 | async-start | bytes 4194304 | tf_op jit(solution)/shard_map/all_to_all | solution.py:1913
  782.8 31.4 %all-to-all-start.22 = ((bf16[8,2,16,16,256]{4,3,2,1,0:T(8,128)(2,1)}), bf16[8,2,16,16,256]{4,3,2,1,0:T(8,128)(2,1)}, u32[]{:S(2)}, u32[]{:S(2)}) async-start(bf16[8,2,16,16,256]{4,3,2,1,0:T(8,128)(2,1)} %get-tuple-element.291), calls=%async_computation.22 | async-start | bytes 4194304 | tf_op jit(solution)/shard_map/all_to_all | solution.py:1913
  787.2 65.5 %all-gather.14.cloned.1.call-start = ((), (), s32[]{:S(2)}) async-start(), calls=%async_computation.32 | async-start | bytes 1622016 | tf_op jit(solution)/shard_map/all_gather | solution.py:2344
  814.2 23.8 %all-to-all-start.23 = ((bf16[8,16,16,256]{3,2,1,0:T(8,128)(2,1)}), bf16[8,16,16,256]{3,2,1,0:T(8,128)(2,1)S(1)}, u32[]{:S(2)}, u32[]{:S(2)}) async-start(bf16[8,16,16,256]{3,2,1,0:T(8,128)(2,1)} %bitcast.85), calls=%async_computation.24 | async-start | bytes 2097152 | tf_op jit(solution)/shard_map/all_to_all | solution.py:1913
  838.0 13.5 %copy-start.14 = (bf16[8,16,16,256]{3,2,1,0:T(8,128)(2,1)}, bf16[8,16,16,256]{3,2,1,0:T(8,128)(2,1)S(1)}, u32[]{:S(2)}) copy-start(bf16[8,16,16,256]{3,2,1,0:T(8,128)(2,1)S(1)} %all-to-all-done.23.refs_0_) | copy-start | bytes 3145732
  838.0 19.9 %all-to-all-start.24 = ((bf16[8,16,16,256]{3,2,1,0:T(8,128)(2,1)}), bf16[8,16,16,256]{3,2,1,0:T(8,128)(2,1)}, u32[]{:S(2)}, u32[]{:S(2)}) async-start(bf16[8,16,16,256]{3,2,1,0:T(8,128)(2,1)} %bitcast.84), calls=%async_computation.25 | async-start | bytes 2097152 | tf_op jit(solution)/shard_map/all_to_all | solution.py:1913
  918.8 31.3 %all-to-all-start.26 = ((bf16[8,21,24,128]{3,2,1,0:T(8,128)(2,1)}), bf16[8,21,24,128]{3,2,1,0:T(8,128)(2,1)S(1)}, u32[]{:S(2)}, u32[]{:S(2)}) async-start(bf16[8,21,24,128]{3,2,1,0:T(8,128)(2,1)} %pair_gradient.1), calls=%async_computation.27 | async-start | bytes 2064384 | tf_op jit(solution)/shard_map/all_to_all | solution.py:1913
  960.3 52.6 %all-to-all-start.28 = ((bf16[4,8,256,128]{3,2,1,0:T(8,128)(2,1)}), bf16[4,8,256,128]{3,2,1,0:T(8,128)(2,1)}, u32[]{:S(2)}, u32[]{:S(2)}) async-start(bf16[4,8,256,128]{3,2,1,0:T(8,128)(2,1)} %bitcast.78), calls=%async_computation.29 | async-start | bytes 4194304 | tf_op jit(solution)/shard_map/all_to_all | solution.py:1913
  964.8 1.9 copy-start.20
  996.2 20.3 %copy-start.37 = (f32[8,128]{1,0:T(8,128)S(1)}, f32[8,128]{1,0:T(8,128)}, u32[]{:S(2)}) copy-start(f32[8,128]{1,0:T(8,128)} %get-tuple-element.343) | copy-start | bytes 12292
  1012.9 27.9 %all-to-all-start.29 = ((bf16[4,8,256,128]{3,2,1,0:T(8,128)(2,1)}), bf16[4,8,256,128]{3,2,1,0:T(8,128)(2,1)S(1)}, u32[]{:S(2)}, u32[]{:S(2)}) async-start(bf16[4,8,256,128]{3,2,1,0:T(8,128)(2,1)} %all-to-all-done.28), calls=%async_computation.30 | async-start | bytes 4194304 | tf_op jit(solution)/shard_map/all_to_all | solution.py:1913
  (7 other events, 7.0 us)
Sparse Core Ops, SparseCore 0:
  21.9 25.2 all-gather.15
  91.1 54.4 all-gather.17
  171.0 63.1 all-gather.19
  635.4 117.1 reduce-scatter.1
  791.7 60.8 all-gather.13

commit v8 on v7

--- a/solution.py
+++ b/solution.py
@@ -1902,7 +1902,7 @@
     ] + [(matrix.shape, F32) for matrix in matrices] + [((8, width), F32)]
     ins = [state, back, project, kv, bias, alive, weights[(SINGLE, VECTORS)]] + matrices
     final, grad, sent, query_grad, gate_grad, *found, vecs = whole_call(
-        single_kernel, "single_path", [(array, None) for array in ins], outs, [], 15
+        single_kernel, "single_path", [(array, None) for array in ins], outs, [], 1
     )
     grads = dict(zip(names, found))
     grads[(SINGLE, NORM_GAIN)], grads[(SINGLE, NORM_BIAS)] = vecs[0], vecs[1]
@@ -1955,6 +1955,18 @@
         return moved
 
     return send
+
+
+def along_line(values, axis):
+    count = values.shape[0]
+    here = lax.axis_index(axis)
+    moved = jnp.zeros_like(values)
+    for step in range(count):
+        part = lax.dynamic_slice_in_dim(values, lax.rem(here + step, count), 1)
+        if step:
+            part = lax.ppermute(part, axis, [(place, (place + step) % count) for place in range(count)])
+        moved = lax.dynamic_update_slice_in_dim(moved, part, lax.rem(here + count - step, count), 0)
+    return moved
 
 
 def pair_path(pair, info, alive, orders, weights, cotangent, middle, between, meet, send, group, parts):
@@ -2053,7 +2065,6 @@
         ],
         [(state_shape, F32, 0), ((TA_HEADS, rows, length), BF16, 1)], [tri_scratch, head_scratch],
     )
-    (bias,) = meet(7, bias)
     bias_one = lax.all_gather(bias, group, axis=0, tiled=False)
     flipped, totals_one, mixed_one, bias = run_rows(
         starting_kernel, "starting_attention", steps,
@@ -2067,15 +2078,14 @@
     )
     state_three = Both([send(flipped, group)])
     bias_two = lax.all_gather(bias, group, axis=0, tiled=False)
-    cotangent, bias_two = after(cotangent, bias_two)
-    cotangent = send(cotangent.reshape((parts, cores) + flip_shape[1:]), "z").reshape(flip_shape)
+    cotangent = along_line(cotangent.reshape((parts, cores) + flip_shape[1:]), "z").reshape(flip_shape)
     state_four, totals_two, mixed_two = run_rows(
         ending_kernel, "ending_attention", steps,
         [
             (alive, None), (state_three, 1), (bias_two, None), (cols(ENDING), None),
             (turned((ENDING, QKVG)), None), (turned((ENDING, OUTPUT)), None),
         ],
-        [(state_shape, F32, 0)] + attend_saves, [table],
+        [(state_shape, F32, 0)] + attend_saves, [table], 1,
     )
     pair_cols, attend_cols = cols(PAIR), cols(ATTEND)
     state_five, pair_out, single_bias = run_rows(
@@ -2085,7 +2095,7 @@
             (attend_cols, None), (turned((ATTEND, PAIR_PROJ)), None),
         ],
         [(state_shape, F32, 0), ((length, rows, width), BF16, 1), ((devices, rows, SA_HEADS * rows), BF16, 1)],
-        [flip_scratch, ((SA_HEADS, block, length), F32)],
+        [flip_scratch, ((SA_HEADS, block, length), F32)], 1,
     )
     single_sent = send(middle(send(single_bias, group)), group)
     between(2, single_sent)
@@ -2294,8 +2304,6 @@
             others = [held["projected"][1]]
         elif number == 3:
             others = [reduced[3]]
-        elif number == 7:
-            others = [held["projected"][2]]
         elif number == 8:
             others = [single_grads[(ATTEND, QKVG)]]
         elif number == 4:

time: 1060 us -> 1040 us (0.981)
  blocking collectives: 287 us -> 241 us
  starting transfers between devices: 96.7 us -> 114 us
    all_to_all x7 -> x5, blocking collectives: 178 us -> 152 us  [swap(): lax.all_to_all(values, group, split_axis=0, concat_axis=0, tiled=True)]
    all_gather x1, blocking collectives: 31.7 us -> 12.2 us  [pair_path(): bias_one = lax.all_gather(bias, group, axis=0, tiled=False)]
    all_to_all x23 -> x24, starting transfers between devices: 96.6 us -> 109 us  [swap(): lax.all_to_all(values, group, split_axis=0, concat_axis=0, tiled=True)]
    all_to_all x23 -> x24, waiting for transfers between devices: 192 us -> 187 us  [swap(): lax.all_to_all(values, group, split_axis=0, concat_axis=0, tiled=True)]
  transfers between devices with their start and end apart: 28 -> 32, of which waited for: 16 -> 19; matrix products, arithmetic and copies ran while one was open for 3% -> 4% of each run, Pallas kernels for 36% -> 38%
where the time goes in v8:
time: 1040 us; the launch traced here: 1030 us
  Pallas kernels  413 us (40%)
  blocking collectives  241 us (23%)
  waiting for transfers between devices  193 us (19%)
  starting transfers between devices  114 us (11%)
  local copies, waits for them, and re-layouts  28.1 us (3%)
  other arithmetic  19 us (2%)
  between operations  17.2 us (2%)
    pallas_call x20, Pallas kernels, run_rows(): pl.pallas_call(run, grid=(grid,), in_specs=in_specs, out_specs=out_specs,...  314 us
    all_to_all x24, waiting for transfers between devices, swap(): lax.all_to_all(values, group, split_axis=0, concat_axis=0, tiled=True)  187 us
    all_to_all x5, blocking collectives, swap(): lax.all_to_all(values, group, split_axis=0, concat_axis=0, tiled=True)  152 us
    all_to_all x24, starting transfers between devices, swap(): lax.all_to_all(values, group, split_axis=0, concat_axis=0, tiled=True)  109 us
    pallas_call x8, Pallas kernels, whole_call(): pl.pallas_call(kernel, in_specs=[spec(axis) for array, axis in ins], out_...  98.4 us
    all_gather x1, blocking collectives, pair_path(): bias_two = lax.all_gather(bias, group, axis=0, tiled=False)  31.7 us
  transfers between devices with their start and end apart: 32, of which 19 were waited for; matrix products, arithmetic and copies ran while one was open for 4% of the time, Pallas kernels for 38%

profile of v8, /device:TPU:0, one launch (start us, length us, event | category | flops | bytes accessed | tf_op | source)
XLA Modules:
  0.0 1027.0 jit_solution(10088749967742821461)
XLA Ops:
  7.2 5.3 all-to-all-start
  14.3 5.9 parameter_runs.1
  21.9 16.3 %all-to-all-done = bf16[4,8,256,128]{3,2,1,0:T(8,128)(2,1)} async-done(((bf16[4,8,256,128]{3,2,1,0:T(8,128)(2,1)}), bf16[4,8,256,128]{3,2,1,0:T(8,128)(2,1)}, u32[]{:S(2)}, u32[]{:S(2)}) %all-to-all-start) | async-done | bytes 2097184 | tf_op jit(solution)/shard_map/all_to_all | solution.py:1913
  38.2 5.1 all-to-all-start.1
  45.3 8.9 all-reduce.2
  55.7 8.0 pair_weights.1
  63.7 27.2 %all-to-all-done.1 = bf16[4,8,256,128]{3,2,1,0:T(8,128)(2,1)S(1)} async-done(((bf16[4,8,256,128]{3,2,1,0:T(8,128)(2,1)}), bf16[4,8,256,128]{3,2,1,0:T(8,128)(2,1)S(1)}, u32[]{:S(2)}, u32[]{:S(2)}) %all-to-all-start.1) | async-done | bytes 2097184 | tf_op jit(solution)/shard_map/all_to_all | solution.py:1913
  92.9 10.2 outgoing_in.1
  103.1 53.5 %all_to_all.145.refs_0_.refs_2_ = bf16[8,2,16,32,256]{4,3,2,1,0:T(8,128)(2,1)} all-to-all(bf16[8,2,16,32,256]{4,3,2,1,0:T(8,128)(2,1)} %outgoing_in.1), channel_id=1, replica_groups=mesh['crop'=4,'z'=4,'core'=2] {'crop','core'}, dimensions={0} | all-to-all | bytes 8388608 | tf_op jit(solution)/shard_map/all_to_all | solution.py:1913
  156.6 6.2 outgoing_product.1
  167.9 14.0 %all-to-all-done.3 = bf16[8,16,16,256]{3,2,1,0:T(8,128)(2,1)S(1)} async-done(((bf16[8,16,16,256]{3,2,1,0:T(8,128)(2,1)}), bf16[8,16,16,256]{3,2,1,0:T(8,128)(2,1)S(1)}, u32[]{:S(2)}, u32[]{:S(2)}) %all-to-all-start.3) | async-done | bytes 1048608 | tf_op jit(solution)/shard_map/all_to_all | solution.py:1913
  185.9 11.1 %outgoing_out_incoming_in.2 = (f32[32,128,256]{2,1,0:T(8,128)}, bf16[8,2,16,16,256]{4,3,2,1,0:T(8,128)(2,1)}) custom-call(s32[16]{0:T(128)} %get-tuple-element.355.refs_0_, f32[8,256]{1,0:T(8,128)} %broadcast_in_dim.32.refs_1_.refs_0_.alive, bf16[32,256,128]{2,1,0:T(8,128)(2,1)} %bitcast.74, bf16[128,16,256]{2,1,0:T(8,128)(2,1)} %bitcast.85, ...), custom_call_target="tpu_custom_call" | custom-call | flops 11000000512 | bytes 33000000 | tf_op jit(solution)/shard_map/outgoing_out_incoming_in/pallas_call | solution.py:762
  197.1 5.6 all-to-all-done.4
  207.4 11.1 %outgoing_out_incoming_in.3 = (f32[32,128,256]{2,1,0:T(8,128)}, bf16[8,2,16,16,256]{4,3,2,1,0:T(8,128)(2,1)}) custom-call(s32[16]{0:T(128)} %get-tuple-element.356.refs_0_, f32[8,256]{1,0:T(8,128)} %broadcast_in_dim.32.refs_1_.refs_0_.alive, bf16[32,256,128]{2,1,0:T(8,128)(2,1)} %bitcast.75, ...), custom_call_target="tpu_custom_call", output_to_operand_aliasing={{0}: (9, {})} | custom-call | flops 11000000512 | bytes 33000000 | tf_op jit(solution)/shard_map/outgoing_out_incoming_in/pallas_call | solution.py:762
  218.6 18.2 %all-to-all-done.5.refs_0_.refs_2_ = bf16[8,2,16,16,256]{4,3,2,1,0:T(8,128)(2,1)S(1)} async-done(((bf16[8,2,16,16,256]{4,3,2,1,0:T(8,128)(2,1)}), bf16[8,2,16,16,256]{4,3,2,1,0:T(8,128)(2,1)S(1)}, u32[]{:S(2)}, u32[]{:S(2)}) %all-to-all-start.5) | async-done | bytes 2097184 | tf_op jit(solution)/shard_map/all_to_all | solution.py:1913
  238.1 4.3 all-to-all-start.6
  244.0 28.4 %single_weights.1 = (bf16[384,1536]{1,0:T(8,128)(2,1)}, bf16[384,384]{1,0:T(8,128)(2,1)}, bf16[384,3072]{1,0:T(8,128)(2,1)}, bf16[1536,384]{1,0:T(8,128)(2,1)}, ...) custom-call(bf16[8,105,24,128]{3,2,1,0:T(8,128)(2,1)} %bitcast.102), custom_call_target="tpu_custom_call" | custom-call | flops 8000000000 | bytes 24000000 | tf_op jit(solution)/shard_map/single_weights/pallas_call | solution.py:1692
  272.4 6.3 incoming_product.1
  278.7 4.5 all-to-all-start.7
  288.3 21.5 %all-to-all-done.7 = bf16[8,16,32,256]{3,2,1,0:T(8,128)(2,1)} async-done(((bf16[8,16,32,256]{3,2,1,0:T(8,128)(2,1)}), bf16[8,16,32,256]{3,2,1,0:T(8,128)(2,1)}, u32[]{:S(2)}, u32[]{:S(2)}) %all-to-all-start.7) | async-done | bytes 2097184 | tf_op jit(solution)/shard_map/all_to_all | solution.py:1913
  314.3 12.1 %incoming_out_starting_bias.1 = (f32[32,128,256]{2,1,0:T(8,128)}, bf16[4,32,256]{2,1,0:T(8,128)(2,1)}) custom-call(f32[32,128,256]{2,1,0:T(8,128)} %get-tuple-element.189.refs_0_.refs_6_.refs_2_, bf16[128,32,256]{2,1,0:T(8,128)(2,1)} %bitcast.14.refs_1_.refs_7_, f32[128,8]{1,0:T(8,128)} %get-tuple-element.186.refs_7_.refs_2_.refs_8_.refs_6_, ...), custom_call_target="tpu_custom_call" | custom-call | flops 15000000512 | bytes 45000000 | tf_op jit(solution)/shard_map/incoming_out_starting_bias/pallas_call | solution.py:762
  326.4 12.2 %all-gather.4 = bf16[32,32,256]{2,1,0:T(8,128)(2,1)} all-gather(bf16[4,32,256]{2,1,0:T(8,128)(2,1)} %get-tuple-element.206), channel_id=7, replica_groups=mesh['crop'=4,'z'=4,'core'=2] {'crop','core'}, dimensions={0}, use_global_device_ids=true | all-gather | bytes 589824 | tf_op jit(solution)/shard_map/all_gather | solution.py:2068
  343.0 20.0 %starting_attention.1 = (bf16[8,32,32,128]{3,2,1,0:T(8,128)(2,1)}, f32[32,4,256]{2,1,0:T(4,128)}, bf16[32,128,256]{2,1,0:T(8,128)(2,1)}, bf16[4,32,256]{2,1,0:T(8,128)(2,1)}) custom-call(f32[8,256]{1,0:T(8,128)} %broadcast_in_dim.32.refs_1_.refs_0_.alive, f32[32,128,256]{2,1,0:T(8,128)} %get-tuple-element.205.refs_1_.refs_0_, ...), custom_call_target="tpu_custom_call" | custom-call | flops 20999999488 | bytes 63000000 | tf_op jit(solution)/shard_map/starting_attention/pallas_call | solution.py:762
  363.0 6.6 all-to-all-done.9
  369.5 4.5 all-to-all-start.10
  374.1 31.7 %all-gather.5 = bf16[32,32,256]{2,1,0:T(8,128)(2,1)} all-gather(bf16[4,32,256]{2,1,0:T(8,128)(2,1)S(1)} %copy-done.19), channel_id=8, replica_groups=mesh['crop'=4,'z'=4,'core'=2] {'crop','core'}, dimensions={0}, use_global_device_ids=true | all-gather | bytes 589824 | tf_op jit(solution)/shard_map/all_gather | solution.py:2080
  409.2 16.6 %ending_attention.1 = (f32[32,128,256]{2,1,0:T(8,128)}, f32[32,4,256]{2,1,0:T(4,128)}, bf16[32,128,256]{2,1,0:T(8,128)(2,1)}) custom-call(f32[8,256]{1,0:T(8,128)} %broadcast_in_dim.32.refs_1_.refs_0_.alive, bf16[8,32,32,128]{3,2,1,0:T(8,128)(2,1)} %all-to-all-done.10.refs_1_.refs_0_, bf16[8,4,32,256]{3,2,1,0:T(8,128)(2,1)} %bitcast.95, ...), custom_call_target="tpu_custom_call" | custom-call | flops 1000000000 | bytes 3000000 | tf_op jit(solution)/shard_map/ending_attention/pallas_call | solution.py:762
  425.8 14.7 %pair_transition.1 = (f32[32,128,256]{2,1,0:T(8,128)}, bf16[256,32,128]{2,1,0:T(8,128)(2,1)}, bf16[8,32,512]{2,1,0:T(8,128)(2,1)}) custom-call(f32[32,128,256]{2,1,0:T(8,128)} %get-tuple-element.218.refs_0_, f32[128,8]{1,0:T(8,128)} %get-tuple-element.219.refs_1_.refs_4_, bf16[1024,128]{1,0:T(8,128)(2,1)} %get-tuple-element.220.refs_2_.refs_5_, ...), custom_call_target="tpu_custom_call" | custom-call | flops 1000000000 | bytes 3000000 | tf_op jit(solution)/shard_map/pair_transition/pallas_call | solution.py:762
  451.4 10.1 single_path.1
  466.9 4.3 collective-permute-done.1
  476.9 13.2 %all-to-all-start.13 = ((bf16[4,64,32,128]{3,2,1,0:T(8,128)(2,1)}), bf16[4,64,32,128]{3,2,1,0:T(8,128)(2,1)S(1)}, u32[]{:S(2)}, u32[]{:S(2)}) async-start(bf16[4,64,32,128]{3,2,1,0:T(8,128)(2,1)} %bitcast.79), calls=%async_computation.13 | async-start | bytes 4194304 | tf_op jit(solution)/shard_map/all_to_all | solution.py:1913
  490.1 28.8 %pair_transition_back.1 = (f32[32,128,256]{2,1,0:T(8,128)}, f32[128,1024]{1,0:T(8,128)}, f32[512,128]{1,0:T(8,128)}, f32[128,16]{1,0:T(8,128)}, f32[8,128]{1,0:T(8,128)}) custom-call(f32[32,128,256]{2,1,0:T(8,128)} %get-tuple-element.218.refs_0_, f32[32,128,256]{2,1,0:T(8,128)} %get-tuple-element.232.refs_1_, bf16[8,32,32,128]{3,2,1,0:T(8,128)(2,1)} %bitcast.70, ...), custom_call_target="tpu_custom_call" | custom-call | flops 30000001024 | bytes 90000000 | tf_op jit(solution)/shard_map/pair_transition_back/pallas_call | solution.py:762
  519.0 31.5 %attention_back.2 = (bf16[32,128,256]{2,1,0:T(8,128)(2,1)}, bf16[8,4,32,256]{3,2,1,0:T(8,128)(2,1)}, f32[128,512]{1,0:T(8,128)}, f32[128,128]{1,0:T(8,128)}) custom-call(f32[8,256]{1,0:T(8,128)} %broadcast_in_dim.32.refs_1_.refs_0_.alive, bf16[8,32,32,128]{3,2,1,0:T(8,128)(2,1)} %all-to-all-done.10.refs_1_.refs_0_, ...), custom_call_target="tpu_custom_call" | custom-call | flops 33999998976 | bytes 102000000 | tf_op jit(solution)/shard_map/attention_back/pallas_call | solution.py:762
  557.8 6.6 all-to-all-done.14.refs_3_
  564.4 10.7 %ending_attention_end.1 = (bf16[8,32,32,128]{3,2,1,0:T(8,128)(2,1)}, f32[128,8]{1,0:T(8,128)}, f32[8,128]{1,0:T(8,128)}) custom-call(bf16[8,32,32,128]{3,2,1,0:T(8,128)(2,1)} %all-to-all-done.10.refs_1_.refs_0_, f32[32,128,256]{2,1,0:T(8,128)} %get-tuple-element.236.refs_2_.refs_1_, bf16[32,128,256]{2,1,0:T(8,128)(2,1)} %get-tuple-element.241.refs_2_, ...), custom_call_target="tpu_custom_call" | custom-call | flops 15000000512 | bytes 45000000 | tf_op jit(solution)/shard_map/ending_attention_end/pallas_call | solution.py:762
  580.8 30.2 %single_gradient.1 = bf16[8,104,24,128]{3,2,1,0:T(8,128)(2,1)} custom-call(f32[384,1536]{1,0:T(8,128)} %fusion.2.refs_0_, f32[384,384]{1,0:T(8,128)} %get-tuple-element.253.refs_1_, f32[384,3072]{1,0:T(8,128)} %get-tuple-element.254.refs_2_, f32[1536,384]{1,0:T(8,128)} %get-tuple-element.255.refs_3_, f32[128,16]{1,0:T(8,128)} %get-tuple-element.256.refs_4_, ...), custom_call_target="tpu_custom_call" | custom-call | flops 8000000000 | bytes 24000000 | tf_op jit(solution)/shard_map/single_gradient/pallas_call | solution.py:1692
  616.5 32.0 %attention_back.3 = (bf16[32,128,256]{2,1,0:T(8,128)(2,1)}, bf16[8,4,32,256]{3,2,1,0:T(8,128)(2,1)}, f32[128,512]{1,0:T(8,128)}, f32[128,128]{1,0:T(8,128)}) custom-call(f32[8,256]{1,0:T(8,128)} %broadcast_in_dim.32.refs_1_.refs_0_.alive, f32[32,128,256]{2,1,0:T(8,128)} %get-tuple-element.205.refs_1_.refs_0_, bf16[8,32,32,128]{3,2,1,0:T(8,128)(2,1)} %copy-done.9, ...), custom_call_target="tpu_custom_call" | custom-call | flops 33999998976 | bytes 102000000 | tf_op jit(solution)/shard_map/attention_back/pallas_call | solution.py:762
  648.5 14.1 %all_to_all.146.refs_3_ = bf16[8,4,32,256]{3,2,1,0:T(8,128)(2,1)} all-to-all(bf16[8,4,32,256]{3,2,1,0:T(8,128)(2,1)} %get-tuple-element.266), channel_id=1, replica_groups=mesh['crop'=4,'z'=4,'core'=2] {'crop','core'}, dimensions={0} | all-to-all | bytes 1048576 | tf_op jit(solution)/shard_map/all_to_all | solution.py:1913
  662.6 15.3 %starting_end_incoming_out_back.2 = (f32[32,128,256]{2,1,0:T(8,128)}, bf16[128,16,256]{2,1,0:T(8,128)(2,1)}, bf16[32,128,256]{2,1,0:T(8,128)(2,1)}, f32[128,8]{1...) custom-call(f32[32,128,256]{2,1,0:T(8,128)} %get-tuple-element.205.refs_1_.refs_0_, ...), custom_call_target="tpu_custom_call" | custom-call | flops 12999999488 | bytes 39000000 | tf_op jit(solution)/shard_map/starting_end_incoming_out_back/pallas_call | solution.py:762
  681.6 15.3 %starting_end_incoming_out_back.3 = (f32[32,128,256]{2,1,0:T(8,128)}, bf16[128,16,256]{2,1,0:T(8,128)(2,1)}, bf16[32,128,256]{2,1,0:T(8,128)(2,1)}, f32[128,8]{1...) custom-call(f32[32,128,256]{2,1,0:T(8,128)} %get-tuple-element.205.r, ...), custom_call_target="tpu_custom_call", output_to_operand_aliasing={{0}: (13, {}), {2}: (14, {}), {3}: (15, {}), {4}: (16, {}),... | custom-call | flops 12999999488 | bytes 39000000 | tf_op jit(solution)/shard_map/starting_end_incoming_out_back/pallas_call | solution.py:762
  699.3 20.7 %all_to_all.147.refs_1_ = bf16[8,16,16,256]{3,2,1,0:T(8,128)(2,1)} all-to-all(bf16[8,16,16,256]{3,2,1,0:T(8,128)(2,1)} %bitcast.90), channel_id=1, replica_groups=mesh['crop'=4,'z'=4,'core'=2] {'crop','core'}, dimensions={0} | all-to-all | bytes 2097152 | tf_op jit(solution)/shard_map/all_to_all | solution.py:1913
  720.0 7.4 incoming_product_back.1
  727.4 4.5 all-to-all-start.20
  732.3 26.3 %all-to-all-done.20.refs_3_ = bf16[8,2,16,16,256]{4,3,2,1,0:T(8,128)(2,1)} async-done(((bf16[8,2,16,16,256]{4,3,2,1,0:T(8,128)(2,1)}), bf16[8,2,16,16,256]{4,3,2,1,0:T(8,128)(2,1)}, u32[]{:S(2)}, u32[]{:S(2)}) %all-to-all-start.20) | async-done | bytes 2097184 | tf_op jit(solution)/shard_map/all_to_all | solution.py:1913
  758.6 4.4 all-to-all-start.21
  763.7 20.0 %incoming_in_outgoing_out_back.2 = (f32[32,128,256]{2,1,0:T(8,128)}, bf16[128,16,256]{2,1,0:T(8,128)(2,1)}, bf16[32,128,256]{2,1,0:T(8,128)(2,1)}, f32[128,512]{...) custom-call(s32[16]{0:T(128)} %get-tuple-element.355.refs_0_, ...), custom_call_target="tpu_custom_call" | custom-call | flops 18499999744 | bytes 55500000 | tf_op jit(solution)/shard_map/incoming_in_outgoing_out_back/pallas_call | solution.py:762
  783.7 6.3 all-to-all-done.21.refs_3_
  793.9 19.9 %incoming_in_outgoing_out_back.3 = (f32[32,128,256]{2,1,0:T(8,128)}, bf16[128,16,256]{2,1,0:T(8,128)(2,1)}, bf16[32,128,256]{2,1,0:T(8,128)(2,1)}, f32[128,512]{...) custom-call(s32[16]{0:T(128)} %get-tuple-element.356.refs_0_, ...), custom_call_target="tpu_custom_call", output_to_operand_aliasing={{0}: (16, {}), {2}: (17, {}), {3}: (18, {}), {4}: (19, {}),... | custom-call | flops 18499999744 | bytes 55500000 | tf_op jit(solution)/shard_map/incoming_in_outgoing_out_back/pallas_call | solution.py:762
  813.9 4.4 all-to-all-start.23
  819.9 7.5 pair_gradient.1
  828.4 5.3 all-to-all-done.23.refs_1_
  833.7 7.3 outgoing_product_back.1
  841.0 53.5 %all_to_all.148.refs_3_ = bf16[8,2,16,32,256]{4,3,2,1,0:T(8,128)(2,1)} all-to-all(bf16[8,2,16,32,256]{4,3,2,1,0:T(8,128)(2,1)} %outgoing_product_back.1), channel_id=1, replica_groups=mesh['crop'=4,'z'=4,'core'=2] {'crop','core'}, dimensions={0} | all-to-all | bytes 8388608 | tf_op jit(solution)/shard_map/all_to_all | solution.py:1913
  894.6 5.1 all-to-all-start.25
  899.6 17.7 %outgoing_in_back.1 = (bf16[32,256,128]{2,1,0:T(8,128)(2,1)}, f32[128,512]{1,0:T(8,128)}, f32[8,128]{1,0:T(8,128)}) custom-call(s32[32]{0:T(128)} %dynamic-slice_convert_fusion.refs_0_, f32[8,256]{1,0:T(8,128)} %broadcast_in_dim.32.refs_1_.refs_0_.alive, bf16[32,256,128]{2,1,0:T(8,128)(2,1)} %bitcast.78, bf16[8,2,16,32,256]{4,3,2,1,0:T(8,128)(2,1)} %all_to_all.148.refs_3_, ...), custom_call_target="tpu_custom_call" | custom-call | flops 20000000000 | bytes 60000000 | tf_op jit(solution)/shard_map/outgoing_in_back/pallas_call | solution.py:762
  919.6 6.3 all-to-all-done.25
  925.9 10.3 %all_to_all.149 = bf16[8,3,24,128]{3,2,1,0:T(8,128)(2,1)S(1)} all-to-all(bf16[8,3,24,128]{3,2,1,0:T(8,128)(2,1)} %outgoing_gradient.1), channel_id=1, replica_groups=mesh['crop'=4,'z'=4,'core'=2] {'z','core'}, dimensions={0} | all-to-all | bytes 294912 | tf_op jit(solution)/shard_map/all_to_all | solution.py:1913
  936.2 4.4 all-to-all-start.27
  942.6 10.3 %all-gather.7 = bf16[104,24,128]{2,1,0:T(8,128)(2,1)} all-gather(bf16[26,24,128]{2,1,0:T(8,128)(2,1)S(1)} %bitcast.97), channel_id=10, replica_groups=mesh['crop'=4,'z'=4,'core'=2] {'crop'}, dimensions={0}, use_global_device_ids=true | all-gather | bytes 798720 | tf_op jit(solution)/shard_map/all_gather | solution.py:2394
  954.5 11.6 %all-gather.6 = bf16[96,24,128]{2,1,0:T(8,128)(2,1)} all-gather(bf16[24,24,128]{2,1,0:T(8,128)(2,1)S(1)} %pad_maximum_fusion), channel_id=9, replica_groups=mesh['crop'=4,'z'=4,'core'=2] {'crop'}, dimensions={0}, use_global_device_ids=true | all-gather | bytes 737280 | tf_op jit(solution)/shard_map/all_gather | solution.py:2393
  966.1 5.9 gradient_share.1
  972.1 16.7 %all-to-all-done.27 = bf16[4,8,256,128]{3,2,1,0:T(8,128)(2,1)} async-done(((bf16[4,8,256,128]{3,2,1,0:T(8,128)(2,1)}), bf16[4,8,256,128]{3,2,1,0:T(8,128)(2,1)}, u32[]{:S(2)}, u32[]{:S(2)}) %all-to-all-start.27) | async-done | bytes 2097184 | tf_op jit(solution)/shard_map/all_to_all | solution.py:1913
  992.4 14.0 %all-gather.8 = f32[64,128]{1,0:T(8,128)S(1)} all-gather(f32[8,128]{1,0:T(8,128)S(1)} %copy-done.26), channel_id=11, replica_groups=mesh['crop'=4,'z'=4,'core'=2] {'z','core'}, dimensions={0}, use_global_device_ids=true | all-gather | bytes 36864 | tf_op jit(solution)/shard_map/all_gather | solution.py:2402
  1007.7 7.5 multiply_subtract_fusion
  (160 shorter events, 110.5 us)
Async XLA Ops:
  7.2 5.3 copy-start.1
  7.2 31.0 %all-to-all-start = ((bf16[4,8,256,128]{3,2,1,0:T(8,128)(2,1)}), bf16[4,8,256,128]{3,2,1,0:T(8,128)(2,1)}, u32[]{:S(2)}, u32[]{:S(2)}) async-start(bf16[4,8,256,128]{3,2,1,0:T(8,128)(2,1)} %bitcast.71), calls=%async_computation | async-start | bytes 4194304 | tf_op jit(solution)/shard_map/all_to_all | solution.py:1913
  12.5 43.2 %all-gather.16.cloned.1.call-start = ((), (), s32[]{:S(2)}) async-start(), calls=%async_computation.32 | async-start | bytes 1327104 | tf_op jit(solution)/shard_map/all_gather | solution.py:2274
  21.8 22.1 %copy-start.31 = (u32[32]{0:T(128)S(1)}, u32[32]{0:T(128)}, u32[]{:S(2)}) copy-start(u32[32]{0:T(128)} %constant.133) | copy-start | bytes 388
  21.9 32.3 %copy-start.17 = (bf16[128,24,128]{2,1,0:T(8,128)(2,1)S(1)}, bf16[128,24,128]{2,1,0:T(8,128)(2,1)}, u32[]{:S(2)}) copy-start(bf16[128,24,128]{2,1,0:T(8,128)(2,1)} %parameter_runs.1) | copy-start | bytes 2359300
  38.2 52.7 %all-to-all-start.1 = ((bf16[4,8,256,128]{3,2,1,0:T(8,128)(2,1)}), bf16[4,8,256,128]{3,2,1,0:T(8,128)(2,1)S(1)}, u32[]{:S(2)}, u32[]{:S(2)}) async-start(bf16[4,8,256,128]{3,2,1,0:T(8,128)(2,1)} %all-to-all-done), calls=%async_computation.1 | async-start | bytes 4194304 | tf_op jit(solution)/shard_map/all_to_all | solution.py:1913
  43.3 164.1 %all-gather.18.cloned.1.call-start = ((), (), s32[]{:S(2)}) async-start(), calls=%async_computation.33 | async-start | bytes 5806080 | tf_op jit(solution)/shard_map/all_gather | solution.py:2333
  55.7 35.2 %copy-start.28 = (f32[256]{0:T(256)S(1)}, f32[256]{0:T(256)}, u32[]{:S(2)}) copy-start(f32[256]{0:T(256)} %constant.118.clone) | copy-start | bytes 3076
  90.9 1.9 copy-start.7
  162.8 3.8 copy-start.24
  162.8 3.8 copy-start.25
  162.8 4.5 copy-start.27
  162.8 19.0 %all-to-all-start.3 = ((bf16[8,16,16,256]{3,2,1,0:T(8,128)(2,1)}), bf16[8,16,16,256]{3,2,1,0:T(8,128)(2,1)S(1)}, u32[]{:S(2)}, u32[]{:S(2)}) async-start(bf16[8,16,16,256]{3,2,1,0:T(8,128)(2,1)} %get-tuple-element.180), calls=%async_computation.3 | async-start | bytes 2097152 | tf_op jit(solution)/shard_map/all_to_all | solution.py:1913
  166.5 75.9 %all-gather.20.cloned.1.call-start = ((), (), s32[]{:S(2)}) async-start(), calls=%async_computation.34 | async-start | bytes 1622016 | tf_op jit(solution)/shard_map/all_gather | solution.py:2338
  181.9 4.0 copy-start.13
  181.9 20.8 %all-to-all-start.4 = ((bf16[8,16,16,256]{3,2,1,0:T(8,128)(2,1)}), bf16[8,16,16,256]{3,2,1,0:T(8,128)(2,1)S(1)}, u32[]{:S(2)}, u32[]{:S(2)}) async-start(bf16[8,16,16,256]{3,2,1,0:T(8,128)(2,1)} %get-tuple-element.181), calls=%async_computation.4 | async-start | bytes 2097152 | tf_op jit(solution)/shard_map/all_to_all | solution.py:1913
  202.7 1.0 copy-start.12
  203.6 33.1 %all-to-all-start.5 = ((bf16[8,2,16,16,256]{4,3,2,1,0:T(8,128)(2,1)}), bf16[8,2,16,16,256]{4,3,2,1,0:T(8,128)(2,1)S(1)}, u32[]{:S(2)}, u32[]{:S(2)}) async-start(bf16[8,2,16,16,256]{4,3,2,1,0:T(8,128)(2,1)} %get-tuple-element.191), calls=%async_computation.5 | async-start | bytes 4194304 | tf_op jit(solution)/shard_map/all_to_all | solution.py:1913
  236.7 1.3 copy-start.8
  238.1 34.3 %all-to-all-start.6 = ((bf16[8,2,16,16,256]{4,3,2,1,0:T(8,128)(2,1)}), bf16[8,2,16,16,256]{4,3,2,1,0:T(8,128)(2,1)}, u32[]{:S(2)}, u32[]{:S(2)}) async-start(bf16[8,2,16,16,256]{4,3,2,1,0:T(8,128)(2,1)} %get-tuple-element.193), calls=%async_computation.6 | async-start | bytes 4194304 | tf_op jit(solution)/shard_map/all_to_all | solution.py:1913
  278.7 4.5 copy-start.6
  278.7 31.1 %all-to-all-start.7 = ((bf16[8,16,32,256]{3,2,1,0:T(8,128)(2,1)}), bf16[8,16,32,256]{3,2,1,0:T(8,128)(2,1)}, u32[]{:S(2)}, u32[]{:S(2)}) async-start(bf16[8,16,32,256]{3,2,1,0:T(8,128)(2,1)} %incoming_product.1), calls=%async_computation.7 | async-start | bytes 4194304 | tf_op jit(solution)/shard_map/all_to_all | solution.py:1913
  283.2 4.8 copy-start.2
  287.1 39.3 %copy-start.29 = (f32[32]{0:T(128)}, f32[32]{0:T(128)S(1)}, u32[]{:S(2)}) copy-start(f32[32]{0:T(128)S(1)} %multiply_reduce_fusion.2) | copy-start | bytes 388
  288.3 22.3 %copy-start.16 = (f32[32,1536]{1,0:T(8,128)}, f32[32,1536]{1,0:T(8,128)S(1)}, u32[]{:S(2)}) copy-start(f32[32,1536]{1,0:T(8,128)S(1)} %fusion.8.project) | copy-start | bytes 589828
  310.6 28.0 %all-to-all-start.8 = ((bf16[8,32,768]{2,1,0:T(8,128)(2,1)}), bf16[8,32,768]{2,1,0:T(8,128)(2,1)S(1)}, u32[]{:S(2)}, u32[]{:S(2)}) async-start(bf16[8,32,768]{2,1,0:T(8,128)(2,1)} %broadcast_in_dim.33), calls=%async_computation.8 | async-start | bytes 786432 | tf_op jit(solution)/shard_map/all_to_all | solution.py:1913
  338.6 0.8 copy-start.10
  339.4 30.2 %all-to-all-start.9 = ((bf16[8,32,32,128]{3,2,1,0:T(8,128)(2,1)}), bf16[8,32,32,128]{3,2,1,0:T(8,128)(2,1)S(1)}, u32[]{:S(2)}, u32[]{:S(2)}) async-start(bf16[8,32,32,128]{3,2,1,0:T(8,128)(2,1)} %bitcast.68), calls=%async_computation.9 | async-start | bytes 4194304 | tf_op jit(solution)/shard_map/all_to_all | solution.py:1913
  369.5 4.5 copy-start.19
  369.5 39.6 %all-to-all-start.10 = ((bf16[8,32,32,128]{3,2,1,0:T(8,128)(2,1)}), bf16[8,32,32,128]{3,2,1,0:T(8,128)(2,1)}, u32[]{:S(2)}, u32[]{:S(2)}) async-start(bf16[8,32,32,128]{3,2,1,0:T(8,128)(2,1)} %get-tuple-element.214), calls=%async_computation.10 | async-start | bytes 4194304 | tf_op jit(solution)/shard_map/all_to_all | solution.py:1913
  407.4 1.4 copy-start.3
  408.8 57.0 %collective-permute-start = (bf16[1,2,32,32,128]{4,3,2,1,0:T(8,128)(2,1)}, bf16[1,2,32,32,128]{4,3,2,1,0:T(8,128)(2,1)}, u32[]{:S(2)}, u32[]{:S(2)}) collective-permute-start(bf16[1,2,32,32,128]{4,3,2,1,0:T(8,128)(2,1)} %get-tuple-element.348), channel_id=1, source_target_pairs={{0,2},{2,4},{4,6},{6,0},{1,3},{3,5},{5,7},{7,1},{8,10},{10,12},{12... | collective-permute-start | bytes 1572872 | tf_op jit(solution)/shard_map/ppermute | solution.py:1967
  440.4 10.3 %all-to-all-start.11 = ((bf16[8,32,512]{2,1,0:T(8,128)(2,1)}), bf16[8,32,512]{2,1,0:T(8,128)(2,1)S(1)}, u32[]{:S(2)}, u32[]{:S(2)}) async-start(bf16[8,32,512]{2,1,0:T(8,128)(2,1)} %get-tuple-element.226), calls=%async_computation.11 | async-start | bytes 524288 | tf_op jit(solution)/shard_map/all_to_all | solution.py:1913
  443.9 27.3 %collective-permute-start.1 = (bf16[1,2,32,32,128]{4,3,2,1,0:T(8,128)(2,1)}, bf16[1,2,32,32,128]{4,3,2,1,0:T(8,128)(2,1)}, u32[]{:S(2)}, u32[]{:S(2)}) collective-permute-start(bf16[1,2,32,32,128]{4,3,2,1,0:T(8,128)(2,1)} %get-tuple-element.347), channel_id=1, source_target_pairs={{0,4},{2,6},{4,0},{6,2},{1,5},{3,7},{5,1},{7,3},{8,12},{10,14},{12... | collective-permute-start | bytes 1572872 | tf_op jit(solution)/shard_map/ppermute | solution.py:1967
  446.3 26.0 %collective-permute-start.2 = (bf16[1,2,32,32,128]{4,3,2,1,0:T(8,128)(2,1)}, bf16[1,2,32,32,128]{4,3,2,1,0:T(8,128)(2,1)}, u32[]{:S(2)}, u32[]{:S(2)}) collective-permute-start(bf16[1,2,32,32,128]{4,3,2,1,0:T(8,128)(2,1)} %get-tuple-element.346), channel_id=1, source_target_pairs={{0,6},{2,0},{4,2},{6,4},{1,7},{3,1},{5,3},{7,5},{8,14},{10,8},{12,... | collective-permute-start | bytes 1572872 | tf_op jit(solution)/shard_map/ppermute | solution.py:1967
  450.7 0.7 copy-start.11
  451.4 14.3 %copy-start.4 = (bf16[4,2,32,32,128]{4,3,2,1,0:T(8,128)(2,1)S(1)}, bf16[4,2,32,32,128]{4,3,2,1,0:T(8,128)(2,1)}, u32[]{:S(2)}) copy-start(bf16[4,2,32,32,128]{4,3,2,1,0:T(8,128)(2,1)} %copy-done.3) | copy-start | bytes 6291460
  461.5 15.4 %all-to-all-start.12 = ((bf16[8,32,1280]{2,1,0:T(8,128)(2,1)}), bf16[8,32,1280]{2,1,0:T(8,128)(2,1)}, u32[]{:S(2)}, u32[]{:S(2)}) async-start(bf16[8,32,1280]{2,1,0:T(8,128)(2,1)} %get-tuple-element.230), calls=%async_computation.12 | async-start | bytes 1310720 | tf_op jit(solution)/shard_map/all_to_all | solution.py:1913
  473.4 3.5 copy-start.5
  476.9 73.6 %all-to-all-start.13 = ((bf16[4,64,32,128]{3,2,1,0:T(8,128)(2,1)}), bf16[4,64,32,128]{3,2,1,0:T(8,128)(2,1)S(1)}, u32[]{:S(2)}, u32[]{:S(2)}) async-start(bf16[4,64,32,128]{3,2,1,0:T(8,128)(2,1)} %bitcast.79), calls=%async_computation.13 | async-start | bytes 4194304 | tf_op jit(solution)/shard_map/all_to_all | solution.py:1913
  519.0 35.7 %copy-start.21 = (f32[32,384]{1,0:T(8,128)S(1)}, f32[32,384]{1,0:T(8,128)}, u32[]{:S(2)}) copy-start(f32[32,384]{1,0:T(8,128)} %get-tuple-element.244) | copy-start | bytes 147460
  519.0 35.7 %copy-start.20 = (f32[32,384]{1,0:T(8,128)S(1)}, f32[32,384]{1,0:T(8,128)}, u32[]{:S(2)}) copy-start(f32[32,384]{1,0:T(8,128)} %get-tuple-element.245) | copy-start | bytes 147460
  550.5 24.7 %copy-start = (bf16[4,64,32,128]{3,2,1,0:T(8,128)(2,1)}, bf16[4,64,32,128]{3,2,1,0:T(8,128)(2,1)S(1)}, u32[]{:S(2)}) copy-start(bf16[4,64,32,128]{3,2,1,0:T(8,128)(2,1)S(1)} %all-to-all-done.13) | copy-start | bytes 6291460
  550.5 13.9 %all-to-all-start.14 = ((bf16[8,4,32,256]{3,2,1,0:T(8,128)(2,1)}), bf16[8,4,32,256]{3,2,1,0:T(8,128)(2,1)}, u32[]{:S(2)}, u32[]{:S(2)}) async-start(bf16[8,4,32,256]{3,2,1,0:T(8,128)(2,1)} %get-tuple-element.243), calls=%async_computation.14 | async-start | bytes 1048576 | tf_op jit(solution)/shard_map/all_to_all | solution.py:1913
  575.2 35.9 %all-to-all-start.15 = ((bf16[8,32,32,128]{3,2,1,0:T(8,128)(2,1)}), bf16[8,32,32,128]{3,2,1,0:T(8,128)(2,1)S(1)}, u32[]{:S(2)}, u32[]{:S(2)}) async-start(bf16[8,32,32,128]{3,2,1,0:T(8,128)(2,1)} %get-tuple-element.251), calls=%async_computation.15 | async-start | bytes 4194304 | tf_op jit(solution)/shard_map/all_to_all | solution.py:1913
  578.8 184.9 %reduce-scatter.2.cloned.1.call-start = ((), (), s32[]{:S(2)}) async-start(), calls=%async_computation.30 | async-start | bytes 5271552 | tf_op jit(solution)/shard_map/reduce_scatter | solution.py:2366
  611.1 1.3 copy-start.9
  612.4 36.1 %all-to-all-start.16 = ((bf16[8,32,32,128]{3,2,1,0:T(8,128)(2,1)}), bf16[8,32,32,128]{3,2,1,0:T(8,128)(2,1)S(1)}, u32[]{:S(2)}, u32[]{:S(2)}) async-start(bf16[8,32,32,128]{3,2,1,0:T(8,128)(2,1)} %bitcast.67), calls=%async_computation.16 | async-start | bytes 4194304 | tf_op jit(solution)/shard_map/all_to_all | solution.py:1913
  677.8 21.5 %all-to-all-start.18 = ((bf16[8,16,16,256]{3,2,1,0:T(8,128)(2,1)}), bf16[8,16,16,256]{3,2,1,0:T(8,128)(2,1)S(1)}, u32[]{:S(2)}, u32[]{:S(2)}) async-start(bf16[8,16,16,256]{3,2,1,0:T(8,128)(2,1)} %bitcast.89), calls=%async_computation.18 | async-start | bytes 2097152 | tf_op jit(solution)/shard_map/all_to_all | solution.py:1913
  699.3 20.7 %copy-start.15 = (bf16[8,16,16,256]{3,2,1,0:T(8,128)(2,1)}, bf16[8,16,16,256]{3,2,1,0:T(8,128)(2,1)S(1)}, u32[]{:S(2)}) copy-start(bf16[8,16,16,256]{3,2,1,0:T(8,128)(2,1)S(1)} %all-to-all-done.18.refs_0_) | copy-start | bytes 3145732
  727.4 4.5 copy-start.30
  727.4 4.7 copy-start.22
  727.4 4.8 copy-start.23
  727.4 31.2 %all-to-all-start.20 = ((bf16[8,2,16,16,256]{4,3,2,1,0:T(8,128)(2,1)}), bf16[8,2,16,16,256]{4,3,2,1,0:T(8,128)(2,1)}, u32[]{:S(2)}, u32[]{:S(2)}) async-start(bf16[8,2,16,16,256]{4,3,2,1,0:T(8,128)(2,1)} %get-tuple-element.282), calls=%async_computation.20 | async-start | bytes 4194304 | tf_op jit(solution)/shard_map/all_to_all | solution.py:1913
  758.6 31.4 %all-to-all-start.21 = ((bf16[8,2,16,16,256]{4,3,2,1,0:T(8,128)(2,1)}), bf16[8,2,16,16,256]{4,3,2,1,0:T(8,128)(2,1)}, u32[]{:S(2)}, u32[]{:S(2)}) async-start(bf16[8,2,16,16,256]{4,3,2,1,0:T(8,128)(2,1)} %get-tuple-element.283), calls=%async_computation.21 | async-start | bytes 4194304 | tf_op jit(solution)/shard_map/all_to_all | solution.py:1913
  763.0 65.5 %all-gather.14.cloned.1.call-start = ((), (), s32[]{:S(2)}) async-start(), calls=%async_computation.31 | async-start | bytes 1622016 | tf_op jit(solution)/shard_map/all_gather | solution.py:2352
  790.0 23.9 %all-to-all-start.22 = ((bf16[8,16,16,256]{3,2,1,0:T(8,128)(2,1)}), bf16[8,16,16,256]{3,2,1,0:T(8,128)(2,1)S(1)}, u32[]{:S(2)}, u32[]{:S(2)}) async-start(bf16[8,16,16,256]{3,2,1,0:T(8,128)(2,1)} %bitcast.88), calls=%async_computation.23 | async-start | bytes 2097152 | tf_op jit(solution)/shard_map/all_to_all | solution.py:1913
  813.9 13.5 %copy-start.14 = (bf16[8,16,16,256]{3,2,1,0:T(8,128)(2,1)}, bf16[8,16,16,256]{3,2,1,0:T(8,128)(2,1)S(1)}, u32[]{:S(2)}) copy-start(bf16[8,16,16,256]{3,2,1,0:T(8,128)(2,1)S(1)} %all-to-all-done.22.refs_0_) | copy-start | bytes 3145732
  813.9 19.9 %all-to-all-start.23 = ((bf16[8,16,16,256]{3,2,1,0:T(8,128)(2,1)}), bf16[8,16,16,256]{3,2,1,0:T(8,128)(2,1)}, u32[]{:S(2)}, u32[]{:S(2)}) async-start(bf16[8,16,16,256]{3,2,1,0:T(8,128)(2,1)} %bitcast.87), calls=%async_computation.24 | async-start | bytes 2097152 | tf_op jit(solution)/shard_map/all_to_all | solution.py:1913
  894.6 31.3 %all-to-all-start.25 = ((bf16[8,21,24,128]{3,2,1,0:T(8,128)(2,1)}), bf16[8,21,24,128]{3,2,1,0:T(8,128)(2,1)S(1)}, u32[]{:S(2)}, u32[]{:S(2)}) async-start(bf16[8,21,24,128]{3,2,1,0:T(8,128)(2,1)} %pair_gradient.1), calls=%async_computation.26 | async-start | bytes 2064384 | tf_op jit(solution)/shard_map/all_to_all | solution.py:1913
  936.2 52.6 %all-to-all-start.27 = ((bf16[4,8,256,128]{3,2,1,0:T(8,128)(2,1)}), bf16[4,8,256,128]{3,2,1,0:T(8,128)(2,1)}, u32[]{:S(2)}, u32[]{:S(2)}) async-start(bf16[4,8,256,128]{3,2,1,0:T(8,128)(2,1)} %bitcast.81), calls=%async_computation.28 | async-start | bytes 4194304 | tf_op jit(solution)/shard_map/all_to_all | solution.py:1913
  940.6 1.9 copy-start.18
  972.1 20.3 %copy-start.26 = (f32[8,128]{1,0:T(8,128)S(1)}, f32[8,128]{1,0:T(8,128)}, u32[]{:S(2)}) copy-start(f32[8,128]{1,0:T(8,128)} %get-tuple-element.335) | copy-start | bytes 12292
  988.7 27.9 %all-to-all-start.28 = ((bf16[4,8,256,128]{3,2,1,0:T(8,128)(2,1)}), bf16[4,8,256,128]{3,2,1,0:T(8,128)(2,1)S(1)}, u32[]{:S(2)}, u32[]{:S(2)}) async-start(bf16[4,8,256,128]{3,2,1,0:T(8,128)(2,1)} %all-to-all-done.27), calls=%async_computation.29 | async-start | bytes 4194304 | tf_op jit(solution)/shard_map/all_to_all | solution.py:1913
Sparse Core Ops, SparseCore 0:
  22.0 25.1 all-gather.15
  91.1 54.5 all-gather.17
  171.0 63.1 all-gather.19
  611.2 117.2 reduce-scatter.1
  767.5 60.9 all-gather.13

commit v9 on v8

--- a/solution.py
+++ b/solution.py
@@ -1506,7 +1506,7 @@
         ).astype(BF16)
         return carry
 
-    lax.fori_loop(0, shards * lanes, one, 0, unroll=4)
+    lax.fori_loop(0, shards * lanes, one, 0, unroll=16 if shards * lanes % 16 == 0 else 8)
 
 
 def row_height(base, first_lane, last_lane, total):
@@ -2183,6 +2183,7 @@
         [grad_tri, product_two], product_half,
     )
     product_grad = swap_all(product_grad)
+    between(9, grads)
     product_grad = [*meet(4, product_grad[0]), product_grad[1]]
     (
         grad_one, grad_tri, gate_back, grads[(INCOMING, PROJ_GATE)], grads[(OUTGOING, PROJ_OUT)],
@@ -2211,7 +2212,7 @@
         "outgoing_product_back", functools.partial(tri_product_back_kernel, False),
         [grad_tri, product_one], product_shape,
     )
-    (product_grad,) = swap_all(product_grad)
+    (product_grad,) = meet(6, *swap_all(product_grad))
     between(6, grads)
     pair_grad, grads[(OUTGOING, PROJ_GATE)], vecs = run_rows(
         functools.partial(tri_first_back_kernel, read_first, order_back), "outgoing_in_back", steps,
@@ -2306,8 +2307,11 @@
             others = [reduced[3]]
         elif number == 8:
             others = [single_grads[(ATTEND, QKVG)]]
+        elif number == 6:
+            values, reduced[5] = after(*values, reduced[5])
+            return [values]
         elif number == 4:
-            values, reduced[2] = after(*values, reduced[2])
+            values, reduced[2], _ = after(*values, reduced[2], reduced[4])
             return [values]
         else:
             values, held["both"], reduced[1] = after(*values, held["both"], reduced[1])
@@ -2322,6 +2326,9 @@
     late_lanes = -(-table[(OUTGOING, OUT_GAIN)][0] * STRIDE // count)
     late_end = table[(OUTGOING, GATE_OUT)][0]
     early = table[(OUTGOING, PROJ_OUT)][0]
+    attend_lanes = -(-table[(STARTING, NORM_GAIN)][0] * STRIDE // count)
+    first_row = table[(STARTING, NORM_GAIN)][0]
+    last_row = table[(STARTING, BIAS_PROJ)][0]
 
     def lines():
         values = jnp.concatenate([single_grads[name].reshape(1, S) for name in SINGLE_VECTORS], axis=0)
@@ -2365,13 +2372,23 @@
             sent = sent.reshape((devices * parts, -1) + sent.shape[2:])
             reduced[2] = lax.psum_scatter(sent, line + ("crop",), scatter_dimension=0, tiled=False)
             return
-        taken = -(-(pair_lanes * count - (attend + 2 * S // STRIDE) * STRIDE) // (4 * S))
+        vectors = [name for name in HELD if name in grads]
+        if number == 9:
+            taken = -(-(pair_lanes * count - (attend + 2 * S // STRIDE) * STRIDE) // (4 * S))
+            sent = pack(
+                "attention_gradient", table, total, devices, (attend_lanes, pair_lanes), first_row,
+                [(name, grads[name]) for name in PAIR_MATRICES if table[name][0] >= first_row]
+                + [(name, grads[name]) for name in ((STARTING, BIAS_PROJ), (ENDING, BIAS_PROJ))]
+                + [vector_part(grads, table, name, first_row, attend) for name in vectors]
+                + [(lines_held[:2], lines()), ((ATTEND, QKVG), single_grads[(ATTEND, QKVG)][: -(-taken // 8) * 8])],
+            )
+            reduced[4] = sent
+            reduced[5] = lax.psum_scatter(sent, line, scatter_dimension=0, tiled=False)
+            return
         sent = pack(
-            "pair_gradient", table, total, devices, (late_lanes, pair_lanes), early,
-            [(name, grads[name]) for name in PAIR_MATRICES if table[name][0] >= early]
-            + [(name, grads[name]) for name in ((STARTING, BIAS_PROJ), (ENDING, BIAS_PROJ))]
-            + [vector_part(grads, table, name, early, attend) for name in HELD if name in grads]
-            + [(lines_held[:2], lines()), ((ATTEND, QKVG), single_grads[(ATTEND, QKVG)][: -(-taken // 8) * 8])],
+            "pair_gradient", table, total, devices, (late_lanes, attend_lanes), early,
+            [(name, grads[name]) for name in PAIR_MATRICES if early <= table[name][0] < last_row]
+            + [vector_part(grads, table, name, early, last_row) for name in vectors],
         )
         reduced[1] = sent
 
@@ -2390,7 +2407,7 @@
     both = both[:, lax.axis_index("crop"), lax.axis_index("core"), lax.axis_index("z")]
     both = both.reshape(rows, 2 * width)
     single_out, single_grad = both[:, :width], both[:, width:].astype(F32)
-    summed = lax.all_gather(jnp.concatenate([reduced[0], reduced[1]], axis=0), "crop")
+    summed = lax.all_gather(jnp.concatenate([reduced[0], reduced[1], reduced[5]], axis=0), "crop")
     others = lax.all_gather(reduced[2], "crop")
     shard, squares = whole_call(
         functools.partial(shard_kernel, shard_size), "gradient_share",

time: 1040 us -> 1030 us (level)
  blocking collectives: 241 us -> 189 us
  waiting for transfers between devices: 193 us -> 242 us
    all_to_all x5 -> x4, blocking collectives: 152 us -> 100 us  [swap(): lax.all_to_all(values, group, split_axis=0, concat_axis=0, tiled=True)]
    all_to_all x24 -> x25, waiting for transfers between devices: 187 us -> 237 us  [swap(): lax.all_to_all(values, group, split_axis=0, concat_axis=0, tiled=True)]
    pallas_call x8 -> x9, Pallas kernels: 98.4 us -> 90.2 us  [whole_call(): pl.pallas_call(kernel, in_specs=[spec(axis) for array, axis in ins], out_...]
    all_to_all x24 -> x25, starting transfers between devices: 109 us -> 114 us  [swap(): lax.all_to_all(values, group, split_axis=0, concat_axis=0, tiled=True)]
  transfers between devices with their start and end apart: 32 -> 34, of which waited for: 19 -> 19; matrix products, arithmetic and copies ran while one was open for 4% -> 4% of each run, Pallas kernels for 38% -> 37%
where the time goes in v9:
time: 1030 us; the launch traced here: 1020 us
  Pallas kernels  404 us (39%)
  waiting for transfers between devices  242 us (23%)
  blocking collectives  189 us (18%)
  starting transfers between devices  118 us (11%)
  local copies, waits for them, and re-layouts  28.1 us (3%)
  other arithmetic  19 us (2%)
  between operations  17.5 us (2%)
    pallas_call x20, Pallas kernels, run_rows(): pl.pallas_call(run, grid=(grid,), in_specs=in_specs, out_specs=out_specs,...  314 us
    all_to_all x25, waiting for transfers between devices, swap(): lax.all_to_all(values, group, split_axis=0, concat_axis=0, tiled=True)  237 us
    all_to_all x25, starting transfers between devices, swap(): lax.all_to_all(values, group, split_axis=0, concat_axis=0, tiled=True)  114 us
    all_to_all x4, blocking collectives, swap(): lax.all_to_all(values, group, split_axis=0, concat_axis=0, tiled=True)  100 us
    pallas_call x9, Pallas kernels, whole_call(): pl.pallas_call(kernel, in_specs=[spec(axis) for array, axis in ins], out_...  90.2 us
    all_gather x1, blocking collectives, pair_path(): bias_two = lax.all_gather(bias, group, axis=0, tiled=False)  31.7 us
  transfers between devices with their start and end apart: 34, of which 19 were waited for; matrix products, arithmetic and copies ran while one was open for 4% of the time, Pallas kernels for 37%

profile of v9, /device:TPU:0, one launch (start us, length us, event | category | flops | bytes accessed | tf_op | source)
XLA Modules:
  0.0 1020.7 jit_solution(11386708809900877344)
XLA Ops:
  7.2 5.3 all-to-all-start
  14.4 5.9 parameter_runs.1
  21.9 16.3 %all-to-all-done = bf16[4,8,256,128]{3,2,1,0:T(8,128)(2,1)} async-done(((bf16[4,8,256,128]{3,2,1,0:T(8,128)(2,1)}), bf16[4,8,256,128]{3,2,1,0:T(8,128)(2,1)}, u32[]{:S(2)}, u32[]{:S(2)}) %all-to-all-start) | async-done | bytes 2097184 | tf_op jit(solution)/shard_map/all_to_all | solution.py:1913
  38.2 5.1 all-to-all-start.1
  45.3 8.9 all-reduce.2
  55.7 8.0 pair_weights.1
  63.7 27.2 %all-to-all-done.1 = bf16[4,8,256,128]{3,2,1,0:T(8,128)(2,1)S(1)} async-done(((bf16[4,8,256,128]{3,2,1,0:T(8,128)(2,1)}), bf16[4,8,256,128]{3,2,1,0:T(8,128)(2,1)S(1)}, u32[]{:S(2)}, u32[]{:S(2)}) %all-to-all-start.1) | async-done | bytes 2097184 | tf_op jit(solution)/shard_map/all_to_all | solution.py:1913
  92.9 10.2 %outgoing_in.1 = bf16[8,2,16,32,256]{4,3,2,1,0:T(8,128)(2,1)} custom-call(s32[32]{0:T(128)} %dynamic-slice_convert_fusion.refs_0_, f32[8,256]{1,0:T(8,128)} %broadcast_in_dim.32.refs_1_.refs_0_.alive, bf16[32,256,128]{2,1,0:T(8,128)(2,1)} %bitcast.75, f32[128,8]{1,0:T(8,128)} %get-tuple-element.177.refs_3_.refs_4_.refs_11_.refs_6_, ...), custom_call_target="tpu_custom_call" | custom-call | flops 12999999488 | bytes 39000000 | tf_op jit(solution)/shard_map/outgoing_in/pallas_call | solution.py:762
  103.1 53.5 %all_to_all.145.refs_0_.refs_2_ = bf16[8,2,16,32,256]{4,3,2,1,0:T(8,128)(2,1)} all-to-all(bf16[8,2,16,32,256]{4,3,2,1,0:T(8,128)(2,1)} %outgoing_in.1), channel_id=1, replica_groups=mesh['crop'=4,'z'=4,'core'=2] {'crop','core'}, dimensions={0} | all-to-all | bytes 8388608 | tf_op jit(solution)/shard_map/all_to_all | solution.py:1913
  156.6 6.2 outgoing_product.1
  167.9 14.0 %all-to-all-done.3 = bf16[8,16,16,256]{3,2,1,0:T(8,128)(2,1)S(1)} async-done(((bf16[8,16,16,256]{3,2,1,0:T(8,128)(2,1)}), bf16[8,16,16,256]{3,2,1,0:T(8,128)(2,1)S(1)}, u32[]{:S(2)}, u32[]{:S(2)}) %all-to-all-start.3) | async-done | bytes 1048608 | tf_op jit(solution)/shard_map/all_to_all | solution.py:1913
  185.8 11.1 %outgoing_out_incoming_in.2 = (f32[32,128,256]{2,1,0:T(8,128)}, bf16[8,2,16,16,256]{4,3,2,1,0:T(8,128)(2,1)}) custom-call(s32[16]{0:T(128)} %get-tuple-element.359.refs_0_, f32[8,256]{1,0:T(8,128)} %broadcast_in_dim.32.refs_1_.refs_0_.alive, bf16[32,256,128]{2,1,0:T(8,128)(2,1)} %bitcast.76, bf16[128,16,256]{2,1,0:T(8,128)(2,1)} %bitcast.87, ...), custom_call_target="tpu_custom_call" | custom-call | flops 11000000512 | bytes 33000000 | tf_op jit(solution)/shard_map/outgoing_out_incoming_in/pallas_call | solution.py:762
  196.9 5.6 all-to-all-done.4
  207.6 11.1 %outgoing_out_incoming_in.3 = (f32[32,128,256]{2,1,0:T(8,128)}, bf16[8,2,16,16,256]{4,3,2,1,0:T(8,128)(2,1)}) custom-call(s32[16]{0:T(128)} %get-tuple-element.360.refs_0_, f32[8,256]{1,0:T(8,128)} %broadcast_in_dim.32.refs_1_.refs_0_.alive, bf16[32,256,128]{2,1,0:T(8,128)(2,1)} %bitcast.77, ...), custom_call_target="tpu_custom_call", output_to_operand_aliasing={{0}: (9, {})} | custom-call | flops 11000000512 | bytes 33000000 | tf_op jit(solution)/shard_map/outgoing_out_incoming_in/pallas_call | solution.py:762
  218.8 18.2 %all-to-all-done.5.refs_0_.refs_2_ = bf16[8,2,16,16,256]{4,3,2,1,0:T(8,128)(2,1)S(1)} async-done(((bf16[8,2,16,16,256]{4,3,2,1,0:T(8,128)(2,1)}), bf16[8,2,16,16,256]{4,3,2,1,0:T(8,128)(2,1)S(1)}, u32[]{:S(2)}, u32[]{:S(2)}) %all-to-all-start.5) | async-done | bytes 2097184 | tf_op jit(solution)/shard_map/all_to_all | solution.py:1913
  238.2 4.4 all-to-all-start.6
  244.2 28.4 %single_weights.1 = (bf16[384,1536]{1,0:T(8,128)(2,1)}, bf16[384,384]{1,0:T(8,128)(2,1)}, bf16[384,3072]{1,0:T(8,128)(2,1)}, bf16[1536,384]{1,0:T(8,128)(2,1)}, ...) custom-call(bf16[8,105,24,128]{3,2,1,0:T(8,128)(2,1)} %bitcast.105), custom_call_target="tpu_custom_call" | custom-call | flops 8000000000 | bytes 24000000 | tf_op jit(solution)/shard_map/single_weights/pallas_call | solution.py:1692
  272.6 6.3 incoming_product.1
  278.8 4.5 all-to-all-start.7
  288.5 21.5 %all-to-all-done.7 = bf16[8,16,32,256]{3,2,1,0:T(8,128)(2,1)} async-done(((bf16[8,16,32,256]{3,2,1,0:T(8,128)(2,1)}), bf16[8,16,32,256]{3,2,1,0:T(8,128)(2,1)}, u32[]{:S(2)}, u32[]{:S(2)}) %all-to-all-start.7) | async-done | bytes 2097184 | tf_op jit(solution)/shard_map/all_to_all | solution.py:1913
  314.4 12.1 %incoming_out_starting_bias.1 = (f32[32,128,256]{2,1,0:T(8,128)}, bf16[4,32,256]{2,1,0:T(8,128)(2,1)}) custom-call(f32[32,128,256]{2,1,0:T(8,128)} %get-tuple-element.191.refs_0_.refs_6_.refs_2_, bf16[128,32,256]{2,1,0:T(8,128)(2,1)} %bitcast.14.refs_1_.refs_7_, f32[128,8]{1,0:T(8,128)} %get-tuple-element.188.refs_7_.refs_2_.refs_8_.refs_6_, ...), custom_call_target="tpu_custom_call" | custom-call | flops 15000000512 | bytes 45000000 | tf_op jit(solution)/shard_map/incoming_out_starting_bias/pallas_call | solution.py:762
  326.5 12.2 %all-gather.4 = bf16[32,32,256]{2,1,0:T(8,128)(2,1)} all-gather(bf16[4,32,256]{2,1,0:T(8,128)(2,1)} %get-tuple-element.208), channel_id=7, replica_groups=mesh['crop'=4,'z'=4,'core'=2] {'crop','core'}, dimensions={0}, use_global_device_ids=true | all-gather | bytes 589824 | tf_op jit(solution)/shard_map/all_gather | solution.py:2068
  343.0 20.0 %starting_attention.1 = (bf16[8,32,32,128]{3,2,1,0:T(8,128)(2,1)}, f32[32,4,256]{2,1,0:T(4,128)}, bf16[32,128,256]{2,1,0:T(8,128)(2,1)}, bf16[4,32,256]{2,1,0:T(8,128)(2,1)}) custom-call(f32[8,256]{1,0:T(8,128)} %broadcast_in_dim.32.refs_1_.refs_0_.alive, f32[32,128,256]{2,1,0:T(8,128)} %get-tuple-element.207.refs_1_.refs_0_, ...), custom_call_target="tpu_custom_call" | custom-call | flops 20999999488 | bytes 63000000 | tf_op jit(solution)/shard_map/starting_attention/pallas_call | solution.py:762
  363.0 6.6 all-to-all-done.9
  369.6 4.5 all-to-all-start.10
  374.1 31.7 %all-gather.5 = bf16[32,32,256]{2,1,0:T(8,128)(2,1)} all-gather(bf16[4,32,256]{2,1,0:T(8,128)(2,1)S(1)} %copy-done.20), channel_id=8, replica_groups=mesh['crop'=4,'z'=4,'core'=2] {'crop','core'}, dimensions={0}, use_global_device_ids=true | all-gather | bytes 589824 | tf_op jit(solution)/shard_map/all_gather | solution.py:2080
  409.1 16.6 %ending_attention.1 = (f32[32,128,256]{2,1,0:T(8,128)}, f32[32,4,256]{2,1,0:T(4,128)}, bf16[32,128,256]{2,1,0:T(8,128)(2,1)}) custom-call(f32[8,256]{1,0:T(8,128)} %broadcast_in_dim.32.refs_1_.refs_0_.alive, bf16[8,32,32,128]{3,2,1,0:T(8,128)(2,1)} %all-to-all-done.10.refs_1_.refs_0_, bf16[8,4,32,256]{3,2,1,0:T(8,128)(2,1)} %bitcast.97, ...), custom_call_target="tpu_custom_call" | custom-call | flops 1000000000 | bytes 3000000 | tf_op jit(solution)/shard_map/ending_attention/pallas_call | solution.py:762
  425.6 14.9 %pair_transition.1 = (f32[32,128,256]{2,1,0:T(8,128)}, bf16[256,32,128]{2,1,0:T(8,128)(2,1)}, bf16[8,32,512]{2,1,0:T(8,128)(2,1)}) custom-call(f32[32,128,256]{2,1,0:T(8,128)} %get-tuple-element.220.refs_0_, f32[128,8]{1,0:T(8,128)} %get-tuple-element.221.refs_1_.refs_4_, bf16[1024,128]{1,0:T(8,128)(2,1)} %get-tuple-element.222.refs_2_.refs_5_, ...), custom_call_target="tpu_custom_call" | custom-call | flops 1000000000 | bytes 3000000 | tf_op jit(solution)/shard_map/pair_transition/pallas_call | solution.py:762
  451.6 10.1 single_path.1
  467.0 4.3 collective-permute-done.1
  477.0 13.0 %all-to-all-start.13 = ((bf16[4,64,32,128]{3,2,1,0:T(8,128)(2,1)}), bf16[4,64,32,128]{3,2,1,0:T(8,128)(2,1)S(1)}, u32[]{:S(2)}, u32[]{:S(2)}) async-start(bf16[4,64,32,128]{3,2,1,0:T(8,128)(2,1)} %bitcast.81), calls=%async_computation.13 | async-start | bytes 4194304 | tf_op jit(solution)/shard_map/all_to_all | solution.py:1913
  490.0 28.8 %pair_transition_back.1 = (f32[32,128,256]{2,1,0:T(8,128)}, f32[128,1024]{1,0:T(8,128)}, f32[512,128]{1,0:T(8,128)}, f32[128,16]{1,0:T(8,128)}, f32[8,128]{1,0:T(8,128)}) custom-call(f32[32,128,256]{2,1,0:T(8,128)} %get-tuple-element.220.refs_0_, f32[32,128,256]{2,1,0:T(8,128)} %get-tuple-element.234.refs_1_, bf16[8,32,32,128]{3,2,1,0:T(8,128)(2,1)} %bitcast.72, ...), custom_call_target="tpu_custom_call" | custom-call | flops 30000001024 | bytes 90000000 | tf_op jit(solution)/shard_map/pair_transition_back/pallas_call | solution.py:762
  518.9 31.4 %attention_back.2 = (bf16[32,128,256]{2,1,0:T(8,128)(2,1)}, bf16[8,4,32,256]{3,2,1,0:T(8,128)(2,1)}, f32[128,512]{1,0:T(8,128)}, f32[128,128]{1,0:T(8,128)}) custom-call(f32[8,256]{1,0:T(8,128)} %broadcast_in_dim.32.refs_1_.refs_0_.alive, bf16[8,32,32,128]{3,2,1,0:T(8,128)(2,1)} %all-to-all-done.10.refs_1_.refs_0_, ...), custom_call_target="tpu_custom_call" | custom-call | flops 33999998976 | bytes 102000000 | tf_op jit(solution)/shard_map/attention_back/pallas_call | solution.py:762
  557.6 6.6 all-to-all-done.14.refs_3_
  564.3 10.7 %ending_attention_end.1 = (bf16[8,32,32,128]{3,2,1,0:T(8,128)(2,1)}, f32[128,8]{1,0:T(8,128)}, f32[8,128]{1,0:T(8,128)}) custom-call(bf16[8,32,32,128]{3,2,1,0:T(8,128)(2,1)} %all-to-all-done.10.refs_1_.refs_0_, f32[32,128,256]{2,1,0:T(8,128)} %get-tuple-element.238.refs_2_.refs_1_, bf16[32,128,256]{2,1,0:T(8,128)(2,1)} %get-tuple-element.243.refs_2_, ...), custom_call_target="tpu_custom_call" | custom-call | flops 15000000512 | bytes 45000000 | tf_op jit(solution)/shard_map/ending_attention_end/pallas_call | solution.py:762
  580.6 21.9 %single_gradient.1 = bf16[8,104,24,128]{3,2,1,0:T(8,128)(2,1)} custom-call(f32[384,1536]{1,0:T(8,128)} %fusion.2.refs_0_, f32[384,384]{1,0:T(8,128)} %get-tuple-element.255.refs_1_, f32[384,3072]{1,0:T(8,128)} %get-tuple-element.256.refs_2_, f32[1536,384]{1,0:T(8,128)} %get-tuple-element.257.refs_3_, f32[128,16]{1,0:T(8,128)} %get-tuple-element.258.refs_4_, ...), custom_call_target="tpu_custom_call" | custom-call | flops 8000000000 | bytes 24000000 | tf_op jit(solution)/shard_map/single_gradient/pallas_call | solution.py:1692
  610.1 32.1 %attention_back.3 = (bf16[32,128,256]{2,1,0:T(8,128)(2,1)}, bf16[8,4,32,256]{3,2,1,0:T(8,128)(2,1)}, f32[128,512]{1,0:T(8,128)}, f32[128,128]{1,0:T(8,128)}) custom-call(f32[8,256]{1,0:T(8,128)} %broadcast_in_dim.32.refs_1_.refs_0_.alive, f32[32,128,256]{2,1,0:T(8,128)} %get-tuple-element.207.refs_1_.refs_0_, bf16[8,32,32,128]{3,2,1,0:T(8,128)(2,1)} %copy-done.9, ...), custom_call_target="tpu_custom_call" | custom-call | flops 33999998976 | bytes 102000000 | tf_op jit(solution)/shard_map/attention_back/pallas_call | solution.py:762
  642.2 14.0 %all_to_all.146.refs_3_ = bf16[8,4,32,256]{3,2,1,0:T(8,128)(2,1)} all-to-all(bf16[8,4,32,256]{3,2,1,0:T(8,128)(2,1)} %get-tuple-element.268), channel_id=1, replica_groups=mesh['crop'=4,'z'=4,'core'=2] {'crop','core'}, dimensions={0} | all-to-all | bytes 1048576 | tf_op jit(solution)/shard_map/all_to_all | solution.py:1913
  656.2 15.2 %starting_end_incoming_out_back.2 = (f32[32,128,256]{2,1,0:T(8,128)}, bf16[128,16,256]{2,1,0:T(8,128)(2,1)}, bf16[32,128,256]{2,1,0:T(8,128)(2,1)}, f32[128,8]{1...) custom-call(f32[32,128,256]{2,1,0:T(8,128)} %get-tuple-element.207.refs_1_.refs_0_, ...), custom_call_target="tpu_custom_call" | custom-call | flops 12999999488 | bytes 39000000 | tf_op jit(solution)/shard_map/starting_end_incoming_out_back/pallas_call | solution.py:762
  675.1 15.2 %starting_end_incoming_out_back.3 = (f32[32,128,256]{2,1,0:T(8,128)}, bf16[128,16,256]{2,1,0:T(8,128)(2,1)}, bf16[32,128,256]{2,1,0:T(8,128)(2,1)}, f32[128,8]{1...) custom-call(f32[32,128,256]{2,1,0:T(8,128)} %get-tuple-element.207.r, ...), custom_call_target="tpu_custom_call", output_to_operand_aliasing={{0}: (13, {}), {2}: (14, {}), {3}: (15, {}), {4}: (16, {}),... | custom-call | flops 12999999488 | bytes 39000000 | tf_op jit(solution)/shard_map/starting_end_incoming_out_back/pallas_call | solution.py:762
  692.8 20.7 %all_to_all.147.refs_1_ = bf16[8,16,16,256]{3,2,1,0:T(8,128)(2,1)} all-to-all(bf16[8,16,16,256]{3,2,1,0:T(8,128)(2,1)} %bitcast.92), channel_id=1, replica_groups=mesh['crop'=4,'z'=4,'core'=2] {'crop','core'}, dimensions={0} | all-to-all | bytes 2097152 | tf_op jit(solution)/shard_map/all_to_all | solution.py:1913
  713.5 7.3 incoming_product_back.1
  720.9 4.5 all-to-all-start.20
  728.0 24.4 %all-to-all-done.20.refs_3_ = bf16[8,2,16,16,256]{4,3,2,1,0:T(8,128)(2,1)} async-done(((bf16[8,2,16,16,256]{4,3,2,1,0:T(8,128)(2,1)}), bf16[8,2,16,16,256]{4,3,2,1,0:T(8,128)(2,1)}, u32[]{:S(2)}, u32[]{:S(2)}) %all-to-all-start.20) | async-done | bytes 2097184 | tf_op jit(solution)/shard_map/all_to_all | solution.py:1913
  752.4 4.6 all-to-all-start.21
  757.0 5.1 attention_gradient.1
  762.1 19.7 %incoming_in_outgoing_out_back.2 = (f32[32,128,256]{2,1,0:T(8,128)}, bf16[128,16,256]{2,1,0:T(8,128)(2,1)}, bf16[32,128,256]{2,1,0:T(8,128)(2,1)}, f32[128,512]{...) custom-call(s32[16]{0:T(128)} %get-tuple-element.359.refs_0_, ...), custom_call_target="tpu_custom_call" | custom-call | flops 18499999744 | bytes 55500000 | tf_op jit(solution)/shard_map/incoming_in_outgoing_out_back/pallas_call | solution.py:762
  781.9 5.6 all-to-all-done.21.refs_3_
  791.4 19.9 %incoming_in_outgoing_out_back.3 = (f32[32,128,256]{2,1,0:T(8,128)}, bf16[128,16,256]{2,1,0:T(8,128)(2,1)}, bf16[32,128,256]{2,1,0:T(8,128)(2,1)}, f32[128,512]{...) custom-call(s32[16]{0:T(128)} %get-tuple-element.360.refs_0_, ...), custom_call_target="tpu_custom_call", output_to_operand_aliasing={{0}: (16, {}), {2}: (17, {}), {3}: (18, {}), {4}: (19, {}),... | custom-call | flops 18499999744 | bytes 55500000 | tf_op jit(solution)/shard_map/incoming_in_outgoing_out_back/pallas_call | solution.py:762
  811.3 4.3 all-to-all-start.23
  818.3 12.7 %all-to-all-done.23.refs_1_ = bf16[8,16,16,256]{3,2,1,0:T(8,128)(2,1)} async-done(((bf16[8,16,16,256]{3,2,1,0:T(8,128)(2,1)}), bf16[8,16,16,256]{3,2,1,0:T(8,128)(2,1)}, u32[]{:S(2)}, u32[]{:S(2)}) %all-to-all-start.23) | async-done | bytes 1048608 | tf_op jit(solution)/shard_map/all_to_all | solution.py:1913
  831.0 7.3 outgoing_product_back.1
  838.3 4.7 all-to-all-start.24
  843.6 48.5 %all-to-all-done.24.refs_3_ = bf16[8,2,16,32,256]{4,3,2,1,0:T(8,128)(2,1)} async-done(((bf16[8,2,16,32,256]{4,3,2,1,0:T(8,128)(2,1)}), bf16[8,2,16,32,256]{4,3,2,1,0:T(8,128)(2,1)}, u32[]{:S(2)}, u32[]{:S(2)}) %all-to-all-start.24) | async-done | bytes 4194336 | tf_op jit(solution)/shard_map/all_to_all | solution.py:1913
  892.1 5.5 all-to-all-start.25
  897.7 17.6 %outgoing_in_back.1 = (bf16[32,256,128]{2,1,0:T(8,128)(2,1)}, f32[128,512]{1,0:T(8,128)}, f32[8,128]{1,0:T(8,128)}) custom-call(s32[32]{0:T(128)} %dynamic-slice_convert_fusion.refs_0_, f32[8,256]{1,0:T(8,128)} %broadcast_in_dim.32.refs_1_.refs_0_.alive, bf16[32,256,128]{2,1,0:T(8,128)(2,1)} %bitcast.80, ...), custom_call_target="tpu_custom_call" | custom-call | flops 20000000000 | bytes 60000000 | tf_op jit(solution)/shard_map/outgoing_in_back/pallas_call | solution.py:762
  917.5 12.1 %all_to_all.148 = bf16[8,3,24,128]{3,2,1,0:T(8,128)(2,1)S(1)} all-to-all(bf16[8,3,24,128]{3,2,1,0:T(8,128)(2,1)} %outgoing_gradient.1), channel_id=1, replica_groups=mesh['crop'=4,'z'=4,'core'=2] {'z','core'}, dimensions={0} | all-to-all | bytes 294912 | tf_op jit(solution)/shard_map/all_to_all | solution.py:1913
  929.6 4.5 all-to-all-start.27
  936.0 10.3 %all-gather.7 = bf16[104,24,128]{2,1,0:T(8,128)(2,1)} all-gather(bf16[26,24,128]{2,1,0:T(8,128)(2,1)S(1)} %bitcast.99), channel_id=10, replica_groups=mesh['crop'=4,'z'=4,'core'=2] {'crop'}, dimensions={0}, use_global_device_ids=true | all-gather | bytes 798720 | tf_op jit(solution)/shard_map/all_gather | solution.py:2411
  947.8 11.7 %all-gather.6 = bf16[96,24,128]{2,1,0:T(8,128)(2,1)} all-gather(bf16[24,24,128]{2,1,0:T(8,128)(2,1)S(1)} %pad_maximum_fusion), channel_id=9, replica_groups=mesh['crop'=4,'z'=4,'core'=2] {'crop'}, dimensions={0}, use_global_device_ids=true | all-gather | bytes 737280 | tf_op jit(solution)/shard_map/all_gather | solution.py:2410
  959.5 5.9 gradient_share.1
  965.4 16.7 %all-to-all-done.27 = bf16[4,8,256,128]{3,2,1,0:T(8,128)(2,1)} async-done(((bf16[4,8,256,128]{3,2,1,0:T(8,128)(2,1)}), bf16[4,8,256,128]{3,2,1,0:T(8,128)(2,1)}, u32[]{:S(2)}, u32[]{:S(2)}) %all-to-all-start.27) | async-done | bytes 2097184 | tf_op jit(solution)/shard_map/all_to_all | solution.py:1913
  985.8 14.0 %all-gather.8 = f32[64,128]{1,0:T(8,128)S(1)} all-gather(f32[8,128]{1,0:T(8,128)S(1)} %copy-done.27), channel_id=11, replica_groups=mesh['crop'=4,'z'=4,'core'=2] {'z','core'}, dimensions={0}, use_global_device_ids=true | all-gather | bytes 36864 | tf_op jit(solution)/shard_map/all_gather | solution.py:2419
  1001.1 7.5 multiply_subtract_fusion
  (167 shorter events, 114.5 us)
Async XLA Ops:
  7.2 5.3 copy-start.1
  7.2 31.0 %all-to-all-start = ((bf16[4,8,256,128]{3,2,1,0:T(8,128)(2,1)}), bf16[4,8,256,128]{3,2,1,0:T(8,128)(2,1)}, u32[]{:S(2)}, u32[]{:S(2)}) async-start(bf16[4,8,256,128]{3,2,1,0:T(8,128)(2,1)} %bitcast.73), calls=%async_computation | async-start | bytes 4194304 | tf_op jit(solution)/shard_map/all_to_all | solution.py:1913
  12.5 43.2 %all-gather.16.cloned.1.call-start = ((), (), s32[]{:S(2)}) async-start(), calls=%async_computation.33 | async-start | bytes 1327104 | tf_op jit(solution)/shard_map/all_gather | solution.py:2275
  21.9 22.1 %copy-start.32 = (u32[32]{0:T(128)S(1)}, u32[32]{0:T(128)}, u32[]{:S(2)}) copy-start(u32[32]{0:T(128)} %constant.133) | copy-start | bytes 388
  21.9 32.3 %copy-start.17 = (bf16[128,24,128]{2,1,0:T(8,128)(2,1)S(1)}, bf16[128,24,128]{2,1,0:T(8,128)(2,1)}, u32[]{:S(2)}) copy-start(bf16[128,24,128]{2,1,0:T(8,128)(2,1)} %parameter_runs.1) | copy-start | bytes 2359300
  38.2 52.7 %all-to-all-start.1 = ((bf16[4,8,256,128]{3,2,1,0:T(8,128)(2,1)}), bf16[4,8,256,128]{3,2,1,0:T(8,128)(2,1)S(1)}, u32[]{:S(2)}, u32[]{:S(2)}) async-start(bf16[4,8,256,128]{3,2,1,0:T(8,128)(2,1)} %all-to-all-done), calls=%async_computation.1 | async-start | bytes 4194304 | tf_op jit(solution)/shard_map/all_to_all | solution.py:1913
  43.3 164.3 %all-gather.18.cloned.1.call-start = ((), (), s32[]{:S(2)}) async-start(), calls=%async_computation.34 | async-start | bytes 5806080 | tf_op jit(solution)/shard_map/all_gather | solution.py:2340
  55.7 35.2 %copy-start.29 = (f32[256]{0:T(256)S(1)}, f32[256]{0:T(256)}, u32[]{:S(2)}) copy-start(f32[256]{0:T(256)} %constant.118.clone) | copy-start | bytes 3076
  90.9 1.9 copy-start.7
  162.8 3.8 copy-start.25
  162.8 3.8 copy-start.26
  162.8 4.5 copy-start.28
  162.9 19.0 %all-to-all-start.3 = ((bf16[8,16,16,256]{3,2,1,0:T(8,128)(2,1)}), bf16[8,16,16,256]{3,2,1,0:T(8,128)(2,1)S(1)}, u32[]{:S(2)}, u32[]{:S(2)}) async-start(bf16[8,16,16,256]{3,2,1,0:T(8,128)(2,1)} %get-tuple-element.182), calls=%async_computation.3 | async-start | bytes 2097152 | tf_op jit(solution)/shard_map/all_to_all | solution.py:1913
  166.6 76.1 %all-gather.20.cloned.1.call-start = ((), (), s32[]{:S(2)}) async-start(), calls=%async_computation.35 | async-start | bytes 1622016 | tf_op jit(solution)/shard_map/all_gather | solution.py:2345
  181.9 3.9 copy-start.13
  181.9 20.6 %all-to-all-start.4 = ((bf16[8,16,16,256]{3,2,1,0:T(8,128)(2,1)}), bf16[8,16,16,256]{3,2,1,0:T(8,128)(2,1)S(1)}, u32[]{:S(2)}, u32[]{:S(2)}) async-start(bf16[8,16,16,256]{3,2,1,0:T(8,128)(2,1)} %get-tuple-element.183), calls=%async_computation.4 | async-start | bytes 2097152 | tf_op jit(solution)/shard_map/all_to_all | solution.py:1913
  203.5 33.5 %all-to-all-start.5 = ((bf16[8,2,16,16,256]{4,3,2,1,0:T(8,128)(2,1)}), bf16[8,2,16,16,256]{4,3,2,1,0:T(8,128)(2,1)S(1)}, u32[]{:S(2)}, u32[]{:S(2)}) async-start(bf16[8,2,16,16,256]{4,3,2,1,0:T(8,128)(2,1)} %get-tuple-element.193), calls=%async_computation.5 | async-start | bytes 4194304 | tf_op jit(solution)/shard_map/all_to_all | solution.py:1913
  236.9 1.3 copy-start.8
  238.2 34.3 %all-to-all-start.6 = ((bf16[8,2,16,16,256]{4,3,2,1,0:T(8,128)(2,1)}), bf16[8,2,16,16,256]{4,3,2,1,0:T(8,128)(2,1)}, u32[]{:S(2)}, u32[]{:S(2)}) async-start(bf16[8,2,16,16,256]{4,3,2,1,0:T(8,128)(2,1)} %get-tuple-element.195), calls=%async_computation.6 | async-start | bytes 4194304 | tf_op jit(solution)/shard_map/all_to_all | solution.py:1913
  278.8 4.5 copy-start.6
  278.8 31.1 %all-to-all-start.7 = ((bf16[8,16,32,256]{3,2,1,0:T(8,128)(2,1)}), bf16[8,16,32,256]{3,2,1,0:T(8,128)(2,1)}, u32[]{:S(2)}, u32[]{:S(2)}) async-start(bf16[8,16,32,256]{3,2,1,0:T(8,128)(2,1)} %incoming_product.1), calls=%async_computation.7 | async-start | bytes 4194304 | tf_op jit(solution)/shard_map/all_to_all | solution.py:1913
  283.3 4.8 copy-start.2
  287.3 39.2 %copy-start.30 = (f32[32]{0:T(128)}, f32[32]{0:T(128)S(1)}, u32[]{:S(2)}) copy-start(f32[32]{0:T(128)S(1)} %multiply_reduce_fusion.2) | copy-start | bytes 388
  288.5 22.3 %copy-start.16 = (f32[32,1536]{1,0:T(8,128)}, f32[32,1536]{1,0:T(8,128)S(1)}, u32[]{:S(2)}) copy-start(f32[32,1536]{1,0:T(8,128)S(1)} %fusion.8.project) | copy-start | bytes 589828
  310.7 27.9 %all-to-all-start.8 = ((bf16[8,32,768]{2,1,0:T(8,128)(2,1)}), bf16[8,32,768]{2,1,0:T(8,128)(2,1)S(1)}, u32[]{:S(2)}, u32[]{:S(2)}) async-start(bf16[8,32,768]{2,1,0:T(8,128)(2,1)} %broadcast_in_dim.33), calls=%async_computation.8 | async-start | bytes 786432 | tf_op jit(solution)/shard_map/all_to_all | solution.py:1913
  339.4 30.2 %all-to-all-start.9 = ((bf16[8,32,32,128]{3,2,1,0:T(8,128)(2,1)}), bf16[8,32,32,128]{3,2,1,0:T(8,128)(2,1)S(1)}, u32[]{:S(2)}, u32[]{:S(2)}) async-start(bf16[8,32,32,128]{3,2,1,0:T(8,128)(2,1)} %bitcast.70), calls=%async_computation.9 | async-start | bytes 4194304 | tf_op jit(solution)/shard_map/all_to_all | solution.py:1913
  369.6 4.5 copy-start.20
  369.6 39.4 %all-to-all-start.10 = ((bf16[8,32,32,128]{3,2,1,0:T(8,128)(2,1)}), bf16[8,32,32,128]{3,2,1,0:T(8,128)(2,1)}, u32[]{:S(2)}, u32[]{:S(2)}) async-start(bf16[8,32,32,128]{3,2,1,0:T(8,128)(2,1)} %get-tuple-element.216), calls=%async_computation.10 | async-start | bytes 4194304 | tf_op jit(solution)/shard_map/all_to_all | solution.py:1913
  407.5 1.3 copy-start.3
  408.9 57.0 %collective-permute-start = (bf16[1,2,32,32,128]{4,3,2,1,0:T(8,128)(2,1)}, bf16[1,2,32,32,128]{4,3,2,1,0:T(8,128)(2,1)}, u32[]{:S(2)}, u32[]{:S(2)}) collective-permute-start(bf16[1,2,32,32,128]{4,3,2,1,0:T(8,128)(2,1)} %get-tuple-element.352), channel_id=1, source_target_pairs={{0,2},{2,4},{4,6},{6,0},{1,3},{3,5},{5,7},{7,1},{8,10},{10,12},{12... | collective-permute-start | bytes 1572872 | tf_op jit(solution)/shard_map/ppermute | solution.py:1967
  440.6 10.3 %all-to-all-start.11 = ((bf16[8,32,512]{2,1,0:T(8,128)(2,1)}), bf16[8,32,512]{2,1,0:T(8,128)(2,1)S(1)}, u32[]{:S(2)}, u32[]{:S(2)}) async-start(bf16[8,32,512]{2,1,0:T(8,128)(2,1)} %get-tuple-element.228), calls=%async_computation.11 | async-start | bytes 524288 | tf_op jit(solution)/shard_map/all_to_all | solution.py:1913
  444.0 27.3 %collective-permute-start.1 = (bf16[1,2,32,32,128]{4,3,2,1,0:T(8,128)(2,1)}, bf16[1,2,32,32,128]{4,3,2,1,0:T(8,128)(2,1)}, u32[]{:S(2)}, u32[]{:S(2)}) collective-permute-start(bf16[1,2,32,32,128]{4,3,2,1,0:T(8,128)(2,1)} %get-tuple-element.351), channel_id=1, source_target_pairs={{0,4},{2,6},{4,0},{6,2},{1,5},{3,7},{5,1},{7,3},{8,12},{10,14},{12... | collective-permute-start | bytes 1572872 | tf_op jit(solution)/shard_map/ppermute | solution.py:1967
  446.2 26.2 %collective-permute-start.2 = (bf16[1,2,32,32,128]{4,3,2,1,0:T(8,128)(2,1)}, bf16[1,2,32,32,128]{4,3,2,1,0:T(8,128)(2,1)}, u32[]{:S(2)}, u32[]{:S(2)}) collective-permute-start(bf16[1,2,32,32,128]{4,3,2,1,0:T(8,128)(2,1)} %get-tuple-element.350), channel_id=1, source_target_pairs={{0,6},{2,0},{4,2},{6,4},{1,7},{3,1},{5,3},{7,5},{8,14},{10,8},{12,... | collective-permute-start | bytes 1572872 | tf_op jit(solution)/shard_map/ppermute | solution.py:1967
  451.6 14.3 %copy-start.4 = (bf16[4,2,32,32,128]{4,3,2,1,0:T(8,128)(2,1)S(1)}, bf16[4,2,32,32,128]{4,3,2,1,0:T(8,128)(2,1)}, u32[]{:S(2)}) copy-start(bf16[4,2,32,32,128]{4,3,2,1,0:T(8,128)(2,1)} %copy-done.3) | copy-start | bytes 6291460
  461.7 15.4 %all-to-all-start.12 = ((bf16[8,32,1280]{2,1,0:T(8,128)(2,1)}), bf16[8,32,1280]{2,1,0:T(8,128)(2,1)}, u32[]{:S(2)}, u32[]{:S(2)}) async-start(bf16[8,32,1280]{2,1,0:T(8,128)(2,1)} %get-tuple-element.232), calls=%async_computation.12 | async-start | bytes 1310720 | tf_op jit(solution)/shard_map/all_to_all | solution.py:1913
  473.5 3.5 copy-start.5
  477.0 73.3 %all-to-all-start.13 = ((bf16[4,64,32,128]{3,2,1,0:T(8,128)(2,1)}), bf16[4,64,32,128]{3,2,1,0:T(8,128)(2,1)S(1)}, u32[]{:S(2)}, u32[]{:S(2)}) async-start(bf16[4,64,32,128]{3,2,1,0:T(8,128)(2,1)} %bitcast.81), calls=%async_computation.13 | async-start | bytes 4194304 | tf_op jit(solution)/shard_map/all_to_all | solution.py:1913
  518.9 35.7 %copy-start.22 = (f32[32,384]{1,0:T(8,128)S(1)}, f32[32,384]{1,0:T(8,128)}, u32[]{:S(2)}) copy-start(f32[32,384]{1,0:T(8,128)} %get-tuple-element.246) | copy-start | bytes 147460
  518.9 35.7 %copy-start.21 = (f32[32,384]{1,0:T(8,128)S(1)}, f32[32,384]{1,0:T(8,128)}, u32[]{:S(2)}) copy-start(f32[32,384]{1,0:T(8,128)} %get-tuple-element.247) | copy-start | bytes 147460
  550.3 24.6 %copy-start = (bf16[4,64,32,128]{3,2,1,0:T(8,128)(2,1)}, bf16[4,64,32,128]{3,2,1,0:T(8,128)(2,1)S(1)}, u32[]{:S(2)}) copy-start(bf16[4,64,32,128]{3,2,1,0:T(8,128)(2,1)S(1)} %all-to-all-done.13) | copy-start | bytes 6291460
  550.3 13.9 %all-to-all-start.14 = ((bf16[8,4,32,256]{3,2,1,0:T(8,128)(2,1)}), bf16[8,4,32,256]{3,2,1,0:T(8,128)(2,1)}, u32[]{:S(2)}, u32[]{:S(2)}) async-start(bf16[8,4,32,256]{3,2,1,0:T(8,128)(2,1)} %get-tuple-element.245), calls=%async_computation.14 | async-start | bytes 1048576 | tf_op jit(solution)/shard_map/all_to_all | solution.py:1913
  575.0 30.2 %all-to-all-start.15 = ((bf16[8,32,32,128]{3,2,1,0:T(8,128)(2,1)}), bf16[8,32,32,128]{3,2,1,0:T(8,128)(2,1)S(1)}, u32[]{:S(2)}, u32[]{:S(2)}) async-start(bf16[8,32,32,128]{3,2,1,0:T(8,128)(2,1)} %get-tuple-element.253), calls=%async_computation.15 | async-start | bytes 4194304 | tf_op jit(solution)/shard_map/all_to_all | solution.py:1913
  578.6 183.5 %reduce-scatter.5.cloned.1.call-start = ((), (), s32[]{:S(2)}) async-start(), calls=%async_computation.31 | async-start | bytes 5271552 | tf_op jit(solution)/shard_map/reduce_scatter | solution.py:2373
  605.2 1.3 copy-start.9
  606.5 35.7 %all-to-all-start.16 = ((bf16[8,32,32,128]{3,2,1,0:T(8,128)(2,1)}), bf16[8,32,32,128]{3,2,1,0:T(8,128)(2,1)S(1)}, u32[]{:S(2)}, u32[]{:S(2)}) async-start(bf16[8,32,32,128]{3,2,1,0:T(8,128)(2,1)} %bitcast.69), calls=%async_computation.16 | async-start | bytes 4194304 | tf_op jit(solution)/shard_map/all_to_all | solution.py:1913
  671.4 21.4 %all-to-all-start.18 = ((bf16[8,16,16,256]{3,2,1,0:T(8,128)(2,1)}), bf16[8,16,16,256]{3,2,1,0:T(8,128)(2,1)S(1)}, u32[]{:S(2)}, u32[]{:S(2)}) async-start(bf16[8,16,16,256]{3,2,1,0:T(8,128)(2,1)} %bitcast.91), calls=%async_computation.18 | async-start | bytes 2097152 | tf_op jit(solution)/shard_map/all_to_all | solution.py:1913
  692.8 20.7 %copy-start.15 = (bf16[8,16,16,256]{3,2,1,0:T(8,128)(2,1)}, bf16[8,16,16,256]{3,2,1,0:T(8,128)(2,1)S(1)}, u32[]{:S(2)}) copy-start(bf16[8,16,16,256]{3,2,1,0:T(8,128)(2,1)S(1)} %all-to-all-done.18.refs_0_) | copy-start | bytes 3145732
  720.9 6.1 copy-start.31
  720.9 6.3 copy-start.23
  720.9 6.3 copy-start.24
  720.9 31.5 %all-to-all-start.20 = ((bf16[8,2,16,16,256]{4,3,2,1,0:T(8,128)(2,1)}), bf16[8,2,16,16,256]{4,3,2,1,0:T(8,128)(2,1)}, u32[]{:S(2)}, u32[]{:S(2)}) async-start(bf16[8,2,16,16,256]{4,3,2,1,0:T(8,128)(2,1)} %get-tuple-element.284), calls=%async_computation.20 | async-start | bytes 4194304 | tf_op jit(solution)/shard_map/all_to_all | solution.py:1913
  725.4 92.9 %all-gather.14.cloned.1.call-start = ((), (), s32[]{:S(2)}) async-start(), calls=%async_computation.32 | async-start | bytes 1622016 | tf_op jit(solution)/shard_map/all_gather | solution.py:2359
  752.4 35.0 %all-to-all-start.21 = ((bf16[8,2,16,16,256]{4,3,2,1,0:T(8,128)(2,1)}), bf16[8,2,16,16,256]{4,3,2,1,0:T(8,128)(2,1)}, u32[]{:S(2)}, u32[]{:S(2)}) async-start(bf16[8,2,16,16,256]{4,3,2,1,0:T(8,128)(2,1)} %get-tuple-element.285), calls=%async_computation.21 | async-start | bytes 4194304 | tf_op jit(solution)/shard_map/all_to_all | solution.py:1913
  787.4 23.9 %all-to-all-start.22 = ((bf16[8,16,16,256]{3,2,1,0:T(8,128)(2,1)}), bf16[8,16,16,256]{3,2,1,0:T(8,128)(2,1)S(1)}, u32[]{:S(2)}, u32[]{:S(2)}) async-start(bf16[8,16,16,256]{3,2,1,0:T(8,128)(2,1)} %bitcast.90), calls=%async_computation.23 | async-start | bytes 2097152 | tf_op jit(solution)/shard_map/all_to_all | solution.py:1913
  811.3 7.0 copy-start.14
  811.3 19.7 %all-to-all-start.23 = ((bf16[8,16,16,256]{3,2,1,0:T(8,128)(2,1)}), bf16[8,16,16,256]{3,2,1,0:T(8,128)(2,1)}, u32[]{:S(2)}, u32[]{:S(2)}) async-start(bf16[8,16,16,256]{3,2,1,0:T(8,128)(2,1)} %bitcast.89), calls=%async_computation.24 | async-start | bytes 2097152 | tf_op jit(solution)/shard_map/all_to_all | solution.py:1913
  838.3 53.9 %all-to-all-start.24 = ((bf16[8,2,16,32,256]{4,3,2,1,0:T(8,128)(2,1)}), bf16[8,2,16,32,256]{4,3,2,1,0:T(8,128)(2,1)}, u32[]{:S(2)}, u32[]{:S(2)}) async-start(bf16[8,2,16,32,256]{4,3,2,1,0:T(8,128)(2,1)} %outgoing_product_back.1), calls=%async_computation.25 | async-start | bytes 8388608 | tf_op jit(solution)/shard_map/all_to_all | solution.py:1913
  843.0 49.1 %reduce-scatter.7.cloned.1.call-start = ((), (), s32[]{:S(2)}) async-start(), calls=%async_computation.36 | async-start | bytes 829440
  892.1 25.3 %all-to-all-start.25 = ((bf16[8,6,24,128]{3,2,1,0:T(8,128)(2,1)}), bf16[8,6,24,128]{3,2,1,0:T(8,128)(2,1)S(1)}, u32[]{:S(2)}, u32[]{:S(2)}) async-start(bf16[8,6,24,128]{3,2,1,0:T(8,128)(2,1)} %pair_gradient.1), calls=%async_computation.26 | async-start | bytes 589824 | tf_op jit(solution)/shard_map/all_to_all | solution.py:1913
  929.6 52.6 %all-to-all-start.27 = ((bf16[4,8,256,128]{3,2,1,0:T(8,128)(2,1)}), bf16[4,8,256,128]{3,2,1,0:T(8,128)(2,1)}, u32[]{:S(2)}, u32[]{:S(2)}) async-start(bf16[4,8,256,128]{3,2,1,0:T(8,128)(2,1)} %bitcast.83), calls=%async_computation.28 | async-start | bytes 4194304 | tf_op jit(solution)/shard_map/all_to_all | solution.py:1913
  934.0 2.0 copy-start.18
  934.0 13.7 %copy-start.19 = (bf16[1,15,24,128]{3,2,1,0:T(8,128)(2,1)S(1)}, bf16[1,15,24,128]{3,2,1,0:T(8,128)(2,1)}, u32[]{:S(2)}) copy-start(bf16[1,15,24,128]{3,2,1,0:T(8,128)(2,1)} %reduce-scatter.7.cloned.1.call-done) | copy-start | bytes 276484
  965.4 20.4 %copy-start.27 = (f32[8,128]{1,0:T(8,128)S(1)}, f32[8,128]{1,0:T(8,128)}, u32[]{:S(2)}) copy-start(f32[8,128]{1,0:T(8,128)} %get-tuple-element.339) | copy-start | bytes 12292
  982.1 27.9 %all-to-all-start.28 = ((bf16[4,8,256,128]{3,2,1,0:T(8,128)(2,1)}), bf16[4,8,256,128]{3,2,1,0:T(8,128)(2,1)S(1)}, u32[]{:S(2)}, u32[]{:S(2)}) async-start(bf16[4,8,256,128]{3,2,1,0:T(8,128)(2,1)} %all-to-all-done.27), calls=%async_computation.29 | async-start | bytes 4194304 | tf_op jit(solution)/shard_map/all_to_all | solution.py:1913
  (3 other events, 2.5 us)
Sparse Core Ops, SparseCore 0:
  22.0 25.2 all-gather.15
  91.1 54.5 all-gather.17
  171.0 63.0 all-gather.19
  602.7 119.1 reduce-scatter.4
  730.0 66.8 all-gather.13
  845.9 33.9 reduce-scatter.6

commit v10 on v9

--- a/solution.py
+++ b/solution.py
@@ -2182,9 +2182,9 @@
         "incoming_product_back", functools.partial(tri_product_back_kernel, True),
         [grad_tri, product_two], product_half,
     )
-    product_grad = swap_all(product_grad)
+    arrived = send(product_grad[0], group)
     between(9, grads)
-    product_grad = [*meet(4, product_grad[0]), product_grad[1]]
+    product_grad = [*meet(4, arrived), send(*meet(7, product_grad[1]), group)]
     (
         grad_one, grad_tri, gate_back, grads[(INCOMING, PROJ_GATE)], grads[(OUTGOING, PROJ_OUT)],
         grads[(OUTGOING, GATE_OUT)], vecs,
@@ -2311,8 +2311,10 @@
             values, reduced[5] = after(*values, reduced[5])
             return [values]
         elif number == 4:
-            values, reduced[2], _ = after(*values, reduced[2], reduced[4])
+            values, reduced[2] = after(*values, reduced[2])
             return [values]
+        elif number == 7:
+            others = [reduced[4]]
         else:
             values, held["both"], reduced[1] = after(*values, held["both"], reduced[1])
             return [values]

time: 1030 us -> 1020 us (level)
    all_to_all x25, waiting for transfers between devices: 237 us -> 225 us  [swap(): lax.all_to_all(values, group, split_axis=0, concat_axis=0, tiled=True)]
  transfers between devices with their start and end apart: 34 -> 34, of which waited for: 19 -> 20; matrix products, arithmetic and copies ran while one was open for 4% -> 4% of each run, Pallas kernels for 37% -> 37%
where the time goes in v10:
time: 1020 us
  Pallas kernels  404 us (40%)
  waiting for transfers between devices  238 us (23%)
  blocking collectives  189 us (19%)
  starting transfers between devices  118 us (12%)
  local copies, waits for them, and re-layouts  28.1 us (3%)
  other arithmetic  19 us (2%)
  between operations  17.5 us (2%)
    pallas_call x20, Pallas kernels, run_rows(): pl.pallas_call(run, grid=(grid,), in_specs=in_specs, out_specs=out_specs,...  314 us
    all_to_all x25, waiting for transfers between devices, swap(): lax.all_to_all(values, group, split_axis=0, concat_axis=0, tiled=True)  225 us
    all_to_all x25, starting transfers between devices, swap(): lax.all_to_all(values, group, split_axis=0, concat_axis=0, tiled=True)  113 us
    all_to_all x4, blocking collectives, swap(): lax.all_to_all(values, group, split_axis=0, concat_axis=0, tiled=True)  100 us
    pallas_call x9, Pallas kernels, whole_call(): pl.pallas_call(kernel, in_specs=[spec(axis) for array, axis in ins], out_...  90.2 us
    all_gather x1, blocking collectives, pair_path(): bias_two = lax.all_gather(bias, group, axis=0, tiled=False)  31.7 us
  transfers between devices with their start and end apart: 34, of which 20 were waited for; matrix products, arithmetic and copies ran while one was open for 4% of the time, Pallas kernels for 37%

profile of v10, /device:TPU:0, one launch (start us, length us, event | category | flops | bytes accessed | tf_op | source)
XLA Modules:
  0.0 1016.4 jit_solution(14515944350299454079)
XLA Ops:
  7.2 5.3 all-to-all-start
  14.4 5.9 parameter_runs.1
  21.9 16.3 %all-to-all-done = bf16[4,8,256,128]{3,2,1,0:T(8,128)(2,1)} async-done(((bf16[4,8,256,128]{3,2,1,0:T(8,128)(2,1)}), bf16[4,8,256,128]{3,2,1,0:T(8,128)(2,1)}, u32[]{:S(2)}, u32[]{:S(2)}) %all-to-all-start) | async-done | bytes 2097184 | tf_op jit(solution)/shard_map/all_to_all | solution.py:1913
  38.2 5.1 all-to-all-start.1
  45.3 8.9 all-reduce.2
  55.7 8.0 pair_weights.1
  63.7 27.2 %all-to-all-done.1 = bf16[4,8,256,128]{3,2,1,0:T(8,128)(2,1)S(1)} async-done(((bf16[4,8,256,128]{3,2,1,0:T(8,128)(2,1)}), bf16[4,8,256,128]{3,2,1,0:T(8,128)(2,1)S(1)}, u32[]{:S(2)}, u32[]{:S(2)}) %all-to-all-start.1) | async-done | bytes 2097184 | tf_op jit(solution)/shard_map/all_to_all | solution.py:1913
  92.9 10.2 %outgoing_in.1 = bf16[8,2,16,32,256]{4,3,2,1,0:T(8,128)(2,1)} custom-call(s32[32]{0:T(128)} %dynamic-slice_convert_fusion.refs_0_, f32[8,256]{1,0:T(8,128)} %broadcast_in_dim.32.refs_1_.refs_0_.alive, bf16[32,256,128]{2,1,0:T(8,128)(2,1)} %bitcast.75, f32[128,8]{1,0:T(8,128)} %get-tuple-element.178.refs_3_.refs_4_.refs_11_.refs_6_, ...), custom_call_target="tpu_custom_call" | custom-call | flops 12999999488 | bytes 39000000 | tf_op jit(solution)/shard_map/outgoing_in/pallas_call | solution.py:762
  103.1 53.5 %all_to_all.145.refs_0_.refs_2_ = bf16[8,2,16,32,256]{4,3,2,1,0:T(8,128)(2,1)} all-to-all(bf16[8,2,16,32,256]{4,3,2,1,0:T(8,128)(2,1)} %outgoing_in.1), channel_id=1, replica_groups=mesh['crop'=4,'z'=4,'core'=2] {'crop','core'}, dimensions={0} | all-to-all | bytes 8388608 | tf_op jit(solution)/shard_map/all_to_all | solution.py:1913
  156.6 6.2 outgoing_product.1
  167.9 14.0 %all-to-all-done.3 = bf16[8,16,16,256]{3,2,1,0:T(8,128)(2,1)S(1)} async-done(((bf16[8,16,16,256]{3,2,1,0:T(8,128)(2,1)}), bf16[8,16,16,256]{3,2,1,0:T(8,128)(2,1)S(1)}, u32[]{:S(2)}, u32[]{:S(2)}) %all-to-all-start.3) | async-done | bytes 1048608 | tf_op jit(solution)/shard_map/all_to_all | solution.py:1913
  185.8 11.1 %outgoing_out_incoming_in.2 = (f32[32,128,256]{2,1,0:T(8,128)}, bf16[8,2,16,16,256]{4,3,2,1,0:T(8,128)(2,1)}) custom-call(s32[16]{0:T(128)} %get-tuple-element.361.refs_0_, f32[8,256]{1,0:T(8,128)} %broadcast_in_dim.32.refs_1_.refs_0_.alive, bf16[32,256,128]{2,1,0:T(8,128)(2,1)} %bitcast.76, bf16[128,16,256]{2,1,0:T(8,128)(2,1)} %bitcast.87, ...), custom_call_target="tpu_custom_call" | custom-call | flops 11000000512 | bytes 33000000 | tf_op jit(solution)/shard_map/outgoing_out_incoming_in/pallas_call | solution.py:762
  196.9 5.6 all-to-all-done.4
  207.6 11.1 %outgoing_out_incoming_in.3 = (f32[32,128,256]{2,1,0:T(8,128)}, bf16[8,2,16,16,256]{4,3,2,1,0:T(8,128)(2,1)}) custom-call(s32[16]{0:T(128)} %get-tuple-element.362.refs_0_, f32[8,256]{1,0:T(8,128)} %broadcast_in_dim.32.refs_1_.refs_0_.alive, bf16[32,256,128]{2,1,0:T(8,128)(2,1)} %bitcast.77, ...), custom_call_target="tpu_custom_call", output_to_operand_aliasing={{0}: (9, {})} | custom-call | flops 11000000512 | bytes 33000000 | tf_op jit(solution)/shard_map/outgoing_out_incoming_in/pallas_call | solution.py:762
  218.8 18.2 %all-to-all-done.5.refs_0_.refs_2_ = bf16[8,2,16,16,256]{4,3,2,1,0:T(8,128)(2,1)S(1)} async-done(((bf16[8,2,16,16,256]{4,3,2,1,0:T(8,128)(2,1)}), bf16[8,2,16,16,256]{4,3,2,1,0:T(8,128)(2,1)S(1)}, u32[]{:S(2)}, u32[]{:S(2)}) %all-to-all-start.5) | async-done | bytes 2097184 | tf_op jit(solution)/shard_map/all_to_all | solution.py:1913
  238.2 4.4 all-to-all-start.6
  244.2 28.4 %single_weights.1 = (bf16[384,1536]{1,0:T(8,128)(2,1)}, bf16[384,384]{1,0:T(8,128)(2,1)}, bf16[384,3072]{1,0:T(8,128)(2,1)}, bf16[1536,384]{1,0:T(8,128)(2,1)}, ...) custom-call(bf16[8,105,24,128]{3,2,1,0:T(8,128)(2,1)} %bitcast.105), custom_call_target="tpu_custom_call" | custom-call | flops 8000000000 | bytes 24000000 | tf_op jit(solution)/shard_map/single_weights/pallas_call | solution.py:1692
  272.6 6.3 incoming_product.1
  278.8 4.5 all-to-all-start.7
  288.5 21.5 %all-to-all-done.7 = bf16[8,16,32,256]{3,2,1,0:T(8,128)(2,1)} async-done(((bf16[8,16,32,256]{3,2,1,0:T(8,128)(2,1)}), bf16[8,16,32,256]{3,2,1,0:T(8,128)(2,1)}, u32[]{:S(2)}, u32[]{:S(2)}) %all-to-all-start.7) | async-done | bytes 2097184 | tf_op jit(solution)/shard_map/all_to_all | solution.py:1913
  314.4 12.1 %incoming_out_starting_bias.1 = (f32[32,128,256]{2,1,0:T(8,128)}, bf16[4,32,256]{2,1,0:T(8,128)(2,1)}) custom-call(f32[32,128,256]{2,1,0:T(8,128)} %get-tuple-element.192.refs_0_.refs_6_.refs_2_, bf16[128,32,256]{2,1,0:T(8,128)(2,1)} %bitcast.14.refs_1_.refs_7_, f32[128,8]{1,0:T(8,128)} %get-tuple-element.189.refs_7_.refs_2_.refs_8_.refs_6_, ...), custom_call_target="tpu_custom_call" | custom-call | flops 15000000512 | bytes 45000000 | tf_op jit(solution)/shard_map/incoming_out_starting_bias/pallas_call | solution.py:762
  326.5 12.2 %all-gather.4 = bf16[32,32,256]{2,1,0:T(8,128)(2,1)} all-gather(bf16[4,32,256]{2,1,0:T(8,128)(2,1)} %get-tuple-element.209), channel_id=7, replica_groups=mesh['crop'=4,'z'=4,'core'=2] {'crop','core'}, dimensions={0}, use_global_device_ids=true | all-gather | bytes 589824 | tf_op jit(solution)/shard_map/all_gather | solution.py:2068
  343.0 20.0 %starting_attention.1 = (bf16[8,32,32,128]{3,2,1,0:T(8,128)(2,1)}, f32[32,4,256]{2,1,0:T(4,128)}, bf16[32,128,256]{2,1,0:T(8,128)(2,1)}, bf16[4,32,256]{2,1,0:T(8,128)(2,1)}) custom-call(f32[8,256]{1,0:T(8,128)} %broadcast_in_dim.32.refs_1_.refs_0_.alive, f32[32,128,256]{2,1,0:T(8,128)} %get-tuple-element.208.refs_1_.refs_0_, ...), custom_call_target="tpu_custom_call" | custom-call | flops 20999999488 | bytes 63000000 | tf_op jit(solution)/shard_map/starting_attention/pallas_call | solution.py:762
  363.0 6.6 all-to-all-done.9
  369.6 4.5 all-to-all-start.10
  374.1 31.7 %all-gather.5 = bf16[32,32,256]{2,1,0:T(8,128)(2,1)} all-gather(bf16[4,32,256]{2,1,0:T(8,128)(2,1)S(1)} %copy-done.20), channel_id=8, replica_groups=mesh['crop'=4,'z'=4,'core'=2] {'crop','core'}, dimensions={0}, use_global_device_ids=true | all-gather | bytes 589824 | tf_op jit(solution)/shard_map/all_gather | solution.py:2080
  409.1 16.6 %ending_attention.1 = (f32[32,128,256]{2,1,0:T(8,128)}, f32[32,4,256]{2,1,0:T(4,128)}, bf16[32,128,256]{2,1,0:T(8,128)(2,1)}) custom-call(f32[8,256]{1,0:T(8,128)} %broadcast_in_dim.32.refs_1_.refs_0_.alive, bf16[8,32,32,128]{3,2,1,0:T(8,128)(2,1)} %all-to-all-done.10.refs_1_.refs_0_, bf16[8,4,32,256]{3,2,1,0:T(8,128)(2,1)} %bitcast.97, ...), custom_call_target="tpu_custom_call" | custom-call | flops 1000000000 | bytes 3000000 | tf_op jit(solution)/shard_map/ending_attention/pallas_call | solution.py:762
  425.6 14.9 %pair_transition.1 = (f32[32,128,256]{2,1,0:T(8,128)}, bf16[256,32,128]{2,1,0:T(8,128)(2,1)}, bf16[8,32,512]{2,1,0:T(8,128)(2,1)}) custom-call(f32[32,128,256]{2,1,0:T(8,128)} %get-tuple-element.221.refs_0_, f32[128,8]{1,0:T(8,128)} %get-tuple-element.222.refs_1_.refs_4_, bf16[1024,128]{1,0:T(8,128)(2,1)} %get-tuple-element.223.refs_2_.refs_5_, ...), custom_call_target="tpu_custom_call" | custom-call | flops 1000000000 | bytes 3000000 | tf_op jit(solution)/shard_map/pair_transition/pallas_call | solution.py:762
  451.6 10.1 single_path.1
  467.0 4.3 collective-permute-done.1
  477.0 13.0 %all-to-all-start.13 = ((bf16[4,64,32,128]{3,2,1,0:T(8,128)(2,1)}), bf16[4,64,32,128]{3,2,1,0:T(8,128)(2,1)S(1)}, u32[]{:S(2)}, u32[]{:S(2)}) async-start(bf16[4,64,32,128]{3,2,1,0:T(8,128)(2,1)} %bitcast.81), calls=%async_computation.13 | async-start | bytes 4194304 | tf_op jit(solution)/shard_map/all_to_all | solution.py:1913
  490.0 28.8 %pair_transition_back.1 = (f32[32,128,256]{2,1,0:T(8,128)}, f32[128,1024]{1,0:T(8,128)}, f32[512,128]{1,0:T(8,128)}, f32[128,16]{1,0:T(8,128)}, f32[8,128]{1,0:T(8,128)}) custom-call(f32[32,128,256]{2,1,0:T(8,128)} %get-tuple-element.221.refs_0_, f32[32,128,256]{2,1,0:T(8,128)} %get-tuple-element.235.refs_1_, bf16[8,32,32,128]{3,2,1,0:T(8,128)(2,1)} %bitcast.72, ...), custom_call_target="tpu_custom_call" | custom-call | flops 30000001024 | bytes 90000000 | tf_op jit(solution)/shard_map/pair_transition_back/pallas_call | solution.py:762
  518.9 31.4 %attention_back.2 = (bf16[32,128,256]{2,1,0:T(8,128)(2,1)}, bf16[8,4,32,256]{3,2,1,0:T(8,128)(2,1)}, f32[128,512]{1,0:T(8,128)}, f32[128,128]{1,0:T(8,128)}) custom-call(f32[8,256]{1,0:T(8,128)} %broadcast_in_dim.32.refs_1_.refs_0_.alive, bf16[8,32,32,128]{3,2,1,0:T(8,128)(2,1)} %all-to-all-done.10.refs_1_.refs_0_, ...), custom_call_target="tpu_custom_call" | custom-call | flops 33999998976 | bytes 102000000 | tf_op jit(solution)/shard_map/attention_back/pallas_call | solution.py:762
  557.6 6.6 all-to-all-done.14.refs_3_
  564.3 10.7 %ending_attention_end.1 = (bf16[8,32,32,128]{3,2,1,0:T(8,128)(2,1)}, f32[128,8]{1,0:T(8,128)}, f32[8,128]{1,0:T(8,128)}) custom-call(bf16[8,32,32,128]{3,2,1,0:T(8,128)(2,1)} %all-to-all-done.10.refs_1_.refs_0_, f32[32,128,256]{2,1,0:T(8,128)} %get-tuple-element.239.refs_2_.refs_1_, bf16[32,128,256]{2,1,0:T(8,128)(2,1)} %get-tuple-element.244.refs_2_, ...), custom_call_target="tpu_custom_call" | custom-call | flops 15000000512 | bytes 45000000 | tf_op jit(solution)/shard_map/ending_attention_end/pallas_call | solution.py:762
  580.6 21.9 %single_gradient.1 = bf16[8,104,24,128]{3,2,1,0:T(8,128)(2,1)} custom-call(f32[384,1536]{1,0:T(8,128)} %fusion.2.refs_0_, f32[384,384]{1,0:T(8,128)} %get-tuple-element.256.refs_1_, f32[384,3072]{1,0:T(8,128)} %get-tuple-element.257.refs_2_, f32[1536,384]{1,0:T(8,128)} %get-tuple-element.258.refs_3_, f32[128,16]{1,0:T(8,128)} %get-tuple-element.259.refs_4_, ...), custom_call_target="tpu_custom_call" | custom-call | flops 8000000000 | bytes 24000000 | tf_op jit(solution)/shard_map/single_gradient/pallas_call | solution.py:1692
  610.1 32.1 %attention_back.3 = (bf16[32,128,256]{2,1,0:T(8,128)(2,1)}, bf16[8,4,32,256]{3,2,1,0:T(8,128)(2,1)}, f32[128,512]{1,0:T(8,128)}, f32[128,128]{1,0:T(8,128)}) custom-call(f32[8,256]{1,0:T(8,128)} %broadcast_in_dim.32.refs_1_.refs_0_.alive, f32[32,128,256]{2,1,0:T(8,128)} %get-tuple-element.208.refs_1_.refs_0_, bf16[8,32,32,128]{3,2,1,0:T(8,128)(2,1)} %copy-done.9, ...), custom_call_target="tpu_custom_call" | custom-call | flops 33999998976 | bytes 102000000 | tf_op jit(solution)/shard_map/attention_back/pallas_call | solution.py:762
  642.2 14.0 %all_to_all.146.refs_3_ = bf16[8,4,32,256]{3,2,1,0:T(8,128)(2,1)} all-to-all(bf16[8,4,32,256]{3,2,1,0:T(8,128)(2,1)} %get-tuple-element.269), channel_id=1, replica_groups=mesh['crop'=4,'z'=4,'core'=2] {'crop','core'}, dimensions={0} | all-to-all | bytes 1048576 | tf_op jit(solution)/shard_map/all_to_all | solution.py:1913
  656.2 15.2 %starting_end_incoming_out_back.2 = (f32[32,128,256]{2,1,0:T(8,128)}, bf16[128,16,256]{2,1,0:T(8,128)(2,1)}, bf16[32,128,256]{2,1,0:T(8,128)(2,1)}, f32[128,8]{1...) custom-call(f32[32,128,256]{2,1,0:T(8,128)} %get-tuple-element.208.refs_1_.refs_0_, ...), custom_call_target="tpu_custom_call" | custom-call | flops 12999999488 | bytes 39000000 | tf_op jit(solution)/shard_map/starting_end_incoming_out_back/pallas_call | solution.py:762
  675.1 15.2 %starting_end_incoming_out_back.3 = (f32[32,128,256]{2,1,0:T(8,128)}, bf16[128,16,256]{2,1,0:T(8,128)(2,1)}, bf16[32,128,256]{2,1,0:T(8,128)(2,1)}, f32[128,8]{1...) custom-call(f32[32,128,256]{2,1,0:T(8,128)} %get-tuple-element.208.r, ...), custom_call_target="tpu_custom_call", output_to_operand_aliasing={{0}: (13, {}), {2}: (14, {}), {3}: (15, {}), {4}: (16, {}),... | custom-call | flops 12999999488 | bytes 39000000 | tf_op jit(solution)/shard_map/starting_end_incoming_out_back/pallas_call | solution.py:762
  692.8 20.7 %all_to_all.147.refs_1_ = bf16[8,16,16,256]{3,2,1,0:T(8,128)(2,1)} all-to-all(bf16[8,16,16,256]{3,2,1,0:T(8,128)(2,1)} %bitcast.92), channel_id=1, replica_groups=mesh['crop'=4,'z'=4,'core'=2] {'crop','core'}, dimensions={0} | all-to-all | bytes 2097152 | tf_op jit(solution)/shard_map/all_to_all | solution.py:1913
  713.5 7.4 incoming_product_back.1
  720.9 4.5 all-to-all-start.20
  727.3 5.1 attention_gradient.1
  732.5 19.7 %all-to-all-done.20.refs_3_ = bf16[8,2,16,16,256]{4,3,2,1,0:T(8,128)(2,1)} async-done(((bf16[8,2,16,16,256]{4,3,2,1,0:T(8,128)(2,1)}), bf16[8,2,16,16,256]{4,3,2,1,0:T(8,128)(2,1)}, u32[]{:S(2)}, u32[]{:S(2)}) %all-to-all-start.20) | async-done | bytes 2097184 | tf_op jit(solution)/shard_map/all_to_all | solution.py:1913
  752.1 4.3 all-to-all-start.21
  757.2 19.9 %incoming_in_outgoing_out_back.2 = (f32[32,128,256]{2,1,0:T(8,128)}, bf16[128,16,256]{2,1,0:T(8,128)(2,1)}, bf16[32,128,256]{2,1,0:T(8,128)(2,1)}, f32[128,512]{...) custom-call(s32[16]{0:T(128)} %get-tuple-element.361.refs_0_, ...), custom_call_target="tpu_custom_call" | custom-call | flops 18499999744 | bytes 55500000 | tf_op jit(solution)/shard_map/incoming_in_outgoing_out_back/pallas_call | solution.py:762
  777.1 6.3 all-to-all-done.21.refs_3_
  787.4 19.9 %incoming_in_outgoing_out_back.3 = (f32[32,128,256]{2,1,0:T(8,128)}, bf16[128,16,256]{2,1,0:T(8,128)(2,1)}, bf16[32,128,256]{2,1,0:T(8,128)(2,1)}, f32[128,512]{...) custom-call(s32[16]{0:T(128)} %get-tuple-element.362.refs_0_, ...), custom_call_target="tpu_custom_call", output_to_operand_aliasing={{0}: (16, {}), {2}: (17, {}), {3}: (18, {}), {4}: (19, {}),... | custom-call | flops 18499999744 | bytes 55500000 | tf_op jit(solution)/shard_map/incoming_in_outgoing_out_back/pallas_call | solution.py:762
  814.4 7.6 all-gather.14.cloned.1.call-done
  822.0 5.1 all-to-all-done.23.refs_1_
  827.1 7.3 outgoing_product_back.1
  834.4 4.7 all-to-all-start.24
  839.7 48.5 %all-to-all-done.24.refs_3_ = bf16[8,2,16,32,256]{4,3,2,1,0:T(8,128)(2,1)} async-done(((bf16[8,2,16,32,256]{4,3,2,1,0:T(8,128)(2,1)}), bf16[8,2,16,32,256]{4,3,2,1,0:T(8,128)(2,1)}, u32[]{:S(2)}, u32[]{:S(2)}) %all-to-all-start.24) | async-done | bytes 4194336 | tf_op jit(solution)/shard_map/all_to_all | solution.py:1913
  888.2 5.1 all-to-all-start.25
  893.3 17.6 %outgoing_in_back.1 = (bf16[32,256,128]{2,1,0:T(8,128)(2,1)}, f32[128,512]{1,0:T(8,128)}, f32[8,128]{1,0:T(8,128)}) custom-call(s32[32]{0:T(128)} %dynamic-slice_convert_fusion.refs_0_, f32[8,256]{1,0:T(8,128)} %broadcast_in_dim.32.refs_1_.refs_0_.alive, bf16[32,256,128]{2,1,0:T(8,128)(2,1)} %bitcast.80, ...), custom_call_target="tpu_custom_call" | custom-call | flops 20000000000 | bytes 60000000 | tf_op jit(solution)/shard_map/outgoing_in_back/pallas_call | solution.py:762
  913.1 12.1 %all_to_all.148 = bf16[8,3,24,128]{3,2,1,0:T(8,128)(2,1)S(1)} all-to-all(bf16[8,3,24,128]{3,2,1,0:T(8,128)(2,1)} %outgoing_gradient.1), channel_id=1, replica_groups=mesh['crop'=4,'z'=4,'core'=2] {'z','core'}, dimensions={0} | all-to-all | bytes 294912 | tf_op jit(solution)/shard_map/all_to_all | solution.py:1913
  925.2 4.5 all-to-all-start.27
  931.7 10.3 %all-gather.7 = bf16[104,24,128]{2,1,0:T(8,128)(2,1)} all-gather(bf16[26,24,128]{2,1,0:T(8,128)(2,1)S(1)} %bitcast.99), channel_id=10, replica_groups=mesh['crop'=4,'z'=4,'core'=2] {'crop'}, dimensions={0}, use_global_device_ids=true | all-gather | bytes 798720 | tf_op jit(solution)/shard_map/all_gather | solution.py:2413
  943.5 11.7 %all-gather.6 = bf16[96,24,128]{2,1,0:T(8,128)(2,1)} all-gather(bf16[24,24,128]{2,1,0:T(8,128)(2,1)S(1)} %pad_maximum_fusion), channel_id=9, replica_groups=mesh['crop'=4,'z'=4,'core'=2] {'crop'}, dimensions={0}, use_global_device_ids=true | all-gather | bytes 737280 | tf_op jit(solution)/shard_map/all_gather | solution.py:2412
  955.1 5.9 gradient_share.1
  961.1 16.7 %all-to-all-done.27 = bf16[4,8,256,128]{3,2,1,0:T(8,128)(2,1)} async-done(((bf16[4,8,256,128]{3,2,1,0:T(8,128)(2,1)}), bf16[4,8,256,128]{3,2,1,0:T(8,128)(2,1)}, u32[]{:S(2)}, u32[]{:S(2)}) %all-to-all-start.27) | async-done | bytes 2097184 | tf_op jit(solution)/shard_map/all_to_all | solution.py:1913
  981.4 14.0 %all-gather.8 = f32[64,128]{1,0:T(8,128)S(1)} all-gather(f32[8,128]{1,0:T(8,128)S(1)} %copy-done.27), channel_id=11, replica_groups=mesh['crop'=4,'z'=4,'core'=2] {'z','core'}, dimensions={0}, use_global_device_ids=true | all-gather | bytes 36864 | tf_op jit(solution)/shard_map/all_gather | solution.py:2421
  996.8 7.5 multiply_subtract_fusion
  (167 shorter events, 118.8 us)
Async XLA Ops:
  7.2 5.3 copy-start.1
  7.2 31.0 %all-to-all-start = ((bf16[4,8,256,128]{3,2,1,0:T(8,128)(2,1)}), bf16[4,8,256,128]{3,2,1,0:T(8,128)(2,1)}, u32[]{:S(2)}, u32[]{:S(2)}) async-start(bf16[4,8,256,128]{3,2,1,0:T(8,128)(2,1)} %bitcast.73), calls=%async_computation | async-start | bytes 4194304 | tf_op jit(solution)/shard_map/all_to_all | solution.py:1913
  12.5 43.2 %all-gather.16.cloned.1.call-start = ((), (), s32[]{:S(2)}) async-start(), calls=%async_computation.33 | async-start | bytes 1327104 | tf_op jit(solution)/shard_map/all_gather | solution.py:2275
  21.9 22.1 %copy-start.32 = (u32[32]{0:T(128)S(1)}, u32[32]{0:T(128)}, u32[]{:S(2)}) copy-start(u32[32]{0:T(128)} %constant.133) | copy-start | bytes 388
  21.9 32.3 %copy-start.17 = (bf16[128,24,128]{2,1,0:T(8,128)(2,1)S(1)}, bf16[128,24,128]{2,1,0:T(8,128)(2,1)}, u32[]{:S(2)}) copy-start(bf16[128,24,128]{2,1,0:T(8,128)(2,1)} %parameter_runs.1) | copy-start | bytes 2359300
  38.2 52.7 %all-to-all-start.1 = ((bf16[4,8,256,128]{3,2,1,0:T(8,128)(2,1)}), bf16[4,8,256,128]{3,2,1,0:T(8,128)(2,1)S(1)}, u32[]{:S(2)}, u32[]{:S(2)}) async-start(bf16[4,8,256,128]{3,2,1,0:T(8,128)(2,1)} %all-to-all-done), calls=%async_computation.1 | async-start | bytes 4194304 | tf_op jit(solution)/shard_map/all_to_all | solution.py:1913
  43.3 164.3 %all-gather.18.cloned.1.call-start = ((), (), s32[]{:S(2)}) async-start(), calls=%async_computation.34 | async-start | bytes 5806080 | tf_op jit(solution)/shard_map/all_gather | solution.py:2342
  55.7 35.2 %copy-start.29 = (f32[256]{0:T(256)S(1)}, f32[256]{0:T(256)}, u32[]{:S(2)}) copy-start(f32[256]{0:T(256)} %constant.118.clone) | copy-start | bytes 3076
  90.9 1.9 copy-start.7
  162.8 3.8 copy-start.25
  162.8 3.8 copy-start.26
  162.8 4.5 copy-start.28
  162.9 19.0 %all-to-all-start.3 = ((bf16[8,16,16,256]{3,2,1,0:T(8,128)(2,1)}), bf16[8,16,16,256]{3,2,1,0:T(8,128)(2,1)S(1)}, u32[]{:S(2)}, u32[]{:S(2)}) async-start(bf16[8,16,16,256]{3,2,1,0:T(8,128)(2,1)} %get-tuple-element.183), calls=%async_computation.3 | async-start | bytes 2097152 | tf_op jit(solution)/shard_map/all_to_all | solution.py:1913
  166.6 76.1 %all-gather.20.cloned.1.call-start = ((), (), s32[]{:S(2)}) async-start(), calls=%async_computation.35 | async-start | bytes 1622016 | tf_op jit(solution)/shard_map/all_gather | solution.py:2347
  181.9 3.9 copy-start.13
  181.9 20.6 %all-to-all-start.4 = ((bf16[8,16,16,256]{3,2,1,0:T(8,128)(2,1)}), bf16[8,16,16,256]{3,2,1,0:T(8,128)(2,1)S(1)}, u32[]{:S(2)}, u32[]{:S(2)}) async-start(bf16[8,16,16,256]{3,2,1,0:T(8,128)(2,1)} %get-tuple-element.184), calls=%async_computation.4 | async-start | bytes 2097152 | tf_op jit(solution)/shard_map/all_to_all | solution.py:1913
  203.5 33.5 %all-to-all-start.5 = ((bf16[8,2,16,16,256]{4,3,2,1,0:T(8,128)(2,1)}), bf16[8,2,16,16,256]{4,3,2,1,0:T(8,128)(2,1)S(1)}, u32[]{:S(2)}, u32[]{:S(2)}) async-start(bf16[8,2,16,16,256]{4,3,2,1,0:T(8,128)(2,1)} %get-tuple-element.194), calls=%async_computation.5 | async-start | bytes 4194304 | tf_op jit(solution)/shard_map/all_to_all | solution.py:1913
  236.9 1.3 copy-start.8
  238.2 34.3 %all-to-all-start.6 = ((bf16[8,2,16,16,256]{4,3,2,1,0:T(8,128)(2,1)}), bf16[8,2,16,16,256]{4,3,2,1,0:T(8,128)(2,1)}, u32[]{:S(2)}, u32[]{:S(2)}) async-start(bf16[8,2,16,16,256]{4,3,2,1,0:T(8,128)(2,1)} %get-tuple-element.196), calls=%async_computation.6 | async-start | bytes 4194304 | tf_op jit(solution)/shard_map/all_to_all | solution.py:1913
  278.8 4.5 copy-start.6
  278.8 31.1 %all-to-all-start.7 = ((bf16[8,16,32,256]{3,2,1,0:T(8,128)(2,1)}), bf16[8,16,32,256]{3,2,1,0:T(8,128)(2,1)}, u32[]{:S(2)}, u32[]{:S(2)}) async-start(bf16[8,16,32,256]{3,2,1,0:T(8,128)(2,1)} %incoming_product.1), calls=%async_computation.7 | async-start | bytes 4194304 | tf_op jit(solution)/shard_map/all_to_all | solution.py:1913
  283.3 4.8 copy-start.2
  287.3 39.2 %copy-start.30 = (f32[32]{0:T(128)}, f32[32]{0:T(128)S(1)}, u32[]{:S(2)}) copy-start(f32[32]{0:T(128)S(1)} %multiply_reduce_fusion.2) | copy-start | bytes 388
  288.5 22.3 %copy-start.16 = (f32[32,1536]{1,0:T(8,128)}, f32[32,1536]{1,0:T(8,128)S(1)}, u32[]{:S(2)}) copy-start(f32[32,1536]{1,0:T(8,128)S(1)} %fusion.8.project) | copy-start | bytes 589828
  310.7 27.9 %all-to-all-start.8 = ((bf16[8,32,768]{2,1,0:T(8,128)(2,1)}), bf16[8,32,768]{2,1,0:T(8,128)(2,1)S(1)}, u32[]{:S(2)}, u32[]{:S(2)}) async-start(bf16[8,32,768]{2,1,0:T(8,128)(2,1)} %broadcast_in_dim.33), calls=%async_computation.8 | async-start | bytes 786432 | tf_op jit(solution)/shard_map/all_to_all | solution.py:1913
  339.4 30.2 %all-to-all-start.9 = ((bf16[8,32,32,128]{3,2,1,0:T(8,128)(2,1)}), bf16[8,32,32,128]{3,2,1,0:T(8,128)(2,1)S(1)}, u32[]{:S(2)}, u32[]{:S(2)}) async-start(bf16[8,32,32,128]{3,2,1,0:T(8,128)(2,1)} %bitcast.70), calls=%async_computation.9 | async-start | bytes 4194304 | tf_op jit(solution)/shard_map/all_to_all | solution.py:1913
  369.6 4.5 copy-start.20
  369.6 39.4 %all-to-all-start.10 = ((bf16[8,32,32,128]{3,2,1,0:T(8,128)(2,1)}), bf16[8,32,32,128]{3,2,1,0:T(8,128)(2,1)}, u32[]{:S(2)}, u32[]{:S(2)}) async-start(bf16[8,32,32,128]{3,2,1,0:T(8,128)(2,1)} %get-tuple-element.217), calls=%async_computation.10 | async-start | bytes 4194304 | tf_op jit(solution)/shard_map/all_to_all | solution.py:1913
  407.5 1.3 copy-start.3
  408.9 57.0 %collective-permute-start = (bf16[1,2,32,32,128]{4,3,2,1,0:T(8,128)(2,1)}, bf16[1,2,32,32,128]{4,3,2,1,0:T(8,128)(2,1)}, u32[]{:S(2)}, u32[]{:S(2)}) collective-permute-start(bf16[1,2,32,32,128]{4,3,2,1,0:T(8,128)(2,1)} %get-tuple-element.354), channel_id=1, source_target_pairs={{0,2},{2,4},{4,6},{6,0},{1,3},{3,5},{5,7},{7,1},{8,10},{10,12},{12... | collective-permute-start | bytes 1572872 | tf_op jit(solution)/shard_map/ppermute | solution.py:1967
  440.6 10.3 %all-to-all-start.11 = ((bf16[8,32,512]{2,1,0:T(8,128)(2,1)}), bf16[8,32,512]{2,1,0:T(8,128)(2,1)S(1)}, u32[]{:S(2)}, u32[]{:S(2)}) async-start(bf16[8,32,512]{2,1,0:T(8,128)(2,1)} %get-tuple-element.229), calls=%async_computation.11 | async-start | bytes 524288 | tf_op jit(solution)/shard_map/all_to_all | solution.py:1913
  444.0 27.3 %collective-permute-start.1 = (bf16[1,2,32,32,128]{4,3,2,1,0:T(8,128)(2,1)}, bf16[1,2,32,32,128]{4,3,2,1,0:T(8,128)(2,1)}, u32[]{:S(2)}, u32[]{:S(2)}) collective-permute-start(bf16[1,2,32,32,128]{4,3,2,1,0:T(8,128)(2,1)} %get-tuple-element.353), channel_id=1, source_target_pairs={{0,4},{2,6},{4,0},{6,2},{1,5},{3,7},{5,1},{7,3},{8,12},{10,14},{12... | collective-permute-start | bytes 1572872 | tf_op jit(solution)/shard_map/ppermute | solution.py:1967
  446.2 26.2 %collective-permute-start.2 = (bf16[1,2,32,32,128]{4,3,2,1,0:T(8,128)(2,1)}, bf16[1,2,32,32,128]{4,3,2,1,0:T(8,128)(2,1)}, u32[]{:S(2)}, u32[]{:S(2)}) collective-permute-start(bf16[1,2,32,32,128]{4,3,2,1,0:T(8,128)(2,1)} %get-tuple-element.352), channel_id=1, source_target_pairs={{0,6},{2,0},{4,2},{6,4},{1,7},{3,1},{5,3},{7,5},{8,14},{10,8},{12,... | collective-permute-start | bytes 1572872 | tf_op jit(solution)/shard_map/ppermute | solution.py:1967
  451.6 14.3 %copy-start.4 = (bf16[4,2,32,32,128]{4,3,2,1,0:T(8,128)(2,1)S(1)}, bf16[4,2,32,32,128]{4,3,2,1,0:T(8,128)(2,1)}, u32[]{:S(2)}) copy-start(bf16[4,2,32,32,128]{4,3,2,1,0:T(8,128)(2,1)} %copy-done.3) | copy-start | bytes 6291460
  461.7 15.4 %all-to-all-start.12 = ((bf16[8,32,1280]{2,1,0:T(8,128)(2,1)}), bf16[8,32,1280]{2,1,0:T(8,128)(2,1)}, u32[]{:S(2)}, u32[]{:S(2)}) async-start(bf16[8,32,1280]{2,1,0:T(8,128)(2,1)} %get-tuple-element.233), calls=%async_computation.12 | async-start | bytes 1310720 | tf_op jit(solution)/shard_map/all_to_all | solution.py:1913
  473.5 3.5 copy-start.5
  477.0 73.3 %all-to-all-start.13 = ((bf16[4,64,32,128]{3,2,1,0:T(8,128)(2,1)}), bf16[4,64,32,128]{3,2,1,0:T(8,128)(2,1)S(1)}, u32[]{:S(2)}, u32[]{:S(2)}) async-start(bf16[4,64,32,128]{3,2,1,0:T(8,128)(2,1)} %bitcast.81), calls=%async_computation.13 | async-start | bytes 4194304 | tf_op jit(solution)/shard_map/all_to_all | solution.py:1913
  518.9 35.7 %copy-start.22 = (f32[32,384]{1,0:T(8,128)S(1)}, f32[32,384]{1,0:T(8,128)}, u32[]{:S(2)}) copy-start(f32[32,384]{1,0:T(8,128)} %get-tuple-element.247) | copy-start | bytes 147460
  518.9 35.7 %copy-start.21 = (f32[32,384]{1,0:T(8,128)S(1)}, f32[32,384]{1,0:T(8,128)}, u32[]{:S(2)}) copy-start(f32[32,384]{1,0:T(8,128)} %get-tuple-element.248) | copy-start | bytes 147460
  550.3 24.6 %copy-start = (bf16[4,64,32,128]{3,2,1,0:T(8,128)(2,1)}, bf16[4,64,32,128]{3,2,1,0:T(8,128)(2,1)S(1)}, u32[]{:S(2)}) copy-start(bf16[4,64,32,128]{3,2,1,0:T(8,128)(2,1)S(1)} %all-to-all-done.13) | copy-start | bytes 6291460
  550.3 13.9 %all-to-all-start.14 = ((bf16[8,4,32,256]{3,2,1,0:T(8,128)(2,1)}), bf16[8,4,32,256]{3,2,1,0:T(8,128)(2,1)}, u32[]{:S(2)}, u32[]{:S(2)}) async-start(bf16[8,4,32,256]{3,2,1,0:T(8,128)(2,1)} %get-tuple-element.246), calls=%async_computation.14 | async-start | bytes 1048576 | tf_op jit(solution)/shard_map/all_to_all | solution.py:1913
  575.0 30.2 %all-to-all-start.15 = ((bf16[8,32,32,128]{3,2,1,0:T(8,128)(2,1)}), bf16[8,32,32,128]{3,2,1,0:T(8,128)(2,1)S(1)}, u32[]{:S(2)}, u32[]{:S(2)}) async-start(bf16[8,32,32,128]{3,2,1,0:T(8,128)(2,1)} %get-tuple-element.254), calls=%async_computation.15 | async-start | bytes 4194304 | tf_op jit(solution)/shard_map/all_to_all | solution.py:1913
  578.6 178.6 %reduce-scatter.5.cloned.1.call-start = ((), (), s32[]{:S(2)}) async-start(), calls=%async_computation.31 | async-start | bytes 5271552 | tf_op jit(solution)/shard_map/reduce_scatter | solution.py:2375
  605.2 1.3 copy-start.9
  606.5 35.7 %all-to-all-start.16 = ((bf16[8,32,32,128]{3,2,1,0:T(8,128)(2,1)}), bf16[8,32,32,128]{3,2,1,0:T(8,128)(2,1)S(1)}, u32[]{:S(2)}, u32[]{:S(2)}) async-start(bf16[8,32,32,128]{3,2,1,0:T(8,128)(2,1)} %bitcast.69), calls=%async_computation.16 | async-start | bytes 4194304 | tf_op jit(solution)/shard_map/all_to_all | solution.py:1913
  671.4 21.4 %all-to-all-start.18 = ((bf16[8,16,16,256]{3,2,1,0:T(8,128)(2,1)}), bf16[8,16,16,256]{3,2,1,0:T(8,128)(2,1)S(1)}, u32[]{:S(2)}, u32[]{:S(2)}) async-start(bf16[8,16,16,256]{3,2,1,0:T(8,128)(2,1)} %bitcast.91), calls=%async_computation.18 | async-start | bytes 2097152 | tf_op jit(solution)/shard_map/all_to_all | solution.py:1913
  692.8 20.7 %copy-start.15 = (bf16[8,16,16,256]{3,2,1,0:T(8,128)(2,1)}, bf16[8,16,16,256]{3,2,1,0:T(8,128)(2,1)S(1)}, u32[]{:S(2)}) copy-start(bf16[8,16,16,256]{3,2,1,0:T(8,128)(2,1)S(1)} %all-to-all-done.18.refs_0_) | copy-start | bytes 3145732
  720.9 6.1 copy-start.31
  720.9 6.3 copy-start.23
  720.9 6.3 copy-start.24
  720.9 31.2 %all-to-all-start.20 = ((bf16[8,2,16,16,256]{4,3,2,1,0:T(8,128)(2,1)}), bf16[8,2,16,16,256]{4,3,2,1,0:T(8,128)(2,1)}, u32[]{:S(2)}, u32[]{:S(2)}) async-start(bf16[8,2,16,16,256]{4,3,2,1,0:T(8,128)(2,1)} %get-tuple-element.296), calls=%async_computation.20 | async-start | bytes 4194304 | tf_op jit(solution)/shard_map/all_to_all | solution.py:1913
  752.1 31.4 %all-to-all-start.21 = ((bf16[8,2,16,16,256]{4,3,2,1,0:T(8,128)(2,1)}), bf16[8,2,16,16,256]{4,3,2,1,0:T(8,128)(2,1)}, u32[]{:S(2)}, u32[]{:S(2)}) async-start(bf16[8,2,16,16,256]{4,3,2,1,0:T(8,128)(2,1)} %get-tuple-element.297), calls=%async_computation.21 | async-start | bytes 4194304 | tf_op jit(solution)/shard_map/all_to_all | solution.py:1913
  756.5 65.5 %all-gather.14.cloned.1.call-start = ((), (), s32[]{:S(2)}) async-start(), calls=%async_computation.32 | async-start | bytes 1622016 | tf_op jit(solution)/shard_map/all_gather | solution.py:2361
  783.5 23.9 %all-to-all-start.22 = ((bf16[8,16,16,256]{3,2,1,0:T(8,128)(2,1)}), bf16[8,16,16,256]{3,2,1,0:T(8,128)(2,1)S(1)}, u32[]{:S(2)}, u32[]{:S(2)}) async-start(bf16[8,16,16,256]{3,2,1,0:T(8,128)(2,1)} %bitcast.90), calls=%async_computation.23 | async-start | bytes 2097152 | tf_op jit(solution)/shard_map/all_to_all | solution.py:1913
  807.4 7.0 copy-start.14
  807.4 19.7 %all-to-all-start.23 = ((bf16[8,16,16,256]{3,2,1,0:T(8,128)(2,1)}), bf16[8,16,16,256]{3,2,1,0:T(8,128)(2,1)}, u32[]{:S(2)}, u32[]{:S(2)}) async-start(bf16[8,16,16,256]{3,2,1,0:T(8,128)(2,1)} %bitcast.89), calls=%async_computation.24 | async-start | bytes 2097152 | tf_op jit(solution)/shard_map/all_to_all | solution.py:1913
  834.4 53.9 %all-to-all-start.24 = ((bf16[8,2,16,32,256]{4,3,2,1,0:T(8,128)(2,1)}), bf16[8,2,16,32,256]{4,3,2,1,0:T(8,128)(2,1)}, u32[]{:S(2)}, u32[]{:S(2)}) async-start(bf16[8,2,16,32,256]{4,3,2,1,0:T(8,128)(2,1)} %outgoing_product_back.1), calls=%async_computation.25 | async-start | bytes 8388608 | tf_op jit(solution)/shard_map/all_to_all | solution.py:1913
  839.1 49.1 %reduce-scatter.7.cloned.1.call-start = ((), (), s32[]{:S(2)}) async-start(), calls=%async_computation.36 | async-start | bytes 829440
  888.2 24.9 %all-to-all-start.25 = ((bf16[8,6,24,128]{3,2,1,0:T(8,128)(2,1)}), bf16[8,6,24,128]{3,2,1,0:T(8,128)(2,1)S(1)}, u32[]{:S(2)}, u32[]{:S(2)}) async-start(bf16[8,6,24,128]{3,2,1,0:T(8,128)(2,1)} %pair_gradient.1), calls=%async_computation.26 | async-start | bytes 589824 | tf_op jit(solution)/shard_map/all_to_all | solution.py:1913
  925.2 52.6 %all-to-all-start.27 = ((bf16[4,8,256,128]{3,2,1,0:T(8,128)(2,1)}), bf16[4,8,256,128]{3,2,1,0:T(8,128)(2,1)}, u32[]{:S(2)}, u32[]{:S(2)}) async-start(bf16[4,8,256,128]{3,2,1,0:T(8,128)(2,1)} %bitcast.83), calls=%async_computation.28 | async-start | bytes 4194304 | tf_op jit(solution)/shard_map/all_to_all | solution.py:1913
  929.7 2.0 copy-start.18
  929.7 13.7 %copy-start.19 = (bf16[1,15,24,128]{3,2,1,0:T(8,128)(2,1)S(1)}, bf16[1,15,24,128]{3,2,1,0:T(8,128)(2,1)}, u32[]{:S(2)}) copy-start(bf16[1,15,24,128]{3,2,1,0:T(8,128)(2,1)} %reduce-scatter.7.cloned.1.call-done) | copy-start | bytes 276484
  961.1 20.4 %copy-start.27 = (f32[8,128]{1,0:T(8,128)S(1)}, f32[8,128]{1,0:T(8,128)}, u32[]{:S(2)}) copy-start(f32[8,128]{1,0:T(8,128)} %get-tuple-element.341) | copy-start | bytes 12292
  977.8 27.9 %all-to-all-start.28 = ((bf16[4,8,256,128]{3,2,1,0:T(8,128)(2,1)}), bf16[4,8,256,128]{3,2,1,0:T(8,128)(2,1)S(1)}, u32[]{:S(2)}, u32[]{:S(2)}) async-start(bf16[4,8,256,128]{3,2,1,0:T(8,128)(2,1)} %all-to-all-done.27), calls=%async_computation.29 | async-start | bytes 4194304 | tf_op jit(solution)/shard_map/all_to_all | solution.py:1913
  (3 other events, 2.5 us)
Sparse Core Ops, SparseCore 0:
  22.0 25.2 all-gather.15
  91.1 54.5 all-gather.17
  171.0 63.0 all-gather.19
  602.7 119.1 reduce-scatter.4
  761.0 60.9 all-gather.13
  842.0 33.5 reduce-scatter.6
